TPU v7x, 512 devices: a whole 4x4x16 slice. The times are simulated.
512 devices in a mesh: section: 32 (over x, y, core), tensor: 16 (over z).
Axes of the slice: x: 4, y: 4, z: 16, core: 2. Of those that a mesh axis runs over, the one named last changes fastest.
Arguments:
- section_inputs: bfloat16 [32, 1, 512, 2304], P('section', None, 'tensor'), may hold values from -6 to 6
- later_grad: bfloat16 [32, 1, 512, 2304], P('section', None, 'tensor'), may hold values from -6 to 6
- attn_gain: bfloat16 [32, 2304], P('section'), may hold values from 0.5 to 1.5
- w_query: bfloat16 [32, 2304, 4096], P('section', None, 'tensor'), may hold values from -0.125 to 0.125
- w_key: bfloat16 [32, 2304, 2048], P('section', None, 'tensor'), may hold values from -0.125 to 0.125
- w_value: bfloat16 [32, 2304, 2048], P('section', None, 'tensor'), may hold values from -0.125 to 0.125
- w_out: bfloat16 [32, 4096, 2304], P('section', 'tensor'), may hold values from -0.09375 to 0.09375
- final_gain: bfloat16 [2304], replicated, may hold values from 0.5 to 1.5
- reward_head: bfloat16 [2304], replicated, may hold values from -0.125 to 0.125
- rankings: int32 [1, 8], replicated, may hold values from 0 to 7, each once within a row
- lengths: int32 [1, 8], replicated, may hold values from 1 to 64, as said below
Outputs:
- arrived: bfloat16 [32, 1, 512, 2304], P('section', None, 'tensor')
- sent_back: bfloat16 [32, 1, 512, 2304], P('section', None, 'tensor')
Inputs may be any that keep to these rules, and one draw needn't show every extreme that they name: `rankings`: each row names every response once; entry j is the response ranked j-th best. `lengths`: each list has a response that fills all 64 slots.
All inputs are finite; a program needn't handle non-finite values.
Results may differ from a plain program's by a relative error of at most 0.04.
Values may be sent and summed in bfloat16 or wider, within the bound.
No kernel may reach another device: no remote copies, remote signals or barrier semaphores. Data moves between devices by JAX's collectives and lax.ppermute only.
A program may use at most 64 MiB of HBM per device.

v0:
```python
import jax
import jax.numpy as jnp
from jax import lax
from jax.sharding import PartitionSpec as P

HEAD_DIM = 128
RESP = 8
MICRO = 1


EPSILON = 1e-06
SOFT_CAP = 50.0
QUERY_SCALE = 1.0 / 12.0
LOSS_SCALE = 64.0


def from_behind(value, axis, steps):
    count = lax.axis_size(axis)
    leading, last = (max(0, -steps), min(count, count - steps))
    return lax.ppermute(value, axis, [(source, source + steps) for source in range(leading, last)])


def inv_rms(values):
    return lax.rsqrt(jnp.mean(values * values, axis=-1, keepdims=True) + EPSILON)


def causal_mask(length):
    places = jnp.arange(length)
    return (places[:, None] >= places[None, :]).astype(jnp.float32)


def attend(queries, key_row_block, value_rows, length):
    groups = key_row_block.shape[1] // HEAD_DIM
    q_split = queries.reshape(RESP, length, groups, 2, HEAD_DIM)
    k_split = key_row_block.reshape(RESP, length, groups, HEAD_DIM)
    v_split = value_rows.reshape(RESP, length, groups, HEAD_DIM)
    raw_score = jnp.einsum(
        "rqgjd,rkgd->rgjqk", q_split, k_split, preferred_element_type=jnp.float32
    )
    capped = jnp.tanh(raw_score * (QUERY_SCALE / SOFT_CAP))
    exp_score = jnp.exp(SOFT_CAP * capped) * causal_mask(length)
    attn_prob = exp_score / jnp.sum(exp_score, axis=-1, keepdims=True)
    prob_bf = attn_prob.astype(jnp.bfloat16)
    context = jnp.einsum("rgjqk,rkgd->rqgjd", prob_bf, v_split, preferred_element_type=jnp.float32)
    context = context.reshape(queries.shape[0], -1).astype(jnp.bfloat16)
    return (context, (capped, attn_prob, prob_bf))


def attend_back(grad_ctx, queries, key_row_block, value_rows, attn_state, length):
    capped, attn_prob, prob_bf = attn_state
    groups = key_row_block.shape[1] // HEAD_DIM
    q_split = queries.reshape(RESP, length, groups, 2, HEAD_DIM)
    k_split = key_row_block.reshape(RESP, length, groups, HEAD_DIM)
    v_split = value_rows.reshape(RESP, length, groups, HEAD_DIM)
    context_split = grad_ctx.reshape(RESP, length, groups, 2, HEAD_DIM)
    grad_prob = jnp.einsum(
        "rqgjd,rkgd->rgjqk", context_split, v_split, preferred_element_type=jnp.float32
    )
    grad_score = attn_prob * (grad_prob - jnp.sum(attn_prob * grad_prob, axis=-1, keepdims=True))
    grad_raw = (grad_score * (1.0 - capped * capped) * QUERY_SCALE).astype(jnp.bfloat16)
    total_rows = queries.shape[0]
    grad_query = jnp.einsum(
        "rgjqk,rkgd->rqgjd", grad_raw, k_split, preferred_element_type=jnp.float32
    )
    grad_key = jnp.einsum(
        "rgjqk,rqgjd->rkgd", grad_raw, q_split, preferred_element_type=jnp.float32
    )
    grad_value = jnp.einsum(
        "rgjqk,rqgjd->rkgd", prob_bf, context_split, preferred_element_type=jnp.float32
    )
    return (
        grad_query.reshape(total_rows, -1).astype(jnp.bfloat16),
        grad_key.reshape(total_rows, -1).astype(jnp.bfloat16),
        grad_value.reshape(total_rows, -1).astype(jnp.bfloat16),
    )


def dot_trans(left_mat, right_mat):
    return lax.dot_general(
        left_mat, right_mat, (((1,), (1,)), ((), ())), preferred_element_type=jnp.float32
    )


def rank_grad(reward_scores, rankings):
    slots = jnp.arange(RESP)
    order_hot = (rankings[:, :, None] == slots[None, None, :]).astype(jnp.float32)
    ordered = jnp.einsum("mji,mi->mj", order_hot, reward_scores, precision=lax.Precision.HIGHEST)
    exp_order = jnp.exp(ordered)
    upper = (slots[:, None] >= slots[None, :]).astype(jnp.float32)
    suffix = jnp.dot(exp_order, upper, precision=lax.Precision.HIGHEST)
    cumulative = jnp.dot(1.0 / suffix, upper.T, precision=lax.Precision.HIGHEST)
    grad_order = LOSS_SCALE / MICRO * (exp_order * cumulative - 1.0)
    return jnp.einsum("mji,mj->mi", order_hot, grad_order, precision=lax.Precision.HIGHEST)


def shards(
    section_inputs,
    later_grad,
    attn_gain,
    w_query,
    w_key,
    w_value,
    w_out,
    final_gain,
    reward_head,
    rankings,
    lengths,
):
    inputs = section_inputs[0]
    own_count = inputs.shape[1]
    tensor_count = lax.axis_size("tensor")
    tensor_pos = lax.axis_index("tensor")
    total_rows = own_count * tensor_count
    length = total_rows // RESP
    norm_gain = attn_gain[0].astype(jnp.float32)
    query_w = w_query[0]
    key_w = w_key[0]
    value_w = w_value[0]
    out_w = w_out[0]
    query_cols = query_w.shape[1]
    kv_cols = key_w.shape[1]
    micro_idx = 0
    x_own = inputs[micro_idx]
    x_float = lax.all_gather(x_own, "tensor", axis=0, tiled=True).astype(jnp.float32)
    normed = (x_float * inv_rms(x_float) * norm_gain).astype(jnp.bfloat16)
    projected = jnp.concatenate(
        [
            jnp.dot(normed, query_w, preferred_element_type=jnp.float32),
            jnp.dot(normed, key_w, preferred_element_type=jnp.float32),
            jnp.dot(normed, value_w, preferred_element_type=jnp.float32),
        ],
        axis=1,
    ).astype(jnp.bfloat16)
    queries = projected[:, :query_cols]
    key_row_block = projected[:, query_cols : query_cols + kv_cols]
    value_rows = projected[:, query_cols + kv_cols :]
    context, attn_state = attend(queries, key_row_block, value_rows, length)
    mixed_all = lax.psum(
        jnp.dot(context, out_w, preferred_element_type=jnp.float32).astype(jnp.bfloat16), "tensor"
    ).astype(jnp.float32)
    mixed_own = lax.dynamic_slice_in_dim(mixed_all, tensor_pos * own_count, own_count, 0)
    hidden_list = [(x_own.astype(jnp.float32) + mixed_own).astype(jnp.bfloat16)]
    kept_state = [(queries, key_row_block, value_rows, attn_state)]
    hidden = jnp.stack(hidden_list)
    arrived = from_behind(hidden, "section", 1)
    hidden_f = hidden.astype(jnp.float32)
    inv_norm = inv_rms(hidden_f)
    head_vec = final_gain.astype(jnp.float32) * reward_head.astype(jnp.float32)
    score_per_row = jnp.sum(hidden_f * inv_norm * head_vec, axis=-1)
    positions = jnp.arange(RESP)[None, :] * length + lengths - 1
    global_rows = tensor_pos * own_count + jnp.arange(own_count)
    selection_onehot = (positions[:, :, None] == global_rows[None, None, :]).astype(jnp.float32)
    local_portion = jnp.einsum(
        "hgn,hn->hg", selection_onehot, score_per_row, precision=lax.Precision.HIGHEST
    )
    reward_scores = lax.psum(local_portion, "tensor")
    gradient_of_scores = rank_grad(reward_scores, rankings)
    gradient_per_row = jnp.einsum(
        "jsc,js->jc", selection_onehot, gradient_of_scores, precision=lax.Precision.HIGHEST
    )
    scaled = gradient_per_row[:, :, None] * head_vec
    last_grad = inv_norm * scaled - hidden_f * inv_norm**3 * jnp.mean(
        scaled * hidden_f, axis=-1, keepdims=True
    )
    last_grad = last_grad.astype(jnp.bfloat16)
    at_end = lax.axis_index("section") == lax.axis_size("section") - 1
    cotangent = jnp.where(at_end, last_grad, later_grad[0])
    micro_idx = 0
    grad_own = cotangent[micro_idx]
    queries, key_row_block, value_rows, attn_state = kept_state[micro_idx]
    grad_ctx = dot_trans(lax.all_gather(grad_own, "tensor", axis=0, tiled=True), out_w).astype(
        jnp.bfloat16
    )
    grad_query, grad_key, grad_value = attend_back(
        grad_ctx, queries, key_row_block, value_rows, attn_state, length
    )
    back_all = lax.psum(
        (
            dot_trans(grad_query, query_w)
            + dot_trans(grad_key, key_w)
            + dot_trans(grad_value, value_w)
        ).astype(jnp.bfloat16),
        "tensor",
    ).astype(jnp.float32)
    back_own = lax.dynamic_slice_in_dim(back_all, tensor_pos * own_count, own_count, 0)
    x_float = inputs[micro_idx].astype(jnp.float32)
    inv_x = inv_rms(x_float)
    scaled_x = back_own * norm_gain
    grad_x = inv_x * scaled_x - x_float * inv_x**3 * jnp.mean(
        scaled_x * x_float, axis=-1, keepdims=True
    )
    returned = [(grad_own.astype(jnp.float32) + grad_x).astype(jnp.bfloat16)]
    sent_back = from_behind(jnp.stack(returned), "section", -1)
    return (arrived[None], sent_back[None])


def solution(mesh):
    return jax.shard_map(
        shards,
        mesh=mesh,
        in_specs=(
            P("section", None, "tensor", None),
            P("section", None, "tensor", None),
            P("section", None),
            P("section", None, "tensor"),
            P("section", None, "tensor"),
            P("section", None, "tensor"),
            P("section", "tensor", None),
            P(),
            P(),
            P(),
            P(),
        ),
        out_specs=(P("section", None, "tensor", None), P("section", None, "tensor", None)),
        check_vma=False,
    )
```

profile of v0, /device:TPU:1, one launch (start us, length us, event | category | flops | bytes accessed | tf_op | source)
XLA Modules:
  0.0 517.1 jit_solution(6171687732435128681)
XLA Ops:
  7.2 0.7 all-gather.6.cloned.1.call-update
  8.0 0.6 fusion.57
  8.6 0.7 convert_reduce_fusion
  9.3 71.2 %all-gather.6.cloned.1.call-done = bf16[1,1,512,2304]{3,2,1,0:T(8,128)(2,1)} async-done(((bf16[1,1,32,2304]{3,2,1,0:T(8,128)(2,1)}), bf16[1,1,512,2304]{3,2,1,0:T(8,128)(2,1)}) %all-gather.6.cloned.1.call-update) | async-done | bytes 2359312 | tf_op jit(solution)/shard_map/all_gather | solution.py:124
  80.5 2.3 fusion
  82.9 2.8 convolution_convert_fusion.4
  85.7 1.7 reshape.332
  87.4 2.0 convolution_convert_fusion.5
  89.5 0.4 fusion.28
  89.9 0.9 convolution_convert_fusion.6
  90.8 0.3 fusion.10
  91.1 0.3 copy.21
  91.5 2.2 convolution_convert_fusion
  93.8 0.5 copy-done.21
  94.4 142.2 %all-reduce.3.cloned.1.call-done = bf16[512,2304]{1,0:T(8,128)(2,1)} async-done(((bf16[512,2304]{1,0:T(8,128)(2,1)}), bf16[512,2304]{1,0:T(8,128)(2,1)}) %all-reduce.3.cloned.1.call-update) | async-done | bytes 2359312 | tf_op jit(solution)/shard_map/psum | solution.py:138
  236.6 1.1 fusion.31
  237.7 0.2 fusion.33
  237.9 0.2 convolution_bitcast_fusion.8
  238.1 21.9 %psum.22 = f32[8]{0:T(128)S(1)} all-reduce(f32[8]{0:T(128)S(1)} %convolution_bitcast_fusion.8), channel_id=1, replica_groups=mesh['section'=32,'tensor'=16] {'tensor'}, use_global_device_ids=true, to_apply=%region_5.0 | all-reduce | flops 8 | bytes 64 | tf_op jit(solution)/shard_map/psum | solution.py:156
  260.0 0.2 fusion.14
  260.3 0.1 fusion.18
  260.4 0.2 convolution_bitcast_fusion.4
  260.6 0.2 convolution_bitcast_fusion.3
  260.8 0.2 fusion.35
  261.1 0.8 fusion.56
  262.0 77.2 %all-gather.4.cloned.1.call-done = bf16[512,2304]{1,0:T(8,128)(2,1)} async-done(((bf16[32,2304]{1,0:T(8,128)(2,1)}), bf16[512,2304]{1,0:T(8,128)(2,1)}) %all-gather.4.cloned.1.call-update) | async-done | bytes 2359312 | tf_op jit(solution)/shard_map/all_gather | solution.py:171
  339.2 2.5 convolution_convert_fusion.2
  341.8 0.3 fusion.13
  342.1 0.5 copy-done.24
  342.6 0.4 multiply_reduce_fusion
  343.0 0.2 fusion.43
  343.3 0.3 copy-done.6
  343.6 0.3 fusion.12
  343.8 0.3 fusion.11
  344.1 0.3 copy.24
  344.4 0.8 fusion.7
  345.2 0.2 copy-done.7
  345.5 0.8 convolution_add_fusion.1
  346.3 0.3 copy-done.9
  346.5 2.2 fusion.3
  348.8 13.1 %collective-permute-start = (bf16[1,32,2304]{2,1,0:T(8,128)(2,1)S(1)}, bf16[1,32,2304]{2,1,0:T(8,128)(2,1)S(1)}, u32[]{:S(2)}, u32[]{:S(2)}) collective-permute-start(bf16[1,32,2304]{2,1,0:T(8,128)(2,1)S(1)} %bitcast.190), channel_id=1, source_target_pairs={{0,16},{16,32},{32,48},{48,64},{64,80},{80,96},{96,112},{112,128},... | collective-permute-start | bytes 442376 | tf_op jit(solution)/shard_map/ppermute | solution.py:20
  361.8 129.7 %all-reduce.5.cloned.1.call-done = bf16[512,2304]{1,0:T(8,128)(2,1)} async-done(((bf16[512,2304]{1,0:T(8,128)(2,1)}), bf16[512,2304]{1,0:T(8,128)(2,1)}) %all-reduce.5.cloned.1.call-update) | async-done | bytes 2359312 | tf_op jit(solution)/shard_map/psum | solution.py:177
  491.5 1.1 fusion.37
  492.6 1.1 fusion.55
  493.7 11.5 %collective-permute-start.1 = (bf16[1,32,2304]{2,1,0:T(8,128)(2,1)S(1)}, bf16[1,32,2304]{2,1,0:T(8,128)(2,1)S(1)}, u32[]{:S(2)}, u32[]{:S(2)}) collective-permute-start(bf16[1,32,2304]{2,1,0:T(8,128)(2,1)S(1)} %fusion.55), channel_id=1, source_target_pairs={{16,0},{32,16},{48,32},{64,48},{80,64},{96,80},{112,96},{128,112},... | collective-permute-start | bytes 442376 | tf_op jit(solution)/shard_map/ppermute | solution.py:20
  505.2 4.0 collective-permute-done.1
  509.2 0.7 copy.59
  509.9 0.7 copy.60
  (62 shorter events, 0.7 us)
Async XLA Ops:
  7.2 84.3 %copy-start = (bf16[1,256,2304]{2,1,0:T(8,128)(2,1)S(1)}, bf16[1,256,2304]{2,1,0:T(8,128)(2,1)}, u32[]{:S(2)}) copy-start(bf16[1,256,2304]{2,1,0:T(8,128)(2,1)} %param.17) | copy-start | bytes 3538948
  7.2 73.3 %all-gather.6.cloned.1.call-start = ((), (), s32[]{:S(2)}) async-start(), calls=%async_computation.3 | async-start | bytes 2506752 | tf_op jit(solution)/shard_map/all_gather | solution.py:124
  7.9 228.7 %all-reduce.3.cloned.1.call-start = ((), (), s32[]{:S(2)}) async-start(), calls=%async_computation | async-start | bytes 4718592 | tf_op jit(solution)/shard_map/psum | solution.py:138
  80.5 2.4 copy-start.1
  87.4 2.0 copy-start.5
  87.4 2.0 copy-start.15
  87.4 2.5 copy-start.8
  89.4 1.4 copy-start.13
  89.9 0.9 copy-start.10
  89.9 0.9 copy-start.17
  90.8 0.7 copy-start.23
  93.7 0.7 copy-start.21
  93.7 0.7 copy-start.19
  93.7 0.7 copy-start.20
  93.7 142.9 %copy-start.2 = (bf16[1,1,32,2304]{3,2,1,0:T(8,128)(2,1)S(1)}, bf16[1,1,32,2304]{3,2,1,0:T(8,128)(2,1)}, u32[]{:S(2)}) copy-start(bf16[1,1,32,2304]{3,2,1,0:T(8,128)(2,1)} %param.11) | copy-start | bytes 442372
  93.7 166.3 %copy-start.22 = (s32[1,8]{1,0:T(1,128)S(1)}, s32[1,8]{1,0:T(1,128)}, u32[]{:S(2)}) copy-start(s32[1,8]{1,0:T(1,128)} %param.20) | copy-start | bytes 100
  93.7 167.4 %copy-start.12 = (bf16[1,1,32,2304]{3,2,1,0:T(8,128)(2,1)S(1)}, bf16[1,1,32,2304]{3,2,1,0:T(8,128)(2,1)}, u32[]{:S(2)}) copy-start(bf16[1,1,32,2304]{3,2,1,0:T(8,128)(2,1)} %param.12) | copy-start | bytes 442372
  93.7 245.5 %all-gather.4.cloned.1.call-start = ((), (), s32[]{:S(2)}) async-start(), calls=%async_computation.1 | async-start | bytes 2506752 | tf_op jit(solution)/shard_map/all_gather | solution.py:171
  261.9 79.9 %copy-start.11 = (f32[8,64,64,2]{2,1,3,0:T(8,128)S(1)}, f32[8,64,64,2]{2,1,3,0:T(8,128)}, u32[]{:S(2)}) copy-start(f32[8,64,64,2]{2,1,3,0:T(8,128)} %copy-done.10) | copy-start | bytes 786436
  261.9 79.9 %copy-start.16 = (f32[64,64]{0,1:T(8,128)S(1)}, f32[64,64]{0,1:T(8,128)}, u32[]{:S(2)}) copy-start(f32[64,64]{0,1:T(8,128)} %fusion.57) | copy-start | bytes 49156
  261.9 79.9 %copy-start.18 = (f32[8,2,64]{2,1,0:T(2,128)S(1)}, f32[8,2,64]{2,1,0:T(2,128)}, u32[]{:S(2)}) copy-start(f32[8,2,64]{2,1,0:T(2,128)} %copy-done.17) | copy-start | bytes 12292
  262.0 229.6 %all-reduce.5.cloned.1.call-start = ((), (), s32[]{:S(2)}) async-start(), calls=%async_computation.2 | async-start | bytes 4718592 | tf_op jit(solution)/shard_map/psum | solution.py:177
  341.7 0.9 copy-start.24
  342.6 0.9 copy-start.6
  342.6 1.2 copy-start.14
  342.6 1.8 copy-start.4
  344.4 1.1 copy-start.7
  345.5 1.1 copy-start.9
  348.7 143.9 %copy-start.3 = (bf16[32,2304]{1,0:T(8,128)(2,1)S(1)}, bf16[32,2304]{1,0:T(8,128)(2,1)}, u32[]{:S(2)}) copy-start(bf16[32,2304]{1,0:T(8,128)(2,1)} %fusion.56) | copy-start | bytes 442372
  348.8 156.5 %collective-permute-start = (bf16[1,32,2304]{2,1,0:T(8,128)(2,1)S(1)}, bf16[1,32,2304]{2,1,0:T(8,128)(2,1)S(1)}, u32[]{:S(2)}, u32[]{:S(2)}) collective-permute-start(bf16[1,32,2304]{2,1,0:T(8,128)(2,1)S(1)} %bitcast.190), channel_id=1, source_target_pairs={{0,16},{16,32},{32,48},{48,64},{64,80},{80,96},{96,112},{112,128},... | collective-permute-start | bytes 442376 | tf_op jit(solution)/shard_map/ppermute | solution.py:20
  493.7 15.5 %collective-permute-start.1 = (bf16[1,32,2304]{2,1,0:T(8,128)(2,1)S(1)}, bf16[1,32,2304]{2,1,0:T(8,128)(2,1)S(1)}, u32[]{:S(2)}, u32[]{:S(2)}) collective-permute-start(bf16[1,32,2304]{2,1,0:T(8,128)(2,1)S(1)} %fusion.55), channel_id=1, source_target_pairs={{16,0},{32,16},{48,32},{64,48},{80,64},{96,80},{112,96},{128,112},... | collective-permute-start | bytes 442376 | tf_op jit(solution)/shard_map/ppermute | solution.py:20
Sparse Core Ops, SparseCore 0:
  10.1 70.3 all-gather.5
  93.8 142.7 all-reduce.2
  262.1 77.1 all-gather.3
  348.9 142.5 all-reduce.4
where the time goes:
time: 518 us; the launch traced here: 517 us
  waiting for transfers between devices  425 us (82%)
  starting transfers between devices  24.7 us (5%)
  blocking collectives  21.9 us (4%)
  matrix products  17.1 us (3%)
  between operations  14.1 us (3%)
  other arithmetic  8.48 us (2%)
  local copies, waits for them, and re-layouts  5.75 us (1%)
    psum x1, waiting for transfers between devices, shards(): lax.psum(jnp.dot(context, out_w, preferred_element_type=jnp.float32).asty...  142 us
    psum x1, waiting for transfers between devices, shards(): lax.psum((dot_trans(grad_query, query_w) + dot_trans(grad_key, key_w) + d...  130 us
    all_gather x1, waiting for transfers between devices, shards(): lax.all_gather(grad_own, 'tensor', axis=0, tiled=True)  77.2 us
    all_gather x1, waiting for transfers between devices, shards(): lax.all_gather(x_own, 'tensor', axis=0, tiled=True).astype(jnp.float32)  71.2 us
    ppermute x2, starting transfers between devices, from_behind(): lax.ppermute(value, axis, [(source, source + steps) for source in range(l...  24.6 us
    psum x1, blocking collectives, shards(): reward_scores = lax.psum(local_portion, 'tensor')  21.9 us
  transfers between devices with their start and end apart: 6, of which 5 were waited for; matrix products, arithmetic and copies ran while one was open for 1% of the time, Pallas kernels for 0%

commit v1 on v0

v1 whole, which is shorter than its diff:
```python
import functools

import jax
import jax.numpy as jnp
from jax import lax
from jax.experimental import pallas as pl
from jax.experimental.pallas import tpu as pltpu
from jax.sharding import PartitionSpec as P

HEAD_DIM = 128
RESP = 8

EPSILON = 1e-06
SOFT_CAP = 50.0
QUERY_SCALE = 1.0 / 12.0
LOSS_SCALE = 64.0

F32 = jnp.float32
BF16 = jnp.bfloat16
VMEM_LIMIT = 48 * 1024 * 1024


def shift(value, steps):
    count = lax.axis_size("tensor")
    return lax.ppermute(value, "tensor", [(i, (i + steps) % count) for i in range(count)])


def from_behind(value, steps):
    count = lax.axis_size("section")
    leading, last = (max(0, -steps), min(count, count - steps))
    return lax.ppermute(value, "section", [(i, i + steps) for i in range(leading, last)])


def dot(left, right):
    return lax.dot_general(left, right, (((1,), (0,)), ((), ())), preferred_element_type=F32)


def dot_nt(left, right):
    return lax.dot_general(left, right, (((1,), (1,)), ((), ())), preferred_element_type=F32)


def dot_tn(left, right):
    return lax.dot_general(left, right, (((0,), (0,)), ((), ())), preferred_element_type=F32)


def inv_rms(values):
    return lax.rsqrt(jnp.mean(values * values, axis=-1, keepdims=True) + EPSILON)


def pair_mask(block, length):
    row = lax.broadcasted_iota(jnp.int32, (block, block), 0)
    col = lax.broadcasted_iota(jnp.int32, (block, block), 1)
    return ((row // length == col // length) & (col <= row)).astype(F32)


def row_picks(positions, rows):
    return (positions == lax.broadcasted_iota(jnp.int32, (RESP, rows), 1)).astype(BF16)


def attention(query, keys, mask):
    capped = jnp.tanh(dot_nt(query, keys) * (QUERY_SCALE / SOFT_CAP))
    exp_score = jnp.exp(SOFT_CAP * capped) * mask
    prob = exp_score / jnp.sum(exp_score, axis=-1, keepdims=True)
    return capped, prob


def forward_kernel(
    offsets, length, me_ref, positions_ref, gain_ref, wq_ref, wk_ref, wv_ref, wo_ref, *refs
):
    count = len(offsets)
    chunks = refs[:count]
    qkv_ref, mixed_ref, rows_x_ref, rows_m_ref, x_all, normed, context = refs[count:]
    own, feats = chunks[0].shape
    rows = own * count
    gain = gain_ref[...].astype(F32)
    for offset, chunk in zip(offsets, chunks):
        place = pl.multiple_of(lax.rem(me_ref[0] + (offset + count), count) * own, own)
        x = chunk[...]
        x_float = x.astype(F32)
        x_all[pl.ds(place, own), :] = x
        normed[pl.ds(place, own), :] = (x_float * inv_rms(x_float) * gain).astype(BF16)
    q_cols, kv_cols = wq_ref.shape[1], wk_ref.shape[1]
    qkv_ref[:, :q_cols] = dot(normed[...], wq_ref[...]).astype(BF16)
    qkv_ref[:, q_cols : q_cols + kv_cols] = dot(normed[...], wk_ref[...]).astype(BF16)
    qkv_ref[:, q_cols + kv_cols :] = dot(normed[...], wv_ref[...]).astype(BF16)
    block = 2 * length
    mask = pair_mask(block, length)
    for start in range(0, rows, block):
        span = slice(start, start + block)
        keys = qkv_ref[span, q_cols : q_cols + kv_cols]
        values = qkv_ref[span, q_cols + kv_cols :]
        for col in range(0, q_cols, HEAD_DIM):
            _, prob = attention(qkv_ref[span, col : col + HEAD_DIM], keys, mask)
            context[span, col : col + HEAD_DIM] = dot(prob.astype(BF16), values).astype(BF16)
    tile = 256

    @pl.loop(0, feats // tile)
    def _(i):
        cols = pl.ds(pl.multiple_of(i * tile, tile), tile)
        mixed_ref[:, cols] = dot(context[...], wo_ref[:, cols]).astype(BF16)

    picks = row_picks(positions_ref[...], rows)
    rows_x_ref[...] = dot(picks, x_all[...])
    rows_m_ref[...] = dot(dot(picks, context[...]).astype(BF16), wo_ref[...])


def forward_part(me, positions, gain, weights, chunks, offsets, length):
    own, feats = chunks[0].shape
    rows = own * len(chunks)
    vmem = pl.BlockSpec(memory_space=pltpu.VMEM)
    smem = pl.BlockSpec(memory_space=pltpu.SMEM)
    cols = sum(w.shape[1] for w in weights[:3])
    return pl.pallas_call(
        functools.partial(forward_kernel, offsets, length),
        out_shape=(
            jax.ShapeDtypeStruct((rows, cols), BF16),
            jax.ShapeDtypeStruct((rows, feats), BF16),
            jax.ShapeDtypeStruct((RESP, feats), F32),
            jax.ShapeDtypeStruct((RESP, feats), F32),
        ),
        in_specs=[smem] + [vmem] * (6 + len(chunks)),
        out_specs=[vmem] * 4,
        scratch_shapes=[
            pltpu.VMEM((rows, feats), BF16),
            pltpu.VMEM((rows, feats), BF16),
            pltpu.VMEM((rows, weights[0].shape[1]), BF16),
        ],
        compiler_params=pltpu.CompilerParams(vmem_limit_bytes=VMEM_LIMIT),
        name="layer_forward",
    )(me, positions, gain, *weights, *chunks)


def backward_kernel(
    offsets,
    length,
    me_ref,
    positions_ref,
    row_grads_ref,
    cot_ref,
    qkv_ref,
    wq_ref,
    wk_ref,
    wv_ref,
    wo_ref,
    *refs,
):
    count = len(offsets)
    outs = refs[:count]
    grads, turned = refs[count:]
    own, feats = outs[0].shape
    rows = own * count
    q_cols, kv_cols = wq_ref.shape[1], wk_ref.shape[1]
    picks = row_picks(positions_ref[...], rows)
    gathered_ctx = dot_nt(cot_ref[...], wo_ref[...]).astype(BF16)
    few = dot_nt(row_grads_ref[...].astype(BF16), wo_ref[...]).astype(BF16)
    placed_ctx = dot_tn(picks, few).astype(BF16)
    grad_ctx = jnp.where(me_ref[1] == 1, placed_ctx, gathered_ctx)
    block = 2 * length
    mask = pair_mask(block, length)
    for start in range(0, rows, block):
        span = slice(start, start + block)
        keys = qkv_ref[span, q_cols : q_cols + kv_cols]
        values = qkv_ref[span, q_cols + kv_cols :]
        grad_key = jnp.zeros((block, kv_cols), F32)
        grad_value = jnp.zeros((block, kv_cols), F32)
        for col in range(0, q_cols, HEAD_DIM):
            query = qkv_ref[span, col : col + HEAD_DIM]
            ctx = grad_ctx[span, col : col + HEAD_DIM]
            capped, prob = attention(query, keys, mask)
            grad_prob = dot_nt(ctx, values)
            grad_score = prob * (grad_prob - jnp.sum(prob * grad_prob, axis=-1, keepdims=True))
            grad_raw = (grad_score * (1.0 - capped * capped) * QUERY_SCALE).astype(BF16)
            grads[span, col : col + HEAD_DIM] = dot(grad_raw, keys).astype(BF16)
            grad_key += dot_tn(grad_raw, query)
            grad_value += dot_tn(prob.astype(BF16), ctx)
        grads[span, q_cols : q_cols + kv_cols] = grad_key.astype(BF16)
        grads[span, q_cols + kv_cols :] = grad_value.astype(BF16)
    for i, offset in enumerate(offsets):
        place = pl.multiple_of(lax.rem(me_ref[0] + (offset + count), count) * own, own)
        turned[i * own : (i + 1) * own, :] = grads[pl.ds(place, own), :]
    tile = 256

    @pl.loop(0, feats // tile)
    def _(i):
        cols = pl.ds(pl.multiple_of(i * tile, tile), tile)
        back = (
            dot_nt(turned[:, :q_cols], wq_ref[cols, :])
            + dot_nt(turned[:, q_cols : q_cols + kv_cols], wk_ref[cols, :])
            + dot_nt(turned[:, q_cols + kv_cols :], wv_ref[cols, :])
        ).astype(BF16)
        for j, out in enumerate(outs):
            out[:, cols] = back[j * own : (j + 1) * own, :]


def backward_part(me, positions, row_grads, cotangent, qkv, weights, offsets, length):
    rows, feats = cotangent.shape
    own = rows // len(offsets)
    vmem = pl.BlockSpec(memory_space=pltpu.VMEM)
    smem = pl.BlockSpec(memory_space=pltpu.SMEM)
    return pl.pallas_call(
        functools.partial(backward_kernel, offsets, length),
        out_shape=[jax.ShapeDtypeStruct((own, feats), BF16)] * len(offsets),
        in_specs=[smem] + [vmem] * 8,
        out_specs=[vmem] * len(offsets),
        scratch_shapes=[pltpu.VMEM(qkv.shape, BF16), pltpu.VMEM(qkv.shape, BF16)],
        compiler_params=pltpu.CompilerParams(vmem_limit_bytes=VMEM_LIMIT),
        name="layer_backward",
    )(me, positions, row_grads, cotangent, qkv, *weights)


def rank_grad(reward_scores, rankings):
    slots = jnp.arange(RESP)
    order_hot = (rankings[0][:, None] == slots[None, :]).astype(F32)
    ordered = jnp.sum(order_hot * reward_scores[None, :], axis=1)
    exp_order = jnp.exp(ordered)
    upper = (slots[:, None] >= slots[None, :]).astype(F32)
    suffix = jnp.sum(exp_order[:, None] * upper, axis=0)
    cumulative = jnp.sum((1.0 / suffix)[None, :] * upper, axis=1)
    grad_order = LOSS_SCALE * (exp_order * cumulative - 1.0)
    return jnp.sum(order_hot * grad_order[:, None], axis=0)


def gather_ring(block):
    count = lax.axis_size("tensor")
    blocks, offsets = [block], [0]
    up = down = block
    for step in range(1, count // 2 + 1):
        up = shift(up, 1)
        blocks.append(up)
        offsets.append(-step)
        if step < count - count // 2:
            down = shift(down, -1)
            blocks.append(down)
            offsets.append(step)
    return blocks, offsets


def scatter_ring(terms):
    count = lax.axis_size("tensor")
    half = count // 2
    up = terms[half]
    down = terms[-(count - half - 1)]
    for step in range(half):
        left = half - step - 1
        up = shift(up, 1)
        if left:
            up = (up.astype(F32) + terms[left].astype(F32)).astype(BF16)
        if left:
            down = shift(down, -1)
            if left > 1:
                down = (down.astype(F32) + terms[1 - left].astype(F32)).astype(BF16)
    return up, down


def sum_rows(value):
    step = 1
    while step < lax.axis_size("tensor"):
        value = value + shift(value, step)
        step *= 2
    return value


def shards(
    section_inputs,
    later_grad,
    attn_gain,
    w_query,
    w_key,
    w_value,
    w_out,
    final_gain,
    reward_head,
    rankings,
    lengths,
):
    x_own = section_inputs[0, 0]
    later_own = later_grad[0, 0]
    own_count = x_own.shape[0]
    tensor_count = lax.axis_size("tensor")
    tensor_pos = lax.axis_index("tensor")
    total_rows = own_count * tensor_count
    length = total_rows // RESP
    weights = (w_query[0], w_key[0], w_value[0], w_out[0])
    at_end = lax.axis_index("section") == lax.axis_size("section") - 1
    positions = jnp.arange(RESP) * length + lengths[0] - 1
    places = positions[:, None].astype(jnp.int32)
    me = jnp.stack([tensor_pos, at_end.astype(jnp.int32)])

    later_all = lax.all_gather(later_own, "tensor", axis=0, tiled=True)
    chunks, offsets = gather_ring(x_own)
    qkv, mixed, rows_x, rows_mixed = forward_part(
        me, places, attn_gain, weights, chunks, offsets, length
    )
    mixed_own = lax.psum_scatter(mixed, "tensor", scatter_dimension=0, tiled=True)

    rows_hidden = (rows_x + sum_rows(rows_mixed)).astype(BF16).astype(F32)
    inv_norm = inv_rms(rows_hidden)
    head_vec = final_gain.astype(F32) * reward_head.astype(F32)
    reward_scores = jnp.sum(rows_hidden * inv_norm * head_vec, axis=-1)
    scaled = rank_grad(reward_scores, rankings)[:, None] * head_vec
    row_grads = inv_norm * scaled - rows_hidden * inv_norm**3 * jnp.mean(
        scaled * rows_hidden, axis=-1, keepdims=True
    )
    row_grads = row_grads.astype(BF16).astype(F32)

    back_offsets = list(range(-(tensor_count - tensor_count // 2 - 1), tensor_count // 2 + 1))
    back = backward_part(
        me, places, row_grads, later_all, qkv, weights, back_offsets, length
    )
    terms = dict(zip(back_offsets, back))
    up, down = scatter_ring(terms)
    back_own = terms[0].astype(F32) + up.astype(F32) + down.astype(F32)

    own_rows = tensor_pos * own_count + jnp.arange(own_count)
    own_picks = (own_rows[:, None] == positions[None, :]).astype(F32)
    last_own = jnp.sum(own_picks[:, :, None] * row_grads[None], axis=1)
    grad_own = jnp.where(at_end, last_own, later_own.astype(F32))
    x_float = x_own.astype(F32)
    inv_x = inv_rms(x_float)
    scaled_x = back_own * attn_gain[0].astype(F32)
    grad_x = inv_x * scaled_x - x_float * inv_x**3 * jnp.mean(
        scaled_x * x_float, axis=-1, keepdims=True
    )
    returned = (grad_own + grad_x).astype(BF16)
    sent_back = from_behind(returned, -1)
    hidden = (x_float + mixed_own.astype(F32)).astype(BF16)
    arrived = from_behind(hidden, 1)
    return (arrived[None, None], sent_back[None, None])


def solution(mesh):
    return jax.shard_map(
        shards,
        mesh=mesh,
        in_specs=(
            P("section", None, "tensor", None),
            P("section", None, "tensor", None),
            P("section", None),
            P("section", None, "tensor"),
            P("section", None, "tensor"),
            P("section", None, "tensor"),
            P("section", "tensor", None),
            P(),
            P(),
            P(),
            P(),
        ),
        out_specs=(P("section", None, "tensor", None), P("section", None, "tensor", None)),
        check_vma=False,
    )
```

time: 518 us -> 281 us (0.54)
  waiting for transfers between devices: 425 us -> 68.2 us
  starting transfers between devices: 24.7 us -> 134 us
  local copies, waits for them, and re-layouts: 5.75 us -> 31.7 us
  blocking collectives: 21.9 us -> 0 us
  Pallas kernels: 0 us -> 20.8 us
  matrix products: 17.1 us -> 0 us
    psum x2 -> x0, waiting for transfers between devices: 272 us -> none  [the longest x1 142 us: shards(): lax.psum(jnp.dot(context, out_w, preferred_element_type=jnp.float32).asty...]
    all_gather x2 -> x1, waiting for transfers between devices: 148 us -> 0.02 us  [shards(): later_all = lax.all_gather(later_own, 'tensor', axis=0, tiled=True)]
    ppermute x2 -> x36, starting transfers between devices: 24.6 us -> 134 us  [the longest x34 118 us: shift(): lax.ppermute(value, 'tensor', [(i, (i + steps) % count) for i in range(co...]
    ppermute x2 -> x36, waiting for transfers between devices: 3.98 us -> 51.2 us  [the longest x34 49.1 us: shift(): lax.ppermute(value, 'tensor', [(i, (i + steps) % count) for i in range(co...]
    unnamed x52 -> x126, local copies, waits for them, and re-layouts: 3.41 us -> 30.9 us
    psum x1 -> x0, blocking collectives: 21.9 us -> none  [shards(): reward_scores = lax.psum(local_portion, 'tensor')]
    pallas_call x0 -> x2, Pallas kernels: none -> 20.8 us  [the longest x1 10.6 us: forward_part(): pl.pallas_call(functools.partial(forward_kernel, offsets, length), out_sh...]
    dot_general x20 -> x0, matrix products: 17.1 us -> none  [the longest x4 6.26 us: dot_trans(): lax.dot_general(left_mat, right_mat, (((1,), (1,)), ((), ())), preferred_...]
  transfers between devices with their start and end apart: 6 -> 38, of which waited for: 5 -> 22; matrix products, arithmetic and copies ran while one was open for 1% -> 2% of each run, Pallas kernels for 0% -> 4%
where the time goes in v1:
time: 281 us; the launch traced here: 276 us
  starting transfers between devices  134 us (48%)
  waiting for transfers between devices  68.2 us (24%)
  local copies, waits for them, and re-layouts  31.7 us (11%)
  Pallas kernels  20.8 us (7%)
  between operations  14.9 us (5%)
  other arithmetic  6.17 us (2%)
    ppermute x34, starting transfers between devices, shift(): lax.ppermute(value, 'tensor', [(i, (i + steps) % count) for i in range(co...  118 us
    ppermute x34, waiting for transfers between devices, shift(): lax.ppermute(value, 'tensor', [(i, (i + steps) % count) for i in range(co...  49.1 us
    unnamed x126, local copies, waits for them, and re-layouts  30.9 us
    reduce_scatter x1, waiting for transfers between devices, shards(): lax.psum_scatter(mixed, 'tensor', scatter_dimension=0, tiled=True)  17 us
    ppermute x2, starting transfers between devices, from_behind(): lax.ppermute(value, 'section', [(i, i + steps) for i in range(leading, la...  15.8 us
    pallas_call x1, Pallas kernels, forward_part(): pl.pallas_call(functools.partial(forward_kernel, offsets, length), out_sh...  10.6 us
    pallas_call x1, Pallas kernels, backward_part(): pl.pallas_call(functools.partial(backward_kernel, offsets, length), out_s...  10.2 us
  transfers between devices with their start and end apart: 38, of which 22 were waited for; matrix products, arithmetic and copies ran while one was open for 2% of the time, Pallas kernels for 4%

profile of v1, /device:TPU:1, one launch (start us, length us, event | category | flops | bytes accessed | tf_op | source)
XLA Modules:
  0.0 276.1 jit_solution(5130571791638450684)
XLA Ops:
  7.2 4.4 %collective-permute-start = (bf16[32,2304]{1,0:T(8,128)(2,1)}, bf16[32,2304]{1,0:T(8,128)(2,1)S(1)}, u32[]{:S(2)}, u32[]{:S(2)}) collective-permute-start(bf16[32,2304]{1,0:T(8,128)(2,1)} %bitcast.27), channel_id=1, source_target_pairs={{0,1},{1,2},{2,3},{3,4},{4,5},{5,6},{6,7},{7,8},{8,9},{9,10},{10,1... | collective-permute-start | bytes 442376 | tf_op jit(solution)/shard_map/ppermute | solution.py:25
  11.7 9.5 %collective-permute-start.1 = (bf16[32,2304]{1,0:T(8,128)(2,1)}, bf16[32,2304]{1,0:T(8,128)(2,1)S(1)}, u32[]{:S(2)}, u32[]{:S(2)}) collective-permute-start(bf16[32,2304]{1,0:T(8,128)(2,1)} %bitcast.28), channel_id=1, source_target_pairs={{0,15},{1,0},{2,1},{3,2},{4,3},{5,4},{6,5},{7,6},{8,7},{9,8},{10,9... | collective-permute-start | bytes 442376 | tf_op jit(solution)/shard_map/ppermute | solution.py:25
  22.9 1.9 collective-permute-start.2
  24.9 4.6 %collective-permute-start.3 = (bf16[32,2304]{1,0:T(8,128)(2,1)S(1)}, bf16[32,2304]{1,0:T(8,128)(2,1)S(1)}, u32[]{:S(2)}, u32[]{:S(2)}) collective-permute-start(bf16[32,2304]{1,0:T(8,128)(2,1)S(1)} %collective-permute-done.1.refs_2_), channel_id=1, source_target_pairs={{0,15},{1,0},{2,1},{3,2},{4,3},{5,4},{6,5},{7,6},{8,7},{9,8},{10,9... | collective-permute-start | bytes 442376 | tf_op jit(solution)/shard_map/ppermute | solution.py:25
  30.0 1.9 collective-permute-start.4
  32.0 4.6 %collective-permute-start.5 = (bf16[32,2304]{1,0:T(8,128)(2,1)S(1)}, bf16[32,2304]{1,0:T(8,128)(2,1)S(1)}, u32[]{:S(2)}, u32[]{:S(2)}) collective-permute-start(bf16[32,2304]{1,0:T(8,128)(2,1)S(1)} %collective-permute-done.3.refs_4_), channel_id=1, source_target_pairs={{0,15},{1,0},{2,1},{3,2},{4,3},{5,4},{6,5},{7,6},{8,7},{9,8},{10,9... | collective-permute-start | bytes 442376 | tf_op jit(solution)/shard_map/ppermute | solution.py:25
  36.5 2.7 collective-permute-done.4.refs_5_
  39.2 1.9 collective-permute-start.6
  41.8 4.6 %collective-permute-start.7 = (bf16[32,2304]{1,0:T(8,128)(2,1)S(1)}, bf16[32,2304]{1,0:T(8,128)(2,1)S(1)}, u32[]{:S(2)}, u32[]{:S(2)}) collective-permute-start(bf16[32,2304]{1,0:T(8,128)(2,1)S(1)} %collective-permute-done.5.refs_6_), channel_id=1, source_target_pairs={{0,15},{1,0},{2,1},{3,2},{4,3},{5,4},{6,5},{7,6},{8,7},{9,8},{10,9... | collective-permute-start | bytes 442376 | tf_op jit(solution)/shard_map/ppermute | solution.py:25
  47.5 2.1 collective-permute-start.8
  50.2 4.6 %collective-permute-start.9 = (bf16[32,2304]{1,0:T(8,128)(2,1)S(1)}, bf16[32,2304]{1,0:T(8,128)(2,1)S(1)}, u32[]{:S(2)}, u32[]{:S(2)}) collective-permute-start(bf16[32,2304]{1,0:T(8,128)(2,1)S(1)} %collective-permute-done.7.refs_8_), channel_id=1, source_target_pairs={{0,15},{1,0},{2,1},{3,2},{4,3},{5,4},{6,5},{7,6},{8,7},{9,8},{10,9... | collective-permute-start | bytes 442376 | tf_op jit(solution)/shard_map/ppermute | solution.py:25
  55.9 1.9 collective-permute-start.10
  58.5 4.8 %collective-permute-start.11 = (bf16[32,2304]{1,0:T(8,128)(2,1)S(1)}, bf16[32,2304]{1,0:T(8,128)(2,1)S(1)}, u32[]{:S(2)}, u32[]{:S(2)}) collective-permute-start(bf16[32,2304]{1,0:T(8,128)(2,1)S(1)} %collective-permute-done.9.refs_10_), channel_id=1, source_target_pairs={{0,15},{1,0},{2,1},{3,2},{4,3},{5,4},{6,5},{7,6},{8,7},{9,8},{10,9... | collective-permute-start | bytes 442376 | tf_op jit(solution)/shard_map/ppermute | solution.py:25
  64.3 1.9 collective-permute-start.12
  67.7 4.6 %collective-permute-start.13 = (bf16[32,2304]{1,0:T(8,128)(2,1)S(1)}, bf16[32,2304]{1,0:T(8,128)(2,1)S(1)}, u32[]{:S(2)}, u32[]{:S(2)}) collective-permute-start(bf16[32,2304]{1,0:T(8,128)(2,1)S(1)} %collective-permute-done.11.refs_12_), channel_id=1, source_target_pairs={{0,15},{1,0},{2,1},{3,2},{4,3},{5,4},{6,5},{7,6},{8,7},{9,8},{10,9... | collective-permute-start | bytes 442376 | tf_op jit(solution)/shard_map/ppermute | solution.py:25
  72.9 1.9 collective-permute-start.14
  76.2 5.5 %collective-permute-done.14.refs_15_ = bf16[32,2304]{1,0:T(8,128)(2,1)S(1)} collective-permute-done((bf16[32,2304]{1,0:T(8,128)(2,1)S(1)}, bf16[32,2304]{1,0:T(8,128)(2,1)S(1)}, u32[]{:S(2)}, u32[]{:S(2)}) %collective-permute-start.14) | collective-permute-done | bytes 147488 | tf_op jit(solution)/shard_map/ppermute | solution.py:25
  97.4 10.6 %layer_forward.1 = (bf16[512,512]{1,0:T(8,128)(2,1)S(1)}, bf16[512,2304]{1,0:T(8,128)(2,1)}, f32[8,2304]{1,0:T(8,128)S(1)}, f32[8,2304]{1,0:T(8,128)S(1)}) custom-call(s32[2]{0:T(128)S(1)} %pad_add_fusion.me_ref, s32[8,1]{1,0:T(8,128)S(1)} %add_add_fusion.positions_ref, bf16[1,2304]{1,0:T(2,128)(2,1)S(1)} %copy-done.51, bf16[2304,256]{1,0:T(8,128)(2,1)S(1)} %bitcast.21, ...), custom_call_target="tpu_custom_call" | custom-call | tf_op jit(solution)/shard_map/layer_forward/pallas_call | solution.py:113
  108.0 1.9 collective-permute-start.16
  109.9 4.4 %collective-permute-done.16 = f32[8,2304]{1,0:T(8,128)S(1)} collective-permute-done((f32[8,2304]{1,0:T(8,128)S(1)}, f32[8,2304]{1,0:T(8,128)S(1)}, u32[]{:S(2)}, u32[]{:S(2)}) %collective-permute-start.16) | collective-permute-done | bytes 73760 | tf_op jit(solution)/shard_map/ppermute | solution.py:25
  114.3 1.9 collective-permute-start.17
  116.3 5.6 %collective-permute-done.17 = f32[8,2304]{1,0:T(8,128)S(1)} collective-permute-done((f32[8,2304]{1,0:T(8,128)S(1)}, f32[8,2304]{1,0:T(8,128)S(1)}, u32[]{:S(2)}, u32[]{:S(2)}) %collective-permute-start.17) | collective-permute-done | bytes 73760 | tf_op jit(solution)/shard_map/ppermute | solution.py:25
  121.9 2.3 collective-permute-start.18
  124.7 8.0 %collective-permute-done.18 = f32[8,2304]{1,0:T(8,128)S(1)} collective-permute-done((f32[8,2304]{1,0:T(8,128)S(1)}, f32[8,2304]{1,0:T(8,128)S(1)}, u32[]{:S(2)}, u32[]{:S(2)}) %collective-permute-start.18) | collective-permute-done | bytes 73760 | tf_op jit(solution)/shard_map/ppermute | solution.py:25
  132.7 8.7 %collective-permute-start.19 = (f32[8,2304]{1,0:T(8,128)S(1)}, f32[8,2304]{1,0:T(8,128)S(1)}, u32[]{:S(2)}, u32[]{:S(2)}) collective-permute-start(f32[8,2304]{1,0:T(8,128)S(1)} %add.137), channel_id=1, source_target_pairs={{0,8},{1,9},{2,10},{3,11},{4,12},{5,13},{6,14},{7,15},{8,0},{9,1},... | collective-permute-start | bytes 221192 | tf_op jit(solution)/shard_map/ppermute | solution.py:25
  142.0 4.7 %collective-permute-done.19 = f32[8,2304]{1,0:T(8,128)S(1)} collective-permute-done((f32[8,2304]{1,0:T(8,128)S(1)}, f32[8,2304]{1,0:T(8,128)S(1)}, u32[]{:S(2)}, u32[]{:S(2)}) %collective-permute-start.19) | collective-permute-done | bytes 73760 | tf_op jit(solution)/shard_map/ppermute | solution.py:25
  148.9 10.2 %layer_backward.1 = (bf16[32,2304]{1,0:T(8,128)(2,1)S(1)}, bf16[32,2304]{1,0:T(8,128)(2,1)S(1)}, bf16[32,2304]{1,0:T(8,128)(2,1)S(1)}, bf16[32,2304]{1,0:T(8,128...) custom-call(s32[2]{0:T(128)S(1)} %pad_add_fusion.me_ref, ...), custom_call_target="tpu_custom_call" | custom-call | tf_op jit(solution)/shard_map/layer_backward/pallas_call | solution.py:200
  166.4 2.1 collective-permute-start.20
  168.6 4.7 %collective-permute-start.28 = (bf16[32,2304]{1,0:T(8,128)(2,1)S(1)}, bf16[32,2304]{1,0:T(8,128)(2,1)S(1)}, u32[]{:S(2)}, u32[]{:S(2)}) collective-permute-start(bf16[32,2304]{1,0:T(8,128)(2,1)S(1)} %copy-done.54), channel_id=1, source_target_pairs={{0,15},{1,0},{2,1},{3,2},{4,3},{5,4},{6,5},{7,6},{8,7},{9,8},{10,9... | collective-permute-start | bytes 442376 | tf_op jit(solution)/shard_map/ppermute | solution.py:25
  173.9 1.9 collective-permute-start.21
  175.9 4.6 %collective-permute-start.29 = (bf16[32,2304]{1,0:T(8,128)(2,1)S(1)}, bf16[32,2304]{1,0:T(8,128)(2,1)S(1)}, u32[]{:S(2)}, u32[]{:S(2)}) collective-permute-start(bf16[32,2304]{1,0:T(8,128)(2,1)S(1)} %add_convert_fusion.5), channel_id=1, source_target_pairs={{0,15},{1,0},{2,1},{3,2},{4,3},{5,4},{6,5},{7,6},{8,7},{9,8},{10,9... | collective-permute-start | bytes 442376 | tf_op jit(solution)/shard_map/ppermute | solution.py:25
  181.0 1.9 collective-permute-start.22
  183.0 4.7 %collective-permute-start.30 = (bf16[32,2304]{1,0:T(8,128)(2,1)S(1)}, bf16[32,2304]{1,0:T(8,128)(2,1)S(1)}, u32[]{:S(2)}, u32[]{:S(2)}) collective-permute-start(bf16[32,2304]{1,0:T(8,128)(2,1)S(1)} %add_convert_fusion.4), channel_id=1, source_target_pairs={{0,15},{1,0},{2,1},{3,2},{4,3},{5,4},{6,5},{7,6},{8,7},{9,8},{10,9... | collective-permute-start | bytes 442376 | tf_op jit(solution)/shard_map/ppermute | solution.py:25
  187.7 1.9 collective-permute-done.22
  189.7 2.1 collective-permute-start.23
  191.8 4.6 %collective-permute-start.31 = (bf16[32,2304]{1,0:T(8,128)(2,1)S(1)}, bf16[32,2304]{1,0:T(8,128)(2,1)S(1)}, u32[]{:S(2)}, u32[]{:S(2)}) collective-permute-start(bf16[32,2304]{1,0:T(8,128)(2,1)S(1)} %add_convert_fusion.3), channel_id=1, source_target_pairs={{0,15},{1,0},{2,1},{3,2},{4,3},{5,4},{6,5},{7,6},{8,7},{9,8},{10,9... | collective-permute-start | bytes 442376 | tf_op jit(solution)/shard_map/ppermute | solution.py:25
  197.8 1.9 collective-permute-start.24
  199.8 4.6 %collective-permute-start.32 = (bf16[32,2304]{1,0:T(8,128)(2,1)S(1)}, bf16[32,2304]{1,0:T(8,128)(2,1)S(1)}, u32[]{:S(2)}, u32[]{:S(2)}) collective-permute-start(bf16[32,2304]{1,0:T(8,128)(2,1)S(1)} %add_convert_fusion.2), channel_id=1, source_target_pairs={{0,15},{1,0},{2,1},{3,2},{4,3},{5,4},{6,5},{7,6},{8,7},{9,8},{10,9... | collective-permute-start | bytes 442376 | tf_op jit(solution)/shard_map/ppermute | solution.py:25
  204.4 2.3 collective-permute-done.24
  206.8 1.9 collective-permute-start.25
  208.8 4.6 %collective-permute-start.33 = (bf16[32,2304]{1,0:T(8,128)(2,1)S(1)}, bf16[32,2304]{1,0:T(8,128)(2,1)S(1)}, u32[]{:S(2)}, u32[]{:S(2)}) collective-permute-start(bf16[32,2304]{1,0:T(8,128)(2,1)S(1)} %add_convert_fusion.1), channel_id=1, source_target_pairs={{0,15},{1,0},{2,1},{3,2},{4,3},{5,4},{6,5},{7,6},{8,7},{9,8},{10,9... | collective-permute-start | bytes 442376 | tf_op jit(solution)/shard_map/ppermute | solution.py:25
  214.3 2.5 collective-permute-start.26
  216.9 4.2 %collective-permute-start.34 = (bf16[32,2304]{1,0:T(8,128)(2,1)S(1)}, bf16[32,2304]{1,0:T(8,128)(2,1)S(1)}, u32[]{:S(2)}, u32[]{:S(2)}) collective-permute-start(bf16[32,2304]{1,0:T(8,128)(2,1)S(1)} %add_convert_fusion), channel_id=1, source_target_pairs={{0,15},{1,0},{2,1},{3,2},{4,3},{5,4},{6,5},{7,6},{8,7},{9,8},{10,9... | collective-permute-start | bytes 442376 | tf_op jit(solution)/shard_map/ppermute | solution.py:25
  222.6 2.4 collective-permute-start.27
  226.1 5.7 %collective-permute-done.27 = bf16[32,2304]{1,0:T(8,128)(2,1)S(1)} collective-permute-done((bf16[32,2304]{1,0:T(8,128)(2,1)S(1)}, bf16[32,2304]{1,0:T(8,128)(2,1)S(1)}, u32[]{:S(2)}, u32[]{:S(2)}) %collective-permute-start.27) | collective-permute-done | bytes 147488 | tf_op jit(solution)/shard_map/ppermute | solution.py:25
  232.0 17.0 %reduce-scatter.2.cloned.1.call-done = bf16[32,2304]{1,0:T(8,128)(2,1)} async-done(((bf16[512,2304]{1,0:T(8,128)(2,1)}), bf16[32,2304]{1,0:T(8,128)(2,1)}) %reduce-scatter.2.cloned.1.call-update) | async-done | bytes 147472 | tf_op jit(solution)/shard_map/reduce_scatter | solution.py:294
  250.1 11.9 %collective-permute-start.35 = (bf16[32,2304]{1,0:T(8,128)(2,1)S(1)}, bf16[32,2304]{1,0:T(8,128)(2,1)S(1)}, u32[]{:S(2)}, u32[]{:S(2)}) collective-permute-start(bf16[32,2304]{1,0:T(8,128)(2,1)S(1)} %get-tuple-element.46), channel_id=1, source_target_pairs={{16,0},{32,16},{48,32},{64,48},{80,64},{96,80},{112,96},{128,112},... | collective-permute-start | bytes 442376 | tf_op jit(solution)/shard_map/ppermute | solution.py:31
  262.0 3.9 %collective-permute-start.15 = (bf16[32,2304]{1,0:T(8,128)(2,1)S(1)}, bf16[32,2304]{1,0:T(8,128)(2,1)S(1)}, u32[]{:S(2)}, u32[]{:S(2)}) collective-permute-start(bf16[32,2304]{1,0:T(8,128)(2,1)S(1)} %get-tuple-element.47), channel_id=1, source_target_pairs={{0,16},{16,32},{32,48},{48,64},{64,80},{80,96},{96,112},{112,128},... | collective-permute-start | bytes 442376 | tf_op jit(solution)/shard_map/ppermute | solution.py:31
  (200 shorter events, 48.5 us)
Async XLA Ops:
  7.2 141.6 %all-gather.3.cloned.1.call-start = ((), (), s32[]{:S(2)}) async-start(), calls=%async_computation.2 | async-start | bytes 2506752 | tf_op jit(solution)/shard_map/all_gather | solution.py:289
  7.2 15.7 %collective-permute-start = (bf16[32,2304]{1,0:T(8,128)(2,1)}, bf16[32,2304]{1,0:T(8,128)(2,1)S(1)}, u32[]{:S(2)}, u32[]{:S(2)}) collective-permute-start(bf16[32,2304]{1,0:T(8,128)(2,1)} %bitcast.27), channel_id=1, source_target_pairs={{0,1},{1,2},{2,3},{3,4},{4,5},{5,6},{6,7},{7,8},{8,9},{9,10},{10,1... | collective-permute-start | bytes 442376 | tf_op jit(solution)/shard_map/ppermute | solution.py:25
  11.6 237.4 %reduce-scatter.2.cloned.1.call-start = ((), (), s32[]{:S(2)}) async-start(), calls=%async_computation.1 | async-start | bytes 2506752 | tf_op jit(solution)/shard_map/reduce_scatter | solution.py:294
  11.7 13.2 %collective-permute-start.1 = (bf16[32,2304]{1,0:T(8,128)(2,1)}, bf16[32,2304]{1,0:T(8,128)(2,1)S(1)}, u32[]{:S(2)}, u32[]{:S(2)}) collective-permute-start(bf16[32,2304]{1,0:T(8,128)(2,1)} %bitcast.28), channel_id=1, source_target_pairs={{0,15},{1,0},{2,1},{3,2},{4,3},{5,4},{6,5},{7,6},{8,7},{9,8},{10,9... | collective-permute-start | bytes 442376 | tf_op jit(solution)/shard_map/ppermute | solution.py:25
  22.9 7.1 %collective-permute-start.2 = (bf16[32,2304]{1,0:T(8,128)(2,1)S(1)}, bf16[32,2304]{1,0:T(8,128)(2,1)S(1)}, u32[]{:S(2)}, u32[]{:S(2)}) collective-permute-start(bf16[32,2304]{1,0:T(8,128)(2,1)S(1)} %collective-permute-done.refs_1_), channel_id=1, source_target_pairs={{0,1},{1,2},{2,3},{3,4},{4,5},{5,6},{6,7},{7,8},{8,9},{9,10},{10,1... | collective-permute-start | bytes 442376 | tf_op jit(solution)/shard_map/ppermute | solution.py:25
  24.9 7.1 %collective-permute-start.3 = (bf16[32,2304]{1,0:T(8,128)(2,1)S(1)}, bf16[32,2304]{1,0:T(8,128)(2,1)S(1)}, u32[]{:S(2)}, u32[]{:S(2)}) collective-permute-start(bf16[32,2304]{1,0:T(8,128)(2,1)S(1)} %collective-permute-done.1.refs_2_), channel_id=1, source_target_pairs={{0,15},{1,0},{2,1},{3,2},{4,3},{5,4},{6,5},{7,6},{8,7},{9,8},{10,9... | collective-permute-start | bytes 442376 | tf_op jit(solution)/shard_map/ppermute | solution.py:25
  30.0 9.2 %collective-permute-start.4 = (bf16[32,2304]{1,0:T(8,128)(2,1)S(1)}, bf16[32,2304]{1,0:T(8,128)(2,1)S(1)}, u32[]{:S(2)}, u32[]{:S(2)}) collective-permute-start(bf16[32,2304]{1,0:T(8,128)(2,1)S(1)} %collective-permute-done.2.refs_3_), channel_id=1, source_target_pairs={{0,1},{1,2},{2,3},{3,4},{4,5},{5,6},{6,7},{7,8},{8,9},{9,10},{10,1... | collective-permute-start | bytes 442376 | tf_op jit(solution)/shard_map/ppermute | solution.py:25
  32.0 9.8 %collective-permute-start.5 = (bf16[32,2304]{1,0:T(8,128)(2,1)S(1)}, bf16[32,2304]{1,0:T(8,128)(2,1)S(1)}, u32[]{:S(2)}, u32[]{:S(2)}) collective-permute-start(bf16[32,2304]{1,0:T(8,128)(2,1)S(1)} %collective-permute-done.3.refs_4_), channel_id=1, source_target_pairs={{0,15},{1,0},{2,1},{3,2},{4,3},{5,4},{6,5},{7,6},{8,7},{9,8},{10,9... | collective-permute-start | bytes 442376 | tf_op jit(solution)/shard_map/ppermute | solution.py:25
  39.2 8.3 %collective-permute-start.6 = (bf16[32,2304]{1,0:T(8,128)(2,1)S(1)}, bf16[32,2304]{1,0:T(8,128)(2,1)S(1)}, u32[]{:S(2)}, u32[]{:S(2)}) collective-permute-start(bf16[32,2304]{1,0:T(8,128)(2,1)S(1)} %collective-permute-done.4.refs_5_), channel_id=1, source_target_pairs={{0,1},{1,2},{2,3},{3,4},{4,5},{5,6},{6,7},{7,8},{8,9},{9,10},{10,1... | collective-permute-start | bytes 442376 | tf_op jit(solution)/shard_map/ppermute | solution.py:25
  41.8 8.4 %collective-permute-start.7 = (bf16[32,2304]{1,0:T(8,128)(2,1)S(1)}, bf16[32,2304]{1,0:T(8,128)(2,1)S(1)}, u32[]{:S(2)}, u32[]{:S(2)}) collective-permute-start(bf16[32,2304]{1,0:T(8,128)(2,1)S(1)} %collective-permute-done.5.refs_6_), channel_id=1, source_target_pairs={{0,15},{1,0},{2,1},{3,2},{4,3},{5,4},{6,5},{7,6},{8,7},{9,8},{10,9... | collective-permute-start | bytes 442376 | tf_op jit(solution)/shard_map/ppermute | solution.py:25
  47.5 8.4 %collective-permute-start.8 = (bf16[32,2304]{1,0:T(8,128)(2,1)S(1)}, bf16[32,2304]{1,0:T(8,128)(2,1)S(1)}, u32[]{:S(2)}, u32[]{:S(2)}) collective-permute-start(bf16[32,2304]{1,0:T(8,128)(2,1)S(1)} %collective-permute-done.6.refs_7_), channel_id=1, source_target_pairs={{0,1},{1,2},{2,3},{3,4},{4,5},{5,6},{6,7},{7,8},{8,9},{9,10},{10,1... | collective-permute-start | bytes 442376 | tf_op jit(solution)/shard_map/ppermute | solution.py:25
  50.2 8.3 %collective-permute-start.9 = (bf16[32,2304]{1,0:T(8,128)(2,1)S(1)}, bf16[32,2304]{1,0:T(8,128)(2,1)S(1)}, u32[]{:S(2)}, u32[]{:S(2)}) collective-permute-start(bf16[32,2304]{1,0:T(8,128)(2,1)S(1)} %collective-permute-done.7.refs_8_), channel_id=1, source_target_pairs={{0,15},{1,0},{2,1},{3,2},{4,3},{5,4},{6,5},{7,6},{8,7},{9,8},{10,9... | collective-permute-start | bytes 442376 | tf_op jit(solution)/shard_map/ppermute | solution.py:25
  55.9 8.5 %collective-permute-start.10 = (bf16[32,2304]{1,0:T(8,128)(2,1)S(1)}, bf16[32,2304]{1,0:T(8,128)(2,1)S(1)}, u32[]{:S(2)}, u32[]{:S(2)}) collective-permute-start(bf16[32,2304]{1,0:T(8,128)(2,1)S(1)} %collective-permute-done.8.refs_9_), channel_id=1, source_target_pairs={{0,1},{1,2},{2,3},{3,4},{4,5},{5,6},{6,7},{7,8},{8,9},{9,10},{10,1... | collective-permute-start | bytes 442376 | tf_op jit(solution)/shard_map/ppermute | solution.py:25
  58.5 9.2 %collective-permute-start.11 = (bf16[32,2304]{1,0:T(8,128)(2,1)S(1)}, bf16[32,2304]{1,0:T(8,128)(2,1)S(1)}, u32[]{:S(2)}, u32[]{:S(2)}) collective-permute-start(bf16[32,2304]{1,0:T(8,128)(2,1)S(1)} %collective-permute-done.9.refs_10_), channel_id=1, source_target_pairs={{0,15},{1,0},{2,1},{3,2},{4,3},{5,4},{6,5},{7,6},{8,7},{9,8},{10,9... | collective-permute-start | bytes 442376 | tf_op jit(solution)/shard_map/ppermute | solution.py:25
  64.3 8.5 %collective-permute-start.12 = (bf16[32,2304]{1,0:T(8,128)(2,1)S(1)}, bf16[32,2304]{1,0:T(8,128)(2,1)S(1)}, u32[]{:S(2)}, u32[]{:S(2)}) collective-permute-start(bf16[32,2304]{1,0:T(8,128)(2,1)S(1)} %collective-permute-done.10.refs_11_), channel_id=1, source_target_pairs={{0,1},{1,2},{2,3},{3,4},{4,5},{5,6},{6,7},{7,8},{8,9},{9,10},{10,1... | collective-permute-start | bytes 442376 | tf_op jit(solution)/shard_map/ppermute | solution.py:25
  67.7 7.9 %collective-permute-start.13 = (bf16[32,2304]{1,0:T(8,128)(2,1)S(1)}, bf16[32,2304]{1,0:T(8,128)(2,1)S(1)}, u32[]{:S(2)}, u32[]{:S(2)}) collective-permute-start(bf16[32,2304]{1,0:T(8,128)(2,1)S(1)} %collective-permute-done.11.refs_12_), channel_id=1, source_target_pairs={{0,15},{1,0},{2,1},{3,2},{4,3},{5,4},{6,5},{7,6},{8,7},{9,8},{10,9... | collective-permute-start | bytes 442376 | tf_op jit(solution)/shard_map/ppermute | solution.py:25
  72.9 8.8 %collective-permute-start.14 = (bf16[32,2304]{1,0:T(8,128)(2,1)S(1)}, bf16[32,2304]{1,0:T(8,128)(2,1)S(1)}, u32[]{:S(2)}, u32[]{:S(2)}) collective-permute-start(bf16[32,2304]{1,0:T(8,128)(2,1)S(1)} %collective-permute-done.12.refs_13_), channel_id=1, source_target_pairs={{0,1},{1,2},{2,3},{3,4},{4,5},{5,6},{6,7},{7,8},{8,9},{9,10},{10,1... | collective-permute-start | bytes 442376 | tf_op jit(solution)/shard_map/ppermute | solution.py:25
  97.4 50.6 %copy-start.61 = (s32[1,8]{1,0:T(1,128)S(1)}, s32[1,8]{1,0:T(1,128)}, u32[]{:S(2)}) copy-start(s32[1,8]{1,0:T(1,128)} %param.20) | copy-start | bytes 100
  97.4 51.5 %copy-start.1 = (bf16[1,2304,256]{2,1,0:T(8,128)(2,1)S(1)}, bf16[1,2304,256]{2,1,0:T(8,128)(2,1)}, u32[]{:S(2)}) copy-start(bf16[1,2304,256]{2,1,0:T(8,128)(2,1)} %param.14) | copy-start | bytes 3538948
  97.4 51.5 %copy-start.3 = (bf16[1,2304,128]{2,1,0:T(8,128)(2,1)S(1)}, bf16[1,2304,128]{2,1,0:T(8,128)(2,1)}, u32[]{:S(2)}) copy-start(bf16[1,2304,128]{2,1,0:T(8,128)(2,1)} %param.15) | copy-start | bytes 1769476
  97.4 51.5 %copy-start.5 = (bf16[1,2304,128]{2,1,0:T(8,128)(2,1)S(1)}, bf16[1,2304,128]{2,1,0:T(8,128)(2,1)}, u32[]{:S(2)}) copy-start(bf16[1,2304,128]{2,1,0:T(8,128)(2,1)} %param.16) | copy-start | bytes 1769476
  108.0 6.3 %collective-permute-start.16 = (f32[8,2304]{1,0:T(8,128)S(1)}, f32[8,2304]{1,0:T(8,128)S(1)}, u32[]{:S(2)}, u32[]{:S(2)}) collective-permute-start(f32[8,2304]{1,0:T(8,128)S(1)} %get-tuple-element.24), channel_id=1, source_target_pairs={{0,1},{1,2},{2,3},{3,4},{4,5},{5,6},{6,7},{7,8},{8,9},{9,10},{10,1... | collective-permute-start | bytes 221192 | tf_op jit(solution)/shard_map/ppermute | solution.py:25
  114.3 7.5 %collective-permute-start.17 = (f32[8,2304]{1,0:T(8,128)S(1)}, f32[8,2304]{1,0:T(8,128)S(1)}, u32[]{:S(2)}, u32[]{:S(2)}) collective-permute-start(f32[8,2304]{1,0:T(8,128)S(1)} %add.135), channel_id=1, source_target_pairs={{0,2},{1,3},{2,4},{3,5},{4,6},{5,7},{6,8},{7,9},{8,10},{9,11},{10,... | collective-permute-start | bytes 221192 | tf_op jit(solution)/shard_map/ppermute | solution.py:25
  121.9 10.8 %collective-permute-start.18 = (f32[8,2304]{1,0:T(8,128)S(1)}, f32[8,2304]{1,0:T(8,128)S(1)}, u32[]{:S(2)}, u32[]{:S(2)}) collective-permute-start(f32[8,2304]{1,0:T(8,128)S(1)} %add.136), channel_id=1, source_target_pairs={{0,4},{1,5},{2,6},{3,7},{4,8},{5,9},{6,10},{7,11},{8,12},{9,13},{1... | collective-permute-start | bytes 221192 | tf_op jit(solution)/shard_map/ppermute | solution.py:25
  132.7 14.0 %collective-permute-start.19 = (f32[8,2304]{1,0:T(8,128)S(1)}, f32[8,2304]{1,0:T(8,128)S(1)}, u32[]{:S(2)}, u32[]{:S(2)}) collective-permute-start(f32[8,2304]{1,0:T(8,128)S(1)} %add.137), channel_id=1, source_target_pairs={{0,8},{1,9},{2,10},{3,11},{4,12},{5,13},{6,14},{7,15},{8,0},{9,1},... | collective-permute-start | bytes 221192 | tf_op jit(solution)/shard_map/ppermute | solution.py:25
  166.4 7.4 %collective-permute-start.20 = (bf16[32,2304]{1,0:T(8,128)(2,1)}, bf16[32,2304]{1,0:T(8,128)(2,1)S(1)}, u32[]{:S(2)}, u32[]{:S(2)}) collective-permute-start(bf16[32,2304]{1,0:T(8,128)(2,1)} %get-tuple-element.27), channel_id=1, source_target_pairs={{0,1},{1,2},{2,3},{3,4},{4,5},{5,6},{6,7},{7,8},{8,9},{9,10},{10,1... | collective-permute-start | bytes 442376 | tf_op jit(solution)/shard_map/ppermute | solution.py:25
  168.5 31.3 %copy-start.35 = (bf16[32,2304]{1,0:T(8,128)(2,1)S(1)}, bf16[32,2304]{1,0:T(8,128)(2,1)}, u32[]{:S(2)}) copy-start(bf16[32,2304]{1,0:T(8,128)(2,1)} %copy-done.34) | copy-start | bytes 442372
  168.6 38.2 %copy-start.33 = (bf16[32,2304]{1,0:T(8,128)(2,1)S(1)}, bf16[32,2304]{1,0:T(8,128)(2,1)}, u32[]{:S(2)}) copy-start(bf16[32,2304]{1,0:T(8,128)(2,1)} %copy-done.32) | copy-start | bytes 442372
  168.6 40.1 %copy-start.31 = (bf16[32,2304]{1,0:T(8,128)(2,1)S(1)}, bf16[32,2304]{1,0:T(8,128)(2,1)}, u32[]{:S(2)}) copy-start(bf16[32,2304]{1,0:T(8,128)(2,1)} %copy-done.30) | copy-start | bytes 442372
  168.6 7.2 %collective-permute-start.28 = (bf16[32,2304]{1,0:T(8,128)(2,1)S(1)}, bf16[32,2304]{1,0:T(8,128)(2,1)S(1)}, u32[]{:S(2)}, u32[]{:S(2)}) collective-permute-start(bf16[32,2304]{1,0:T(8,128)(2,1)S(1)} %copy-done.54), channel_id=1, source_target_pairs={{0,15},{1,0},{2,1},{3,2},{4,3},{5,4},{6,5},{7,6},{8,7},{9,8},{10,9... | collective-permute-start | bytes 442376 | tf_op jit(solution)/shard_map/ppermute | solution.py:25
  173.9 7.1 %collective-permute-start.21 = (bf16[32,2304]{1,0:T(8,128)(2,1)S(1)}, bf16[32,2304]{1,0:T(8,128)(2,1)S(1)}, u32[]{:S(2)}, u32[]{:S(2)}) collective-permute-start(bf16[32,2304]{1,0:T(8,128)(2,1)S(1)} %add_convert_fusion.12), channel_id=1, source_target_pairs={{0,1},{1,2},{2,3},{3,4},{4,5},{5,6},{6,7},{7,8},{8,9},{9,10},{10,1... | collective-permute-start | bytes 442376 | tf_op jit(solution)/shard_map/ppermute | solution.py:25
  175.9 7.1 %collective-permute-start.29 = (bf16[32,2304]{1,0:T(8,128)(2,1)S(1)}, bf16[32,2304]{1,0:T(8,128)(2,1)S(1)}, u32[]{:S(2)}, u32[]{:S(2)}) collective-permute-start(bf16[32,2304]{1,0:T(8,128)(2,1)S(1)} %add_convert_fusion.5), channel_id=1, source_target_pairs={{0,15},{1,0},{2,1},{3,2},{4,3},{5,4},{6,5},{7,6},{8,7},{9,8},{10,9... | collective-permute-start | bytes 442376 | tf_op jit(solution)/shard_map/ppermute | solution.py:25
  181.0 44.0 %copy-start.52 = (bf16[1,2304]{1,0:T(2,128)(2,1)S(1)}, bf16[1,2304]{1,0:T(2,128)(2,1)}, u32[]{:S(2)}) copy-start(bf16[1,2304]{1,0:T(2,128)(2,1)} %gain_ref.1) | copy-start | bytes 13828
  181.0 8.7 %collective-permute-start.22 = (bf16[32,2304]{1,0:T(8,128)(2,1)S(1)}, bf16[32,2304]{1,0:T(8,128)(2,1)S(1)}, u32[]{:S(2)}, u32[]{:S(2)}) collective-permute-start(bf16[32,2304]{1,0:T(8,128)(2,1)S(1)} %add_convert_fusion.11), channel_id=1, source_target_pairs={{0,1},{1,2},{2,3},{3,4},{4,5},{5,6},{6,7},{7,8},{8,9},{9,10},{10,1... | collective-permute-start | bytes 442376 | tf_op jit(solution)/shard_map/ppermute | solution.py:25
  182.9 48.8 %copy-start.7 = (bf16[1,1,32,2304]{3,2,1,0:T(8,128)(2,1)S(1)}, bf16[1,1,32,2304]{3,2,1,0:T(8,128)(2,1)}, u32[]{:S(2)}) copy-start(bf16[1,1,32,2304]{3,2,1,0:T(8,128)(2,1)} %param.11) | copy-start | bytes 442372
  183.0 8.8 %collective-permute-start.30 = (bf16[32,2304]{1,0:T(8,128)(2,1)S(1)}, bf16[32,2304]{1,0:T(8,128)(2,1)S(1)}, u32[]{:S(2)}, u32[]{:S(2)}) collective-permute-start(bf16[32,2304]{1,0:T(8,128)(2,1)S(1)} %add_convert_fusion.4), channel_id=1, source_target_pairs={{0,15},{1,0},{2,1},{3,2},{4,3},{5,4},{6,5},{7,6},{8,7},{9,8},{10,9... | collective-permute-start | bytes 442376 | tf_op jit(solution)/shard_map/ppermute | solution.py:25
  189.7 59.3 %copy-start.55 = (bf16[1,1,32,2304]{3,2,1,0:T(8,128)(2,1)S(1)}, bf16[1,1,32,2304]{3,2,1,0:T(8,128)(2,1)}, u32[]{:S(2)}) copy-start(bf16[1,1,32,2304]{3,2,1,0:T(8,128)(2,1)} %param.12) | copy-start | bytes 442372
  189.7 8.1 %collective-permute-start.23 = (bf16[32,2304]{1,0:T(8,128)(2,1)S(1)}, bf16[32,2304]{1,0:T(8,128)(2,1)S(1)}, u32[]{:S(2)}, u32[]{:S(2)}) collective-permute-start(bf16[32,2304]{1,0:T(8,128)(2,1)S(1)} %add_convert_fusion.10), channel_id=1, source_target_pairs={{0,1},{1,2},{2,3},{3,4},{4,5},{5,6},{6,7},{7,8},{8,9},{9,10},{10,1... | collective-permute-start | bytes 442376 | tf_op jit(solution)/shard_map/ppermute | solution.py:25
  191.8 7.9 %collective-permute-start.31 = (bf16[32,2304]{1,0:T(8,128)(2,1)S(1)}, bf16[32,2304]{1,0:T(8,128)(2,1)S(1)}, u32[]{:S(2)}, u32[]{:S(2)}) collective-permute-start(bf16[32,2304]{1,0:T(8,128)(2,1)S(1)} %add_convert_fusion.3), channel_id=1, source_target_pairs={{0,15},{1,0},{2,1},{3,2},{4,3},{5,4},{6,5},{7,6},{8,7},{9,8},{10,9... | collective-permute-start | bytes 442376 | tf_op jit(solution)/shard_map/ppermute | solution.py:25
  197.8 8.9 %collective-permute-start.24 = (bf16[32,2304]{1,0:T(8,128)(2,1)S(1)}, bf16[32,2304]{1,0:T(8,128)(2,1)S(1)}, u32[]{:S(2)}, u32[]{:S(2)}) collective-permute-start(bf16[32,2304]{1,0:T(8,128)(2,1)S(1)} %add_convert_fusion.9), channel_id=1, source_target_pairs={{0,1},{1,2},{2,3},{3,4},{4,5},{5,6},{6,7},{7,8},{8,9},{9,10},{10,1... | collective-permute-start | bytes 442376 | tf_op jit(solution)/shard_map/ppermute | solution.py:25
  199.8 8.9 %collective-permute-start.32 = (bf16[32,2304]{1,0:T(8,128)(2,1)S(1)}, bf16[32,2304]{1,0:T(8,128)(2,1)S(1)}, u32[]{:S(2)}, u32[]{:S(2)}) collective-permute-start(bf16[32,2304]{1,0:T(8,128)(2,1)S(1)} %add_convert_fusion.2), channel_id=1, source_target_pairs={{0,15},{1,0},{2,1},{3,2},{4,3},{5,4},{6,5},{7,6},{8,7},{9,8},{10,9... | collective-permute-start | bytes 442376 | tf_op jit(solution)/shard_map/ppermute | solution.py:25
  206.8 7.5 %collective-permute-start.25 = (bf16[32,2304]{1,0:T(8,128)(2,1)S(1)}, bf16[32,2304]{1,0:T(8,128)(2,1)S(1)}, u32[]{:S(2)}, u32[]{:S(2)}) collective-permute-start(bf16[32,2304]{1,0:T(8,128)(2,1)S(1)} %add_convert_fusion.8), channel_id=1, source_target_pairs={{0,1},{1,2},{2,3},{3,4},{4,5},{5,6},{6,7},{7,8},{8,9},{9,10},{10,1... | collective-permute-start | bytes 442376 | tf_op jit(solution)/shard_map/ppermute | solution.py:25
  208.8 8.1 %collective-permute-start.33 = (bf16[32,2304]{1,0:T(8,128)(2,1)S(1)}, bf16[32,2304]{1,0:T(8,128)(2,1)S(1)}, u32[]{:S(2)}, u32[]{:S(2)}) collective-permute-start(bf16[32,2304]{1,0:T(8,128)(2,1)S(1)} %add_convert_fusion.1), channel_id=1, source_target_pairs={{0,15},{1,0},{2,1},{3,2},{4,3},{5,4},{6,5},{7,6},{8,7},{9,8},{10,9... | collective-permute-start | bytes 442376 | tf_op jit(solution)/shard_map/ppermute | solution.py:25
  214.3 8.2 %collective-permute-start.26 = (bf16[32,2304]{1,0:T(8,128)(2,1)S(1)}, bf16[32,2304]{1,0:T(8,128)(2,1)S(1)}, u32[]{:S(2)}, u32[]{:S(2)}) collective-permute-start(bf16[32,2304]{1,0:T(8,128)(2,1)S(1)} %add_convert_fusion.7), channel_id=1, source_target_pairs={{0,1},{1,2},{2,3},{3,4},{4,5},{5,6},{6,7},{7,8},{8,9},{9,10},{10,1... | collective-permute-start | bytes 442376 | tf_op jit(solution)/shard_map/ppermute | solution.py:25
  216.9 9.2 %collective-permute-start.34 = (bf16[32,2304]{1,0:T(8,128)(2,1)S(1)}, bf16[32,2304]{1,0:T(8,128)(2,1)S(1)}, u32[]{:S(2)}, u32[]{:S(2)}) collective-permute-start(bf16[32,2304]{1,0:T(8,128)(2,1)S(1)} %add_convert_fusion), channel_id=1, source_target_pairs={{0,15},{1,0},{2,1},{3,2},{4,3},{5,4},{6,5},{7,6},{8,7},{9,8},{10,9... | collective-permute-start | bytes 442376 | tf_op jit(solution)/shard_map/ppermute | solution.py:25
  222.6 9.2 %collective-permute-start.27 = (bf16[32,2304]{1,0:T(8,128)(2,1)S(1)}, bf16[32,2304]{1,0:T(8,128)(2,1)S(1)}, u32[]{:S(2)}, u32[]{:S(2)}) collective-permute-start(bf16[32,2304]{1,0:T(8,128)(2,1)S(1)} %add_convert_fusion.6), channel_id=1, source_target_pairs={{0,1},{1,2},{2,3},{3,4},{4,5},{5,6},{6,7},{7,8},{8,9},{9,10},{10,1... | collective-permute-start | bytes 442376 | tf_op jit(solution)/shard_map/ppermute | solution.py:25
  250.1 16.6 %collective-permute-start.35 = (bf16[32,2304]{1,0:T(8,128)(2,1)S(1)}, bf16[32,2304]{1,0:T(8,128)(2,1)S(1)}, u32[]{:S(2)}, u32[]{:S(2)}) collective-permute-start(bf16[32,2304]{1,0:T(8,128)(2,1)S(1)} %get-tuple-element.46), channel_id=1, source_target_pairs={{16,0},{32,16},{48,32},{64,48},{80,64},{96,80},{112,96},{128,112},... | collective-permute-start | bytes 442376 | tf_op jit(solution)/shard_map/ppermute | solution.py:31
  262.0 6.0 %collective-permute-start.15 = (bf16[32,2304]{1,0:T(8,128)(2,1)S(1)}, bf16[32,2304]{1,0:T(8,128)(2,1)S(1)}, u32[]{:S(2)}, u32[]{:S(2)}) collective-permute-start(bf16[32,2304]{1,0:T(8,128)(2,1)S(1)} %get-tuple-element.47), channel_id=1, source_target_pairs={{0,16},{16,32},{32,48},{48,64},{64,80},{80,96},{96,112},{112,128},... | collective-permute-start | bytes 442376 | tf_op jit(solution)/shard_map/ppermute | solution.py:31
  (52 other events, 268.1 us)
Sparse Core Ops, SparseCore 0:
  11.7 72.4 all-gather.2
  168.7 80.3 reduce-scatter.1

commit v2 on v1

--- a/solution.py
+++ b/solution.py
@@ -17,12 +17,14 @@
 
 F32 = jnp.float32
 BF16 = jnp.bfloat16
-VMEM_LIMIT = 48 * 1024 * 1024
-
-
-def shift(value, steps):
+VMEM_LIMIT = 24 * 1024 * 1024
+
+
+def shift(value, steps, sections=None):
     count = lax.axis_size("tensor")
-    return lax.ppermute(value, "tensor", [(i, (i + steps) % count) for i in range(count)])
+    sections = range(lax.axis_size("section")) if sections is None else sections
+    pairs = [(s * count + i, s * count + (i + steps) % count) for s in sections for i in range(count)]
+    return lax.ppermute(value, ("section", "tensor"), pairs)
 
 
 def from_behind(value, steps):
@@ -57,56 +59,63 @@
     return (positions == lax.broadcasted_iota(jnp.int32, (RESP, rows), 1)).astype(BF16)
 
 
-def attention(query, keys, mask):
-    capped = jnp.tanh(dot_nt(query, keys) * (QUERY_SCALE / SOFT_CAP))
-    exp_score = jnp.exp(SOFT_CAP * capped) * mask
-    prob = exp_score / jnp.sum(exp_score, axis=-1, keepdims=True)
-    return capped, prob
+def attention(queries, keys, mask):
+    raw = [dot_nt(q, k) for q, k in zip(queries, keys)]
+    capped = [jnp.tanh(r * (QUERY_SCALE / SOFT_CAP)) for r in raw]
+    exps = [jnp.exp(SOFT_CAP * c) * mask for c in capped]
+    sums = [jnp.sum(e, axis=-1, keepdims=True) for e in exps]
+    return capped, [e / s for e, s in zip(exps, sums)]
 
 
 def forward_kernel(
     offsets, length, me_ref, positions_ref, gain_ref, wq_ref, wk_ref, wv_ref, wo_ref, *refs
 ):
-    count = len(offsets)
-    chunks = refs[:count]
-    qkv_ref, mixed_ref, rows_x_ref, rows_m_ref, x_all, normed, context = refs[count:]
-    own, feats = chunks[0].shape
-    rows = own * count
+    blocks, (qkv_ref, mixed_ref, rows_ref, context) = refs[: len(offsets)], refs[len(offsets) :]
+    count = sum(len(distances) for distances in offsets)
+    rows, feats = mixed_ref.shape
+    own = rows // count
+    chunks = [b.at[i * own : (i + 1) * own] for b, d in zip(blocks, offsets) for i in range(len(d))]
+    offsets = [distance for distances in offsets for distance in distances]
     gain = gain_ref[...].astype(F32)
-    for offset, chunk in zip(offsets, chunks):
-        place = pl.multiple_of(lax.rem(me_ref[0] + (offset + count), count) * own, own)
-        x = chunk[...]
-        x_float = x.astype(F32)
-        x_all[pl.ds(place, own), :] = x
-        normed[pl.ds(place, own), :] = (x_float * inv_rms(x_float) * gain).astype(BF16)
     q_cols, kv_cols = wq_ref.shape[1], wk_ref.shape[1]
-    qkv_ref[:, :q_cols] = dot(normed[...], wq_ref[...]).astype(BF16)
-    qkv_ref[:, q_cols : q_cols + kv_cols] = dot(normed[...], wk_ref[...]).astype(BF16)
-    qkv_ref[:, q_cols + kv_cols :] = dot(normed[...], wv_ref[...]).astype(BF16)
+    w_kv = jnp.concatenate([wk_ref[...], wv_ref[...]], axis=1)
+    batch = 4
+    for first in range(0, count, batch):
+        normed = []
+        for chunk in chunks[first : first + batch]:
+            x_float = chunk[...].astype(F32)
+            normed.append((x_float * inv_rms(x_float) * gain).astype(BF16))
+        normed = jnp.concatenate(normed, axis=0)
+        q_part = dot(normed, wq_ref[...]).astype(BF16)
+        kv_part = dot(normed, w_kv).astype(BF16)
+        for i, offset in enumerate(offsets[first : first + batch]):
+            place = pl.multiple_of(lax.rem(me_ref[0] + (offset + count), count) * own, own)
+            span = slice(i * own, (i + 1) * own)
+            qkv_ref[pl.ds(place, own), :q_cols] = q_part[span]
+            qkv_ref[pl.ds(place, own), q_cols:] = kv_part[span]
     block = 2 * length
     mask = pair_mask(block, length)
-    for start in range(0, rows, block):
-        span = slice(start, start + block)
-        keys = qkv_ref[span, q_cols : q_cols + kv_cols]
-        values = qkv_ref[span, q_cols + kv_cols :]
-        for col in range(0, q_cols, HEAD_DIM):
-            _, prob = attention(qkv_ref[span, col : col + HEAD_DIM], keys, mask)
-            context[span, col : col + HEAD_DIM] = dot(prob.astype(BF16), values).astype(BF16)
-    tile = 256
-
-    @pl.loop(0, feats // tile)
-    def _(i):
-        cols = pl.ds(pl.multiple_of(i * tile, tile), tile)
+    spans = [slice(start, start + block) for start in range(0, rows, block)]
+    heads = range(0, q_cols, HEAD_DIM)
+    queries = [qkv_ref[s, h : h + HEAD_DIM] for s in spans for h in heads]
+    keys = [qkv_ref[s, q_cols : q_cols + kv_cols] for s in spans for h in heads]
+    values = [qkv_ref[s, q_cols + kv_cols :] for s in spans for h in heads]
+    _, probs = attention(queries, keys, mask)
+    mixes = [dot(p.astype(BF16), v).astype(BF16) for p, v in zip(probs, values)]
+    for i, (s, h) in enumerate((s, h) for s in spans for h in heads):
+        context[s, h : h + HEAD_DIM] = mixes[i]
+    for start in range(0, feats, 256):
+        cols = slice(start, start + 256)
         mixed_ref[:, cols] = dot(context[...], wo_ref[:, cols]).astype(BF16)
-
     picks = row_picks(positions_ref[...], rows)
-    rows_x_ref[...] = dot(picks, x_all[...])
-    rows_m_ref[...] = dot(dot(picks, context[...]).astype(BF16), wo_ref[...])
-
-
-def forward_part(me, positions, gain, weights, chunks, offsets, length):
-    own, feats = chunks[0].shape
-    rows = own * len(chunks)
+    own_picks = row_picks(positions_ref[...] - me_ref[0] * own, own)
+    rows_ref[...] = dot(dot(picks, context[...]).astype(BF16), wo_ref[...]) + dot(
+        own_picks, chunks[offsets.index(0)][...]
+    )
+
+
+def forward_part(me, positions, gain, weights, blocks, offsets, length):
+    rows, feats = sum(b.shape[0] for b in blocks), blocks[0].shape[1]
     vmem = pl.BlockSpec(memory_space=pltpu.VMEM)
     smem = pl.BlockSpec(memory_space=pltpu.SMEM)
     cols = sum(w.shape[1] for w in weights[:3])
@@ -116,18 +125,13 @@
             jax.ShapeDtypeStruct((rows, cols), BF16),
             jax.ShapeDtypeStruct((rows, feats), BF16),
             jax.ShapeDtypeStruct((RESP, feats), F32),
-            jax.ShapeDtypeStruct((RESP, feats), F32),
         ),
-        in_specs=[smem] + [vmem] * (6 + len(chunks)),
-        out_specs=[vmem] * 4,
-        scratch_shapes=[
-            pltpu.VMEM((rows, feats), BF16),
-            pltpu.VMEM((rows, feats), BF16),
-            pltpu.VMEM((rows, weights[0].shape[1]), BF16),
-        ],
+        in_specs=[smem] + [vmem] * (6 + len(blocks)),
+        out_specs=[vmem] * 3,
+        scratch_shapes=[pltpu.VMEM((rows, weights[0].shape[1]), BF16)],
         compiler_params=pltpu.CompilerParams(vmem_limit_bytes=VMEM_LIMIT),
         name="layer_forward",
-    )(me, positions, gain, *weights, *chunks)
+    )(me, positions, gain, *weights, *blocks)
 
 
 def backward_kernel(
@@ -157,37 +161,36 @@
     grad_ctx = jnp.where(me_ref[1] == 1, placed_ctx, gathered_ctx)
     block = 2 * length
     mask = pair_mask(block, length)
-    for start in range(0, rows, block):
-        span = slice(start, start + block)
-        keys = qkv_ref[span, q_cols : q_cols + kv_cols]
-        values = qkv_ref[span, q_cols + kv_cols :]
-        grad_key = jnp.zeros((block, kv_cols), F32)
-        grad_value = jnp.zeros((block, kv_cols), F32)
-        for col in range(0, q_cols, HEAD_DIM):
-            query = qkv_ref[span, col : col + HEAD_DIM]
-            ctx = grad_ctx[span, col : col + HEAD_DIM]
-            capped, prob = attention(query, keys, mask)
-            grad_prob = dot_nt(ctx, values)
-            grad_score = prob * (grad_prob - jnp.sum(prob * grad_prob, axis=-1, keepdims=True))
-            grad_raw = (grad_score * (1.0 - capped * capped) * QUERY_SCALE).astype(BF16)
-            grads[span, col : col + HEAD_DIM] = dot(grad_raw, keys).astype(BF16)
-            grad_key += dot_tn(grad_raw, query)
-            grad_value += dot_tn(prob.astype(BF16), ctx)
-        grads[span, q_cols : q_cols + kv_cols] = grad_key.astype(BF16)
-        grads[span, q_cols + kv_cols :] = grad_value.astype(BF16)
+    spans = [slice(start, start + block) for start in range(0, rows, block)]
+    heads = range(0, q_cols, HEAD_DIM)
+    pairs = [(s, h) for s in spans for h in heads]
+    queries = [qkv_ref[s, h : h + HEAD_DIM] for s, h in pairs]
+    keys = [qkv_ref[s, q_cols : q_cols + kv_cols] for s, h in pairs]
+    values = [qkv_ref[s, q_cols + kv_cols :] for s, h in pairs]
+    ctxs = [grad_ctx[s, h : h + HEAD_DIM] for s, h in pairs]
+    capped, probs = attention(queries, keys, mask)
+    grad_probs = [dot_nt(c, v) for c, v in zip(ctxs, values)]
+    means = [jnp.sum(p * g, axis=-1, keepdims=True) for p, g in zip(probs, grad_probs)]
+    raws = [
+        (p * (g - m) * (1.0 - c * c) * QUERY_SCALE).astype(BF16)
+        for p, g, m, c in zip(probs, grad_probs, means, capped)
+    ]
+    grad_queries = [dot(r, k).astype(BF16) for r, k in zip(raws, keys)]
+    grad_keys = [dot_tn(r, q) for r, q in zip(raws, queries)]
+    grad_values = [dot_tn(p.astype(BF16), c) for p, c in zip(probs, ctxs)]
+    per = len(heads)
+    for i, s in enumerate(spans):
+        for j, h in enumerate(heads):
+            grads[s, h : h + HEAD_DIM] = grad_queries[i * per + j]
+        grads[s, q_cols : q_cols + kv_cols] = sum(grad_keys[i * per : (i + 1) * per]).astype(BF16)
+        grads[s, q_cols + kv_cols :] = sum(grad_values[i * per : (i + 1) * per]).astype(BF16)
     for i, offset in enumerate(offsets):
         place = pl.multiple_of(lax.rem(me_ref[0] + (offset + count), count) * own, own)
         turned[i * own : (i + 1) * own, :] = grads[pl.ds(place, own), :]
-    tile = 256
-
-    @pl.loop(0, feats // tile)
-    def _(i):
-        cols = pl.ds(pl.multiple_of(i * tile, tile), tile)
-        back = (
-            dot_nt(turned[:, :q_cols], wq_ref[cols, :])
-            + dot_nt(turned[:, q_cols : q_cols + kv_cols], wk_ref[cols, :])
-            + dot_nt(turned[:, q_cols + kv_cols :], wv_ref[cols, :])
-        ).astype(BF16)
+    for start in range(0, feats, 256):
+        cols = slice(start, start + 256)
+        all_w = jnp.concatenate([wq_ref[cols, :], wk_ref[cols, :], wv_ref[cols, :]], axis=1)
+        back = dot_nt(turned[...], all_w).astype(BF16)
         for j, out in enumerate(outs):
             out[:, cols] = back[j * own : (j + 1) * own, :]
 
@@ -220,18 +223,29 @@
     return jnp.sum(order_hot * grad_order[:, None], axis=0)
 
 
-def gather_ring(block):
+def gather_ring(block, sections):
     count = lax.axis_size("tensor")
-    blocks, offsets = [block], [0]
+    blocks, offsets = [block], [(0,)]
     up = down = block
     for step in range(1, count // 2 + 1):
-        up = shift(up, 1)
+        up = shift(up, 1, sections)
         blocks.append(up)
-        offsets.append(-step)
+        offsets.append((-step,))
         if step < count - count // 2:
-            down = shift(down, -1)
+            down = shift(down, -1, sections)
             blocks.append(down)
-            offsets.append(step)
+            offsets.append((step,))
+    return blocks, offsets
+
+
+def gather_hops(block, sections):
+    own = block.shape[0]
+    far = jnp.concatenate([block, shift(block, 5, sections), shift(block, -5, sections)])
+    left, right = shift(far, 1, sections), shift(far, -1, sections)
+    left_on, right_on = shift(left, 1, sections), shift(right, -1, sections)
+    across = shift(right[2 * own :], -2, sections)
+    blocks = [far, left, right, left_on, right_on, across]
+    offsets = [(0, -5, 5), (-1, -6, 4), (1, -4, 6), (-2, -7, 3), (2, -3, 7), (8,)]
     return blocks, offsets
 
 
@@ -252,10 +266,10 @@
     return up, down
 
 
-def sum_rows(value):
+def sum_rows(value, sections):
     step = 1
     while step < lax.axis_size("tensor"):
-        value = value + shift(value, step)
+        value = value + shift(value, step, sections)
         step *= 2
     return value
 
@@ -287,21 +301,29 @@
     me = jnp.stack([tensor_pos, at_end.astype(jnp.int32)])
 
     later_all = lax.all_gather(later_own, "tensor", axis=0, tiled=True)
-    chunks, offsets = gather_ring(x_own)
-    qkv, mixed, rows_x, rows_mixed = forward_part(
-        me, places, attn_gain, weights, chunks, offsets, length
-    )
+    last = lax.axis_size("section") - 1
+
+    def forward(blocks, offsets):
+        return forward_part(me, places, attn_gain, weights, blocks, offsets, length)
+
+    def inner_section(x_own):
+        qkv, mixed, rows_part = forward(*gather_ring(x_own, range(last)))
+        return qkv, mixed, rows_part
+
+    def last_section(x_own):
+        qkv, mixed, rows_part = forward(*gather_hops(x_own, [last]))
+        rows_hidden = sum_rows(rows_part, [last]).astype(BF16).astype(F32)
+        inv_norm = inv_rms(rows_hidden)
+        head_vec = final_gain.astype(F32) * reward_head.astype(F32)
+        reward_scores = jnp.sum(rows_hidden * inv_norm * head_vec, axis=-1)
+        scaled = rank_grad(reward_scores, rankings)[:, None] * head_vec
+        row_grads = inv_norm * scaled - rows_hidden * inv_norm**3 * jnp.mean(
+            scaled * rows_hidden, axis=-1, keepdims=True
+        )
+        return qkv, mixed, row_grads.astype(BF16).astype(F32)
+
+    qkv, mixed, row_grads = lax.cond(at_end, last_section, inner_section, x_own)
     mixed_own = lax.psum_scatter(mixed, "tensor", scatter_dimension=0, tiled=True)
-
-    rows_hidden = (rows_x + sum_rows(rows_mixed)).astype(BF16).astype(F32)
-    inv_norm = inv_rms(rows_hidden)
-    head_vec = final_gain.astype(F32) * reward_head.astype(F32)
-    reward_scores = jnp.sum(rows_hidden * inv_norm * head_vec, axis=-1)
-    scaled = rank_grad(reward_scores, rankings)[:, None] * head_vec
-    row_grads = inv_norm * scaled - rows_hidden * inv_norm**3 * jnp.mean(
-        scaled * rows_hidden, axis=-1, keepdims=True
-    )
-    row_grads = row_grads.astype(BF16).astype(F32)
 
     back_offsets = list(range(-(tensor_count - tensor_count // 2 - 1), tensor_count // 2 + 1))
     back = backward_part(

time: 281 us -> 225 us (0.80)
  the two profiles are of different devices: /device:TPU:1 before, /device:TPU:151 now
where the time goes in v2:
time: 225 us; the launch traced here: 224 us
  starting transfers between devices  111 us (49%)
  waiting for transfers between devices  78.8 us (35%)
  between operations  14.4 us (6%)
  Pallas kernels  11.3 us (5%)
  local copies, waits for them, and re-layouts  5.39 us (2%)
  other arithmetic  2.96 us (1%)
    ppermute x30, starting transfers between devices, shift(): return lax.ppermute(value, ('section', 'tensor'), pairs)  94.4 us
    ppermute x30, waiting for transfers between devices, shift(): return lax.ppermute(value, ('section', 'tensor'), pairs)  35.6 us
    reduce_scatter x1, waiting for transfers between devices, shards(): lax.psum_scatter(mixed, 'tensor', scatter_dimension=0, tiled=True)  30.5 us
    ppermute x2, starting transfers between devices, from_behind(): lax.ppermute(value, 'section', [(i, i + steps) for i in range(leading, la...  16.3 us
    ppermute x2, waiting for transfers between devices, from_behind(): lax.ppermute(value, 'section', [(i, i + steps) for i in range(leading, la...  12 us
    pallas_call x1, Pallas kernels, forward_part(): pl.pallas_call(functools.partial(forward_kernel, offsets, length), out_sh...  6.59 us
    pallas_call x1, Pallas kernels, backward_part(): pl.pallas_call(functools.partial(backward_kernel, offsets, length), out_s...  4.69 us
    unnamed x16, local copies, waits for them, and re-layouts  4.58 us
  transfers between devices with their start and end apart: 34, of which 23 were waited for; matrix products, arithmetic and copies ran while one was open for 1% of the time, Pallas kernels for 5%

profile of v2, /device:TPU:151, one launch (start us, length us, event | category | flops | bytes accessed | tf_op | source)
XLA Modules:
  0.0 223.7 jit_solution(5422490656327052270)
XLA Ops:
  8.8 75.2 %conditional.1 = ((bf16[512,512]{1,0:T(8,128)(2,1)S(1)}, bf16[512,2304]{1,0:T(8,128)(2,1)}, f32[8,2304]{1,0:T(8,128)S(1)})) conditional(s32[]{:T(128)} %convert_element_type.175, (bf16[32,2304]{1,0:T(8,128)(2,1)}, s32[2]{0:T(128)S(1)}, s32[8,1]{1,0:T(8,128)S(1)}, bf16[1,2304]{1,0:T(2,128)(2,1)}, bf16[2304,256]{1,0:T(8,128)(2,1)}, ...), branch_computations={%region_0.0_spmd, %region_1.0_spmd} | conditional | flops 450064 | bytes 12323468 | solution.py:325
  8.8 3.5 %collective-permute-start = (bf16[32,2304]{1,0:T(8,128)(2,1)}, bf16[32,2304]{1,0:T(8,128)(2,1)S(1)}, u32[]{:S(2)}, u32[]{:S(2)}) collective-permute-start(bf16[32,2304]{1,0:T(8,128)(2,1)} %get-tuple-element.45.refs_0_), channel_id=1, source_target_pairs={{0,1},{1,2},{2,3},{3,4},{4,5},{5,6},{6,7},{7,8},{8,9},{9,10},{10,1... | collective-permute-start | bytes 442376 | tf_op jit(solution)/shard_map/cond/branch_0_fun/ppermute | solution.py:27
  12.3 2.9 %collective-permute-start.1 = (bf16[32,2304]{1,0:T(8,128)(2,1)}, bf16[32,2304]{1,0:T(8,128)(2,1)S(1)}, u32[]{:S(2)}, u32[]{:S(2)}) collective-permute-start(bf16[32,2304]{1,0:T(8,128)(2,1)} %get-tuple-element.45.refs_0_), channel_id=1, source_target_pairs={{0,15},{1,0},{2,1},{3,2},{4,3},{5,4},{6,5},{7,6},{8,7},{9,8},{10,9... | collective-permute-start | bytes 442376 | tf_op jit(solution)/shard_map/cond/branch_0_fun/ppermute | solution.py:27
  15.3 1.5 collective-permute-done.refs_1_
  16.8 2.3 %collective-permute-start.2 = (bf16[32,2304]{1,0:T(8,128)(2,1)S(1)}, bf16[32,2304]{1,0:T(8,128)(2,1)S(1)}, u32[]{:S(2)}, u32[]{:S(2)}) collective-permute-start(bf16[32,2304]{1,0:T(8,128)(2,1)S(1)} %collective-permute-done.refs_1_), channel_id=1, source_target_pairs={{0,1},{1,2},{2,3},{3,4},{4,5},{5,6},{6,7},{7,8},{8,9},{9,10},{10,1... | collective-permute-start | bytes 442376 | tf_op jit(solution)/shard_map/cond/branch_0_fun/ppermute | solution.py:27
  19.2 4.1 %collective-permute-start.3 = (bf16[32,2304]{1,0:T(8,128)(2,1)S(1)}, bf16[32,2304]{1,0:T(8,128)(2,1)S(1)}, u32[]{:S(2)}, u32[]{:S(2)}) collective-permute-start(bf16[32,2304]{1,0:T(8,128)(2,1)S(1)} %collective-permute-done.1.refs_2_), channel_id=1, source_target_pairs={{0,15},{1,0},{2,1},{3,2},{4,3},{5,4},{6,5},{7,6},{8,7},{9,8},{10,9... | collective-permute-start | bytes 442376 | tf_op jit(solution)/shard_map/cond/branch_0_fun/ppermute | solution.py:27
  23.9 1.9 collective-permute-start.4
  25.8 4.6 %collective-permute-start.5 = (bf16[32,2304]{1,0:T(8,128)(2,1)S(1)}, bf16[32,2304]{1,0:T(8,128)(2,1)S(1)}, u32[]{:S(2)}, u32[]{:S(2)}) collective-permute-start(bf16[32,2304]{1,0:T(8,128)(2,1)S(1)} %collective-permute-done.3.refs_4_), channel_id=1, source_target_pairs={{0,15},{1,0},{2,1},{3,2},{4,3},{5,4},{6,5},{7,6},{8,7},{9,8},{10,9... | collective-permute-start | bytes 442376 | tf_op jit(solution)/shard_map/cond/branch_0_fun/ppermute | solution.py:27
  30.4 2.8 %collective-permute-done.4.refs_5_ = bf16[32,2304]{1,0:T(8,128)(2,1)S(1)} collective-permute-done((bf16[32,2304]{1,0:T(8,128)(2,1)S(1)}, bf16[32,2304]{1,0:T(8,128)(2,1)S(1)}, u32[]{:S(2)}, u32[]{:S(2)}) %collective-permute-start.4) | collective-permute-done | bytes 147488 | tf_op jit(solution)/shard_map/cond/branch_0_fun/ppermute | solution.py:27
  33.1 1.9 collective-permute-start.6
  35.4 4.3 %collective-permute-start.7 = (bf16[32,2304]{1,0:T(8,128)(2,1)S(1)}, bf16[32,2304]{1,0:T(8,128)(2,1)S(1)}, u32[]{:S(2)}, u32[]{:S(2)}) collective-permute-start(bf16[32,2304]{1,0:T(8,128)(2,1)S(1)} %collective-permute-done.5.refs_6_), channel_id=1, source_target_pairs={{0,15},{1,0},{2,1},{3,2},{4,3},{5,4},{6,5},{7,6},{8,7},{9,8},{10,9... | collective-permute-start | bytes 442376 | tf_op jit(solution)/shard_map/cond/branch_0_fun/ppermute | solution.py:27
  39.7 2.9 %collective-permute-done.6.refs_7_ = bf16[32,2304]{1,0:T(8,128)(2,1)S(1)} collective-permute-done((bf16[32,2304]{1,0:T(8,128)(2,1)S(1)}, bf16[32,2304]{1,0:T(8,128)(2,1)S(1)}, u32[]{:S(2)}, u32[]{:S(2)}) %collective-permute-start.6) | collective-permute-done | bytes 147488 | tf_op jit(solution)/shard_map/cond/branch_0_fun/ppermute | solution.py:27
  42.5 1.9 collective-permute-start.8
  44.4 4.6 %collective-permute-start.9 = (bf16[32,2304]{1,0:T(8,128)(2,1)S(1)}, bf16[32,2304]{1,0:T(8,128)(2,1)S(1)}, u32[]{:S(2)}, u32[]{:S(2)}) collective-permute-start(bf16[32,2304]{1,0:T(8,128)(2,1)S(1)} %collective-permute-done.7.refs_8_), channel_id=1, source_target_pairs={{0,15},{1,0},{2,1},{3,2},{4,3},{5,4},{6,5},{7,6},{8,7},{9,8},{10,9... | collective-permute-start | bytes 442376 | tf_op jit(solution)/shard_map/cond/branch_0_fun/ppermute | solution.py:27
  49.0 1.8 collective-permute-done.8.refs_9_
  50.8 1.9 collective-permute-start.10
  52.7 4.6 %collective-permute-start.11 = (bf16[32,2304]{1,0:T(8,128)(2,1)S(1)}, bf16[32,2304]{1,0:T(8,128)(2,1)S(1)}, u32[]{:S(2)}, u32[]{:S(2)}) collective-permute-start(bf16[32,2304]{1,0:T(8,128)(2,1)S(1)} %collective-permute-done.9.refs_10_), channel_id=1, source_target_pairs={{0,15},{1,0},{2,1},{3,2},{4,3},{5,4},{6,5},{7,6},{8,7},{9,8},{10,9... | collective-permute-start | bytes 442376 | tf_op jit(solution)/shard_map/cond/branch_0_fun/ppermute | solution.py:27
  57.3 2.3 %collective-permute-done.10.refs_11_ = bf16[32,2304]{1,0:T(8,128)(2,1)S(1)} collective-permute-done((bf16[32,2304]{1,0:T(8,128)(2,1)S(1)}, bf16[32,2304]{1,0:T(8,128)(2,1)S(1)}, u32[]{:S(2)}, u32[]{:S(2)}) %collective-permute-start.10) | collective-permute-done | bytes 147488 | tf_op jit(solution)/shard_map/cond/branch_0_fun/ppermute | solution.py:27
  59.6 1.9 collective-permute-start.12
  61.5 4.6 %collective-permute-start.13 = (bf16[32,2304]{1,0:T(8,128)(2,1)S(1)}, bf16[32,2304]{1,0:T(8,128)(2,1)S(1)}, u32[]{:S(2)}, u32[]{:S(2)}) collective-permute-start(bf16[32,2304]{1,0:T(8,128)(2,1)S(1)} %collective-permute-done.11.refs_12_), channel_id=1, source_target_pairs={{0,15},{1,0},{2,1},{3,2},{4,3},{5,4},{6,5},{7,6},{8,7},{9,8},{10,9... | collective-permute-start | bytes 442376 | tf_op jit(solution)/shard_map/cond/branch_0_fun/ppermute | solution.py:27
  66.1 1.6 collective-permute-done.12.refs_13_
  67.7 1.9 collective-permute-start.14
  69.6 7.8 %collective-permute-done.14.refs_15_ = bf16[32,2304]{1,0:T(8,128)(2,1)S(1)} collective-permute-done((bf16[32,2304]{1,0:T(8,128)(2,1)S(1)}, bf16[32,2304]{1,0:T(8,128)(2,1)S(1)}, u32[]{:S(2)}, u32[]{:S(2)}) %collective-permute-start.14) | collective-permute-done | bytes 147488 | tf_op jit(solution)/shard_map/cond/branch_0_fun/ppermute | solution.py:27
  77.4 6.6 %layer_forward.2 = (bf16[512,512]{1,0:T(8,128)(2,1)S(1)}, bf16[512,2304]{1,0:T(8,128)(2,1)}, f32[8,2304]{1,0:T(8,128)S(1)}) custom-call(s32[2]{0:T(128)S(1)} %get-tuple-element.38.me_ref, s32[8,1]{1,0:T(8,128)S(1)} %get-tuple-element.39.positions_ref, bf16[1,2304]{1,0:T(2,128)(2,1)} %get-tuple-element.40.gain_ref, ...), custom_call_target="tpu_custom_call" | custom-call | tf_op jit(solution)/shard_map/cond/branch_0_fun/layer_forward/pallas_call | solution.py:122
  85.6 1.7 copy-done
  87.3 4.7 %layer_backward.1 = (bf16[32,2304]{1,0:T(8,128)(2,1)S(1)}, bf16[32,2304]{1,0:T(8,128)(2,1)S(1)}, bf16[32,2304]{1,0:T(8,128)(2,1)S(1)}, bf16[32,2304]{1,0:T(8,128...) custom-call(s32[2]{0:T(128)S(1)} %pad_add_fusion.me_ref, ...), custom_call_target="tpu_custom_call" | custom-call | tf_op jit(solution)/shard_map/layer_backward/pallas_call | solution.py:203
  92.0 1.9 collective-permute-start.27
  94.0 4.6 %collective-permute-start.35 = (bf16[32,2304]{1,0:T(8,128)(2,1)S(1)}, bf16[32,2304]{1,0:T(8,128)(2,1)S(1)}, u32[]{:S(2)}, u32[]{:S(2)}) collective-permute-start(bf16[32,2304]{1,0:T(8,128)(2,1)S(1)} %get-tuple-element.93), channel_id=1, source_target_pairs={{0,15},{1,0},{2,1},{3,2},{4,3},{5,4},{6,5},{7,6},{8,7},{9,8},{10,9... | collective-permute-start | bytes 442376 | tf_op jit(solution)/shard_map/ppermute | solution.py:27
  99.1 1.9 collective-permute-start.28
  101.1 4.8 %collective-permute-start.36 = (bf16[32,2304]{1,0:T(8,128)(2,1)S(1)}, bf16[32,2304]{1,0:T(8,128)(2,1)S(1)}, u32[]{:S(2)}, u32[]{:S(2)}) collective-permute-start(bf16[32,2304]{1,0:T(8,128)(2,1)S(1)} %add_convert_fusion.6), channel_id=1, source_target_pairs={{0,15},{1,0},{2,1},{3,2},{4,3},{5,4},{6,5},{7,6},{8,7},{9,8},{10,9... | collective-permute-start | bytes 442376 | tf_op jit(solution)/shard_map/ppermute | solution.py:27
  105.9 2.1 collective-permute-done.28
  108.0 1.9 collective-permute-start.29
  110.0 4.7 %collective-permute-start.37 = (bf16[32,2304]{1,0:T(8,128)(2,1)S(1)}, bf16[32,2304]{1,0:T(8,128)(2,1)S(1)}, u32[]{:S(2)}, u32[]{:S(2)}) collective-permute-start(bf16[32,2304]{1,0:T(8,128)(2,1)S(1)} %add_convert_fusion.5), channel_id=1, source_target_pairs={{0,15},{1,0},{2,1},{3,2},{4,3},{5,4},{6,5},{7,6},{8,7},{9,8},{10,9... | collective-permute-start | bytes 442376 | tf_op jit(solution)/shard_map/ppermute | solution.py:27
  114.7 1.3 collective-permute-done.29
  116.0 2.1 collective-permute-start.30
  119.0 3.7 %collective-permute-start.38 = (bf16[32,2304]{1,0:T(8,128)(2,1)S(1)}, bf16[32,2304]{1,0:T(8,128)(2,1)S(1)}, u32[]{:S(2)}, u32[]{:S(2)}) collective-permute-start(bf16[32,2304]{1,0:T(8,128)(2,1)S(1)} %add_convert_fusion.4), channel_id=1, source_target_pairs={{0,15},{1,0},{2,1},{3,2},{4,3},{5,4},{6,5},{7,6},{8,7},{9,8},{10,9... | collective-permute-start | bytes 442376 | tf_op jit(solution)/shard_map/ppermute | solution.py:27
  123.3 1.9 collective-permute-start.31
  125.3 4.6 %collective-permute-start.39 = (bf16[32,2304]{1,0:T(8,128)(2,1)S(1)}, bf16[32,2304]{1,0:T(8,128)(2,1)S(1)}, u32[]{:S(2)}, u32[]{:S(2)}) collective-permute-start(bf16[32,2304]{1,0:T(8,128)(2,1)S(1)} %add_convert_fusion.3), channel_id=1, source_target_pairs={{0,15},{1,0},{2,1},{3,2},{4,3},{5,4},{6,5},{7,6},{8,7},{9,8},{10,9... | collective-permute-start | bytes 442376 | tf_op jit(solution)/shard_map/ppermute | solution.py:27
  130.4 1.9 collective-permute-start.32
  132.4 4.6 %collective-permute-start.40 = (bf16[32,2304]{1,0:T(8,128)(2,1)S(1)}, bf16[32,2304]{1,0:T(8,128)(2,1)S(1)}, u32[]{:S(2)}, u32[]{:S(2)}) collective-permute-start(bf16[32,2304]{1,0:T(8,128)(2,1)S(1)} %add_convert_fusion.2), channel_id=1, source_target_pairs={{0,15},{1,0},{2,1},{3,2},{4,3},{5,4},{6,5},{7,6},{8,7},{9,8},{10,9... | collective-permute-start | bytes 442376 | tf_op jit(solution)/shard_map/ppermute | solution.py:27
  137.6 1.9 collective-permute-start.33
  140.7 5.1 %collective-permute-start.41 = (bf16[32,2304]{1,0:T(8,128)(2,1)S(1)}, bf16[32,2304]{1,0:T(8,128)(2,1)S(1)}, u32[]{:S(2)}, u32[]{:S(2)}) collective-permute-start(bf16[32,2304]{1,0:T(8,128)(2,1)S(1)} %add_convert_fusion.1), channel_id=1, source_target_pairs={{0,15},{1,0},{2,1},{3,2},{4,3},{5,4},{6,5},{7,6},{8,7},{9,8},{10,9... | collective-permute-start | bytes 442376 | tf_op jit(solution)/shard_map/ppermute | solution.py:27
  146.6 1.9 collective-permute-start.34
  149.7 5.7 %collective-permute-done.34 = bf16[32,2304]{1,0:T(8,128)(2,1)S(1)} collective-permute-done((bf16[32,2304]{1,0:T(8,128)(2,1)S(1)}, bf16[32,2304]{1,0:T(8,128)(2,1)S(1)}, u32[]{:S(2)}, u32[]{:S(2)}) %collective-permute-start.34) | collective-permute-done | bytes 147488 | tf_op jit(solution)/shard_map/ppermute | solution.py:27
  155.6 30.5 %reduce-scatter.2.cloned.1.call-done = bf16[32,2304]{1,0:T(8,128)(2,1)} async-done(((bf16[512,2304]{1,0:T(8,128)(2,1)}), bf16[32,2304]{1,0:T(8,128)(2,1)}) %reduce-scatter.2.cloned.1.call-update) | async-done | bytes 147472 | tf_op jit(solution)/shard_map/reduce_scatter | solution.py:326
  187.2 14.4 %collective-permute-start.26 = (bf16[32,2304]{1,0:T(8,128)(2,1)S(1)}, bf16[32,2304]{1,0:T(8,128)(2,1)S(1)}, u32[]{:S(2)}, u32[]{:S(2)}) collective-permute-start(bf16[32,2304]{1,0:T(8,128)(2,1)S(1)} %get-tuple-element.113), channel_id=1, source_target_pairs={{0,16},{16,32},{32,48},{48,64},{64,80},{80,96},{96,112},{112,128},... | collective-permute-start | bytes 442376 | tf_op jit(solution)/shard_map/ppermute | solution.py:33
  201.6 1.9 collective-permute-start.42
  203.6 11.9 %collective-permute-done.42 = bf16[32,2304]{1,0:T(8,128)(2,1)S(1)} collective-permute-done((bf16[32,2304]{1,0:T(8,128)(2,1)S(1)}, bf16[32,2304]{1,0:T(8,128)(2,1)S(1)}, u32[]{:S(2)}, u32[]{:S(2)}) %collective-permute-start.42) | collective-permute-done | bytes 147488 | tf_op jit(solution)/shard_map/ppermute | solution.py:33
  (66 shorter events, 13.6 us)
Async XLA Ops:
  7.2 77.5 %all-gather.3.cloned.1.call-start = ((), (), s32[]{:S(2)}) async-start(), calls=%async_computation.2 | async-start | bytes 2506752 | tf_op jit(solution)/shard_map/all_gather | solution.py:303
  7.9 178.2 %reduce-scatter.2.cloned.1.call-start = ((), (), s32[]{:S(2)}) async-start(), calls=%async_computation.1 | async-start | bytes 2506752 | tf_op jit(solution)/shard_map/reduce_scatter | solution.py:326
  8.8 8.0 %collective-permute-start = (bf16[32,2304]{1,0:T(8,128)(2,1)}, bf16[32,2304]{1,0:T(8,128)(2,1)S(1)}, u32[]{:S(2)}, u32[]{:S(2)}) collective-permute-start(bf16[32,2304]{1,0:T(8,128)(2,1)} %get-tuple-element.45.refs_0_), channel_id=1, source_target_pairs={{0,1},{1,2},{2,3},{3,4},{4,5},{5,6},{6,7},{7,8},{8,9},{9,10},{10,1... | collective-permute-start | bytes 442376 | tf_op jit(solution)/shard_map/cond/branch_0_fun/ppermute | solution.py:27
  12.3 6.9 %collective-permute-start.1 = (bf16[32,2304]{1,0:T(8,128)(2,1)}, bf16[32,2304]{1,0:T(8,128)(2,1)S(1)}, u32[]{:S(2)}, u32[]{:S(2)}) collective-permute-start(bf16[32,2304]{1,0:T(8,128)(2,1)} %get-tuple-element.45.refs_0_), channel_id=1, source_target_pairs={{0,15},{1,0},{2,1},{3,2},{4,3},{5,4},{6,5},{7,6},{8,7},{9,8},{10,9... | collective-permute-start | bytes 442376 | tf_op jit(solution)/shard_map/cond/branch_0_fun/ppermute | solution.py:27
  16.8 7.1 %collective-permute-start.2 = (bf16[32,2304]{1,0:T(8,128)(2,1)S(1)}, bf16[32,2304]{1,0:T(8,128)(2,1)S(1)}, u32[]{:S(2)}, u32[]{:S(2)}) collective-permute-start(bf16[32,2304]{1,0:T(8,128)(2,1)S(1)} %collective-permute-done.refs_1_), channel_id=1, source_target_pairs={{0,1},{1,2},{2,3},{3,4},{4,5},{5,6},{6,7},{7,8},{8,9},{9,10},{10,1... | collective-permute-start | bytes 442376 | tf_op jit(solution)/shard_map/cond/branch_0_fun/ppermute | solution.py:27
  19.2 6.6 %collective-permute-start.3 = (bf16[32,2304]{1,0:T(8,128)(2,1)S(1)}, bf16[32,2304]{1,0:T(8,128)(2,1)S(1)}, u32[]{:S(2)}, u32[]{:S(2)}) collective-permute-start(bf16[32,2304]{1,0:T(8,128)(2,1)S(1)} %collective-permute-done.1.refs_2_), channel_id=1, source_target_pairs={{0,15},{1,0},{2,1},{3,2},{4,3},{5,4},{6,5},{7,6},{8,7},{9,8},{10,9... | collective-permute-start | bytes 442376 | tf_op jit(solution)/shard_map/cond/branch_0_fun/ppermute | solution.py:27
  23.9 9.3 %collective-permute-start.4 = (bf16[32,2304]{1,0:T(8,128)(2,1)S(1)}, bf16[32,2304]{1,0:T(8,128)(2,1)S(1)}, u32[]{:S(2)}, u32[]{:S(2)}) collective-permute-start(bf16[32,2304]{1,0:T(8,128)(2,1)S(1)} %collective-permute-done.2.refs_3_), channel_id=1, source_target_pairs={{0,1},{1,2},{2,3},{3,4},{4,5},{5,6},{6,7},{7,8},{8,9},{9,10},{10,1... | collective-permute-start | bytes 442376 | tf_op jit(solution)/shard_map/cond/branch_0_fun/ppermute | solution.py:27
  25.8 9.6 %collective-permute-start.5 = (bf16[32,2304]{1,0:T(8,128)(2,1)S(1)}, bf16[32,2304]{1,0:T(8,128)(2,1)S(1)}, u32[]{:S(2)}, u32[]{:S(2)}) collective-permute-start(bf16[32,2304]{1,0:T(8,128)(2,1)S(1)} %collective-permute-done.3.refs_4_), channel_id=1, source_target_pairs={{0,15},{1,0},{2,1},{3,2},{4,3},{5,4},{6,5},{7,6},{8,7},{9,8},{10,9... | collective-permute-start | bytes 442376 | tf_op jit(solution)/shard_map/cond/branch_0_fun/ppermute | solution.py:27
  33.1 9.4 %collective-permute-start.6 = (bf16[32,2304]{1,0:T(8,128)(2,1)S(1)}, bf16[32,2304]{1,0:T(8,128)(2,1)S(1)}, u32[]{:S(2)}, u32[]{:S(2)}) collective-permute-start(bf16[32,2304]{1,0:T(8,128)(2,1)S(1)} %collective-permute-done.4.refs_5_), channel_id=1, source_target_pairs={{0,1},{1,2},{2,3},{3,4},{4,5},{5,6},{6,7},{7,8},{8,9},{9,10},{10,1... | collective-permute-start | bytes 442376 | tf_op jit(solution)/shard_map/cond/branch_0_fun/ppermute | solution.py:27
  35.4 9.0 %collective-permute-start.7 = (bf16[32,2304]{1,0:T(8,128)(2,1)S(1)}, bf16[32,2304]{1,0:T(8,128)(2,1)S(1)}, u32[]{:S(2)}, u32[]{:S(2)}) collective-permute-start(bf16[32,2304]{1,0:T(8,128)(2,1)S(1)} %collective-permute-done.5.refs_6_), channel_id=1, source_target_pairs={{0,15},{1,0},{2,1},{3,2},{4,3},{5,4},{6,5},{7,6},{8,7},{9,8},{10,9... | collective-permute-start | bytes 442376 | tf_op jit(solution)/shard_map/cond/branch_0_fun/ppermute | solution.py:27
  42.5 8.3 %collective-permute-start.8 = (bf16[32,2304]{1,0:T(8,128)(2,1)S(1)}, bf16[32,2304]{1,0:T(8,128)(2,1)S(1)}, u32[]{:S(2)}, u32[]{:S(2)}) collective-permute-start(bf16[32,2304]{1,0:T(8,128)(2,1)S(1)} %collective-permute-done.6.refs_7_), channel_id=1, source_target_pairs={{0,1},{1,2},{2,3},{3,4},{4,5},{5,6},{6,7},{7,8},{8,9},{9,10},{10,1... | collective-permute-start | bytes 442376 | tf_op jit(solution)/shard_map/cond/branch_0_fun/ppermute | solution.py:27
  44.4 8.3 %collective-permute-start.9 = (bf16[32,2304]{1,0:T(8,128)(2,1)S(1)}, bf16[32,2304]{1,0:T(8,128)(2,1)S(1)}, u32[]{:S(2)}, u32[]{:S(2)}) collective-permute-start(bf16[32,2304]{1,0:T(8,128)(2,1)S(1)} %collective-permute-done.7.refs_8_), channel_id=1, source_target_pairs={{0,15},{1,0},{2,1},{3,2},{4,3},{5,4},{6,5},{7,6},{8,7},{9,8},{10,9... | collective-permute-start | bytes 442376 | tf_op jit(solution)/shard_map/cond/branch_0_fun/ppermute | solution.py:27
  50.8 8.8 %collective-permute-start.10 = (bf16[32,2304]{1,0:T(8,128)(2,1)S(1)}, bf16[32,2304]{1,0:T(8,128)(2,1)S(1)}, u32[]{:S(2)}, u32[]{:S(2)}) collective-permute-start(bf16[32,2304]{1,0:T(8,128)(2,1)S(1)} %collective-permute-done.8.refs_9_), channel_id=1, source_target_pairs={{0,1},{1,2},{2,3},{3,4},{4,5},{5,6},{6,7},{7,8},{8,9},{9,10},{10,1... | collective-permute-start | bytes 442376 | tf_op jit(solution)/shard_map/cond/branch_0_fun/ppermute | solution.py:27
  52.7 8.8 %collective-permute-start.11 = (bf16[32,2304]{1,0:T(8,128)(2,1)S(1)}, bf16[32,2304]{1,0:T(8,128)(2,1)S(1)}, u32[]{:S(2)}, u32[]{:S(2)}) collective-permute-start(bf16[32,2304]{1,0:T(8,128)(2,1)S(1)} %collective-permute-done.9.refs_10_), channel_id=1, source_target_pairs={{0,15},{1,0},{2,1},{3,2},{4,3},{5,4},{6,5},{7,6},{8,7},{9,8},{10,9... | collective-permute-start | bytes 442376 | tf_op jit(solution)/shard_map/cond/branch_0_fun/ppermute | solution.py:27
  59.6 8.1 %collective-permute-start.12 = (bf16[32,2304]{1,0:T(8,128)(2,1)S(1)}, bf16[32,2304]{1,0:T(8,128)(2,1)S(1)}, u32[]{:S(2)}, u32[]{:S(2)}) collective-permute-start(bf16[32,2304]{1,0:T(8,128)(2,1)S(1)} %collective-permute-done.10.refs_11_), channel_id=1, source_target_pairs={{0,1},{1,2},{2,3},{3,4},{4,5},{5,6},{6,7},{7,8},{8,9},{9,10},{10,1... | collective-permute-start | bytes 442376 | tf_op jit(solution)/shard_map/cond/branch_0_fun/ppermute | solution.py:27
  61.5 8.1 %collective-permute-start.13 = (bf16[32,2304]{1,0:T(8,128)(2,1)S(1)}, bf16[32,2304]{1,0:T(8,128)(2,1)S(1)}, u32[]{:S(2)}, u32[]{:S(2)}) collective-permute-start(bf16[32,2304]{1,0:T(8,128)(2,1)S(1)} %collective-permute-done.11.refs_12_), channel_id=1, source_target_pairs={{0,15},{1,0},{2,1},{3,2},{4,3},{5,4},{6,5},{7,6},{8,7},{9,8},{10,9... | collective-permute-start | bytes 442376 | tf_op jit(solution)/shard_map/cond/branch_0_fun/ppermute | solution.py:27
  67.7 9.7 %collective-permute-start.14 = (bf16[32,2304]{1,0:T(8,128)(2,1)S(1)}, bf16[32,2304]{1,0:T(8,128)(2,1)S(1)}, u32[]{:S(2)}, u32[]{:S(2)}) collective-permute-start(bf16[32,2304]{1,0:T(8,128)(2,1)S(1)} %collective-permute-done.12.refs_13_), channel_id=1, source_target_pairs={{0,1},{1,2},{2,3},{3,4},{4,5},{5,6},{6,7},{7,8},{8,9},{9,10},{10,1... | collective-permute-start | bytes 442376 | tf_op jit(solution)/shard_map/cond/branch_0_fun/ppermute | solution.py:27
  84.0 0.7 copy-start.8
  84.0 1.3 copy-start.1
  84.0 1.6 copy-start.2
  85.6 1.7 copy-start
  92.0 7.1 %collective-permute-start.27 = (bf16[32,2304]{1,0:T(8,128)(2,1)S(1)}, bf16[32,2304]{1,0:T(8,128)(2,1)S(1)}, u32[]{:S(2)}, u32[]{:S(2)}) collective-permute-start(bf16[32,2304]{1,0:T(8,128)(2,1)S(1)} %get-tuple-element.85), channel_id=1, source_target_pairs={{0,1},{1,2},{2,3},{3,4},{4,5},{5,6},{6,7},{7,8},{8,9},{9,10},{10,1... | collective-permute-start | bytes 442376 | tf_op jit(solution)/shard_map/ppermute | solution.py:27
  94.0 7.1 %collective-permute-start.35 = (bf16[32,2304]{1,0:T(8,128)(2,1)S(1)}, bf16[32,2304]{1,0:T(8,128)(2,1)S(1)}, u32[]{:S(2)}, u32[]{:S(2)}) collective-permute-start(bf16[32,2304]{1,0:T(8,128)(2,1)S(1)} %get-tuple-element.93), channel_id=1, source_target_pairs={{0,15},{1,0},{2,1},{3,2},{4,3},{5,4},{6,5},{7,6},{8,7},{9,8},{10,9... | collective-permute-start | bytes 442376 | tf_op jit(solution)/shard_map/ppermute | solution.py:27
  99.1 8.8 %collective-permute-start.28 = (bf16[32,2304]{1,0:T(8,128)(2,1)S(1)}, bf16[32,2304]{1,0:T(8,128)(2,1)S(1)}, u32[]{:S(2)}, u32[]{:S(2)}) collective-permute-start(bf16[32,2304]{1,0:T(8,128)(2,1)S(1)} %add_convert_fusion.13), channel_id=1, source_target_pairs={{0,1},{1,2},{2,3},{3,4},{4,5},{5,6},{6,7},{7,8},{8,9},{9,10},{10,1... | collective-permute-start | bytes 442376 | tf_op jit(solution)/shard_map/ppermute | solution.py:27
  101.1 8.8 %collective-permute-start.36 = (bf16[32,2304]{1,0:T(8,128)(2,1)S(1)}, bf16[32,2304]{1,0:T(8,128)(2,1)S(1)}, u32[]{:S(2)}, u32[]{:S(2)}) collective-permute-start(bf16[32,2304]{1,0:T(8,128)(2,1)S(1)} %add_convert_fusion.6), channel_id=1, source_target_pairs={{0,15},{1,0},{2,1},{3,2},{4,3},{5,4},{6,5},{7,6},{8,7},{9,8},{10,9... | collective-permute-start | bytes 442376 | tf_op jit(solution)/shard_map/ppermute | solution.py:27
  107.9 40.6 %copy-start.5 = (bf16[1,2304]{1,0:T(2,128)(2,1)S(1)}, bf16[1,2304]{1,0:T(2,128)(2,1)}, u32[]{:S(2)}) copy-start(bf16[1,2304]{1,0:T(2,128)(2,1)} %param.15) | copy-start | bytes 13828
  108.0 8.0 %collective-permute-start.29 = (bf16[32,2304]{1,0:T(8,128)(2,1)S(1)}, bf16[32,2304]{1,0:T(8,128)(2,1)S(1)}, u32[]{:S(2)}, u32[]{:S(2)}) collective-permute-start(bf16[32,2304]{1,0:T(8,128)(2,1)S(1)} %add_convert_fusion.12), channel_id=1, source_target_pairs={{0,1},{1,2},{2,3},{3,4},{4,5},{5,6},{6,7},{7,8},{8,9},{9,10},{10,1... | collective-permute-start | bytes 442376 | tf_op jit(solution)/shard_map/ppermute | solution.py:27
  109.9 45.4 %copy-start.3 = (bf16[1,1,32,2304]{3,2,1,0:T(8,128)(2,1)S(1)}, bf16[1,1,32,2304]{3,2,1,0:T(8,128)(2,1)}, u32[]{:S(2)}) copy-start(bf16[1,1,32,2304]{3,2,1,0:T(8,128)(2,1)} %param.13) | copy-start | bytes 442372
  110.0 8.9 %collective-permute-start.37 = (bf16[32,2304]{1,0:T(8,128)(2,1)S(1)}, bf16[32,2304]{1,0:T(8,128)(2,1)S(1)}, u32[]{:S(2)}, u32[]{:S(2)}) collective-permute-start(bf16[32,2304]{1,0:T(8,128)(2,1)S(1)} %add_convert_fusion.5), channel_id=1, source_target_pairs={{0,15},{1,0},{2,1},{3,2},{4,3},{5,4},{6,5},{7,6},{8,7},{9,8},{10,9... | collective-permute-start | bytes 442376 | tf_op jit(solution)/shard_map/ppermute | solution.py:27
  116.0 70.1 %copy-start.4 = (bf16[1,1,32,2304]{3,2,1,0:T(8,128)(2,1)S(1)}, bf16[1,1,32,2304]{3,2,1,0:T(8,128)(2,1)}, u32[]{:S(2)}) copy-start(bf16[1,1,32,2304]{3,2,1,0:T(8,128)(2,1)} %param.14) | copy-start | bytes 442372
  116.0 7.2 %collective-permute-start.30 = (bf16[32,2304]{1,0:T(8,128)(2,1)S(1)}, bf16[32,2304]{1,0:T(8,128)(2,1)S(1)}, u32[]{:S(2)}, u32[]{:S(2)}) collective-permute-start(bf16[32,2304]{1,0:T(8,128)(2,1)S(1)} %add_convert_fusion.11), channel_id=1, source_target_pairs={{0,1},{1,2},{2,3},{3,4},{4,5},{5,6},{6,7},{7,8},{8,9},{9,10},{10,1... | collective-permute-start | bytes 442376 | tf_op jit(solution)/shard_map/ppermute | solution.py:27
  119.0 6.2 %collective-permute-start.38 = (bf16[32,2304]{1,0:T(8,128)(2,1)S(1)}, bf16[32,2304]{1,0:T(8,128)(2,1)S(1)}, u32[]{:S(2)}, u32[]{:S(2)}) collective-permute-start(bf16[32,2304]{1,0:T(8,128)(2,1)S(1)} %add_convert_fusion.4), channel_id=1, source_target_pairs={{0,15},{1,0},{2,1},{3,2},{4,3},{5,4},{6,5},{7,6},{8,7},{9,8},{10,9... | collective-permute-start | bytes 442376 | tf_op jit(solution)/shard_map/ppermute | solution.py:27
  123.3 7.1 %collective-permute-start.31 = (bf16[32,2304]{1,0:T(8,128)(2,1)S(1)}, bf16[32,2304]{1,0:T(8,128)(2,1)S(1)}, u32[]{:S(2)}, u32[]{:S(2)}) collective-permute-start(bf16[32,2304]{1,0:T(8,128)(2,1)S(1)} %add_convert_fusion.10), channel_id=1, source_target_pairs={{0,1},{1,2},{2,3},{3,4},{4,5},{5,6},{6,7},{7,8},{8,9},{9,10},{10,1... | collective-permute-start | bytes 442376 | tf_op jit(solution)/shard_map/ppermute | solution.py:27
  125.3 7.1 %collective-permute-start.39 = (bf16[32,2304]{1,0:T(8,128)(2,1)S(1)}, bf16[32,2304]{1,0:T(8,128)(2,1)S(1)}, u32[]{:S(2)}, u32[]{:S(2)}) collective-permute-start(bf16[32,2304]{1,0:T(8,128)(2,1)S(1)} %add_convert_fusion.3), channel_id=1, source_target_pairs={{0,15},{1,0},{2,1},{3,2},{4,3},{5,4},{6,5},{7,6},{8,7},{9,8},{10,9... | collective-permute-start | bytes 442376 | tf_op jit(solution)/shard_map/ppermute | solution.py:27
  130.4 7.1 %collective-permute-start.32 = (bf16[32,2304]{1,0:T(8,128)(2,1)S(1)}, bf16[32,2304]{1,0:T(8,128)(2,1)S(1)}, u32[]{:S(2)}, u32[]{:S(2)}) collective-permute-start(bf16[32,2304]{1,0:T(8,128)(2,1)S(1)} %add_convert_fusion.9), channel_id=1, source_target_pairs={{0,1},{1,2},{2,3},{3,4},{4,5},{5,6},{6,7},{7,8},{8,9},{9,10},{10,1... | collective-permute-start | bytes 442376 | tf_op jit(solution)/shard_map/ppermute | solution.py:27
  132.4 8.2 %collective-permute-start.40 = (bf16[32,2304]{1,0:T(8,128)(2,1)S(1)}, bf16[32,2304]{1,0:T(8,128)(2,1)S(1)}, u32[]{:S(2)}, u32[]{:S(2)}) collective-permute-start(bf16[32,2304]{1,0:T(8,128)(2,1)S(1)} %add_convert_fusion.2), channel_id=1, source_target_pairs={{0,15},{1,0},{2,1},{3,2},{4,3},{5,4},{6,5},{7,6},{8,7},{9,8},{10,9... | collective-permute-start | bytes 442376 | tf_op jit(solution)/shard_map/ppermute | solution.py:27
  137.6 9.1 %collective-permute-start.33 = (bf16[32,2304]{1,0:T(8,128)(2,1)S(1)}, bf16[32,2304]{1,0:T(8,128)(2,1)S(1)}, u32[]{:S(2)}, u32[]{:S(2)}) collective-permute-start(bf16[32,2304]{1,0:T(8,128)(2,1)S(1)} %add_convert_fusion.8), channel_id=1, source_target_pairs={{0,1},{1,2},{2,3},{3,4},{4,5},{5,6},{6,7},{7,8},{8,9},{9,10},{10,1... | collective-permute-start | bytes 442376 | tf_op jit(solution)/shard_map/ppermute | solution.py:27
  140.7 9.0 %collective-permute-start.41 = (bf16[32,2304]{1,0:T(8,128)(2,1)S(1)}, bf16[32,2304]{1,0:T(8,128)(2,1)S(1)}, u32[]{:S(2)}, u32[]{:S(2)}) collective-permute-start(bf16[32,2304]{1,0:T(8,128)(2,1)S(1)} %add_convert_fusion.1), channel_id=1, source_target_pairs={{0,15},{1,0},{2,1},{3,2},{4,3},{5,4},{6,5},{7,6},{8,7},{9,8},{10,9... | collective-permute-start | bytes 442376 | tf_op jit(solution)/shard_map/ppermute | solution.py:27
  146.6 8.7 %collective-permute-start.34 = (bf16[32,2304]{1,0:T(8,128)(2,1)S(1)}, bf16[32,2304]{1,0:T(8,128)(2,1)S(1)}, u32[]{:S(2)}, u32[]{:S(2)}) collective-permute-start(bf16[32,2304]{1,0:T(8,128)(2,1)S(1)} %add_convert_fusion.7), channel_id=1, source_target_pairs={{0,1},{1,2},{2,3},{3,4},{4,5},{5,6},{6,7},{7,8},{8,9},{9,10},{10,1... | collective-permute-start | bytes 442376 | tf_op jit(solution)/shard_map/ppermute | solution.py:27
  187.2 16.5 %collective-permute-start.26 = (bf16[32,2304]{1,0:T(8,128)(2,1)S(1)}, bf16[32,2304]{1,0:T(8,128)(2,1)S(1)}, u32[]{:S(2)}, u32[]{:S(2)}) collective-permute-start(bf16[32,2304]{1,0:T(8,128)(2,1)S(1)} %get-tuple-element.113), channel_id=1, source_target_pairs={{0,16},{16,32},{32,48},{48,64},{64,80},{80,96},{96,112},{112,128},... | collective-permute-start | bytes 442376 | tf_op jit(solution)/shard_map/ppermute | solution.py:33
  201.6 13.9 %collective-permute-start.42 = (bf16[32,2304]{1,0:T(8,128)(2,1)S(1)}, bf16[32,2304]{1,0:T(8,128)(2,1)S(1)}, u32[]{:S(2)}, u32[]{:S(2)}) collective-permute-start(bf16[32,2304]{1,0:T(8,128)(2,1)S(1)} %get-tuple-element.112), channel_id=1, source_target_pairs={{16,0},{32,16},{48,32},{64,48},{80,64},{96,80},{112,96},{128,112},... | collective-permute-start | bytes 442376 | tf_op jit(solution)/shard_map/ppermute | solution.py:33
Sparse Core Ops, SparseCore 0:
  10.1 67.7 all-gather.2
  84.1 101.8 reduce-scatter.1

commit v3 on v2

--- a/solution.py
+++ b/solution.py
@@ -138,8 +138,6 @@
     offsets,
     length,
     me_ref,
-    positions_ref,
-    row_grads_ref,
     cot_ref,
     qkv_ref,
     wq_ref,
@@ -154,11 +152,7 @@
     own, feats = outs[0].shape
     rows = own * count
     q_cols, kv_cols = wq_ref.shape[1], wk_ref.shape[1]
-    picks = row_picks(positions_ref[...], rows)
-    gathered_ctx = dot_nt(cot_ref[...], wo_ref[...]).astype(BF16)
-    few = dot_nt(row_grads_ref[...].astype(BF16), wo_ref[...]).astype(BF16)
-    placed_ctx = dot_tn(picks, few).astype(BF16)
-    grad_ctx = jnp.where(me_ref[1] == 1, placed_ctx, gathered_ctx)
+    grad_ctx = dot_nt(cot_ref[...], wo_ref[...]).astype(BF16)
     block = 2 * length
     mask = pair_mask(block, length)
     spans = [slice(start, start + block) for start in range(0, rows, block)]
@@ -195,7 +189,7 @@
             out[:, cols] = back[j * own : (j + 1) * own, :]
 
 
-def backward_part(me, positions, row_grads, cotangent, qkv, weights, offsets, length):
+def backward_part(me, cotangent, qkv, weights, offsets, length):
     rows, feats = cotangent.shape
     own = rows // len(offsets)
     vmem = pl.BlockSpec(memory_space=pltpu.VMEM)
@@ -203,12 +197,89 @@
     return pl.pallas_call(
         functools.partial(backward_kernel, offsets, length),
         out_shape=[jax.ShapeDtypeStruct((own, feats), BF16)] * len(offsets),
-        in_specs=[smem] + [vmem] * 8,
+        in_specs=[smem] + [vmem] * 6,
         out_specs=[vmem] * len(offsets),
         scratch_shapes=[pltpu.VMEM(qkv.shape, BF16), pltpu.VMEM(qkv.shape, BF16)],
         compiler_params=pltpu.CompilerParams(vmem_limit_bytes=VMEM_LIMIT),
         name="layer_backward",
-    )(me, positions, row_grads, cotangent, qkv, *weights)
+    )(me, cotangent, qkv, *weights)
+
+
+def scored_kernel(
+    count,
+    length,
+    positions_ref,
+    row_grads_ref,
+    qkv_ref,
+    wq_ref,
+    wk_ref,
+    wv_ref,
+    wo_ref,
+    parcels_ref,
+):
+    rows = qkv_ref.shape[0]
+    feats = wq_ref.shape[0]
+    own = rows // count
+    q_cols, kv_cols = wq_ref.shape[1], wk_ref.shape[1]
+    positions = positions_ref[...]
+    picks = row_picks(positions, rows)
+    row = lax.broadcasted_iota(jnp.int32, (RESP, rows), 0)
+    col = lax.broadcasted_iota(jnp.int32, (RESP, rows), 1)
+    mask = ((col // length == row) & (col <= positions)).astype(F32)
+    query_all = dot(picks, qkv_ref[:, :q_cols]).astype(BF16)
+    ctx_all = dot_nt(row_grads_ref[...].astype(BF16), wo_ref[...]).astype(BF16)
+    keys = qkv_ref[:, q_cols : q_cols + kv_cols]
+    values = qkv_ref[:, q_cols + kv_cols :]
+    heads = range(0, q_cols, HEAD_DIM)
+    queries = [query_all[:, h : h + HEAD_DIM] for h in heads]
+    ctxs = [ctx_all[:, h : h + HEAD_DIM] for h in heads]
+    capped, probs = attention(queries, [keys] * len(heads), mask)
+    raws = []
+    for prob, cap, ctx in zip(probs, capped, ctxs):
+        grad_prob = dot_nt(ctx, values)
+        grad_score = prob * (grad_prob - jnp.sum(prob * grad_prob, axis=-1, keepdims=True))
+        raws.append((grad_score * (1.0 - cap * cap) * QUERY_SCALE).astype(BF16))
+    grad_query = jnp.concatenate([dot(raw, keys) for raw in raws], axis=1).astype(BF16)
+    vectors = [dot_nt(q, wk_ref[...]) for q in queries] + [dot_nt(c, wv_ref[...]) for c in ctxs]
+    vectors.append(dot_nt(grad_query, wq_ref[...]))
+    fold_row = lax.broadcasted_iota(jnp.int32, (rows, length), 0)
+    fold_col = lax.broadcasted_iota(jnp.int32, (rows, length), 1)
+    fold = (fold_row % length == fold_col).astype(BF16)
+    shares = [dot(c, fold) for c in raws + [p.astype(BF16) for p in probs] + [picks]]
+    kinds = len(vectors)
+    vectors = jnp.concatenate(vectors, axis=0).astype(BF16)
+    shares = jnp.concatenate(shares, axis=0).astype(BF16)
+    slots = parcels_ref.shape[0] // count
+    out_row = lax.broadcasted_iota(jnp.int32, (count * slots, kinds * RESP), 0)
+    source = lax.broadcasted_iota(jnp.int32, (count * slots, kinds * RESP), 1)
+    owner, slot = out_row // slots, out_row % slots
+    choose = ((slot == source // RESP) & (owner // (length // own) == source % RESP)).astype(BF16)
+    parcels_ref[:, :feats] = dot(choose, vectors).astype(BF16)
+    chosen = dot(choose, shares)
+    half = (lax.broadcasted_iota(jnp.int32, (count * slots, own), 0) // slots) % (length // own)
+    part = jnp.zeros((count * slots, own), F32)
+    for i in range(length // own):
+        part = jnp.where(half == i, chosen[:, i * own : (i + 1) * own], part)
+    tail = jnp.zeros((count * slots, 128 - own), F32)
+    parcels_ref[:, feats:] = jnp.concatenate([part, tail], axis=1).astype(BF16)
+
+
+def scored_part(positions, row_grads, qkv, weights, count, length):
+    feats = row_grads.shape[1]
+    vmem = pl.BlockSpec(memory_space=pltpu.VMEM)
+    slots = 8
+    parcels = pl.pallas_call(
+        functools.partial(scored_kernel, count, length),
+        out_shape=jax.ShapeDtypeStruct((count * slots, feats + 128), BF16),
+        in_specs=[vmem] * 7,
+        out_specs=vmem,
+        compiler_params=pltpu.CompilerParams(vmem_limit_bytes=VMEM_LIMIT),
+        name="scored_backward",
+    )(positions, row_grads, qkv, *weights)
+    parcels = lax.all_to_all(parcels.reshape(count, slots, -1), "tensor", 0, 0)
+    parcels = parcels.reshape(count * slots, -1)
+    own = qkv.shape[0] // count
+    return dot_tn(parcels[:, feats : feats + own], parcels[:, :feats])
 
 
 def rank_grad(reward_scores, rankings):
@@ -223,47 +294,36 @@
     return jnp.sum(order_hot * grad_order[:, None], axis=0)
 
 
-def gather_ring(block, sections):
+def gather_ring(block):
     count = lax.axis_size("tensor")
     blocks, offsets = [block], [(0,)]
     up = down = block
     for step in range(1, count // 2 + 1):
-        up = shift(up, 1, sections)
+        up = shift(up, 1)
         blocks.append(up)
         offsets.append((-step,))
         if step < count - count // 2:
-            down = shift(down, -1, sections)
+            down = shift(down, -1)
             blocks.append(down)
             offsets.append((step,))
     return blocks, offsets
 
 
-def gather_hops(block, sections):
-    own = block.shape[0]
-    far = jnp.concatenate([block, shift(block, 5, sections), shift(block, -5, sections)])
-    left, right = shift(far, 1, sections), shift(far, -1, sections)
-    left_on, right_on = shift(left, 1, sections), shift(right, -1, sections)
-    across = shift(right[2 * own :], -2, sections)
-    blocks = [far, left, right, left_on, right_on, across]
-    offsets = [(0, -5, 5), (-1, -6, 4), (1, -4, 6), (-2, -7, 3), (2, -3, 7), (8,)]
-    return blocks, offsets
-
-
-def scatter_ring(terms):
+def scatter_ring(terms, sections):
     count = lax.axis_size("tensor")
     half = count // 2
     up = terms[half]
     down = terms[-(count - half - 1)]
     for step in range(half):
         left = half - step - 1
-        up = shift(up, 1)
+        up = shift(up, 1, sections)
         if left:
             up = (up.astype(F32) + terms[left].astype(F32)).astype(BF16)
         if left:
-            down = shift(down, -1)
+            down = shift(down, -1, sections)
             if left > 1:
                 down = (down.astype(F32) + terms[1 - left].astype(F32)).astype(BF16)
-    return up, down
+    return terms[0].astype(F32) + up.astype(F32) + down.astype(F32)
 
 
 def sum_rows(value, sections):
@@ -298,20 +358,21 @@
     at_end = lax.axis_index("section") == lax.axis_size("section") - 1
     positions = jnp.arange(RESP) * length + lengths[0] - 1
     places = positions[:, None].astype(jnp.int32)
-    me = jnp.stack([tensor_pos, at_end.astype(jnp.int32)])
+    me = tensor_pos[None].astype(jnp.int32)
 
     later_all = lax.all_gather(later_own, "tensor", axis=0, tiled=True)
     last = lax.axis_size("section") - 1
-
-    def forward(blocks, offsets):
-        return forward_part(me, places, attn_gain, weights, blocks, offsets, length)
-
-    def inner_section(x_own):
-        qkv, mixed, rows_part = forward(*gather_ring(x_own, range(last)))
-        return qkv, mixed, rows_part
-
-    def last_section(x_own):
-        qkv, mixed, rows_part = forward(*gather_hops(x_own, [last]))
+    blocks, offsets = gather_ring(x_own)
+    qkv, mixed, rows_part = forward_part(me, places, attn_gain, weights, blocks, offsets, length)
+    mixed_own = lax.psum_scatter(mixed, "tensor", scatter_dimension=0, tiled=True)
+
+    def inner_section(later_all, qkv, rows_part):
+        far = tensor_count // 2
+        back_offsets = list(range(far + 1 - tensor_count, far + 1))
+        back = backward_part(me, later_all, qkv, weights, back_offsets, length)
+        return scatter_ring(dict(zip(back_offsets, back)), range(last)), jnp.zeros_like(rows_part)
+
+    def last_section(later_all, qkv, rows_part):
         rows_hidden = sum_rows(rows_part, [last]).astype(BF16).astype(F32)
         inv_norm = inv_rms(rows_hidden)
         head_vec = final_gain.astype(F32) * reward_head.astype(F32)
@@ -320,18 +381,12 @@
         row_grads = inv_norm * scaled - rows_hidden * inv_norm**3 * jnp.mean(
             scaled * rows_hidden, axis=-1, keepdims=True
         )
-        return qkv, mixed, row_grads.astype(BF16).astype(F32)
-
-    qkv, mixed, row_grads = lax.cond(at_end, last_section, inner_section, x_own)
-    mixed_own = lax.psum_scatter(mixed, "tensor", scatter_dimension=0, tiled=True)
-
-    back_offsets = list(range(-(tensor_count - tensor_count // 2 - 1), tensor_count // 2 + 1))
-    back = backward_part(
-        me, places, row_grads, later_all, qkv, weights, back_offsets, length
+        row_grads = row_grads.astype(BF16).astype(F32)
+        return scored_part(places, row_grads, qkv, weights, tensor_count, length), row_grads
+
+    back_own, row_grads = lax.cond(
+        at_end, last_section, inner_section, later_all, qkv, rows_part
     )
-    terms = dict(zip(back_offsets, back))
-    up, down = scatter_ring(terms)
-    back_own = terms[0].astype(F32) + up.astype(F32) + down.astype(F32)
 
     own_rows = tensor_pos * own_count + jnp.arange(own_count)
     own_picks = (own_rows[:, None] == positions[None, :]).astype(F32)

time: 225 us -> 212 us (0.942)
  the two profiles are of different devices: /device:TPU:151 before, /device:TPU:30 now
where the time goes in v3:
time: 212 us; the launch traced here: 211 us
  starting transfers between devices  117 us (55%)
  waiting for transfers between devices  57.7 us (27%)
  between operations  14.3 us (7%)
  Pallas kernels  12.3 us (6%)
  local copies, waits for them, and re-layouts  5.73 us (3%)
  other arithmetic  3.78 us (2%)
    ppermute x30, starting transfers between devices, shift(): return lax.ppermute(value, ('section', 'tensor'), pairs)  113 us
    ppermute x30, waiting for transfers between devices, shift(): return lax.ppermute(value, ('section', 'tensor'), pairs)  52.9 us
    pallas_call x1, Pallas kernels, forward_part(): pl.pallas_call(functools.partial(forward_kernel, offsets, length), out_sh...  6.66 us
    pallas_call x1, Pallas kernels, backward_part(): pl.pallas_call(functools.partial(backward_kernel, offsets, length), out_s...  5.68 us
    ppermute x2, starting transfers between devices, from_behind(): lax.ppermute(value, 'section', [(i, i + steps) for i in range(leading, la...  4.33 us
    unnamed x26, local copies, waits for them, and re-layouts  4.28 us
  transfers between devices with their start and end apart: 34, of which 26 were waited for; matrix products, arithmetic and copies ran while one was open for 2% of the time, Pallas kernels for 6%

profile of v3, /device:TPU:30, one launch (start us, length us, event | category | flops | bytes accessed | tf_op | source)
XLA Modules:
  0.0 211.2 jit_solution(2511031542299638351)
XLA Ops:
  7.9 3.8 %collective-permute-start.19 = (bf16[32,2304]{1,0:T(8,128)(2,1)}, bf16[32,2304]{1,0:T(8,128)(2,1)S(1)}, u32[]{:S(2)}, u32[]{:S(2)}) collective-permute-start(bf16[32,2304]{1,0:T(8,128)(2,1)} %bitcast.23), channel_id=1, source_target_pairs={{0,1},{1,2},{2,3},{3,4},{4,5},{5,6},{6,7},{7,8},{8,9},{9,10},{10,1... | collective-permute-start | bytes 442376 | tf_op jit(solution)/shard_map/ppermute | solution.py:27
  11.8 9.5 %collective-permute-start.20 = (bf16[32,2304]{1,0:T(8,128)(2,1)}, bf16[32,2304]{1,0:T(8,128)(2,1)S(1)}, u32[]{:S(2)}, u32[]{:S(2)}) collective-permute-start(bf16[32,2304]{1,0:T(8,128)(2,1)} %bitcast.24), channel_id=1, source_target_pairs={{0,15},{1,0},{2,1},{3,2},{4,3},{5,4},{6,5},{7,6},{8,7},{9,8},{10,9... | collective-permute-start | bytes 442376 | tf_op jit(solution)/shard_map/ppermute | solution.py:27
  21.3 2.1 collective-permute-done.19.refs_1_
  23.4 1.9 collective-permute-start.21
  25.3 5.1 %collective-permute-start.22 = (bf16[32,2304]{1,0:T(8,128)(2,1)S(1)}, bf16[32,2304]{1,0:T(8,128)(2,1)S(1)}, u32[]{:S(2)}, u32[]{:S(2)}) collective-permute-start(bf16[32,2304]{1,0:T(8,128)(2,1)S(1)} %collective-permute-done.20.refs_2_), channel_id=1, source_target_pairs={{0,15},{1,0},{2,1},{3,2},{4,3},{5,4},{6,5},{7,6},{8,7},{9,8},{10,9... | collective-permute-start | bytes 442376 | tf_op jit(solution)/shard_map/ppermute | solution.py:27
  31.6 1.9 collective-permute-start.23
  34.3 5.6 %collective-permute-start.24 = (bf16[32,2304]{1,0:T(8,128)(2,1)S(1)}, bf16[32,2304]{1,0:T(8,128)(2,1)S(1)}, u32[]{:S(2)}, u32[]{:S(2)}) collective-permute-start(bf16[32,2304]{1,0:T(8,128)(2,1)S(1)} %collective-permute-done.22.refs_4_), channel_id=1, source_target_pairs={{0,15},{1,0},{2,1},{3,2},{4,3},{5,4},{6,5},{7,6},{8,7},{9,8},{10,9... | collective-permute-start | bytes 442376 | tf_op jit(solution)/shard_map/ppermute | solution.py:27
  41.6 1.9 collective-permute-start.25
  44.7 5.6 %collective-permute-start.26 = (bf16[32,2304]{1,0:T(8,128)(2,1)S(1)}, bf16[32,2304]{1,0:T(8,128)(2,1)S(1)}, u32[]{:S(2)}, u32[]{:S(2)}) collective-permute-start(bf16[32,2304]{1,0:T(8,128)(2,1)S(1)} %collective-permute-done.24.refs_6_), channel_id=1, source_target_pairs={{0,15},{1,0},{2,1},{3,2},{4,3},{5,4},{6,5},{7,6},{8,7},{9,8},{10,9... | collective-permute-start | bytes 442376 | tf_op jit(solution)/shard_map/ppermute | solution.py:27
  50.5 1.9 collective-permute-start.27
  53.8 5.6 %collective-permute-start.28 = (bf16[32,2304]{1,0:T(8,128)(2,1)S(1)}, bf16[32,2304]{1,0:T(8,128)(2,1)S(1)}, u32[]{:S(2)}, u32[]{:S(2)}) collective-permute-start(bf16[32,2304]{1,0:T(8,128)(2,1)S(1)} %collective-permute-done.26.refs_8_), channel_id=1, source_target_pairs={{0,15},{1,0},{2,1},{3,2},{4,3},{5,4},{6,5},{7,6},{8,7},{9,8},{10,9... | collective-permute-start | bytes 442376 | tf_op jit(solution)/shard_map/ppermute | solution.py:27
  59.8 1.9 collective-permute-start.29
  61.7 1.7 collective-permute-done.28.refs_10_
  63.4 5.6 %collective-permute-start.30 = (bf16[32,2304]{1,0:T(8,128)(2,1)S(1)}, bf16[32,2304]{1,0:T(8,128)(2,1)S(1)}, u32[]{:S(2)}, u32[]{:S(2)}) collective-permute-start(bf16[32,2304]{1,0:T(8,128)(2,1)S(1)} %collective-permute-done.28.refs_10_), channel_id=1, source_target_pairs={{0,15},{1,0},{2,1},{3,2},{4,3},{5,4},{6,5},{7,6},{8,7},{9,8},{10,9... | collective-permute-start | bytes 442376 | tf_op jit(solution)/shard_map/ppermute | solution.py:27
  69.8 1.9 collective-permute-start.31
  73.0 5.6 %collective-permute-start.32 = (bf16[32,2304]{1,0:T(8,128)(2,1)S(1)}, bf16[32,2304]{1,0:T(8,128)(2,1)S(1)}, u32[]{:S(2)}, u32[]{:S(2)}) collective-permute-start(bf16[32,2304]{1,0:T(8,128)(2,1)S(1)} %collective-permute-done.30.refs_12_), channel_id=1, source_target_pairs={{0,15},{1,0},{2,1},{3,2},{4,3},{5,4},{6,5},{7,6},{8,7},{9,8},{10,9... | collective-permute-start | bytes 442376 | tf_op jit(solution)/shard_map/ppermute | solution.py:27
  79.7 1.9 collective-permute-start.33
  81.7 6.8 %collective-permute-done.33.refs_15_ = bf16[32,2304]{1,0:T(8,128)(2,1)S(1)} collective-permute-done((bf16[32,2304]{1,0:T(8,128)(2,1)S(1)}, bf16[32,2304]{1,0:T(8,128)(2,1)S(1)}, u32[]{:S(2)}, u32[]{:S(2)}) %collective-permute-start.33) | collective-permute-done | bytes 147488 | tf_op jit(solution)/shard_map/ppermute | solution.py:27
  90.2 6.7 %layer_forward.1 = (bf16[512,512]{1,0:T(8,128)(2,1)}, bf16[512,2304]{1,0:T(8,128)(2,1)}, f32[8,2304]{1,0:T(8,128)S(1)}) custom-call(s32[1]{0:T(128)} %bitcast.4.me_ref, s32[8,1]{1,0:T(8,128)S(1)} %add_add_fusion.positions_ref, bf16[1,2304]{1,0:T(2,128)(2,1)S(1)} %copy-done.2, bf16[2304,256]{1,0:T(8,128)(2,1)} %bitcast.26, bf16[2304,128]{1,0:T(8,128)(2,1)} %bitcast.32, ...), custom_call_target="tpu_custom_call" | custom-call | tf_op jit(solution)/shard_map/layer_forward/pallas_call | solution.py:122
  98.5 93.0 %conditional.1 = (f32[32,2304]{1,0:T(8,128)S(1)}, f32[8,2304]{1,0:T(8,128)}) conditional(s32[]{:T(128)} %convert_element_type.177, (s32[1]{0:T(128)}, bf16[512,2304]{1,0:T(8,128)(2,1)}, bf16[512,512]{1,0:T(8,128)(2,1)}, bf16[2304,256]{1,0:T(8,128)(2,1)S(1)}, bf16[2304,128]{1,0:T(8,128)(2,1)S(1)}, /*index=5*/bf16[2304,128]{1,0:T(8,128)(2,1)}, ...), branch_computations={%region_1.0_spmd, %region_2.0_spmd} | conditional | flops 19324432 | bytes 15409772 | solution.py:387
  98.5 5.7 %layer_backward.1 = (bf16[32,2304]{1,0:T(8,128)(2,1)S(1)}, bf16[32,2304]{1,0:T(8,128)(2,1)S(1)}, bf16[32,2304]{1,0:T(8,128)(2,1)S(1)}, bf16[32,2304]{1,0:T(8,128...) custom-call(s32[1]{0:T(128)} %get-tuple-element.34.me_ref, ...), custom_call_target="tpu_custom_call" | custom-call | tf_op jit(solution)/shard_map/cond/branch_0_fun/layer_backward/pallas_call | solution.py:197
  104.2 1.9 collective-permute-start
  106.1 5.1 %collective-permute-start.8 = (bf16[32,2304]{1,0:T(8,128)(2,1)S(1)}, bf16[32,2304]{1,0:T(8,128)(2,1)S(1)}, u32[]{:S(2)}, u32[]{:S(2)}) collective-permute-start(bf16[32,2304]{1,0:T(8,128)(2,1)S(1)} %get-tuple-element.50), channel_id=1, source_target_pairs={{0,15},{1,0},{2,1},{3,2},{4,3},{5,4},{6,5},{7,6},{8,7},{9,8},{10,9... | collective-permute-start | bytes 442376 | tf_op jit(solution)/shard_map/cond/branch_0_fun/ppermute | solution.py:27
  111.3 2.6 %collective-permute-done = bf16[32,2304]{1,0:T(8,128)(2,1)S(1)} collective-permute-done((bf16[32,2304]{1,0:T(8,128)(2,1)S(1)}, bf16[32,2304]{1,0:T(8,128)(2,1)S(1)}, u32[]{:S(2)}, u32[]{:S(2)}) %collective-permute-start) | collective-permute-done | bytes 147488 | tf_op jit(solution)/shard_map/cond/branch_0_fun/ppermute | solution.py:27
  113.9 2.4 %collective-permute-start.1 = (bf16[32,2304]{1,0:T(8,128)(2,1)S(1)}, bf16[32,2304]{1,0:T(8,128)(2,1)S(1)}, u32[]{:S(2)}, u32[]{:S(2)}) collective-permute-start(bf16[32,2304]{1,0:T(8,128)(2,1)S(1)} %add_convert_fusion.12), channel_id=1, source_target_pairs={{0,1},{1,2},{2,3},{3,4},{4,5},{5,6},{6,7},{7,8},{8,9},{9,10},{10,1... | collective-permute-start | bytes 442376 | tf_op jit(solution)/shard_map/cond/branch_0_fun/ppermute | solution.py:27
  116.3 4.7 %collective-permute-start.9 = (bf16[32,2304]{1,0:T(8,128)(2,1)S(1)}, bf16[32,2304]{1,0:T(8,128)(2,1)S(1)}, u32[]{:S(2)}, u32[]{:S(2)}) collective-permute-start(bf16[32,2304]{1,0:T(8,128)(2,1)S(1)} %add_convert_fusion.5), channel_id=1, source_target_pairs={{0,15},{1,0},{2,1},{3,2},{4,3},{5,4},{6,5},{7,6},{8,7},{9,8},{10,9... | collective-permute-start | bytes 442376 | tf_op jit(solution)/shard_map/cond/branch_0_fun/ppermute | solution.py:27
  121.0 2.7 %collective-permute-done.1 = bf16[32,2304]{1,0:T(8,128)(2,1)S(1)} collective-permute-done((bf16[32,2304]{1,0:T(8,128)(2,1)S(1)}, bf16[32,2304]{1,0:T(8,128)(2,1)S(1)}, u32[]{:S(2)}, u32[]{:S(2)}) %collective-permute-start.1) | collective-permute-done | bytes 147488 | tf_op jit(solution)/shard_map/cond/branch_0_fun/ppermute | solution.py:27
  123.8 1.9 collective-permute-start.2
  125.7 3.0 %collective-permute-done.9 = bf16[32,2304]{1,0:T(8,128)(2,1)S(1)} collective-permute-done((bf16[32,2304]{1,0:T(8,128)(2,1)S(1)}, bf16[32,2304]{1,0:T(8,128)(2,1)S(1)}, u32[]{:S(2)}, u32[]{:S(2)}) %collective-permute-start.9) | collective-permute-done | bytes 147488 | tf_op jit(solution)/shard_map/cond/branch_0_fun/ppermute | solution.py:27
  128.7 6.0 %collective-permute-start.10 = (bf16[32,2304]{1,0:T(8,128)(2,1)S(1)}, bf16[32,2304]{1,0:T(8,128)(2,1)S(1)}, u32[]{:S(2)}, u32[]{:S(2)}) collective-permute-start(bf16[32,2304]{1,0:T(8,128)(2,1)S(1)} %add_convert_fusion.4), channel_id=1, source_target_pairs={{0,15},{1,0},{2,1},{3,2},{4,3},{5,4},{6,5},{7,6},{8,7},{9,8},{10,9... | collective-permute-start | bytes 442376 | tf_op jit(solution)/shard_map/cond/branch_0_fun/ppermute | solution.py:27
  134.8 1.9 collective-permute-start.3
  136.7 2.0 collective-permute-done.10
  138.8 5.6 %collective-permute-start.11 = (bf16[32,2304]{1,0:T(8,128)(2,1)S(1)}, bf16[32,2304]{1,0:T(8,128)(2,1)S(1)}, u32[]{:S(2)}, u32[]{:S(2)}) collective-permute-start(bf16[32,2304]{1,0:T(8,128)(2,1)S(1)} %add_convert_fusion.3), channel_id=1, source_target_pairs={{0,15},{1,0},{2,1},{3,2},{4,3},{5,4},{6,5},{7,6},{8,7},{9,8},{10,9... | collective-permute-start | bytes 442376 | tf_op jit(solution)/shard_map/cond/branch_0_fun/ppermute | solution.py:27
  144.4 1.9 collective-permute-start.4
  147.5 5.6 %collective-permute-start.12 = (bf16[32,2304]{1,0:T(8,128)(2,1)S(1)}, bf16[32,2304]{1,0:T(8,128)(2,1)S(1)}, u32[]{:S(2)}, u32[]{:S(2)}) collective-permute-start(bf16[32,2304]{1,0:T(8,128)(2,1)S(1)} %add_convert_fusion.2), channel_id=1, source_target_pairs={{0,15},{1,0},{2,1},{3,2},{4,3},{5,4},{6,5},{7,6},{8,7},{9,8},{10,9... | collective-permute-start | bytes 442376 | tf_op jit(solution)/shard_map/cond/branch_0_fun/ppermute | solution.py:27
  153.1 8.4 %collective-permute-done.4 = bf16[32,2304]{1,0:T(8,128)(2,1)S(1)} collective-permute-done((bf16[32,2304]{1,0:T(8,128)(2,1)S(1)}, bf16[32,2304]{1,0:T(8,128)(2,1)S(1)}, u32[]{:S(2)}, u32[]{:S(2)}) %collective-permute-start.4) | collective-permute-done | bytes 147488 | tf_op jit(solution)/shard_map/cond/branch_0_fun/ppermute | solution.py:27
  161.5 1.9 collective-permute-start.5
  163.4 3.2 %collective-permute-done.12 = bf16[32,2304]{1,0:T(8,128)(2,1)S(1)} collective-permute-done((bf16[32,2304]{1,0:T(8,128)(2,1)S(1)}, bf16[32,2304]{1,0:T(8,128)(2,1)S(1)}, u32[]{:S(2)}, u32[]{:S(2)}) %collective-permute-start.12) | collective-permute-done | bytes 147488 | tf_op jit(solution)/shard_map/cond/branch_0_fun/ppermute | solution.py:27
  166.7 5.0 %collective-permute-start.13 = (bf16[32,2304]{1,0:T(8,128)(2,1)S(1)}, bf16[32,2304]{1,0:T(8,128)(2,1)S(1)}, u32[]{:S(2)}, u32[]{:S(2)}) collective-permute-start(bf16[32,2304]{1,0:T(8,128)(2,1)S(1)} %add_convert_fusion.1), channel_id=1, source_target_pairs={{0,15},{1,0},{2,1},{3,2},{4,3},{5,4},{6,5},{7,6},{8,7},{9,8},{10,9... | collective-permute-start | bytes 442376 | tf_op jit(solution)/shard_map/cond/branch_0_fun/ppermute | solution.py:27
  171.6 2.4 %collective-permute-done.5 = bf16[32,2304]{1,0:T(8,128)(2,1)S(1)} collective-permute-done((bf16[32,2304]{1,0:T(8,128)(2,1)S(1)}, bf16[32,2304]{1,0:T(8,128)(2,1)S(1)}, u32[]{:S(2)}, u32[]{:S(2)}) %collective-permute-start.5) | collective-permute-done | bytes 147488 | tf_op jit(solution)/shard_map/cond/branch_0_fun/ppermute | solution.py:27
  174.1 1.9 collective-permute-start.6
  176.0 5.1 %collective-permute-start.14 = (bf16[32,2304]{1,0:T(8,128)(2,1)S(1)}, bf16[32,2304]{1,0:T(8,128)(2,1)S(1)}, u32[]{:S(2)}, u32[]{:S(2)}) collective-permute-start(bf16[32,2304]{1,0:T(8,128)(2,1)S(1)} %add_convert_fusion), channel_id=1, source_target_pairs={{0,15},{1,0},{2,1},{3,2},{4,3},{5,4},{6,5},{7,6},{8,7},{9,8},{10,9... | collective-permute-start | bytes 442376 | tf_op jit(solution)/shard_map/cond/branch_0_fun/ppermute | solution.py:27
  182.5 1.9 collective-permute-start.7
  184.4 6.3 %collective-permute-done.7 = bf16[32,2304]{1,0:T(8,128)(2,1)S(1)} collective-permute-done((bf16[32,2304]{1,0:T(8,128)(2,1)S(1)}, bf16[32,2304]{1,0:T(8,128)(2,1)S(1)}, u32[]{:S(2)}, u32[]{:S(2)}) %collective-permute-start.7) | collective-permute-done | bytes 147488 | tf_op jit(solution)/shard_map/cond/branch_0_fun/ppermute | solution.py:27
  191.6 1.9 multiply_reduce_fusion
  194.6 1.9 collective-permute-start.35
  196.5 2.4 %collective-permute-start.34 = (bf16[32,2304]{1,0:T(8,128)(2,1)S(1)}, bf16[32,2304]{1,0:T(8,128)(2,1)S(1)}, u32[]{:S(2)}, u32[]{:S(2)}) collective-permute-start(bf16[32,2304]{1,0:T(8,128)(2,1)S(1)} %get-tuple-element.92), channel_id=1, source_target_pairs={{0,16},{16,32},{32,48},{48,64},{64,80},{80,96},{96,112},{112,128},... | collective-permute-start | bytes 442376 | tf_op jit(solution)/shard_map/ppermute | solution.py:33
  199.2 3.8 %collective-permute-done.34 = bf16[32,2304]{1,0:T(8,128)(2,1)S(1)} collective-permute-done((bf16[32,2304]{1,0:T(8,128)(2,1)S(1)}, bf16[32,2304]{1,0:T(8,128)(2,1)S(1)}, u32[]{:S(2)}, u32[]{:S(2)}) %collective-permute-start.34) | collective-permute-done | bytes 147488 | tf_op jit(solution)/shard_map/ppermute | solution.py:33
  (77 shorter events, 20.3 us)
Async XLA Ops:
  7.2 90.4 %all-gather.3.cloned.1.call-start = ((), (), s32[]{:S(2)}) async-start(), calls=%async_computation.3 | async-start | bytes 2506752 | tf_op jit(solution)/shard_map/all_gather | solution.py:363
  7.9 185.7 %reduce-scatter.2.cloned.1.call-start = ((), (), s32[]{:S(2)}) async-start(), calls=%async_computation.2 | async-start | bytes 2506752 | tf_op jit(solution)/shard_map/reduce_scatter | solution.py:367
  7.9 15.5 %collective-permute-start.19 = (bf16[32,2304]{1,0:T(8,128)(2,1)}, bf16[32,2304]{1,0:T(8,128)(2,1)S(1)}, u32[]{:S(2)}, u32[]{:S(2)}) collective-permute-start(bf16[32,2304]{1,0:T(8,128)(2,1)} %bitcast.23), channel_id=1, source_target_pairs={{0,1},{1,2},{2,3},{3,4},{4,5},{5,6},{6,7},{7,8},{8,9},{9,10},{10,1... | collective-permute-start | bytes 442376 | tf_op jit(solution)/shard_map/ppermute | solution.py:27
  11.8 13.5 %collective-permute-start.20 = (bf16[32,2304]{1,0:T(8,128)(2,1)}, bf16[32,2304]{1,0:T(8,128)(2,1)S(1)}, u32[]{:S(2)}, u32[]{:S(2)}) collective-permute-start(bf16[32,2304]{1,0:T(8,128)(2,1)} %bitcast.24), channel_id=1, source_target_pairs={{0,15},{1,0},{2,1},{3,2},{4,3},{5,4},{6,5},{7,6},{8,7},{9,8},{10,9... | collective-permute-start | bytes 442376 | tf_op jit(solution)/shard_map/ppermute | solution.py:27
  23.4 8.2 %collective-permute-start.21 = (bf16[32,2304]{1,0:T(8,128)(2,1)S(1)}, bf16[32,2304]{1,0:T(8,128)(2,1)S(1)}, u32[]{:S(2)}, u32[]{:S(2)}) collective-permute-start(bf16[32,2304]{1,0:T(8,128)(2,1)S(1)} %collective-permute-done.19.refs_1_), channel_id=1, source_target_pairs={{0,1},{1,2},{2,3},{3,4},{4,5},{5,6},{6,7},{7,8},{8,9},{9,10},{10,1... | collective-permute-start | bytes 442376 | tf_op jit(solution)/shard_map/ppermute | solution.py:27
  25.3 9.0 %collective-permute-start.22 = (bf16[32,2304]{1,0:T(8,128)(2,1)S(1)}, bf16[32,2304]{1,0:T(8,128)(2,1)S(1)}, u32[]{:S(2)}, u32[]{:S(2)}) collective-permute-start(bf16[32,2304]{1,0:T(8,128)(2,1)S(1)} %collective-permute-done.20.refs_2_), channel_id=1, source_target_pairs={{0,15},{1,0},{2,1},{3,2},{4,3},{5,4},{6,5},{7,6},{8,7},{9,8},{10,9... | collective-permute-start | bytes 442376 | tf_op jit(solution)/shard_map/ppermute | solution.py:27
  31.6 10.0 %collective-permute-start.23 = (bf16[32,2304]{1,0:T(8,128)(2,1)S(1)}, bf16[32,2304]{1,0:T(8,128)(2,1)S(1)}, u32[]{:S(2)}, u32[]{:S(2)}) collective-permute-start(bf16[32,2304]{1,0:T(8,128)(2,1)S(1)} %collective-permute-done.21.refs_3_), channel_id=1, source_target_pairs={{0,1},{1,2},{2,3},{3,4},{4,5},{5,6},{6,7},{7,8},{8,9},{9,10},{10,1... | collective-permute-start | bytes 442376 | tf_op jit(solution)/shard_map/ppermute | solution.py:27
  34.3 10.4 %collective-permute-start.24 = (bf16[32,2304]{1,0:T(8,128)(2,1)S(1)}, bf16[32,2304]{1,0:T(8,128)(2,1)S(1)}, u32[]{:S(2)}, u32[]{:S(2)}) collective-permute-start(bf16[32,2304]{1,0:T(8,128)(2,1)S(1)} %collective-permute-done.22.refs_4_), channel_id=1, source_target_pairs={{0,15},{1,0},{2,1},{3,2},{4,3},{5,4},{6,5},{7,6},{8,7},{9,8},{10,9... | collective-permute-start | bytes 442376 | tf_op jit(solution)/shard_map/ppermute | solution.py:27
  41.6 8.8 %collective-permute-start.25 = (bf16[32,2304]{1,0:T(8,128)(2,1)S(1)}, bf16[32,2304]{1,0:T(8,128)(2,1)S(1)}, u32[]{:S(2)}, u32[]{:S(2)}) collective-permute-start(bf16[32,2304]{1,0:T(8,128)(2,1)S(1)} %collective-permute-done.23.refs_5_), channel_id=1, source_target_pairs={{0,1},{1,2},{2,3},{3,4},{4,5},{5,6},{6,7},{7,8},{8,9},{9,10},{10,1... | collective-permute-start | bytes 442376 | tf_op jit(solution)/shard_map/ppermute | solution.py:27
  44.7 9.1 %collective-permute-start.26 = (bf16[32,2304]{1,0:T(8,128)(2,1)S(1)}, bf16[32,2304]{1,0:T(8,128)(2,1)S(1)}, u32[]{:S(2)}, u32[]{:S(2)}) collective-permute-start(bf16[32,2304]{1,0:T(8,128)(2,1)S(1)} %collective-permute-done.24.refs_6_), channel_id=1, source_target_pairs={{0,15},{1,0},{2,1},{3,2},{4,3},{5,4},{6,5},{7,6},{8,7},{9,8},{10,9... | collective-permute-start | bytes 442376 | tf_op jit(solution)/shard_map/ppermute | solution.py:27
  50.5 9.3 %collective-permute-start.27 = (bf16[32,2304]{1,0:T(8,128)(2,1)S(1)}, bf16[32,2304]{1,0:T(8,128)(2,1)S(1)}, u32[]{:S(2)}, u32[]{:S(2)}) collective-permute-start(bf16[32,2304]{1,0:T(8,128)(2,1)S(1)} %collective-permute-done.25.refs_7_), channel_id=1, source_target_pairs={{0,1},{1,2},{2,3},{3,4},{4,5},{5,6},{6,7},{7,8},{8,9},{9,10},{10,1... | collective-permute-start | bytes 442376 | tf_op jit(solution)/shard_map/ppermute | solution.py:27
  53.8 9.6 %collective-permute-start.28 = (bf16[32,2304]{1,0:T(8,128)(2,1)S(1)}, bf16[32,2304]{1,0:T(8,128)(2,1)S(1)}, u32[]{:S(2)}, u32[]{:S(2)}) collective-permute-start(bf16[32,2304]{1,0:T(8,128)(2,1)S(1)} %collective-permute-done.26.refs_8_), channel_id=1, source_target_pairs={{0,15},{1,0},{2,1},{3,2},{4,3},{5,4},{6,5},{7,6},{8,7},{9,8},{10,9... | collective-permute-start | bytes 442376 | tf_op jit(solution)/shard_map/ppermute | solution.py:27
  59.8 10.0 %collective-permute-start.29 = (bf16[32,2304]{1,0:T(8,128)(2,1)S(1)}, bf16[32,2304]{1,0:T(8,128)(2,1)S(1)}, u32[]{:S(2)}, u32[]{:S(2)}) collective-permute-start(bf16[32,2304]{1,0:T(8,128)(2,1)S(1)} %collective-permute-done.27.refs_9_), channel_id=1, source_target_pairs={{0,1},{1,2},{2,3},{3,4},{4,5},{5,6},{6,7},{7,8},{8,9},{9,10},{10,1... | collective-permute-start | bytes 442376 | tf_op jit(solution)/shard_map/ppermute | solution.py:27
  63.4 9.6 %collective-permute-start.30 = (bf16[32,2304]{1,0:T(8,128)(2,1)S(1)}, bf16[32,2304]{1,0:T(8,128)(2,1)S(1)}, u32[]{:S(2)}, u32[]{:S(2)}) collective-permute-start(bf16[32,2304]{1,0:T(8,128)(2,1)S(1)} %collective-permute-done.28.refs_10_), channel_id=1, source_target_pairs={{0,15},{1,0},{2,1},{3,2},{4,3},{5,4},{6,5},{7,6},{8,7},{9,8},{10,9... | collective-permute-start | bytes 442376 | tf_op jit(solution)/shard_map/ppermute | solution.py:27
  69.8 9.9 %collective-permute-start.31 = (bf16[32,2304]{1,0:T(8,128)(2,1)S(1)}, bf16[32,2304]{1,0:T(8,128)(2,1)S(1)}, u32[]{:S(2)}, u32[]{:S(2)}) collective-permute-start(bf16[32,2304]{1,0:T(8,128)(2,1)S(1)} %collective-permute-done.29.refs_11_), channel_id=1, source_target_pairs={{0,1},{1,2},{2,3},{3,4},{4,5},{5,6},{6,7},{7,8},{8,9},{9,10},{10,1... | collective-permute-start | bytes 442376 | tf_op jit(solution)/shard_map/ppermute | solution.py:27
  73.0 8.7 %collective-permute-start.32 = (bf16[32,2304]{1,0:T(8,128)(2,1)S(1)}, bf16[32,2304]{1,0:T(8,128)(2,1)S(1)}, u32[]{:S(2)}, u32[]{:S(2)}) collective-permute-start(bf16[32,2304]{1,0:T(8,128)(2,1)S(1)} %collective-permute-done.30.refs_12_), channel_id=1, source_target_pairs={{0,15},{1,0},{2,1},{3,2},{4,3},{5,4},{6,5},{7,6},{8,7},{9,8},{10,9... | collective-permute-start | bytes 442376 | tf_op jit(solution)/shard_map/ppermute | solution.py:27
  79.7 8.8 %collective-permute-start.33 = (bf16[32,2304]{1,0:T(8,128)(2,1)S(1)}, bf16[32,2304]{1,0:T(8,128)(2,1)S(1)}, u32[]{:S(2)}, u32[]{:S(2)}) collective-permute-start(bf16[32,2304]{1,0:T(8,128)(2,1)S(1)} %collective-permute-done.31.refs_13_), channel_id=1, source_target_pairs={{0,1},{1,2},{2,3},{3,4},{4,5},{5,6},{6,7},{7,8},{8,9},{9,10},{10,1... | collective-permute-start | bytes 442376 | tf_op jit(solution)/shard_map/ppermute | solution.py:27
  88.5 0.9 copy-start
  89.5 0.7 copy-start.2
  90.2 6.8 %copy-start.10 = (s32[1,8]{1,0:T(1,128)S(1)}, s32[1,8]{1,0:T(1,128)}, u32[]{:S(2)}) copy-start(s32[1,8]{1,0:T(1,128)} %param.23) | copy-start | bytes 100
  90.2 7.4 %copy-start.6 = (bf16[1,2304,128]{2,1,0:T(8,128)(2,1)S(1)}, bf16[1,2304,128]{2,1,0:T(8,128)(2,1)}, u32[]{:S(2)}) copy-start(bf16[1,2304,128]{2,1,0:T(8,128)(2,1)} %param.17) | copy-start | bytes 1769476
  96.8 0.7 copy-start.3
  96.8 1.3 copy-start.4
  96.8 1.6 copy-start.5
  96.8 1.6 copy-start.8
  96.8 1.6 copy-start.9
  96.9 1.6 copy-start.11
  98.5 93.0 %copy-start.1 = (bf16[1,1,32,2304]{3,2,1,0:T(8,128)(2,1)S(1)}, bf16[1,1,32,2304]{3,2,1,0:T(8,128)(2,1)}, u32[]{:S(2)}) copy-start(bf16[1,1,32,2304]{3,2,1,0:T(8,128)(2,1)} %param.13) | copy-start | bytes 442372
  98.5 95.1 %copy-start.7 = (bf16[1,1,32,2304]{3,2,1,0:T(8,128)(2,1)S(1)}, bf16[1,1,32,2304]{3,2,1,0:T(8,128)(2,1)}, u32[]{:S(2)}) copy-start(bf16[1,1,32,2304]{3,2,1,0:T(8,128)(2,1)} %param.14) | copy-start | bytes 442372
  104.2 9.7 %collective-permute-start = (bf16[32,2304]{1,0:T(8,128)(2,1)S(1)}, bf16[32,2304]{1,0:T(8,128)(2,1)S(1)}, u32[]{:S(2)}, u32[]{:S(2)}) collective-permute-start(bf16[32,2304]{1,0:T(8,128)(2,1)S(1)} %get-tuple-element.42), channel_id=1, source_target_pairs={{0,1},{1,2},{2,3},{3,4},{4,5},{5,6},{6,7},{7,8},{8,9},{9,10},{10,1... | collective-permute-start | bytes 442376 | tf_op jit(solution)/shard_map/cond/branch_0_fun/ppermute | solution.py:27
  106.1 10.2 %collective-permute-start.8 = (bf16[32,2304]{1,0:T(8,128)(2,1)S(1)}, bf16[32,2304]{1,0:T(8,128)(2,1)S(1)}, u32[]{:S(2)}, u32[]{:S(2)}) collective-permute-start(bf16[32,2304]{1,0:T(8,128)(2,1)S(1)} %get-tuple-element.50), channel_id=1, source_target_pairs={{0,15},{1,0},{2,1},{3,2},{4,3},{5,4},{6,5},{7,6},{8,7},{9,8},{10,9... | collective-permute-start | bytes 442376 | tf_op jit(solution)/shard_map/cond/branch_0_fun/ppermute | solution.py:27
  113.9 9.8 %collective-permute-start.1 = (bf16[32,2304]{1,0:T(8,128)(2,1)S(1)}, bf16[32,2304]{1,0:T(8,128)(2,1)S(1)}, u32[]{:S(2)}, u32[]{:S(2)}) collective-permute-start(bf16[32,2304]{1,0:T(8,128)(2,1)S(1)} %add_convert_fusion.12), channel_id=1, source_target_pairs={{0,1},{1,2},{2,3},{3,4},{4,5},{5,6},{6,7},{7,8},{8,9},{9,10},{10,1... | collective-permute-start | bytes 442376 | tf_op jit(solution)/shard_map/cond/branch_0_fun/ppermute | solution.py:27
  116.3 12.4 %collective-permute-start.9 = (bf16[32,2304]{1,0:T(8,128)(2,1)S(1)}, bf16[32,2304]{1,0:T(8,128)(2,1)S(1)}, u32[]{:S(2)}, u32[]{:S(2)}) collective-permute-start(bf16[32,2304]{1,0:T(8,128)(2,1)S(1)} %add_convert_fusion.5), channel_id=1, source_target_pairs={{0,15},{1,0},{2,1},{3,2},{4,3},{5,4},{6,5},{7,6},{8,7},{9,8},{10,9... | collective-permute-start | bytes 442376 | tf_op jit(solution)/shard_map/cond/branch_0_fun/ppermute | solution.py:27
  123.8 10.9 %collective-permute-start.2 = (bf16[32,2304]{1,0:T(8,128)(2,1)S(1)}, bf16[32,2304]{1,0:T(8,128)(2,1)S(1)}, u32[]{:S(2)}, u32[]{:S(2)}) collective-permute-start(bf16[32,2304]{1,0:T(8,128)(2,1)S(1)} %add_convert_fusion.11), channel_id=1, source_target_pairs={{0,1},{1,2},{2,3},{3,4},{4,5},{5,6},{6,7},{7,8},{8,9},{9,10},{10,1... | collective-permute-start | bytes 442376 | tf_op jit(solution)/shard_map/cond/branch_0_fun/ppermute | solution.py:27
  128.7 10.0 %collective-permute-start.10 = (bf16[32,2304]{1,0:T(8,128)(2,1)S(1)}, bf16[32,2304]{1,0:T(8,128)(2,1)S(1)}, u32[]{:S(2)}, u32[]{:S(2)}) collective-permute-start(bf16[32,2304]{1,0:T(8,128)(2,1)S(1)} %add_convert_fusion.4), channel_id=1, source_target_pairs={{0,15},{1,0},{2,1},{3,2},{4,3},{5,4},{6,5},{7,6},{8,7},{9,8},{10,9... | collective-permute-start | bytes 442376 | tf_op jit(solution)/shard_map/cond/branch_0_fun/ppermute | solution.py:27
  134.8 9.6 %collective-permute-start.3 = (bf16[32,2304]{1,0:T(8,128)(2,1)S(1)}, bf16[32,2304]{1,0:T(8,128)(2,1)S(1)}, u32[]{:S(2)}, u32[]{:S(2)}) collective-permute-start(bf16[32,2304]{1,0:T(8,128)(2,1)S(1)} %add_convert_fusion.10), channel_id=1, source_target_pairs={{0,1},{1,2},{2,3},{3,4},{4,5},{5,6},{6,7},{7,8},{8,9},{9,10},{10,1... | collective-permute-start | bytes 442376 | tf_op jit(solution)/shard_map/cond/branch_0_fun/ppermute | solution.py:27
  138.8 8.6 %collective-permute-start.11 = (bf16[32,2304]{1,0:T(8,128)(2,1)S(1)}, bf16[32,2304]{1,0:T(8,128)(2,1)S(1)}, u32[]{:S(2)}, u32[]{:S(2)}) collective-permute-start(bf16[32,2304]{1,0:T(8,128)(2,1)S(1)} %add_convert_fusion.3), channel_id=1, source_target_pairs={{0,15},{1,0},{2,1},{3,2},{4,3},{5,4},{6,5},{7,6},{8,7},{9,8},{10,9... | collective-permute-start | bytes 442376 | tf_op jit(solution)/shard_map/cond/branch_0_fun/ppermute | solution.py:27
  144.4 17.0 %collective-permute-start.4 = (bf16[32,2304]{1,0:T(8,128)(2,1)S(1)}, bf16[32,2304]{1,0:T(8,128)(2,1)S(1)}, u32[]{:S(2)}, u32[]{:S(2)}) collective-permute-start(bf16[32,2304]{1,0:T(8,128)(2,1)S(1)} %add_convert_fusion.9), channel_id=1, source_target_pairs={{0,1},{1,2},{2,3},{3,4},{4,5},{5,6},{6,7},{7,8},{8,9},{9,10},{10,1... | collective-permute-start | bytes 442376 | tf_op jit(solution)/shard_map/cond/branch_0_fun/ppermute | solution.py:27
  147.5 19.2 %collective-permute-start.12 = (bf16[32,2304]{1,0:T(8,128)(2,1)S(1)}, bf16[32,2304]{1,0:T(8,128)(2,1)S(1)}, u32[]{:S(2)}, u32[]{:S(2)}) collective-permute-start(bf16[32,2304]{1,0:T(8,128)(2,1)S(1)} %add_convert_fusion.2), channel_id=1, source_target_pairs={{0,15},{1,0},{2,1},{3,2},{4,3},{5,4},{6,5},{7,6},{8,7},{9,8},{10,9... | collective-permute-start | bytes 442376 | tf_op jit(solution)/shard_map/cond/branch_0_fun/ppermute | solution.py:27
  161.5 12.5 %collective-permute-start.5 = (bf16[32,2304]{1,0:T(8,128)(2,1)S(1)}, bf16[32,2304]{1,0:T(8,128)(2,1)S(1)}, u32[]{:S(2)}, u32[]{:S(2)}) collective-permute-start(bf16[32,2304]{1,0:T(8,128)(2,1)S(1)} %add_convert_fusion.8), channel_id=1, source_target_pairs={{0,1},{1,2},{2,3},{3,4},{4,5},{5,6},{6,7},{7,8},{8,9},{9,10},{10,1... | collective-permute-start | bytes 442376 | tf_op jit(solution)/shard_map/cond/branch_0_fun/ppermute | solution.py:27
  166.7 9.3 %collective-permute-start.13 = (bf16[32,2304]{1,0:T(8,128)(2,1)S(1)}, bf16[32,2304]{1,0:T(8,128)(2,1)S(1)}, u32[]{:S(2)}, u32[]{:S(2)}) collective-permute-start(bf16[32,2304]{1,0:T(8,128)(2,1)S(1)} %add_convert_fusion.1), channel_id=1, source_target_pairs={{0,15},{1,0},{2,1},{3,2},{4,3},{5,4},{6,5},{7,6},{8,7},{9,8},{10,9... | collective-permute-start | bytes 442376 | tf_op jit(solution)/shard_map/cond/branch_0_fun/ppermute | solution.py:27
  174.1 8.4 %collective-permute-start.6 = (bf16[32,2304]{1,0:T(8,128)(2,1)S(1)}, bf16[32,2304]{1,0:T(8,128)(2,1)S(1)}, u32[]{:S(2)}, u32[]{:S(2)}) collective-permute-start(bf16[32,2304]{1,0:T(8,128)(2,1)S(1)} %add_convert_fusion.7), channel_id=1, source_target_pairs={{0,1},{1,2},{2,3},{3,4},{4,5},{5,6},{6,7},{7,8},{8,9},{9,10},{10,1... | collective-permute-start | bytes 442376 | tf_op jit(solution)/shard_map/cond/branch_0_fun/ppermute | solution.py:27
  176.0 8.4 %collective-permute-start.14 = (bf16[32,2304]{1,0:T(8,128)(2,1)S(1)}, bf16[32,2304]{1,0:T(8,128)(2,1)S(1)}, u32[]{:S(2)}, u32[]{:S(2)}) collective-permute-start(bf16[32,2304]{1,0:T(8,128)(2,1)S(1)} %add_convert_fusion), channel_id=1, source_target_pairs={{0,15},{1,0},{2,1},{3,2},{4,3},{5,4},{6,5},{7,6},{8,7},{9,8},{10,9... | collective-permute-start | bytes 442376 | tf_op jit(solution)/shard_map/cond/branch_0_fun/ppermute | solution.py:27
  182.5 8.2 %collective-permute-start.7 = (bf16[32,2304]{1,0:T(8,128)(2,1)S(1)}, bf16[32,2304]{1,0:T(8,128)(2,1)S(1)}, u32[]{:S(2)}, u32[]{:S(2)}) collective-permute-start(bf16[32,2304]{1,0:T(8,128)(2,1)S(1)} %add_convert_fusion.6), channel_id=1, source_target_pairs={{0,1},{1,2},{2,3},{3,4},{4,5},{5,6},{6,7},{7,8},{8,9},{9,10},{10,1... | collective-permute-start | bytes 442376 | tf_op jit(solution)/shard_map/cond/branch_0_fun/ppermute | solution.py:27
  194.6 4.6 %collective-permute-start.35 = (bf16[32,2304]{1,0:T(8,128)(2,1)S(1)}, bf16[32,2304]{1,0:T(8,128)(2,1)S(1)}, u32[]{:S(2)}, u32[]{:S(2)}) collective-permute-start(bf16[32,2304]{1,0:T(8,128)(2,1)S(1)} %get-tuple-element.91), channel_id=1, source_target_pairs={{16,0},{32,16},{48,32},{64,48},{80,64},{96,80},{112,96},{128,112},... | collective-permute-start | bytes 442376 | tf_op jit(solution)/shard_map/ppermute | solution.py:33
  196.5 6.5 %collective-permute-start.34 = (bf16[32,2304]{1,0:T(8,128)(2,1)S(1)}, bf16[32,2304]{1,0:T(8,128)(2,1)S(1)}, u32[]{:S(2)}, u32[]{:S(2)}) collective-permute-start(bf16[32,2304]{1,0:T(8,128)(2,1)S(1)} %get-tuple-element.92), channel_id=1, source_target_pairs={{0,16},{16,32},{32,48},{48,64},{64,80},{80,96},{96,112},{112,128},... | collective-permute-start | bytes 442376 | tf_op jit(solution)/shard_map/ppermute | solution.py:33
Sparse Core Ops, SparseCore 0:
  10.1 80.5 all-gather.2
  97.0 84.8 reduce-scatter.1

commit v4 on v3

v4 whole, which is shorter than its diff:
```python
import functools

import jax
import jax.numpy as jnp
from jax import lax
from jax.experimental import pallas as pl
from jax.experimental.pallas import tpu as pltpu
from jax.sharding import PartitionSpec as P

HEAD_DIM = 128
RESP = 8

EPSILON = 1e-06
SOFT_CAP = 50.0
QUERY_SCALE = 1.0 / 12.0
LOSS_SCALE = 64.0

F32 = jnp.float32
BF16 = jnp.bfloat16
VMEM_LIMIT = 24 * 1024 * 1024
BATCH = 8
FIRST_TERMS = 2


def shift(value, steps, sections=None):
    count = lax.axis_size("tensor")
    sections = range(lax.axis_size("section")) if sections is None else sections
    pairs = [(s * count + i, s * count + (i + steps) % count) for s in sections for i in range(count)]
    return lax.ppermute(value, ("section", "tensor"), pairs)


def from_behind(value, steps):
    count = lax.axis_size("section")
    leading, last = (max(0, -steps), min(count, count - steps))
    return lax.ppermute(value, "section", [(i, i + steps) for i in range(leading, last)])


def dot(left, right):
    return lax.dot_general(left, right, (((1,), (0,)), ((), ())), preferred_element_type=F32)


def dot_nt(left, right):
    return lax.dot_general(left, right, (((1,), (1,)), ((), ())), preferred_element_type=F32)


def dot_tn(left, right):
    return lax.dot_general(left, right, (((0,), (0,)), ((), ())), preferred_element_type=F32)


def inv_rms(values):
    return lax.rsqrt(jnp.mean(values * values, axis=-1, keepdims=True) + EPSILON)


def pair_mask(block, length):
    row = lax.broadcasted_iota(jnp.int32, (block, block), 0)
    col = lax.broadcasted_iota(jnp.int32, (block, block), 1)
    return ((row // length == col // length) & (col <= row)).astype(F32)


def row_picks(positions, rows):
    return (positions == lax.broadcasted_iota(jnp.int32, (RESP, rows), 1)).astype(BF16)


def attention(queries, keys, mask):
    raw = [dot_nt(q, k) for q, k in zip(queries, keys)]
    capped = [jnp.tanh(r * (QUERY_SCALE / SOFT_CAP)) for r in raw]
    exps = [jnp.exp(SOFT_CAP * c) * mask for c in capped]
    sums = [jnp.sum(e, axis=-1, keepdims=True) for e in exps]
    return capped, [e / s for e, s in zip(exps, sums)]


def project(me_ref, gain_ref, wq_ref, wk_ref, wv_ref, wo_ref, blocks):
    own = blocks[0].shape[0] // 2
    gain = gain_ref[...].astype(F32)
    normed = []
    for block in blocks:
        x_float = block[:own].astype(F32)
        normed.append((x_float * inv_rms(x_float) * gain).astype(BF16))
    normed = jnp.concatenate(normed, axis=0)
    w_kv = jnp.concatenate([wk_ref[...], wv_ref[...]], axis=1)
    cot = jnp.concatenate([block[own:] for block in blocks], axis=0)
    parts = [dot(normed, wq_ref[...]), dot(normed, w_kv), dot_nt(cot, wo_ref[...])]
    return [part.astype(BF16) for part in parts]


def early_kernel(gain_ref, wq_ref, wk_ref, wv_ref, wo_ref, *refs):
    blocks, out_ref = refs[:-1], refs[-1]
    own = blocks[0].shape[0] // 2
    for first in range(0, len(blocks), BATCH):
        some = blocks[first : first + BATCH]
        parts = project(None, gain_ref, wq_ref, wk_ref, wv_ref, wo_ref, some)
        rows = slice(first * own, (first + len(some)) * own)
        out_ref[rows, :] = jnp.concatenate(parts, axis=1)


def early_part(gain, weights, blocks):
    own, feats = blocks[0].shape[0] // 2, blocks[0].shape[1]
    rows, cols = own * len(blocks), sum(w.shape[1] for w in weights[:3]) + weights[3].shape[0]
    vmem = pl.BlockSpec(memory_space=pltpu.VMEM)
    return pl.pallas_call(
        early_kernel,
        out_shape=jax.ShapeDtypeStruct((rows, cols), BF16),
        in_specs=[vmem] * (5 + len(blocks)),
        out_specs=vmem,
        compiler_params=pltpu.CompilerParams(vmem_limit_bytes=VMEM_LIMIT),
        cost_estimate=pl.CostEstimate(
            flops=2 * rows * cols * feats, bytes_accessed=4 * rows * feats, transcendentals=0
        ),
        name="early_rows",
    )(gain, *weights, *blocks)


def place_all(offsets, me_ref, early_ref, late, qkv_ref, grad_ctx=None):
    count = len(offsets)
    cols = qkv_ref.shape[1]
    own = qkv_ref.shape[0] // count
    for i, offset in enumerate(offsets[:-1]):
        rows = pl.ds(place_of(me_ref, offset, count, own), own)
        qkv_ref[rows, :] = early_ref[i * own : (i + 1) * own, :cols]
        if grad_ctx is not None:
            grad_ctx[rows, :] = early_ref[i * own : (i + 1) * own, cols:]
    rows = pl.ds(place_of(me_ref, offsets[-1], count, own), own)
    qkv_ref[rows, :] = jnp.concatenate(late[:2], axis=1)
    if grad_ctx is not None:
        grad_ctx[rows, :] = late[2]


def place_of(me_ref, offset, count, own):
    return pl.multiple_of(lax.rem(me_ref[0] + (offset + count), count) * own, own)


def pairs_of(qkv_ref, length, q_cols, kv_cols):
    block = 2 * length
    spans = [slice(start, start + block) for start in range(0, qkv_ref.shape[0], block)]
    pairs = [(s, h) for s in spans for h in range(0, q_cols, HEAD_DIM)]
    queries = [qkv_ref[s, h : h + HEAD_DIM] for s, h in pairs]
    keys = [qkv_ref[s, q_cols : q_cols + kv_cols] for s, h in pairs]
    values = [qkv_ref[s, q_cols + kv_cols :] for s, h in pairs]
    return spans, pairs, queries, keys, values


def rows_kernel(
    offsets,
    length,
    me_ref,
    positions_ref,
    gain_ref,
    wq_ref,
    wk_ref,
    wv_ref,
    wo_ref,
    early_ref,
    first_ref,
    late_ref,
    qkv_ref,
    rows_ref,
    context,
):
    own = qkv_ref.shape[0] // len(offsets)
    late = project(me_ref, gain_ref, wq_ref, wk_ref, wv_ref, wo_ref, [late_ref])
    place_all(offsets, me_ref, early_ref, late, qkv_ref)
    q_cols, kv_cols = wq_ref.shape[1], wk_ref.shape[1]
    _, pairs, queries, keys, values = pairs_of(qkv_ref, length, q_cols, kv_cols)
    _, probs = attention(queries, keys, pair_mask(2 * length, length))
    for (s, h), prob, value in zip(pairs, probs, values):
        context[s, h : h + HEAD_DIM] = dot(prob.astype(BF16), value).astype(BF16)
    picks = row_picks(positions_ref[...], qkv_ref.shape[0])
    own_picks = row_picks(positions_ref[...] - me_ref[0] * own, own)
    rows_ref[...] = dot(dot(picks, context[...]).astype(BF16), wo_ref[...]) + dot(
        own_picks, first_ref[:own]
    )


def rows_part_of(me, positions, gain, weights, early, first, late, offsets, length):
    own, feats = late.shape[0] // 2, late.shape[1]
    rows = own * len(offsets)
    vmem = pl.BlockSpec(memory_space=pltpu.VMEM)
    smem = pl.BlockSpec(memory_space=pltpu.SMEM)
    cols = sum(w.shape[1] for w in weights[:3])
    return pl.pallas_call(
        functools.partial(rows_kernel, offsets, length),
        out_shape=(
            jax.ShapeDtypeStruct((rows, cols), BF16),
            jax.ShapeDtypeStruct((RESP, feats), F32),
        ),
        in_specs=[smem] + [vmem] * 9,
        out_specs=[vmem] * 2,
        scratch_shapes=[pltpu.VMEM((rows, weights[0].shape[1]), BF16)],
        compiler_params=pltpu.CompilerParams(vmem_limit_bytes=VMEM_LIMIT),
        name="scored_rows",
    )(me, positions, gain, *weights, early, first, late)


def project_back(turned, wq_ref, wk_ref, wv_ref, wo_ref, outs):
    own, feats = outs[0].shape[0] // 2, outs[0].shape[1]
    at_mix = turned.shape[1] - wo_ref.shape[0]
    for start in range(0, feats, 256):
        cols = slice(start, start + 256)
        all_w = jnp.concatenate([wq_ref[cols, :], wk_ref[cols, :], wv_ref[cols, :]], axis=1)
        back = dot_nt(turned[:, :at_mix], all_w).astype(BF16)
        mixed = dot(turned[:, at_mix:], wo_ref[:, cols]).astype(BF16)
        for j, out in enumerate(outs):
            out[:own, cols] = mixed[j * own : (j + 1) * own]
            out[own:, cols] = back[j * own : (j + 1) * own]


def layer_kernel(
    offsets,
    back_offsets,
    length,
    me_ref,
    gain_ref,
    wq_ref,
    wk_ref,
    wv_ref,
    wo_ref,
    early_ref,
    late_ref,
    *refs,
):
    count = len(offsets)
    outs, rest_ref = refs[:FIRST_TERMS], refs[FIRST_TERMS]
    qkv, grad_ctx, work, first_rows = refs[FIRST_TERMS + 1 :]
    own = late_ref.shape[0] // 2
    q_cols, kv_cols = wq_ref.shape[1], wk_ref.shape[1]
    late = project(me_ref, gain_ref, wq_ref, wk_ref, wv_ref, wo_ref, [late_ref])
    place_all(offsets, me_ref, early_ref, late, qkv, grad_ctx)
    spans, pairs, queries, keys, values = pairs_of(qkv, length, q_cols, kv_cols)
    ctxs = [grad_ctx[s, h : h + HEAD_DIM] for s, h in pairs]
    capped, probs = attention(queries, keys, pair_mask(2 * length, length))
    grad_probs = [dot_nt(c, v) for c, v in zip(ctxs, values)]
    means = [jnp.sum(p * g, axis=-1, keepdims=True) for p, g in zip(probs, grad_probs)]
    raws = [
        (p * (g - m) * (1.0 - c * c) * QUERY_SCALE).astype(BF16)
        for p, g, m, c in zip(probs, grad_probs, means, capped)
    ]
    probs = [p.astype(BF16) for p in probs]
    mixes = [dot(p, v).astype(BF16) for p, v in zip(probs, values)]
    grad_queries = [dot(r, k).astype(BF16) for r, k in zip(raws, keys)]
    grad_keys = [dot_tn(r, q) for r, q in zip(raws, queries)]
    grad_values = [dot_tn(p, c) for p, c in zip(probs, ctxs)]
    per = q_cols // HEAD_DIM
    at_keys, at_values, at_mix = q_cols, q_cols + kv_cols, q_cols + 2 * kv_cols
    for (s, h), grad_query, mix in zip(pairs, grad_queries, mixes):
        work[s, h : h + HEAD_DIM] = grad_query
        work[s, at_mix + h : at_mix + h + HEAD_DIM] = mix
    for i, s in enumerate(spans):
        work[s, at_keys:at_values] = sum(grad_keys[i * per : (i + 1) * per]).astype(BF16)
        work[s, at_values:at_mix] = sum(grad_values[i * per : (i + 1) * per]).astype(BF16)
    for i, offset in enumerate(back_offsets):
        rows = work[pl.ds(place_of(me_ref, offset, count, own), own), :]
        if i < FIRST_TERMS:
            first_rows[i * own : (i + 1) * own, :] = rows
        else:
            rest_ref[(i - FIRST_TERMS) * own : (i - FIRST_TERMS + 1) * own, :] = rows
    project_back(first_rows, wq_ref, wk_ref, wv_ref, wo_ref, outs)


def rest_kernel(wq_ref, wk_ref, wv_ref, wo_ref, rest_ref, *outs):
    project_back(rest_ref, wq_ref, wk_ref, wv_ref, wo_ref, outs)


def layer_part(me, gain, weights, early, late, offsets, back_offsets, length):
    count = len(offsets)
    own, feats = late.shape[0] // 2, late.shape[1]
    rows = own * count
    vmem = pl.BlockSpec(memory_space=pltpu.VMEM)
    smem = pl.BlockSpec(memory_space=pltpu.SMEM)
    cols = sum(w.shape[1] for w in weights[:3])
    q_cols = weights[0].shape[1]
    left = count - FIRST_TERMS
    term = jax.ShapeDtypeStruct(late.shape, BF16)
    *first, rest = pl.pallas_call(
        functools.partial(layer_kernel, offsets, back_offsets, length),
        out_shape=[term] * FIRST_TERMS + [jax.ShapeDtypeStruct((own * left, cols + q_cols), BF16)],
        in_specs=[smem] + [vmem] * 7,
        out_specs=[vmem] * (FIRST_TERMS + 1),
        scratch_shapes=[
            pltpu.VMEM((rows, cols), BF16),
            pltpu.VMEM((rows, q_cols), BF16),
            pltpu.VMEM((rows, cols + q_cols), BF16),
            pltpu.VMEM((own * FIRST_TERMS, cols + q_cols), BF16),
        ],
        compiler_params=pltpu.CompilerParams(vmem_limit_bytes=VMEM_LIMIT),
        name="layer_both_ways",
    )(me, gain, *weights, early, late)
    others = pl.pallas_call(
        rest_kernel,
        out_shape=[term] * left,
        in_specs=[vmem] * 5,
        out_specs=[vmem] * left,
        compiler_params=pltpu.CompilerParams(vmem_limit_bytes=VMEM_LIMIT),
        cost_estimate=pl.CostEstimate(
            flops=2 * rows * (cols + q_cols) * feats, bytes_accessed=0, transcendentals=0
        ),
        name="rest_of_terms",
    )(*weights, rest)
    return dict(zip(back_offsets, [*first, *others]))


def scored_kernel(
    count,
    length,
    positions_ref,
    row_grads_ref,
    qkv_ref,
    wq_ref,
    wk_ref,
    wv_ref,
    wo_ref,
    parcels_ref,
):
    rows = qkv_ref.shape[0]
    feats = wq_ref.shape[0]
    own = rows // count
    q_cols, kv_cols = wq_ref.shape[1], wk_ref.shape[1]
    positions = positions_ref[...]
    picks = row_picks(positions, rows)
    row = lax.broadcasted_iota(jnp.int32, (RESP, rows), 0)
    col = lax.broadcasted_iota(jnp.int32, (RESP, rows), 1)
    mask = ((col // length == row) & (col <= positions)).astype(F32)
    query_all = dot(picks, qkv_ref[:, :q_cols]).astype(BF16)
    ctx_all = dot_nt(row_grads_ref[...].astype(BF16), wo_ref[...]).astype(BF16)
    keys = qkv_ref[:, q_cols : q_cols + kv_cols]
    values = qkv_ref[:, q_cols + kv_cols :]
    heads = range(0, q_cols, HEAD_DIM)
    queries = [query_all[:, h : h + HEAD_DIM] for h in heads]
    ctxs = [ctx_all[:, h : h + HEAD_DIM] for h in heads]
    capped, probs = attention(queries, [keys] * len(heads), mask)
    raws = []
    for prob, cap, ctx in zip(probs, capped, ctxs):
        grad_prob = dot_nt(ctx, values)
        grad_score = prob * (grad_prob - jnp.sum(prob * grad_prob, axis=-1, keepdims=True))
        raws.append((grad_score * (1.0 - cap * cap) * QUERY_SCALE).astype(BF16))
    grad_query = jnp.concatenate([dot(raw, keys) for raw in raws], axis=1).astype(BF16)
    vectors = [dot_nt(q, wk_ref[...]) for q in queries] + [dot_nt(c, wv_ref[...]) for c in ctxs]
    vectors.append(dot_nt(grad_query, wq_ref[...]))
    fold_row = lax.broadcasted_iota(jnp.int32, (rows, length), 0)
    fold_col = lax.broadcasted_iota(jnp.int32, (rows, length), 1)
    fold = (fold_row % length == fold_col).astype(BF16)
    shares = [dot(c, fold) for c in raws + [p.astype(BF16) for p in probs] + [picks]]
    kinds = len(vectors)
    vectors = jnp.concatenate(vectors, axis=0).astype(BF16)
    shares = jnp.concatenate(shares, axis=0).astype(BF16)
    slots = parcels_ref.shape[0] // count
    out_row = lax.broadcasted_iota(jnp.int32, (count * slots, kinds * RESP), 0)
    source = lax.broadcasted_iota(jnp.int32, (count * slots, kinds * RESP), 1)
    owner, slot = out_row // slots, out_row % slots
    choose = ((slot == source // RESP) & (owner // (length // own) == source % RESP)).astype(BF16)
    share = length // own
    half = (lax.broadcasted_iota(jnp.int32, (count * slots, 1), 0) // slots) % share
    width = feats // share
    lanes = jnp.zeros((count * slots, width), F32)
    chosen = dot(choose, shares)
    part = jnp.zeros((count * slots, own), F32)
    for i in range(share):
        lanes = jnp.where(half == i, dot(choose, vectors[:, i * width : (i + 1) * width]), lanes)
        part = jnp.where(half == i, chosen[:, i * own : (i + 1) * own], part)
    parcels_ref[:, :width] = lanes.astype(BF16)
    tail = jnp.zeros((count * slots, 128 - own), F32)
    parcels_ref[:, width:] = jnp.concatenate([part, tail], axis=1).astype(BF16)


def scored_part(positions, row_grads, qkv, weights, count, length, section):
    width = row_grads.shape[1] // 2
    own = qkv.shape[0] // count
    vmem = pl.BlockSpec(memory_space=pltpu.VMEM)
    slots = 8
    parcels = pl.pallas_call(
        functools.partial(scored_kernel, count, length),
        out_shape=jax.ShapeDtypeStruct((count * slots, width + 128), BF16),
        in_specs=[vmem] * 7,
        out_specs=vmem,
        compiler_params=pltpu.CompilerParams(vmem_limit_bytes=VMEM_LIMIT),
        name="scored_backward",
    )(positions, row_grads, qkv, *weights)
    parcels = lax.all_to_all(parcels.reshape(count, slots, -1), "tensor", 0, 0)
    parcels = parcels.reshape(count * slots, -1)
    vectors, shares = parcels[:, :width], parcels[:, width : width + own]
    swaps = [(section * count + i, section * count + (i ^ 1)) for i in range(count)]
    swapped = lax.ppermute(vectors, ("section", "tensor"), swaps)
    mine, theirs = dot_tn(shares, vectors), dot_tn(shares, swapped)
    second = lax.axis_index("tensor") % 2 == 1
    return jnp.concatenate(
        [jnp.where(second, theirs, mine), jnp.where(second, mine, theirs)], axis=1
    )


def rank_grad(reward_scores, rankings):
    slots = jnp.arange(RESP)
    order_hot = (rankings[0][:, None] == slots[None, :]).astype(F32)
    ordered = jnp.sum(order_hot * reward_scores[None, :], axis=1)
    exp_order = jnp.exp(ordered)
    upper = (slots[:, None] >= slots[None, :]).astype(F32)
    suffix = jnp.sum(exp_order[:, None] * upper, axis=0)
    cumulative = jnp.sum((1.0 / suffix)[None, :] * upper, axis=1)
    grad_order = LOSS_SCALE * (exp_order * cumulative - 1.0)
    return jnp.sum(order_hot * grad_order[:, None], axis=0)


def gather_ring(block):
    count = lax.axis_size("tensor")
    blocks, offsets = [block], [0]
    up = down = block
    for step in range(1, count // 2 + 1):
        up = shift(up, 1)
        blocks.append(up)
        offsets.append(-step)
        if step < count - count // 2:
            down = shift(down, -1)
            blocks.append(down)
            offsets.append(step)
    return blocks, offsets


def scatter_ring(terms, sections):
    count = lax.axis_size("tensor")
    half = count // 2
    up = terms[half]
    down = terms[-(count - half - 1)]
    for step in range(half):
        left = half - step - 1
        up = shift(up, 1, sections)
        if left:
            up = (up.astype(F32) + terms[left].astype(F32)).astype(BF16)
        if left:
            down = shift(down, -1, sections)
            if left > 1:
                down = (down.astype(F32) + terms[1 - left].astype(F32)).astype(BF16)
    return terms[0].astype(F32) + up.astype(F32) + down.astype(F32)


def sum_rows(value, sections):
    step = 1
    while step < lax.axis_size("tensor"):
        value = value + shift(value, step, sections)
        step *= 2
    return value


def shards(
    section_inputs,
    later_grad,
    attn_gain,
    w_query,
    w_key,
    w_value,
    w_out,
    final_gain,
    reward_head,
    rankings,
    lengths,
):
    x_own = section_inputs[0, 0]
    later_own = later_grad[0, 0]
    own_count = x_own.shape[0]
    tensor_count = lax.axis_size("tensor")
    tensor_pos = lax.axis_index("tensor")
    total_rows = own_count * tensor_count
    length = total_rows // RESP
    weights = (w_query[0], w_key[0], w_value[0], w_out[0])
    at_end = lax.axis_index("section") == lax.axis_size("section") - 1
    positions = jnp.arange(RESP) * length + lengths[0] - 1
    places = positions[:, None].astype(jnp.int32)
    me = tensor_pos[None].astype(jnp.int32)

    last = lax.axis_size("section") - 1
    blocks, offsets = gather_ring(jnp.concatenate([x_own, later_own]))
    far = tensor_count // 2
    back_offsets = [far, far + 1 - tensor_count]
    back_offsets += [o for o in range(back_offsets[1] + 1, far)]
    early = early_part(attn_gain, weights, blocks[:-1])
    first, late = blocks[0], blocks[-1]

    def inner_section(early, first, late):
        terms = layer_part(me, attn_gain, weights, early, late, offsets, back_offsets, length)
        sums = scatter_ring(terms, range(last))
        return sums, jnp.zeros((RESP, x_own.shape[1]), F32)

    def last_section(early, first, late):
        qkv, rows_part = rows_part_of(
            me, places, attn_gain, weights, early, first, late, offsets, length
        )
        rows_hidden = sum_rows(rows_part, [last]).astype(BF16).astype(F32)
        inv_norm = inv_rms(rows_hidden)
        head_vec = final_gain.astype(F32) * reward_head.astype(F32)
        reward_scores = jnp.sum(rows_hidden * inv_norm * head_vec, axis=-1)
        scaled = rank_grad(reward_scores, rankings)[:, None] * head_vec
        row_grads = inv_norm * scaled - rows_hidden * inv_norm**3 * jnp.mean(
            scaled * rows_hidden, axis=-1, keepdims=True
        )
        row_grads = row_grads.astype(BF16).astype(F32)
        back_own = scored_part(
            places, row_grads, qkv, weights, tensor_count, length, last
        )
        return jnp.concatenate([jnp.zeros_like(back_own), back_own]), row_grads

    sums, row_grads = lax.cond(at_end, last_section, inner_section, early, first, late)
    mixed_own, back_own = sums[:own_count], sums[own_count:]

    own_rows = tensor_pos * own_count + jnp.arange(own_count)
    own_picks = (own_rows[:, None] == positions[None, :]).astype(F32)
    last_own = jnp.sum(own_picks[:, :, None] * row_grads[None], axis=1)
    grad_own = jnp.where(at_end, last_own, later_own.astype(F32))
    x_float = x_own.astype(F32)
    inv_x = inv_rms(x_float)
    scaled_x = back_own * attn_gain[0].astype(F32)
    grad_x = inv_x * scaled_x - x_float * inv_x**3 * jnp.mean(
        scaled_x * x_float, axis=-1, keepdims=True
    )
    returned = (grad_own + grad_x).astype(BF16)
    sent_back = from_behind(returned, -1)
    hidden = (x_float + mixed_own).astype(BF16)
    arrived = from_behind(hidden, 1)
    return (arrived[None, None], sent_back[None, None])


def solution(mesh):
    return jax.shard_map(
        shards,
        mesh=mesh,
        in_specs=(
            P("section", None, "tensor", None),
            P("section", None, "tensor", None),
            P("section", None),
            P("section", None, "tensor"),
            P("section", None, "tensor"),
            P("section", None, "tensor"),
            P("section", "tensor", None),
            P(),
            P(),
            P(),
            P(),
        ),
        out_specs=(P("section", None, "tensor", None), P("section", None, "tensor", None)),
        check_vma=False,
    )
```

time: 212 us -> 202 us (0.953)
  the two profiles are of different devices: /device:TPU:30 before, /device:TPU:1 now
where the time goes in v4:
time: 202 us; the launch traced here: 200 us
  starting transfers between devices  123 us (61%)
  waiting for transfers between devices  54.1 us (27%)
  Pallas kernels  14.6 us (7%)
  other arithmetic  5.42 us (3%)
  local copies, waits for them, and re-layouts  2.05 us (1%)
    ppermute x30, starting transfers between devices, shift(): return lax.ppermute(value, ('section', 'tensor'), pairs)  103 us
    ppermute x30, waiting for transfers between devices, shift(): return lax.ppermute(value, ('section', 'tensor'), pairs)  49.6 us
    ppermute x2, starting transfers between devices, from_behind(): lax.ppermute(value, 'section', [(i, i + steps) for i in range(leading, la...  20.3 us
    pallas_call x1, Pallas kernels, early_part(): pl.pallas_call(early_kernel, out_shape=jax.ShapeDtypeStruct((rows, cols),...  5.42 us
    pallas_call x1, Pallas kernels, layer_part(): pl.pallas_call(functools.partial(layer_kernel, offsets, back_offsets, len...  5.4 us
    ppermute x2, waiting for transfers between devices, from_behind(): lax.ppermute(value, 'section', [(i, i + steps) for i in range(leading, la...  4.53 us
  transfers between devices with their start and end apart: 32, of which 17 were waited for; matrix products, arithmetic and copies ran while one was open for 2% of the time, Pallas kernels for 5%

profile of v4, /device:TPU:1, one launch (start us, length us, event | category | flops | bytes accessed | tf_op | source)
XLA Modules:
  0.0 200.3 jit_solution(9228559716882395882)
XLA Ops:
  1.6 4.4 %collective-permute-start.20 = (bf16[64,2304]{1,0:T(8,128)(2,1)S(1)}, bf16[64,2304]{1,0:T(8,128)(2,1)S(1)}, u32[]{:S(2)}, u32[]{:S(2)}) collective-permute-start(bf16[64,2304]{1,0:T(8,128)(2,1)S(1)} %pad_maximum_fusion.refs_0_), channel_id=1, source_target_pairs={{0,1},{1,2},{2,3},{3,4},{4,5},{5,6},{6,7},{7,8},{8,9},{9,10},{10,1... | collective-permute-start | bytes 884744 | tf_op jit(solution)/shard_map/ppermute | solution.py:29
  6.0 9.5 %collective-permute-start.21 = (bf16[64,2304]{1,0:T(8,128)(2,1)S(1)}, bf16[64,2304]{1,0:T(8,128)(2,1)S(1)}, u32[]{:S(2)}, u32[]{:S(2)}) collective-permute-start(bf16[64,2304]{1,0:T(8,128)(2,1)S(1)} %pad_maximum_fusion.refs_0_), channel_id=1, source_target_pairs={{0,15},{1,0},{2,1},{3,2},{4,3},{5,4},{6,5},{7,6},{8,7},{9,8},{10,9... | collective-permute-start | bytes 884744 | tf_op jit(solution)/shard_map/ppermute | solution.py:29
  15.5 4.8 %collective-permute-done.20.refs_1_ = bf16[64,2304]{1,0:T(8,128)(2,1)S(1)} collective-permute-done((bf16[64,2304]{1,0:T(8,128)(2,1)S(1)}, bf16[64,2304]{1,0:T(8,128)(2,1)S(1)}, u32[]{:S(2)}, u32[]{:S(2)}) %collective-permute-start.20) | collective-permute-done | bytes 294944 | tf_op jit(solution)/shard_map/ppermute | solution.py:29
  20.3 1.9 collective-permute-start.22
  22.3 4.6 %collective-permute-start.23 = (bf16[64,2304]{1,0:T(8,128)(2,1)S(1)}, bf16[64,2304]{1,0:T(8,128)(2,1)S(1)}, u32[]{:S(2)}, u32[]{:S(2)}) collective-permute-start(bf16[64,2304]{1,0:T(8,128)(2,1)S(1)} %collective-permute-done.21.refs_2_), channel_id=1, source_target_pairs={{0,15},{1,0},{2,1},{3,2},{4,3},{5,4},{6,5},{7,6},{8,7},{9,8},{10,9... | collective-permute-start | bytes 884744 | tf_op jit(solution)/shard_map/ppermute | solution.py:29
  26.8 3.9 %collective-permute-done.22.refs_3_ = bf16[64,2304]{1,0:T(8,128)(2,1)S(1)} collective-permute-done((bf16[64,2304]{1,0:T(8,128)(2,1)S(1)}, bf16[64,2304]{1,0:T(8,128)(2,1)S(1)}, u32[]{:S(2)}, u32[]{:S(2)}) %collective-permute-start.22) | collective-permute-done | bytes 294944 | tf_op jit(solution)/shard_map/ppermute | solution.py:29
  32.6 4.6 %collective-permute-start.25 = (bf16[64,2304]{1,0:T(8,128)(2,1)S(1)}, bf16[64,2304]{1,0:T(8,128)(2,1)S(1)}, u32[]{:S(2)}, u32[]{:S(2)}) collective-permute-start(bf16[64,2304]{1,0:T(8,128)(2,1)S(1)} %collective-permute-done.23.refs_4_), channel_id=1, source_target_pairs={{0,15},{1,0},{2,1},{3,2},{4,3},{5,4},{6,5},{7,6},{8,7},{9,8},{10,9... | collective-permute-start | bytes 884744 | tf_op jit(solution)/shard_map/ppermute | solution.py:29
  37.2 2.9 %collective-permute-done.24.refs_5_ = bf16[64,2304]{1,0:T(8,128)(2,1)S(1)} collective-permute-done((bf16[64,2304]{1,0:T(8,128)(2,1)S(1)}, bf16[64,2304]{1,0:T(8,128)(2,1)S(1)}, u32[]{:S(2)}, u32[]{:S(2)}) %collective-permute-start.24) | collective-permute-done | bytes 294944 | tf_op jit(solution)/shard_map/ppermute | solution.py:29
  42.1 4.6 %collective-permute-start.27 = (bf16[64,2304]{1,0:T(8,128)(2,1)S(1)}, bf16[64,2304]{1,0:T(8,128)(2,1)S(1)}, u32[]{:S(2)}, u32[]{:S(2)}) collective-permute-start(bf16[64,2304]{1,0:T(8,128)(2,1)S(1)} %collective-permute-done.25.refs_6_), channel_id=1, source_target_pairs={{0,15},{1,0},{2,1},{3,2},{4,3},{5,4},{6,5},{7,6},{8,7},{9,8},{10,9... | collective-permute-start | bytes 884744 | tf_op jit(solution)/shard_map/ppermute | solution.py:29
  46.6 2.2 %collective-permute-done.26.refs_7_ = bf16[64,2304]{1,0:T(8,128)(2,1)S(1)} collective-permute-done((bf16[64,2304]{1,0:T(8,128)(2,1)S(1)}, bf16[64,2304]{1,0:T(8,128)(2,1)S(1)}, u32[]{:S(2)}, u32[]{:S(2)}) %collective-permute-start.26) | collective-permute-done | bytes 294944 | tf_op jit(solution)/shard_map/ppermute | solution.py:29
  50.7 4.6 %collective-permute-start.29 = (bf16[64,2304]{1,0:T(8,128)(2,1)S(1)}, bf16[64,2304]{1,0:T(8,128)(2,1)S(1)}, u32[]{:S(2)}, u32[]{:S(2)}) collective-permute-start(bf16[64,2304]{1,0:T(8,128)(2,1)S(1)} %collective-permute-done.27.refs_8_), channel_id=1, source_target_pairs={{0,15},{1,0},{2,1},{3,2},{4,3},{5,4},{6,5},{7,6},{8,7},{9,8},{10,9... | collective-permute-start | bytes 884744 | tf_op jit(solution)/shard_map/ppermute | solution.py:29
  55.3 2.2 %collective-permute-done.28.refs_9_ = bf16[64,2304]{1,0:T(8,128)(2,1)S(1)} collective-permute-done((bf16[64,2304]{1,0:T(8,128)(2,1)S(1)}, bf16[64,2304]{1,0:T(8,128)(2,1)S(1)}, u32[]{:S(2)}, u32[]{:S(2)}) %collective-permute-start.28) | collective-permute-done | bytes 294944 | tf_op jit(solution)/shard_map/ppermute | solution.py:29
  57.5 1.9 collective-permute-start.30
  59.4 4.6 %collective-permute-start.31 = (bf16[64,2304]{1,0:T(8,128)(2,1)S(1)}, bf16[64,2304]{1,0:T(8,128)(2,1)S(1)}, u32[]{:S(2)}, u32[]{:S(2)}) collective-permute-start(bf16[64,2304]{1,0:T(8,128)(2,1)S(1)} %collective-permute-done.29.refs_10_), channel_id=1, source_target_pairs={{0,15},{1,0},{2,1},{3,2},{4,3},{5,4},{6,5},{7,6},{8,7},{9,8},{10,9... | collective-permute-start | bytes 884744 | tf_op jit(solution)/shard_map/ppermute | solution.py:29
  64.0 2.2 %collective-permute-done.30.refs_11_ = bf16[64,2304]{1,0:T(8,128)(2,1)S(1)} collective-permute-done((bf16[64,2304]{1,0:T(8,128)(2,1)S(1)}, bf16[64,2304]{1,0:T(8,128)(2,1)S(1)}, u32[]{:S(2)}, u32[]{:S(2)}) %collective-permute-start.30) | collective-permute-done | bytes 294944 | tf_op jit(solution)/shard_map/ppermute | solution.py:29
  66.1 1.9 collective-permute-start.32
  68.7 4.6 %collective-permute-start.33 = (bf16[64,2304]{1,0:T(8,128)(2,1)S(1)}, bf16[64,2304]{1,0:T(8,128)(2,1)}, u32[]{:S(2)}, u32[]{:S(2)}) collective-permute-start(bf16[64,2304]{1,0:T(8,128)(2,1)S(1)} %collective-permute-done.31.refs_12_), channel_id=1, source_target_pairs={{0,15},{1,0},{2,1},{3,2},{4,3},{5,4},{6,5},{7,6},{8,7},{9,8},{10,9... | collective-permute-start | bytes 884744 | tf_op jit(solution)/shard_map/ppermute | solution.py:29
  73.3 1.9 collective-permute-done.32.refs_13_
  75.2 1.9 collective-permute-start.34
  79.2 5.4 %early_rows.1 = bf16[480,768]{1,0:T(8,128)(2,1)} custom-call(bf16[1,2304]{1,0:T(2,128)(2,1)} %gain_ref.1, bf16[2304,256]{1,0:T(8,128)(2,1)} %bitcast.6.wq_ref, bf16[2304,128]{1,0:T(8,128)(2,1)} %bitcast.7.wk_ref, bf16[2304,128]{1,0:T(8,128)(2,1)} %bitcast.8.wv_ref, bf16[256,2304]{1,0:T(8,128)(2,1)} %bitcast.9.wo_ref, bf16[64,2304]{1,0:T(8,128)(2,1)} %copy-done, ...), custom_call_target="tpu_custom_call" | custom-call | flops 1698693120 | bytes 4423680 | tf_op jit(solution)/shard_map/early_rows/pallas_call | solution.py:100
  85.4 87.4 %conditional.1 = (f32[64,2304]{1,0:T(8,128)S(1)}, f32[8,2304]{1,0:T(8,128)S(1)}) conditional(s32[]{:T(128)} %convert_element_type.171, (s32[1]{0:T(128)}, bf16[1,2304]{1,0:T(2,128)(2,1)S(1)}, bf16[2304,256]{1,0:T(8,128)(2,1)}, bf16[2304,128]{1,0:T(8,128)(2,1)}, bf16[2304,128]{1,0:T(8,128)(2,1)}, /*index=5*/bf16[256,2304]{1,0:T(8,128)(2,1)}, ...), branch_computations={%region_0.0_spmd, %region_1.9_spmd} | conditional | flops 1820344320 | bytes 30745196 | solution.py:498
  85.4 5.4 %layer_both_ways.1 = (bf16[64,2304]{1,0:T(8,128)(2,1)S(1)}, bf16[64,2304]{1,0:T(8,128)(2,1)S(1)}, bf16[448,768]{1,0:T(8,128)(2,1)S(1)}) custom-call(s32[1]{0:T(128)} %get-tuple-element.56.me_ref, bf16[1,2304]{1,0:T(2,128)(2,1)S(1)} %get-tuple-element.57.gain_ref, bf16[2304,256]{1,0:T(8,128)(2,1)} %get-tuple-element.52.wq_ref, ...), custom_call_target="tpu_custom_call" | custom-call | tf_op jit(solution)/shard_map/cond/branch_0_fun/layer_both_ways/pallas_call | solution.py:273
  90.8 1.9 collective-permute-start
  92.7 4.6 %collective-permute-start.8 = (bf16[64,2304]{1,0:T(8,128)(2,1)S(1)}, bf16[64,2304]{1,0:T(8,128)(2,1)S(1)}, u32[]{:S(2)}, u32[]{:S(2)}) collective-permute-start(bf16[64,2304]{1,0:T(8,128)(2,1)S(1)} %get-tuple-element.70), channel_id=1, source_target_pairs={{0,15},{1,0},{2,1},{3,2},{4,3},{5,4},{6,5},{7,6},{8,7},{9,8},{10,9... | collective-permute-start | bytes 884744 | tf_op jit(solution)/shard_map/cond/branch_0_fun/ppermute | solution.py:29
  97.3 3.8 %rest_of_terms.1 = (bf16[64,2304]{1,0:T(8,128)(2,1)S(1)}, bf16[64,2304]{1,0:T(8,128)(2,1)S(1)}, bf16[64,2304]{1,0:T(8,128)(2,1)S(1)}, bf16[64,2304]{1,0:T(8,128)...) custom-call(bf16[2304,256]{1,0:T(8,128)(2,1)} %get-tuple-element.52., ...), custom_call_target="tpu_custom_call" | custom-call | flops 1811939328 | tf_op jit(solution)/shard_map/cond/branch_0_fun/rest_of_terms/pallas_call | solution.py:287
  101.2 1.9 collective-permute-start.1
  103.2 4.6 %collective-permute-start.9 = (bf16[64,2304]{1,0:T(8,128)(2,1)S(1)}, bf16[64,2304]{1,0:T(8,128)(2,1)S(1)}, u32[]{:S(2)}, u32[]{:S(2)}) collective-permute-start(bf16[64,2304]{1,0:T(8,128)(2,1)S(1)} %add_convert_fusion.5), channel_id=1, source_target_pairs={{0,15},{1,0},{2,1},{3,2},{4,3},{5,4},{6,5},{7,6},{8,7},{9,8},{10,9... | collective-permute-start | bytes 884744 | tf_op jit(solution)/shard_map/cond/branch_0_fun/ppermute | solution.py:29
  107.7 4.0 %collective-permute-done.1 = bf16[64,2304]{1,0:T(8,128)(2,1)S(1)} collective-permute-done((bf16[64,2304]{1,0:T(8,128)(2,1)S(1)}, bf16[64,2304]{1,0:T(8,128)(2,1)S(1)}, u32[]{:S(2)}, u32[]{:S(2)}) %collective-permute-start.1) | collective-permute-done | bytes 294944 | tf_op jit(solution)/shard_map/cond/branch_0_fun/ppermute | solution.py:29
  111.8 1.9 collective-permute-start.2
  113.9 4.8 %collective-permute-start.10 = (bf16[64,2304]{1,0:T(8,128)(2,1)S(1)}, bf16[64,2304]{1,0:T(8,128)(2,1)S(1)}, u32[]{:S(2)}, u32[]{:S(2)}) collective-permute-start(bf16[64,2304]{1,0:T(8,128)(2,1)S(1)} %add_convert_fusion.4), channel_id=1, source_target_pairs={{0,15},{1,0},{2,1},{3,2},{4,3},{5,4},{6,5},{7,6},{8,7},{9,8},{10,9... | collective-permute-start | bytes 884744 | tf_op jit(solution)/shard_map/cond/branch_0_fun/ppermute | solution.py:29
  118.6 5.1 %collective-permute-done.2 = bf16[64,2304]{1,0:T(8,128)(2,1)S(1)} collective-permute-done((bf16[64,2304]{1,0:T(8,128)(2,1)S(1)}, bf16[64,2304]{1,0:T(8,128)(2,1)S(1)}, u32[]{:S(2)}, u32[]{:S(2)}) %collective-permute-start.2) | collective-permute-done | bytes 294944 | tf_op jit(solution)/shard_map/cond/branch_0_fun/ppermute | solution.py:29
  123.8 1.9 collective-permute-start.3
  125.9 4.8 %collective-permute-start.11 = (bf16[64,2304]{1,0:T(8,128)(2,1)S(1)}, bf16[64,2304]{1,0:T(8,128)(2,1)S(1)}, u32[]{:S(2)}, u32[]{:S(2)}) collective-permute-start(bf16[64,2304]{1,0:T(8,128)(2,1)S(1)} %add_convert_fusion.3), channel_id=1, source_target_pairs={{0,15},{1,0},{2,1},{3,2},{4,3},{5,4},{6,5},{7,6},{8,7},{9,8},{10,9... | collective-permute-start | bytes 884744 | tf_op jit(solution)/shard_map/cond/branch_0_fun/ppermute | solution.py:29
  130.7 4.4 %collective-permute-done.3 = bf16[64,2304]{1,0:T(8,128)(2,1)S(1)} collective-permute-done((bf16[64,2304]{1,0:T(8,128)(2,1)S(1)}, bf16[64,2304]{1,0:T(8,128)(2,1)S(1)}, u32[]{:S(2)}, u32[]{:S(2)}) %collective-permute-start.3) | collective-permute-done | bytes 294944 | tf_op jit(solution)/shard_map/cond/branch_0_fun/ppermute | solution.py:29
  135.2 1.9 collective-permute-start.4
  137.2 4.7 %collective-permute-start.12 = (bf16[64,2304]{1,0:T(8,128)(2,1)S(1)}, bf16[64,2304]{1,0:T(8,128)(2,1)S(1)}, u32[]{:S(2)}, u32[]{:S(2)}) collective-permute-start(bf16[64,2304]{1,0:T(8,128)(2,1)S(1)} %add_convert_fusion.2), channel_id=1, source_target_pairs={{0,15},{1,0},{2,1},{3,2},{4,3},{5,4},{6,5},{7,6},{8,7},{9,8},{10,9... | collective-permute-start | bytes 884744 | tf_op jit(solution)/shard_map/cond/branch_0_fun/ppermute | solution.py:29
  142.0 3.6 %collective-permute-done.4 = bf16[64,2304]{1,0:T(8,128)(2,1)S(1)} collective-permute-done((bf16[64,2304]{1,0:T(8,128)(2,1)S(1)}, bf16[64,2304]{1,0:T(8,128)(2,1)S(1)}, u32[]{:S(2)}, u32[]{:S(2)}) %collective-permute-start.4) | collective-permute-done | bytes 294944 | tf_op jit(solution)/shard_map/cond/branch_0_fun/ppermute | solution.py:29
  145.7 1.9 collective-permute-start.5
  147.7 4.6 %collective-permute-start.13 = (bf16[64,2304]{1,0:T(8,128)(2,1)S(1)}, bf16[64,2304]{1,0:T(8,128)(2,1)S(1)}, u32[]{:S(2)}, u32[]{:S(2)}) collective-permute-start(bf16[64,2304]{1,0:T(8,128)(2,1)S(1)} %add_convert_fusion.1), channel_id=1, source_target_pairs={{0,15},{1,0},{2,1},{3,2},{4,3},{5,4},{6,5},{7,6},{8,7},{9,8},{10,9... | collective-permute-start | bytes 884744 | tf_op jit(solution)/shard_map/cond/branch_0_fun/ppermute | solution.py:29
  152.3 2.9 %collective-permute-done.5 = bf16[64,2304]{1,0:T(8,128)(2,1)S(1)} collective-permute-done((bf16[64,2304]{1,0:T(8,128)(2,1)S(1)}, bf16[64,2304]{1,0:T(8,128)(2,1)S(1)}, u32[]{:S(2)}, u32[]{:S(2)}) %collective-permute-start.5) | collective-permute-done | bytes 294944 | tf_op jit(solution)/shard_map/cond/branch_0_fun/ppermute | solution.py:29
  155.2 1.9 collective-permute-start.6
  157.2 4.6 %collective-permute-start.14 = (bf16[64,2304]{1,0:T(8,128)(2,1)S(1)}, bf16[64,2304]{1,0:T(8,128)(2,1)S(1)}, u32[]{:S(2)}, u32[]{:S(2)}) collective-permute-start(bf16[64,2304]{1,0:T(8,128)(2,1)S(1)} %add_convert_fusion), channel_id=1, source_target_pairs={{0,15},{1,0},{2,1},{3,2},{4,3},{5,4},{6,5},{7,6},{8,7},{9,8},{10,9... | collective-permute-start | bytes 884744 | tf_op jit(solution)/shard_map/cond/branch_0_fun/ppermute | solution.py:29
  161.8 2.1 %collective-permute-done.6 = bf16[64,2304]{1,0:T(8,128)(2,1)S(1)} collective-permute-done((bf16[64,2304]{1,0:T(8,128)(2,1)S(1)}, bf16[64,2304]{1,0:T(8,128)(2,1)S(1)}, u32[]{:S(2)}, u32[]{:S(2)}) %collective-permute-start.6) | collective-permute-done | bytes 294944 | tf_op jit(solution)/shard_map/cond/branch_0_fun/ppermute | solution.py:29
  164.0 1.9 collective-permute-start.7
  165.9 6.7 %collective-permute-done.7 = bf16[64,2304]{1,0:T(8,128)(2,1)S(1)} collective-permute-done((bf16[64,2304]{1,0:T(8,128)(2,1)S(1)}, bf16[64,2304]{1,0:T(8,128)(2,1)S(1)}, u32[]{:S(2)}, u32[]{:S(2)}) %collective-permute-start.7) | collective-permute-done | bytes 294944 | tf_op jit(solution)/shard_map/cond/branch_0_fun/ppermute | solution.py:29
  174.1 18.4 %collective-permute-start.35 = (bf16[32,2304]{1,0:T(8,128)(2,1)S(1)}, bf16[32,2304]{1,0:T(8,128)(2,1)S(1)}, u32[]{:S(2)}, u32[]{:S(2)}) collective-permute-start(bf16[32,2304]{1,0:T(8,128)(2,1)S(1)} %get-tuple-element.114), channel_id=1, source_target_pairs={{0,16},{16,32},{32,48},{48,64},{64,80},{80,96},{96,112},{112,128},... | collective-permute-start | bytes 442376 | tf_op jit(solution)/shard_map/ppermute | solution.py:35
  192.5 1.9 collective-permute-start.36
  194.6 4.4 %collective-permute-done.36 = bf16[32,2304]{1,0:T(8,128)(2,1)S(1)} collective-permute-done((bf16[32,2304]{1,0:T(8,128)(2,1)S(1)}, bf16[32,2304]{1,0:T(8,128)(2,1)S(1)}, u32[]{:S(2)}, u32[]{:S(2)}) %collective-permute-start.36) | collective-permute-done | bytes 147488 | tf_op jit(solution)/shard_map/ppermute | solution.py:35
  (62 shorter events, 14.0 us)
Async XLA Ops:
  1.6 55.8 %copy-start = (bf16[64,2304]{1,0:T(8,128)(2,1)}, bf16[64,2304]{1,0:T(8,128)(2,1)S(1)}, u32[]{:S(2)}) copy-start(bf16[64,2304]{1,0:T(8,128)(2,1)S(1)} %pad_maximum_fusion.refs_0_) | copy-start | bytes 884740
  1.6 18.7 %collective-permute-start.20 = (bf16[64,2304]{1,0:T(8,128)(2,1)S(1)}, bf16[64,2304]{1,0:T(8,128)(2,1)S(1)}, u32[]{:S(2)}, u32[]{:S(2)}) collective-permute-start(bf16[64,2304]{1,0:T(8,128)(2,1)S(1)} %pad_maximum_fusion.refs_0_), channel_id=1, source_target_pairs={{0,1},{1,2},{2,3},{3,4},{4,5},{5,6},{6,7},{7,8},{8,9},{9,10},{10,1... | collective-permute-start | bytes 884744 | tf_op jit(solution)/shard_map/ppermute | solution.py:29
  6.0 16.2 %collective-permute-start.21 = (bf16[64,2304]{1,0:T(8,128)(2,1)S(1)}, bf16[64,2304]{1,0:T(8,128)(2,1)S(1)}, u32[]{:S(2)}, u32[]{:S(2)}) collective-permute-start(bf16[64,2304]{1,0:T(8,128)(2,1)S(1)} %pad_maximum_fusion.refs_0_), channel_id=1, source_target_pairs={{0,15},{1,0},{2,1},{3,2},{4,3},{5,4},{6,5},{7,6},{8,7},{9,8},{10,9... | collective-permute-start | bytes 884744 | tf_op jit(solution)/shard_map/ppermute | solution.py:29
  20.3 10.4 %collective-permute-start.22 = (bf16[64,2304]{1,0:T(8,128)(2,1)S(1)}, bf16[64,2304]{1,0:T(8,128)(2,1)S(1)}, u32[]{:S(2)}, u32[]{:S(2)}) collective-permute-start(bf16[64,2304]{1,0:T(8,128)(2,1)S(1)} %collective-permute-done.20.refs_1_), channel_id=1, source_target_pairs={{0,1},{1,2},{2,3},{3,4},{4,5},{5,6},{6,7},{7,8},{8,9},{9,10},{10,1... | collective-permute-start | bytes 884744 | tf_op jit(solution)/shard_map/ppermute | solution.py:29
  22.3 10.4 %collective-permute-start.23 = (bf16[64,2304]{1,0:T(8,128)(2,1)S(1)}, bf16[64,2304]{1,0:T(8,128)(2,1)S(1)}, u32[]{:S(2)}, u32[]{:S(2)}) collective-permute-start(bf16[64,2304]{1,0:T(8,128)(2,1)S(1)} %collective-permute-done.21.refs_2_), channel_id=1, source_target_pairs={{0,15},{1,0},{2,1},{3,2},{4,3},{5,4},{6,5},{7,6},{8,7},{9,8},{10,9... | collective-permute-start | bytes 884744 | tf_op jit(solution)/shard_map/ppermute | solution.py:29
  30.7 9.4 %collective-permute-start.24 = (bf16[64,2304]{1,0:T(8,128)(2,1)S(1)}, bf16[64,2304]{1,0:T(8,128)(2,1)S(1)}, u32[]{:S(2)}, u32[]{:S(2)}) collective-permute-start(bf16[64,2304]{1,0:T(8,128)(2,1)S(1)} %collective-permute-done.22.refs_3_), channel_id=1, source_target_pairs={{0,1},{1,2},{2,3},{3,4},{4,5},{5,6},{6,7},{7,8},{8,9},{9,10},{10,1... | collective-permute-start | bytes 884744 | tf_op jit(solution)/shard_map/ppermute | solution.py:29
  32.6 9.4 %collective-permute-start.25 = (bf16[64,2304]{1,0:T(8,128)(2,1)S(1)}, bf16[64,2304]{1,0:T(8,128)(2,1)S(1)}, u32[]{:S(2)}, u32[]{:S(2)}) collective-permute-start(bf16[64,2304]{1,0:T(8,128)(2,1)S(1)} %collective-permute-done.23.refs_4_), channel_id=1, source_target_pairs={{0,15},{1,0},{2,1},{3,2},{4,3},{5,4},{6,5},{7,6},{8,7},{9,8},{10,9... | collective-permute-start | bytes 884744 | tf_op jit(solution)/shard_map/ppermute | solution.py:29
  40.1 8.7 %collective-permute-start.26 = (bf16[64,2304]{1,0:T(8,128)(2,1)S(1)}, bf16[64,2304]{1,0:T(8,128)(2,1)S(1)}, u32[]{:S(2)}, u32[]{:S(2)}) collective-permute-start(bf16[64,2304]{1,0:T(8,128)(2,1)S(1)} %collective-permute-done.24.refs_5_), channel_id=1, source_target_pairs={{0,1},{1,2},{2,3},{3,4},{4,5},{5,6},{6,7},{7,8},{8,9},{9,10},{10,1... | collective-permute-start | bytes 884744 | tf_op jit(solution)/shard_map/ppermute | solution.py:29
  42.1 8.7 %collective-permute-start.27 = (bf16[64,2304]{1,0:T(8,128)(2,1)S(1)}, bf16[64,2304]{1,0:T(8,128)(2,1)S(1)}, u32[]{:S(2)}, u32[]{:S(2)}) collective-permute-start(bf16[64,2304]{1,0:T(8,128)(2,1)S(1)} %collective-permute-done.25.refs_6_), channel_id=1, source_target_pairs={{0,15},{1,0},{2,1},{3,2},{4,3},{5,4},{6,5},{7,6},{8,7},{9,8},{10,9... | collective-permute-start | bytes 884744 | tf_op jit(solution)/shard_map/ppermute | solution.py:29
  48.8 8.7 %collective-permute-start.28 = (bf16[64,2304]{1,0:T(8,128)(2,1)S(1)}, bf16[64,2304]{1,0:T(8,128)(2,1)S(1)}, u32[]{:S(2)}, u32[]{:S(2)}) collective-permute-start(bf16[64,2304]{1,0:T(8,128)(2,1)S(1)} %collective-permute-done.26.refs_7_), channel_id=1, source_target_pairs={{0,1},{1,2},{2,3},{3,4},{4,5},{5,6},{6,7},{7,8},{8,9},{9,10},{10,1... | collective-permute-start | bytes 884744 | tf_op jit(solution)/shard_map/ppermute | solution.py:29
  50.7 8.7 %collective-permute-start.29 = (bf16[64,2304]{1,0:T(8,128)(2,1)S(1)}, bf16[64,2304]{1,0:T(8,128)(2,1)S(1)}, u32[]{:S(2)}, u32[]{:S(2)}) collective-permute-start(bf16[64,2304]{1,0:T(8,128)(2,1)S(1)} %collective-permute-done.27.refs_8_), channel_id=1, source_target_pairs={{0,15},{1,0},{2,1},{3,2},{4,3},{5,4},{6,5},{7,6},{8,7},{9,8},{10,9... | collective-permute-start | bytes 884744 | tf_op jit(solution)/shard_map/ppermute | solution.py:29
  57.5 8.7 %collective-permute-start.30 = (bf16[64,2304]{1,0:T(8,128)(2,1)S(1)}, bf16[64,2304]{1,0:T(8,128)(2,1)S(1)}, u32[]{:S(2)}, u32[]{:S(2)}) collective-permute-start(bf16[64,2304]{1,0:T(8,128)(2,1)S(1)} %collective-permute-done.28.refs_9_), channel_id=1, source_target_pairs={{0,1},{1,2},{2,3},{3,4},{4,5},{5,6},{6,7},{7,8},{8,9},{9,10},{10,1... | collective-permute-start | bytes 884744 | tf_op jit(solution)/shard_map/ppermute | solution.py:29
  59.4 9.3 %collective-permute-start.31 = (bf16[64,2304]{1,0:T(8,128)(2,1)S(1)}, bf16[64,2304]{1,0:T(8,128)(2,1)S(1)}, u32[]{:S(2)}, u32[]{:S(2)}) collective-permute-start(bf16[64,2304]{1,0:T(8,128)(2,1)S(1)} %collective-permute-done.29.refs_10_), channel_id=1, source_target_pairs={{0,15},{1,0},{2,1},{3,2},{4,3},{5,4},{6,5},{7,6},{8,7},{9,8},{10,9... | collective-permute-start | bytes 884744 | tf_op jit(solution)/shard_map/ppermute | solution.py:29
  66.1 9.1 %collective-permute-start.32 = (bf16[64,2304]{1,0:T(8,128)(2,1)S(1)}, bf16[64,2304]{1,0:T(8,128)(2,1)}, u32[]{:S(2)}, u32[]{:S(2)}) collective-permute-start(bf16[64,2304]{1,0:T(8,128)(2,1)S(1)} %collective-permute-done.30.refs_11_), channel_id=1, source_target_pairs={{0,1},{1,2},{2,3},{3,4},{4,5},{5,6},{6,7},{7,8},{8,9},{9,10},{10,1... | collective-permute-start | bytes 884744 | tf_op jit(solution)/shard_map/ppermute | solution.py:29
  68.7 10.5 %collective-permute-start.33 = (bf16[64,2304]{1,0:T(8,128)(2,1)S(1)}, bf16[64,2304]{1,0:T(8,128)(2,1)}, u32[]{:S(2)}, u32[]{:S(2)}) collective-permute-start(bf16[64,2304]{1,0:T(8,128)(2,1)S(1)} %collective-permute-done.31.refs_12_), channel_id=1, source_target_pairs={{0,15},{1,0},{2,1},{3,2},{4,3},{5,4},{6,5},{7,6},{8,7},{9,8},{10,9... | collective-permute-start | bytes 884744 | tf_op jit(solution)/shard_map/ppermute | solution.py:29
  75.2 10.1 %collective-permute-start.34 = (bf16[64,2304]{1,0:T(8,128)(2,1)}, bf16[64,2304]{1,0:T(8,128)(2,1)}, u32[]{:S(2)}, u32[]{:S(2)}) collective-permute-start(bf16[64,2304]{1,0:T(8,128)(2,1)} %collective-permute-done.32.refs_13_), channel_id=1, source_target_pairs={{0,1},{1,2},{2,3},{3,4},{4,5},{5,6},{6,7},{7,8},{8,9},{9,10},{10,1... | collective-permute-start | bytes 884744 | tf_op jit(solution)/shard_map/ppermute | solution.py:29
  79.2 6.1 %copy-start.5 = (bf16[1,2304]{1,0:T(2,128)(2,1)S(1)}, bf16[1,2304]{1,0:T(2,128)(2,1)}, u32[]{:S(2)}) copy-start(bf16[1,2304]{1,0:T(2,128)(2,1)} %gain_ref.1) | copy-start | bytes 13828
  79.2 6.1 %copy-start.10 = (s32[1,8]{1,0:T(1,128)S(1)}, s32[1,8]{1,0:T(1,128)}, u32[]{:S(2)}) copy-start(s32[1,8]{1,0:T(1,128)} %param.23) | copy-start | bytes 100
  85.3 87.5 %copy-start.1 = (bf16[1,1,32,2304]{3,2,1,0:T(8,128)(2,1)S(1)}, bf16[1,1,32,2304]{3,2,1,0:T(8,128)(2,1)}, u32[]{:S(2)}) copy-start(bf16[1,1,32,2304]{3,2,1,0:T(8,128)(2,1)} %param.13) | copy-start | bytes 442372
  85.3 87.5 %copy-start.6 = (f32[2304]{0:T(1024)S(1)}, f32[2304]{0:T(1024)}, u32[]{:S(2)}) copy-start(f32[2304]{0:T(1024)} %convert_reduce_fusion) | copy-start | bytes 27652
  85.3 87.6 %copy-start.7 = (f32[32,8]{1,0:T(8,128)S(1)}, f32[32,8]{1,0:T(8,128)}, u32[]{:S(2)}) copy-start(f32[32,8]{1,0:T(8,128)} %copy.19) | copy-start | bytes 3076
  85.3 88.6 %copy-start.4 = (bf16[1,1,32,2304]{3,2,1,0:T(8,128)(2,1)S(1)}, bf16[1,1,32,2304]{3,2,1,0:T(8,128)(2,1)}, u32[]{:S(2)}) copy-start(bf16[1,1,32,2304]{3,2,1,0:T(8,128)(2,1)} %param.14) | copy-start | bytes 442372
  90.8 10.3 %collective-permute-start = (bf16[64,2304]{1,0:T(8,128)(2,1)S(1)}, bf16[64,2304]{1,0:T(8,128)(2,1)S(1)}, u32[]{:S(2)}, u32[]{:S(2)}) collective-permute-start(bf16[64,2304]{1,0:T(8,128)(2,1)S(1)} %get-tuple-element.62), channel_id=1, source_target_pairs={{0,1},{1,2},{2,3},{3,4},{4,5},{5,6},{6,7},{7,8},{8,9},{9,10},{10,1... | collective-permute-start | bytes 884744 | tf_op jit(solution)/shard_map/cond/branch_0_fun/ppermute | solution.py:29
  92.7 10.4 %collective-permute-start.8 = (bf16[64,2304]{1,0:T(8,128)(2,1)S(1)}, bf16[64,2304]{1,0:T(8,128)(2,1)S(1)}, u32[]{:S(2)}, u32[]{:S(2)}) collective-permute-start(bf16[64,2304]{1,0:T(8,128)(2,1)S(1)} %get-tuple-element.70), channel_id=1, source_target_pairs={{0,15},{1,0},{2,1},{3,2},{4,3},{5,4},{6,5},{7,6},{8,7},{9,8},{10,9... | collective-permute-start | bytes 884744 | tf_op jit(solution)/shard_map/cond/branch_0_fun/ppermute | solution.py:29
  101.2 10.6 %collective-permute-start.1 = (bf16[64,2304]{1,0:T(8,128)(2,1)S(1)}, bf16[64,2304]{1,0:T(8,128)(2,1)S(1)}, u32[]{:S(2)}, u32[]{:S(2)}) collective-permute-start(bf16[64,2304]{1,0:T(8,128)(2,1)S(1)} %add_convert_fusion.12), channel_id=1, source_target_pairs={{0,1},{1,2},{2,3},{3,4},{4,5},{5,6},{6,7},{7,8},{8,9},{9,10},{10,1... | collective-permute-start | bytes 884744 | tf_op jit(solution)/shard_map/cond/branch_0_fun/ppermute | solution.py:29
  103.2 10.6 %collective-permute-start.9 = (bf16[64,2304]{1,0:T(8,128)(2,1)S(1)}, bf16[64,2304]{1,0:T(8,128)(2,1)S(1)}, u32[]{:S(2)}, u32[]{:S(2)}) collective-permute-start(bf16[64,2304]{1,0:T(8,128)(2,1)S(1)} %add_convert_fusion.5), channel_id=1, source_target_pairs={{0,15},{1,0},{2,1},{3,2},{4,3},{5,4},{6,5},{7,6},{8,7},{9,8},{10,9... | collective-permute-start | bytes 884744 | tf_op jit(solution)/shard_map/cond/branch_0_fun/ppermute | solution.py:29
  111.8 11.9 %collective-permute-start.2 = (bf16[64,2304]{1,0:T(8,128)(2,1)S(1)}, bf16[64,2304]{1,0:T(8,128)(2,1)S(1)}, u32[]{:S(2)}, u32[]{:S(2)}) collective-permute-start(bf16[64,2304]{1,0:T(8,128)(2,1)S(1)} %add_convert_fusion.11), channel_id=1, source_target_pairs={{0,1},{1,2},{2,3},{3,4},{4,5},{5,6},{6,7},{7,8},{8,9},{9,10},{10,1... | collective-permute-start | bytes 884744 | tf_op jit(solution)/shard_map/cond/branch_0_fun/ppermute | solution.py:29
  113.9 11.9 %collective-permute-start.10 = (bf16[64,2304]{1,0:T(8,128)(2,1)S(1)}, bf16[64,2304]{1,0:T(8,128)(2,1)S(1)}, u32[]{:S(2)}, u32[]{:S(2)}) collective-permute-start(bf16[64,2304]{1,0:T(8,128)(2,1)S(1)} %add_convert_fusion.4), channel_id=1, source_target_pairs={{0,15},{1,0},{2,1},{3,2},{4,3},{5,4},{6,5},{7,6},{8,7},{9,8},{10,9... | collective-permute-start | bytes 884744 | tf_op jit(solution)/shard_map/cond/branch_0_fun/ppermute | solution.py:29
  123.8 11.3 %collective-permute-start.3 = (bf16[64,2304]{1,0:T(8,128)(2,1)S(1)}, bf16[64,2304]{1,0:T(8,128)(2,1)S(1)}, u32[]{:S(2)}, u32[]{:S(2)}) collective-permute-start(bf16[64,2304]{1,0:T(8,128)(2,1)S(1)} %add_convert_fusion.10), channel_id=1, source_target_pairs={{0,1},{1,2},{2,3},{3,4},{4,5},{5,6},{6,7},{7,8},{8,9},{9,10},{10,1... | collective-permute-start | bytes 884744 | tf_op jit(solution)/shard_map/cond/branch_0_fun/ppermute | solution.py:29
  125.9 11.3 %collective-permute-start.11 = (bf16[64,2304]{1,0:T(8,128)(2,1)S(1)}, bf16[64,2304]{1,0:T(8,128)(2,1)S(1)}, u32[]{:S(2)}, u32[]{:S(2)}) collective-permute-start(bf16[64,2304]{1,0:T(8,128)(2,1)S(1)} %add_convert_fusion.3), channel_id=1, source_target_pairs={{0,15},{1,0},{2,1},{3,2},{4,3},{5,4},{6,5},{7,6},{8,7},{9,8},{10,9... | collective-permute-start | bytes 884744 | tf_op jit(solution)/shard_map/cond/branch_0_fun/ppermute | solution.py:29
  135.2 10.4 %collective-permute-start.4 = (bf16[64,2304]{1,0:T(8,128)(2,1)S(1)}, bf16[64,2304]{1,0:T(8,128)(2,1)S(1)}, u32[]{:S(2)}, u32[]{:S(2)}) collective-permute-start(bf16[64,2304]{1,0:T(8,128)(2,1)S(1)} %add_convert_fusion.9), channel_id=1, source_target_pairs={{0,1},{1,2},{2,3},{3,4},{4,5},{5,6},{6,7},{7,8},{8,9},{9,10},{10,1... | collective-permute-start | bytes 884744 | tf_op jit(solution)/shard_map/cond/branch_0_fun/ppermute | solution.py:29
  137.2 10.4 %collective-permute-start.12 = (bf16[64,2304]{1,0:T(8,128)(2,1)S(1)}, bf16[64,2304]{1,0:T(8,128)(2,1)S(1)}, u32[]{:S(2)}, u32[]{:S(2)}) collective-permute-start(bf16[64,2304]{1,0:T(8,128)(2,1)S(1)} %add_convert_fusion.2), channel_id=1, source_target_pairs={{0,15},{1,0},{2,1},{3,2},{4,3},{5,4},{6,5},{7,6},{8,7},{9,8},{10,9... | collective-permute-start | bytes 884744 | tf_op jit(solution)/shard_map/cond/branch_0_fun/ppermute | solution.py:29
  145.7 9.5 %collective-permute-start.5 = (bf16[64,2304]{1,0:T(8,128)(2,1)S(1)}, bf16[64,2304]{1,0:T(8,128)(2,1)S(1)}, u32[]{:S(2)}, u32[]{:S(2)}) collective-permute-start(bf16[64,2304]{1,0:T(8,128)(2,1)S(1)} %add_convert_fusion.8), channel_id=1, source_target_pairs={{0,1},{1,2},{2,3},{3,4},{4,5},{5,6},{6,7},{7,8},{8,9},{9,10},{10,1... | collective-permute-start | bytes 884744 | tf_op jit(solution)/shard_map/cond/branch_0_fun/ppermute | solution.py:29
  147.7 9.4 %collective-permute-start.13 = (bf16[64,2304]{1,0:T(8,128)(2,1)S(1)}, bf16[64,2304]{1,0:T(8,128)(2,1)S(1)}, u32[]{:S(2)}, u32[]{:S(2)}) collective-permute-start(bf16[64,2304]{1,0:T(8,128)(2,1)S(1)} %add_convert_fusion.1), channel_id=1, source_target_pairs={{0,15},{1,0},{2,1},{3,2},{4,3},{5,4},{6,5},{7,6},{8,7},{9,8},{10,9... | collective-permute-start | bytes 884744 | tf_op jit(solution)/shard_map/cond/branch_0_fun/ppermute | solution.py:29
  155.2 8.7 %collective-permute-start.6 = (bf16[64,2304]{1,0:T(8,128)(2,1)S(1)}, bf16[64,2304]{1,0:T(8,128)(2,1)S(1)}, u32[]{:S(2)}, u32[]{:S(2)}) collective-permute-start(bf16[64,2304]{1,0:T(8,128)(2,1)S(1)} %add_convert_fusion.7), channel_id=1, source_target_pairs={{0,1},{1,2},{2,3},{3,4},{4,5},{5,6},{6,7},{7,8},{8,9},{9,10},{10,1... | collective-permute-start | bytes 884744 | tf_op jit(solution)/shard_map/cond/branch_0_fun/ppermute | solution.py:29
  157.2 8.7 %collective-permute-start.14 = (bf16[64,2304]{1,0:T(8,128)(2,1)S(1)}, bf16[64,2304]{1,0:T(8,128)(2,1)S(1)}, u32[]{:S(2)}, u32[]{:S(2)}) collective-permute-start(bf16[64,2304]{1,0:T(8,128)(2,1)S(1)} %add_convert_fusion), channel_id=1, source_target_pairs={{0,15},{1,0},{2,1},{3,2},{4,3},{5,4},{6,5},{7,6},{8,7},{9,8},{10,9... | collective-permute-start | bytes 884744 | tf_op jit(solution)/shard_map/cond/branch_0_fun/ppermute | solution.py:29
  164.0 8.7 %collective-permute-start.7 = (bf16[64,2304]{1,0:T(8,128)(2,1)S(1)}, bf16[64,2304]{1,0:T(8,128)(2,1)S(1)}, u32[]{:S(2)}, u32[]{:S(2)}) collective-permute-start(bf16[64,2304]{1,0:T(8,128)(2,1)S(1)} %add_convert_fusion.6), channel_id=1, source_target_pairs={{0,1},{1,2},{2,3},{3,4},{4,5},{5,6},{6,7},{7,8},{8,9},{9,10},{10,1... | collective-permute-start | bytes 884744 | tf_op jit(solution)/shard_map/cond/branch_0_fun/ppermute | solution.py:29
  174.1 20.5 %collective-permute-start.35 = (bf16[32,2304]{1,0:T(8,128)(2,1)S(1)}, bf16[32,2304]{1,0:T(8,128)(2,1)S(1)}, u32[]{:S(2)}, u32[]{:S(2)}) collective-permute-start(bf16[32,2304]{1,0:T(8,128)(2,1)S(1)} %get-tuple-element.114), channel_id=1, source_target_pairs={{0,16},{16,32},{32,48},{48,64},{64,80},{80,96},{96,112},{112,128},... | collective-permute-start | bytes 442376 | tf_op jit(solution)/shard_map/ppermute | solution.py:35
  192.5 6.5 %collective-permute-start.36 = (bf16[32,2304]{1,0:T(8,128)(2,1)S(1)}, bf16[32,2304]{1,0:T(8,128)(2,1)S(1)}, u32[]{:S(2)}, u32[]{:S(2)}) collective-permute-start(bf16[32,2304]{1,0:T(8,128)(2,1)S(1)} %get-tuple-element.113), channel_id=1, source_target_pairs={{16,0},{32,16},{48,32},{64,48},{80,64},{96,80},{112,96},{128,112},... | collective-permute-start | bytes 442376 | tf_op jit(solution)/shard_map/ppermute | solution.py:35

commit v5 on v4

--- a/solution.py
+++ b/solution.py
@@ -19,7 +19,6 @@
 BF16 = jnp.bfloat16
 VMEM_LIMIT = 24 * 1024 * 1024
 BATCH = 8
-FIRST_TERMS = 2
 
 
 def shift(value, steps, sections=None):
@@ -29,10 +28,12 @@
     return lax.ppermute(value, ("section", "tensor"), pairs)
 
 
-def from_behind(value, steps):
+def swap_sections(value, first):
     count = lax.axis_size("section")
-    leading, last = (max(0, -steps), min(count, count - steps))
-    return lax.ppermute(value, "section", [(i, i + steps) for i in range(leading, last)])
+    pairs = []
+    for s in range(first, count - 1, 2):
+        pairs += [(s, s + 1), (s + 1, s)]
+    return lax.ppermute(value, "section", pairs)
 
 
 def dot(left, right):
@@ -69,7 +70,11 @@
     return capped, [e / s for e, s in zip(exps, sums)]
 
 
-def project(me_ref, gain_ref, wq_ref, wk_ref, wv_ref, wo_ref, blocks):
+def w_in_of(wq_ref, wk_ref, wv_ref):
+    return jnp.concatenate([wq_ref[...], wk_ref[...], wv_ref[...]], axis=1)
+
+
+def project(gain_ref, w_in, wo_ref, blocks):
     own = blocks[0].shape[0] // 2
     gain = gain_ref[...].astype(F32)
     normed = []
@@ -77,18 +82,17 @@
         x_float = block[:own].astype(F32)
         normed.append((x_float * inv_rms(x_float) * gain).astype(BF16))
     normed = jnp.concatenate(normed, axis=0)
-    w_kv = jnp.concatenate([wk_ref[...], wv_ref[...]], axis=1)
     cot = jnp.concatenate([block[own:] for block in blocks], axis=0)
-    parts = [dot(normed, wq_ref[...]), dot(normed, w_kv), dot_nt(cot, wo_ref[...])]
-    return [part.astype(BF16) for part in parts]
+    return dot(normed, w_in).astype(BF16), dot_nt(cot, wo_ref[...]).astype(BF16)
 
 
 def early_kernel(gain_ref, wq_ref, wk_ref, wv_ref, wo_ref, *refs):
     blocks, out_ref = refs[:-1], refs[-1]
+    w_in = w_in_of(wq_ref, wk_ref, wv_ref)
     own = blocks[0].shape[0] // 2
     for first in range(0, len(blocks), BATCH):
         some = blocks[first : first + BATCH]
-        parts = project(None, gain_ref, wq_ref, wk_ref, wv_ref, wo_ref, some)
+        parts = project(gain_ref, w_in, wo_ref, some)
         rows = slice(first * own, (first + len(some)) * own)
         out_ref[rows, :] = jnp.concatenate(parts, axis=1)
 
@@ -120,9 +124,9 @@
         if grad_ctx is not None:
             grad_ctx[rows, :] = early_ref[i * own : (i + 1) * own, cols:]
     rows = pl.ds(place_of(me_ref, offsets[-1], count, own), own)
-    qkv_ref[rows, :] = jnp.concatenate(late[:2], axis=1)
+    qkv_ref[rows, :] = late[0]
     if grad_ctx is not None:
-        grad_ctx[rows, :] = late[2]
+        grad_ctx[rows, :] = late[1]
 
 
 def place_of(me_ref, offset, count, own):
@@ -150,14 +154,14 @@
     wv_ref,
     wo_ref,
     early_ref,
-    first_ref,
+    x_ref,
     late_ref,
     qkv_ref,
     rows_ref,
     context,
 ):
     own = qkv_ref.shape[0] // len(offsets)
-    late = project(me_ref, gain_ref, wq_ref, wk_ref, wv_ref, wo_ref, [late_ref])
+    late = project(gain_ref, w_in_of(wq_ref, wk_ref, wv_ref), wo_ref, [late_ref])
     place_all(offsets, me_ref, early_ref, late, qkv_ref)
     q_cols, kv_cols = wq_ref.shape[1], wk_ref.shape[1]
     _, pairs, queries, keys, values = pairs_of(qkv_ref, length, q_cols, kv_cols)
@@ -167,11 +171,11 @@
     picks = row_picks(positions_ref[...], qkv_ref.shape[0])
     own_picks = row_picks(positions_ref[...] - me_ref[0] * own, own)
     rows_ref[...] = dot(dot(picks, context[...]).astype(BF16), wo_ref[...]) + dot(
-        own_picks, first_ref[:own]
+        own_picks, x_ref[...]
     )
 
 
-def rows_part_of(me, positions, gain, weights, early, first, late, offsets, length):
+def rows_part_of(me, positions, gain, weights, early, x_own, late, offsets, length):
     own, feats = late.shape[0] // 2, late.shape[1]
     rows = own * len(offsets)
     vmem = pl.BlockSpec(memory_space=pltpu.VMEM)
@@ -188,20 +192,20 @@
         scratch_shapes=[pltpu.VMEM((rows, weights[0].shape[1]), BF16)],
         compiler_params=pltpu.CompilerParams(vmem_limit_bytes=VMEM_LIMIT),
         name="scored_rows",
-    )(me, positions, gain, *weights, early, first, late)
-
-
-def project_back(turned, wq_ref, wk_ref, wv_ref, wo_ref, outs):
-    own, feats = outs[0].shape[0] // 2, outs[0].shape[1]
+    )(me, positions, gain, *weights, early, x_own, late)
+
+
+def project_back(turned, wq_ref, wk_ref, wv_ref, wo_ref, mixed_outs, back_outs):
+    own, feats = mixed_outs[0].shape[0], wq_ref.shape[0]
     at_mix = turned.shape[1] - wo_ref.shape[0]
     for start in range(0, feats, 256):
         cols = slice(start, start + 256)
-        all_w = jnp.concatenate([wq_ref[cols, :], wk_ref[cols, :], wv_ref[cols, :]], axis=1)
-        back = dot_nt(turned[:, :at_mix], all_w).astype(BF16)
+        w_in = w_in_of(wq_ref.at[cols], wk_ref.at[cols], wv_ref.at[cols])
+        back = dot_nt(turned[:, :at_mix], w_in).astype(BF16)
         mixed = dot(turned[:, at_mix:], wo_ref[:, cols]).astype(BF16)
-        for j, out in enumerate(outs):
-            out[:own, cols] = mixed[j * own : (j + 1) * own]
-            out[own:, cols] = back[j * own : (j + 1) * own]
+        for j, (mixed_out, back_out) in enumerate(zip(mixed_outs, back_outs)):
+            mixed_out[:, cols] = mixed[j * own : (j + 1) * own]
+            back_out[:, cols] = back[j * own : (j + 1) * own]
 
 
 def layer_kernel(
@@ -216,14 +220,19 @@
     wo_ref,
     early_ref,
     late_ref,
-    *refs,
+    far_mixed_ref,
+    far_back_ref,
+    next_ref,
+    rest_ref,
+    qkv,
+    grad_ctx,
+    work,
+    far_rows,
 ):
     count = len(offsets)
-    outs, rest_ref = refs[:FIRST_TERMS], refs[FIRST_TERMS]
-    qkv, grad_ctx, work, first_rows = refs[FIRST_TERMS + 1 :]
     own = late_ref.shape[0] // 2
     q_cols, kv_cols = wq_ref.shape[1], wk_ref.shape[1]
-    late = project(me_ref, gain_ref, wq_ref, wk_ref, wv_ref, wo_ref, [late_ref])
+    late = project(gain_ref, w_in_of(wq_ref, wk_ref, wv_ref), wo_ref, [late_ref])
     place_all(offsets, me_ref, early_ref, late, qkv, grad_ctx)
     spans, pairs, queries, keys, values = pairs_of(qkv, length, q_cols, kv_cols)
     ctxs = [grad_ctx[s, h : h + HEAD_DIM] for s, h in pairs]
@@ -249,15 +258,20 @@
         work[s, at_values:at_mix] = sum(grad_values[i * per : (i + 1) * per]).astype(BF16)
     for i, offset in enumerate(back_offsets):
         rows = work[pl.ds(place_of(me_ref, offset, count, own), own), :]
-        if i < FIRST_TERMS:
-            first_rows[i * own : (i + 1) * own, :] = rows
+        if i == 0:
+            far_rows[...] = rows
+        elif i <= 2:
+            next_ref[(i - 1) * own : i * own, :] = rows
         else:
-            rest_ref[(i - FIRST_TERMS) * own : (i - FIRST_TERMS + 1) * own, :] = rows
-    project_back(first_rows, wq_ref, wk_ref, wv_ref, wo_ref, outs)
+            rest_ref[(i - 3) * own : (i - 2) * own, :] = rows
+    project_back(far_rows, wq_ref, wk_ref, wv_ref, wo_ref, [far_mixed_ref], [far_back_ref])
 
 
 def rest_kernel(wq_ref, wk_ref, wv_ref, wo_ref, rest_ref, *outs):
-    project_back(rest_ref, wq_ref, wk_ref, wv_ref, wo_ref, outs)
+    own = outs[0].shape[0] // 2
+    mixed_outs = [out.at[:own] for out in outs]
+    back_outs = [out.at[own:] for out in outs]
+    project_back(rest_ref, wq_ref, wk_ref, wv_ref, wo_ref, mixed_outs, back_outs)
 
 
 def layer_part(me, gain, weights, early, late, offsets, back_offsets, length):
@@ -266,36 +280,43 @@
     rows = own * count
     vmem = pl.BlockSpec(memory_space=pltpu.VMEM)
     smem = pl.BlockSpec(memory_space=pltpu.SMEM)
-    cols = sum(w.shape[1] for w in weights[:3])
-    q_cols = weights[0].shape[1]
-    left = count - FIRST_TERMS
-    term = jax.ShapeDtypeStruct(late.shape, BF16)
-    *first, rest = pl.pallas_call(
+    cols, q_cols = sum(w.shape[1] for w in weights[:3]), weights[0].shape[1]
+    far_term = jax.ShapeDtypeStruct((own, feats), BF16)
+    return pl.pallas_call(
         functools.partial(layer_kernel, offsets, back_offsets, length),
-        out_shape=[term] * FIRST_TERMS + [jax.ShapeDtypeStruct((own * left, cols + q_cols), BF16)],
+        out_shape=(
+            far_term,
+            far_term,
+            jax.ShapeDtypeStruct((2 * own, cols + q_cols), BF16),
+            jax.ShapeDtypeStruct((rows - 3 * own, cols + q_cols), BF16),
+        ),
         in_specs=[smem] + [vmem] * 7,
-        out_specs=[vmem] * (FIRST_TERMS + 1),
+        out_specs=[vmem] * 4,
         scratch_shapes=[
             pltpu.VMEM((rows, cols), BF16),
             pltpu.VMEM((rows, q_cols), BF16),
             pltpu.VMEM((rows, cols + q_cols), BF16),
-            pltpu.VMEM((own * FIRST_TERMS, cols + q_cols), BF16),
+            pltpu.VMEM((own, cols + q_cols), BF16),
         ],
         compiler_params=pltpu.CompilerParams(vmem_limit_bytes=VMEM_LIMIT),
         name="layer_both_ways",
     )(me, gain, *weights, early, late)
-    others = pl.pallas_call(
+
+
+def terms_of(weights, turned, own):
+    count, feats = turned.shape[0] // own, weights[0].shape[0]
+    vmem = pl.BlockSpec(memory_space=pltpu.VMEM)
+    return pl.pallas_call(
         rest_kernel,
-        out_shape=[term] * left,
+        out_shape=[jax.ShapeDtypeStruct((2 * own, feats), BF16)] * count,
         in_specs=[vmem] * 5,
-        out_specs=[vmem] * left,
+        out_specs=[vmem] * count,
         compiler_params=pltpu.CompilerParams(vmem_limit_bytes=VMEM_LIMIT),
         cost_estimate=pl.CostEstimate(
-            flops=2 * rows * (cols + q_cols) * feats, bytes_accessed=0, transcendentals=0
+            flops=2 * turned.size * feats, bytes_accessed=0, transcendentals=0
         ),
         name="rest_of_terms",
-    )(*weights, rest)
-    return dict(zip(back_offsets, [*first, *others]))
+    )(*weights, turned)
 
 
 def scored_kernel(
@@ -386,6 +407,37 @@
     )
 
 
+def finish_kernel(
+    me_ref, positions_ref, gain_ref, x_ref, later_ref, sums_ref, row_grads_ref, between_ref, within_ref
+):
+    own = x_ref.shape[0]
+    x = x_ref[...].astype(F32)
+    hidden = x + sums_ref[:own]
+    picks = row_picks(positions_ref[...] - me_ref[0] * own, own)
+    last = dot_tn(picks, row_grads_ref[...].astype(BF16))
+    cotangent = jnp.where(me_ref[2] == 1, last, later_ref[...].astype(F32))
+    inv_x = inv_rms(x)
+    scaled = sums_ref[own:] * gain_ref[...].astype(F32)
+    mean = jnp.mean(scaled * x, axis=-1, keepdims=True)
+    returned = cotangent + inv_x * scaled - x * (inv_x * inv_x * inv_x * mean)
+    odd = me_ref[1] == 1
+    between_ref[...] = jnp.where(odd, hidden, returned).astype(BF16)
+    within_ref[...] = jnp.where(odd, returned, hidden).astype(BF16)
+
+
+def finish_part(me, positions, gain, x_own, later_own, sums, row_grads):
+    vmem = pl.BlockSpec(memory_space=pltpu.VMEM)
+    smem = pl.BlockSpec(memory_space=pltpu.SMEM)
+    return pl.pallas_call(
+        finish_kernel,
+        out_shape=[jax.ShapeDtypeStruct(x_own.shape, BF16)] * 2,
+        in_specs=[smem] + [vmem] * 6,
+        out_specs=[vmem] * 2,
+        compiler_params=pltpu.CompilerParams(vmem_limit_bytes=VMEM_LIMIT),
+        name="finish",
+    )(me, positions, gain, x_own, later_own, sums, row_grads)
+
+
 def rank_grad(reward_scores, rankings):
     slots = jnp.arange(RESP)
     order_hot = (rankings[0][:, None] == slots[None, :]).astype(F32)
@@ -413,20 +465,21 @@
     return blocks, offsets
 
 
-def scatter_ring(terms, sections):
-    count = lax.axis_size("tensor")
-    half = count // 2
-    up = terms[half]
-    down = terms[-(count - half - 1)]
-    for step in range(half):
-        left = half - step - 1
-        up = shift(up, 1, sections)
-        if left:
-            up = (up.astype(F32) + terms[left].astype(F32)).astype(BF16)
-        if left:
-            down = shift(down, -1, sections)
-            if left > 1:
-                down = (down.astype(F32) + terms[1 - left].astype(F32)).astype(BF16)
+def scatter_ring(weights, far_mixed, far_back, next_rows, rest_rows, back_offsets, sections):
+    far = lax.axis_size("tensor") // 2
+    own = far_mixed.shape[0]
+    none = jnp.zeros(far_mixed.shape, F32)
+    up, down = shift(far_mixed, 1, sections), shift(far_back, -1, sections)
+    terms = dict(zip(back_offsets[1:3], terms_of(weights, next_rows, own)))
+    up = jnp.concatenate([up.astype(F32), none])
+    down = jnp.concatenate([none, down.astype(F32)])
+    for left in range(far - 1, 0, -1):
+        up = (up.astype(F32) + terms[left].astype(F32)).astype(BF16)
+        down = (down.astype(F32) + terms[-left].astype(F32)).astype(BF16)
+        if left == far - 1:
+            up, down, rest_rows = lax.optimization_barrier((up, down, rest_rows))
+            terms.update(zip(back_offsets[3:], terms_of(weights, rest_rows, own)))
+        up, down = shift(up, 1, sections), shift(down, -1, sections)
     return terms[0].astype(F32) + up.astype(F32) + down.astype(F32)
 
 
@@ -462,24 +515,23 @@
     at_end = lax.axis_index("section") == lax.axis_size("section") - 1
     positions = jnp.arange(RESP) * length + lengths[0] - 1
     places = positions[:, None].astype(jnp.int32)
-    me = tensor_pos[None].astype(jnp.int32)
+    odd = lax.axis_index("section") % 2
+    me = jnp.stack([tensor_pos, odd, at_end]).astype(jnp.int32)
 
     last = lax.axis_size("section") - 1
     blocks, offsets = gather_ring(jnp.concatenate([x_own, later_own]))
     far = tensor_count // 2
-    back_offsets = [far, far + 1 - tensor_count]
-    back_offsets += [o for o in range(back_offsets[1] + 1, far)]
+    back_offsets = [far, far - 1, 1 - far, *range(2 - far, far - 1)]
     early = early_part(attn_gain, weights, blocks[:-1])
-    first, late = blocks[0], blocks[-1]
-
-    def inner_section(early, first, late):
-        terms = layer_part(me, attn_gain, weights, early, late, offsets, back_offsets, length)
-        sums = scatter_ring(terms, range(last))
+
+    def inner_section(early, late):
+        parts = layer_part(me, attn_gain, weights, early, late, offsets, back_offsets, length)
+        sums = scatter_ring(weights, *parts, back_offsets, range(last))
         return sums, jnp.zeros((RESP, x_own.shape[1]), F32)
 
-    def last_section(early, first, late):
+    def last_section(early, late):
         qkv, rows_part = rows_part_of(
-            me, places, attn_gain, weights, early, first, late, offsets, length
+            me, places, attn_gain, weights, early, x_own, late, offsets, length
         )
         rows_hidden = sum_rows(rows_part, [last]).astype(BF16).astype(F32)
         inv_norm = inv_rms(rows_hidden)
@@ -495,23 +547,12 @@
         )
         return jnp.concatenate([jnp.zeros_like(back_own), back_own]), row_grads
 
-    sums, row_grads = lax.cond(at_end, last_section, inner_section, early, first, late)
-    mixed_own, back_own = sums[:own_count], sums[own_count:]
-
-    own_rows = tensor_pos * own_count + jnp.arange(own_count)
-    own_picks = (own_rows[:, None] == positions[None, :]).astype(F32)
-    last_own = jnp.sum(own_picks[:, :, None] * row_grads[None], axis=1)
-    grad_own = jnp.where(at_end, last_own, later_own.astype(F32))
-    x_float = x_own.astype(F32)
-    inv_x = inv_rms(x_float)
-    scaled_x = back_own * attn_gain[0].astype(F32)
-    grad_x = inv_x * scaled_x - x_float * inv_x**3 * jnp.mean(
-        scaled_x * x_float, axis=-1, keepdims=True
-    )
-    returned = (grad_own + grad_x).astype(BF16)
-    sent_back = from_behind(returned, -1)
-    hidden = (x_float + mixed_own).astype(BF16)
-    arrived = from_behind(hidden, 1)
+    sums, row_grads = lax.cond(at_end, last_section, inner_section, early, blocks[-1])
+    between, within = finish_part(me, places, attn_gain, x_own, later_own, sums, row_grads)
+    between, within = swap_sections(between, 1), swap_sections(within, 0)
+    even = lax.axis_index("section") % 2 == 0
+    arrived = jnp.where(even, between, within)
+    sent_back = jnp.where(even, within, between)
     return (arrived[None, None], sent_back[None, None])
 
 

time: 202 us -> 198 us (0.980)
  the two profiles are of different devices: /device:TPU:1 before, /device:TPU:23 now
where the time goes in v5:
time: 198 us; the launch traced here: 197 us
  starting transfers between devices  133 us (67%)
  waiting for transfers between devices  46.6 us (24%)
  Pallas kernels  12.4 us (6%)
  other arithmetic  2.86 us (1%)
    ppermute x31, starting transfers between devices, shift(): return lax.ppermute(value, ('section', 'tensor'), pairs)  105 us
    ppermute x31, waiting for transfers between devices, shift(): return lax.ppermute(value, ('section', 'tensor'), pairs)  45.2 us
    ppermute x2, starting transfers between devices, swap_sections(): return lax.ppermute(value, 'section', pairs)  28.2 us
    pallas_call x1, Pallas kernels, early_part(): pl.pallas_call(early_kernel, out_shape=jax.ShapeDtypeStruct((rows, cols),...  4.65 us
    pallas_call x1, Pallas kernels, layer_part(): pl.pallas_call(functools.partial(layer_kernel, offsets, back_offsets, len...  4.04 us
  transfers between devices with their start and end apart: 33, of which 20 were waited for; matrix products, arithmetic and copies ran while one was open for 1% of the time, Pallas kernels for 4%

profile of v5, /device:TPU:23, one launch (start us, length us, event | category | flops | bytes accessed | tf_op | source)
XLA Modules:
  0.0 196.7 jit_solution(14689950602604480516)
XLA Ops:
  1.6 3.5 %collective-permute-start.21 = (bf16[64,2304]{1,0:T(8,128)(2,1)S(1)}, bf16[64,2304]{1,0:T(8,128)(2,1)S(1)}, u32[]{:S(2)}, u32[]{:S(2)}) collective-permute-start(bf16[64,2304]{1,0:T(8,128)(2,1)S(1)} %pad_maximum_fusion.refs_0_), channel_id=1, source_target_pairs={{0,1},{1,2},{2,3},{3,4},{4,5},{5,6},{6,7},{7,8},{8,9},{9,10},{10,1... | collective-permute-start | bytes 884744 | tf_op jit(solution)/shard_map/ppermute | solution.py:28
  5.2 9.5 %collective-permute-start.22 = (bf16[64,2304]{1,0:T(8,128)(2,1)S(1)}, bf16[64,2304]{1,0:T(8,128)(2,1)S(1)}, u32[]{:S(2)}, u32[]{:S(2)}) collective-permute-start(bf16[64,2304]{1,0:T(8,128)(2,1)S(1)} %pad_maximum_fusion.refs_0_), channel_id=1, source_target_pairs={{0,15},{1,0},{2,1},{3,2},{4,3},{5,4},{6,5},{7,6},{8,7},{9,8},{10,9... | collective-permute-start | bytes 884744 | tf_op jit(solution)/shard_map/ppermute | solution.py:28
  14.7 4.8 %collective-permute-done.21.refs_1_ = bf16[64,2304]{1,0:T(8,128)(2,1)S(1)} collective-permute-done((bf16[64,2304]{1,0:T(8,128)(2,1)S(1)}, bf16[64,2304]{1,0:T(8,128)(2,1)S(1)}, u32[]{:S(2)}, u32[]{:S(2)}) %collective-permute-start.21) | collective-permute-done | bytes 294944 | tf_op jit(solution)/shard_map/ppermute | solution.py:28
  19.5 1.9 collective-permute-start.23
  21.4 4.6 %collective-permute-start.24 = (bf16[64,2304]{1,0:T(8,128)(2,1)S(1)}, bf16[64,2304]{1,0:T(8,128)(2,1)S(1)}, u32[]{:S(2)}, u32[]{:S(2)}) collective-permute-start(bf16[64,2304]{1,0:T(8,128)(2,1)S(1)} %collective-permute-done.22.refs_2_), channel_id=1, source_target_pairs={{0,15},{1,0},{2,1},{3,2},{4,3},{5,4},{6,5},{7,6},{8,7},{9,8},{10,9... | collective-permute-start | bytes 884744 | tf_op jit(solution)/shard_map/ppermute | solution.py:28
  26.0 3.9 %collective-permute-done.23.refs_3_ = bf16[64,2304]{1,0:T(8,128)(2,1)S(1)} collective-permute-done((bf16[64,2304]{1,0:T(8,128)(2,1)S(1)}, bf16[64,2304]{1,0:T(8,128)(2,1)S(1)}, u32[]{:S(2)}, u32[]{:S(2)}) %collective-permute-start.23) | collective-permute-done | bytes 294944 | tf_op jit(solution)/shard_map/ppermute | solution.py:28
  29.9 1.9 collective-permute-start.25
  31.8 4.6 %collective-permute-start.26 = (bf16[64,2304]{1,0:T(8,128)(2,1)S(1)}, bf16[64,2304]{1,0:T(8,128)(2,1)S(1)}, u32[]{:S(2)}, u32[]{:S(2)}) collective-permute-start(bf16[64,2304]{1,0:T(8,128)(2,1)S(1)} %collective-permute-done.24.refs_4_), channel_id=1, source_target_pairs={{0,15},{1,0},{2,1},{3,2},{4,3},{5,4},{6,5},{7,6},{8,7},{9,8},{10,9... | collective-permute-start | bytes 884744 | tf_op jit(solution)/shard_map/ppermute | solution.py:28
  36.4 2.9 %collective-permute-done.25.refs_5_ = bf16[64,2304]{1,0:T(8,128)(2,1)S(1)} collective-permute-done((bf16[64,2304]{1,0:T(8,128)(2,1)S(1)}, bf16[64,2304]{1,0:T(8,128)(2,1)S(1)}, u32[]{:S(2)}, u32[]{:S(2)}) %collective-permute-start.25) | collective-permute-done | bytes 294944 | tf_op jit(solution)/shard_map/ppermute | solution.py:28
  39.3 1.9 collective-permute-start.27
  41.2 4.6 %collective-permute-start.28 = (bf16[64,2304]{1,0:T(8,128)(2,1)S(1)}, bf16[64,2304]{1,0:T(8,128)(2,1)S(1)}, u32[]{:S(2)}, u32[]{:S(2)}) collective-permute-start(bf16[64,2304]{1,0:T(8,128)(2,1)S(1)} %collective-permute-done.26.refs_6_), channel_id=1, source_target_pairs={{0,15},{1,0},{2,1},{3,2},{4,3},{5,4},{6,5},{7,6},{8,7},{9,8},{10,9... | collective-permute-start | bytes 884744 | tf_op jit(solution)/shard_map/ppermute | solution.py:28
  45.8 2.2 %collective-permute-done.27.refs_7_ = bf16[64,2304]{1,0:T(8,128)(2,1)S(1)} collective-permute-done((bf16[64,2304]{1,0:T(8,128)(2,1)S(1)}, bf16[64,2304]{1,0:T(8,128)(2,1)S(1)}, u32[]{:S(2)}, u32[]{:S(2)}) %collective-permute-start.27) | collective-permute-done | bytes 294944 | tf_op jit(solution)/shard_map/ppermute | solution.py:28
  49.9 4.6 %collective-permute-start.30 = (bf16[64,2304]{1,0:T(8,128)(2,1)S(1)}, bf16[64,2304]{1,0:T(8,128)(2,1)S(1)}, u32[]{:S(2)}, u32[]{:S(2)}) collective-permute-start(bf16[64,2304]{1,0:T(8,128)(2,1)S(1)} %collective-permute-done.28.refs_8_), channel_id=1, source_target_pairs={{0,15},{1,0},{2,1},{3,2},{4,3},{5,4},{6,5},{7,6},{8,7},{9,8},{10,9... | collective-permute-start | bytes 884744 | tf_op jit(solution)/shard_map/ppermute | solution.py:28
  54.5 2.2 %collective-permute-done.29.refs_9_ = bf16[64,2304]{1,0:T(8,128)(2,1)S(1)} collective-permute-done((bf16[64,2304]{1,0:T(8,128)(2,1)S(1)}, bf16[64,2304]{1,0:T(8,128)(2,1)S(1)}, u32[]{:S(2)}, u32[]{:S(2)}) %collective-permute-start.29) | collective-permute-done | bytes 294944 | tf_op jit(solution)/shard_map/ppermute | solution.py:28
  58.6 4.6 %collective-permute-start.32 = (bf16[64,2304]{1,0:T(8,128)(2,1)S(1)}, bf16[64,2304]{1,0:T(8,128)(2,1)}, u32[]{:S(2)}, u32[]{:S(2)}) collective-permute-start(bf16[64,2304]{1,0:T(8,128)(2,1)S(1)} %collective-permute-done.30.refs_10_), channel_id=1, source_target_pairs={{0,15},{1,0},{2,1},{3,2},{4,3},{5,4},{6,5},{7,6},{8,7},{9,8},{10,9... | collective-permute-start | bytes 884744 | tf_op jit(solution)/shard_map/ppermute | solution.py:28
  63.1 2.2 %collective-permute-done.31.refs_11_ = bf16[64,2304]{1,0:T(8,128)(2,1)S(1)} collective-permute-done((bf16[64,2304]{1,0:T(8,128)(2,1)S(1)}, bf16[64,2304]{1,0:T(8,128)(2,1)S(1)}, u32[]{:S(2)}, u32[]{:S(2)}) %collective-permute-start.31) | collective-permute-done | bytes 294944 | tf_op jit(solution)/shard_map/ppermute | solution.py:28
  65.3 1.9 collective-permute-start.33
  68.0 4.6 %collective-permute-start.34 = (bf16[64,2304]{1,0:T(8,128)(2,1)}, bf16[64,2304]{1,0:T(8,128)(2,1)}, u32[]{:S(2)}, u32[]{:S(2)}) collective-permute-start(bf16[64,2304]{1,0:T(8,128)(2,1)} %collective-permute-done.32.refs_12_), channel_id=1, source_target_pairs={{0,15},{1,0},{2,1},{3,2},{4,3},{5,4},{6,5},{7,6},{8,7},{9,8},{10,9... | collective-permute-start | bytes 884744 | tf_op jit(solution)/shard_map/ppermute | solution.py:28
  74.4 1.9 collective-permute-start.35
  76.5 4.7 %early_rows.1 = bf16[480,768]{1,0:T(8,128)(2,1)S(1)} custom-call(bf16[1,2304]{1,0:T(2,128)(2,1)} %gain_ref.3, bf16[2304,256]{1,0:T(8,128)(2,1)} %bitcast.21, bf16[2304,128]{1,0:T(8,128)(2,1)} %bitcast.27, bf16[2304,128]{1,0:T(8,128)(2,1)} %bitcast.30, bf16[256,2304]{1,0:T(8,128)(2,1)} %bitcast.24, bf16[64,2304]{1,0:T(8,128)(2,1)S(1)} %pad_maximum_fusion.refs_0_, ...), custom_call_target="tpu_custom_call" | custom-call | flops 1698693120 | bytes 4423680 | tf_op jit(solution)/shard_map/early_rows/pallas_call | solution.py:104
  81.2 3.3 %collective-permute-done.35 = bf16[64,2304]{1,0:T(8,128)(2,1)} collective-permute-done((bf16[64,2304]{1,0:T(8,128)(2,1)}, bf16[64,2304]{1,0:T(8,128)(2,1)}, u32[]{:S(2)}, u32[]{:S(2)}) %collective-permute-start.35) | collective-permute-done | bytes 294944 | tf_op jit(solution)/shard_map/ppermute | solution.py:28
  84.6 80.8 %conditional.1 = (f32[64,2304]{1,0:T(8,128)S(1)}, f32[8,2304]{1,0:T(8,128)S(1)}) conditional(s32[]{:T(128)} %convert_element_type.155, (s32[3]{0:T(128)S(1)}, bf16[1,2304]{1,0:T(2,128)(2,1)S(1)}, bf16[2304,256]{1,0:T(8,128)(2,1)S(1)}, bf16[2304,128]{1,0:T(8,128)(2,1)S(1)}, bf16[2304,128]{1,0:T(8,128)(2,1)S(1)}, ...), branch_computations={%region_0.1_spmd, %region_1.9_spmd} | conditional | flops 1707687936 | bytes 31335060 | solution.py:550
  84.6 4.0 %layer_both_ways.1 = (bf16[32,2304]{1,0:T(8,128)(2,1)S(1)}, bf16[32,2304]{1,0:T(8,128)(2,1)S(1)}, bf16[64,768]{1,0:T(8,128)(2,1)S(1)}, bf16[416,768]{1,0:T(8,128)(2,1)S(1)}) custom-call(s32[3]{0:T(128)S(1)} %get-tuple-element.46.me_ref, bf16[1,2304]{1,0:T(2,128)(2,1)S(1)} %get-tuple-element.47.gain_ref, bf16[2304,256]{1,0:T(8,128)(2,1)S(1)} %get-tuple-element.42.wq_ref, ...), custom_call_target="tpu_custom_call" | custom-call | tf_op jit(solution)/shard_map/cond/branch_0_fun/layer_both_ways/pallas_call | solution.py:285
  88.6 1.9 collective-permute-start.1
  90.6 3.4 %collective-permute-start = (bf16[32,2304]{1,0:T(8,128)(2,1)S(1)}, bf16[32,2304]{1,0:T(8,128)(2,1)S(1)}, u32[]{:S(2)}, u32[]{:S(2)}) collective-permute-start(bf16[32,2304]{1,0:T(8,128)(2,1)S(1)} %get-tuple-element.50), channel_id=1, source_target_pairs={{0,1},{1,2},{2,3},{3,4},{4,5},{5,6},{6,7},{7,8},{8,9},{9,10},{10,1... | collective-permute-start | bytes 442376 | tf_op jit(solution)/shard_map/cond/branch_0_fun/ppermute | solution.py:28
  95.0 2.6 %collective-permute-done = bf16[32,2304]{1,0:T(8,128)(2,1)S(1)} collective-permute-done((bf16[32,2304]{1,0:T(8,128)(2,1)S(1)}, bf16[32,2304]{1,0:T(8,128)(2,1)S(1)}, u32[]{:S(2)}, u32[]{:S(2)}) %collective-permute-start) | collective-permute-done | bytes 147488 | tf_op jit(solution)/shard_map/cond/branch_0_fun/ppermute | solution.py:28
  97.7 2.2 %collective-permute-start.2 = (bf16[64,2304]{1,0:T(8,128)(2,1)S(1)}, bf16[64,2304]{1,0:T(8,128)(2,1)S(1)}, u32[]{:S(2)}, u32[]{:S(2)}) collective-permute-start(bf16[64,2304]{1,0:T(8,128)(2,1)S(1)} %add_convert_fusion.13), channel_id=1, source_target_pairs={{0,1},{1,2},{2,3},{3,4},{4,5},{5,6},{6,7},{7,8},{8,9},{9,10},{10,1... | collective-permute-start | bytes 884744 | tf_op jit(solution)/shard_map/cond/branch_0_fun/ppermute | solution.py:28
  99.9 4.3 %collective-permute-start.9 = (bf16[64,2304]{1,0:T(8,128)(2,1)S(1)}, bf16[64,2304]{1,0:T(8,128)(2,1)S(1)}, u32[]{:S(2)}, u32[]{:S(2)}) collective-permute-start(bf16[64,2304]{1,0:T(8,128)(2,1)S(1)} %add_convert_fusion.12), channel_id=1, source_target_pairs={{0,15},{1,0},{2,1},{3,2},{4,3},{5,4},{6,5},{7,6},{8,7},{9,8},{10,9... | collective-permute-start | bytes 884744 | tf_op jit(solution)/shard_map/cond/branch_0_fun/ppermute | solution.py:28
  107.8 1.9 collective-permute-start.3
  109.8 4.6 %collective-permute-start.10 = (bf16[64,2304]{1,0:T(8,128)(2,1)S(1)}, bf16[64,2304]{1,0:T(8,128)(2,1)S(1)}, u32[]{:S(2)}, u32[]{:S(2)}) collective-permute-start(bf16[64,2304]{1,0:T(8,128)(2,1)S(1)} %add_convert_fusion.5), channel_id=1, source_target_pairs={{0,15},{1,0},{2,1},{3,2},{4,3},{5,4},{6,5},{7,6},{8,7},{9,8},{10,9... | collective-permute-start | bytes 884744 | tf_op jit(solution)/shard_map/cond/branch_0_fun/ppermute | solution.py:28
  114.4 4.2 %collective-permute-done.3 = bf16[64,2304]{1,0:T(8,128)(2,1)S(1)} collective-permute-done((bf16[64,2304]{1,0:T(8,128)(2,1)S(1)}, bf16[64,2304]{1,0:T(8,128)(2,1)S(1)}, u32[]{:S(2)}, u32[]{:S(2)}) %collective-permute-start.3) | collective-permute-done | bytes 294944 | tf_op jit(solution)/shard_map/cond/branch_0_fun/ppermute | solution.py:28
  118.7 1.9 collective-permute-start.4
  120.7 4.6 %collective-permute-start.11 = (bf16[64,2304]{1,0:T(8,128)(2,1)S(1)}, bf16[64,2304]{1,0:T(8,128)(2,1)S(1)}, u32[]{:S(2)}, u32[]{:S(2)}) collective-permute-start(bf16[64,2304]{1,0:T(8,128)(2,1)S(1)} %add_convert_fusion.4), channel_id=1, source_target_pairs={{0,15},{1,0},{2,1},{3,2},{4,3},{5,4},{6,5},{7,6},{8,7},{9,8},{10,9... | collective-permute-start | bytes 884744 | tf_op jit(solution)/shard_map/cond/branch_0_fun/ppermute | solution.py:28
  125.3 3.3 %collective-permute-done.4 = bf16[64,2304]{1,0:T(8,128)(2,1)S(1)} collective-permute-done((bf16[64,2304]{1,0:T(8,128)(2,1)S(1)}, bf16[64,2304]{1,0:T(8,128)(2,1)S(1)}, u32[]{:S(2)}, u32[]{:S(2)}) %collective-permute-start.4) | collective-permute-done | bytes 294944 | tf_op jit(solution)/shard_map/cond/branch_0_fun/ppermute | solution.py:28
  128.6 1.9 collective-permute-start.5
  130.6 4.6 %collective-permute-start.12 = (bf16[64,2304]{1,0:T(8,128)(2,1)S(1)}, bf16[64,2304]{1,0:T(8,128)(2,1)S(1)}, u32[]{:S(2)}, u32[]{:S(2)}) collective-permute-start(bf16[64,2304]{1,0:T(8,128)(2,1)S(1)} %add_convert_fusion.3), channel_id=1, source_target_pairs={{0,15},{1,0},{2,1},{3,2},{4,3},{5,4},{6,5},{7,6},{8,7},{9,8},{10,9... | collective-permute-start | bytes 884744 | tf_op jit(solution)/shard_map/cond/branch_0_fun/ppermute | solution.py:28
  135.2 2.1 %collective-permute-done.5 = bf16[64,2304]{1,0:T(8,128)(2,1)S(1)} collective-permute-done((bf16[64,2304]{1,0:T(8,128)(2,1)S(1)}, bf16[64,2304]{1,0:T(8,128)(2,1)S(1)}, u32[]{:S(2)}, u32[]{:S(2)}) %collective-permute-start.5) | collective-permute-done | bytes 294944 | tf_op jit(solution)/shard_map/cond/branch_0_fun/ppermute | solution.py:28
  137.4 1.9 collective-permute-start.6
  139.4 4.6 %collective-permute-start.13 = (bf16[64,2304]{1,0:T(8,128)(2,1)S(1)}, bf16[64,2304]{1,0:T(8,128)(2,1)S(1)}, u32[]{:S(2)}, u32[]{:S(2)}) collective-permute-start(bf16[64,2304]{1,0:T(8,128)(2,1)S(1)} %add_convert_fusion.2), channel_id=1, source_target_pairs={{0,15},{1,0},{2,1},{3,2},{4,3},{5,4},{6,5},{7,6},{8,7},{9,8},{10,9... | collective-permute-start | bytes 884744 | tf_op jit(solution)/shard_map/cond/branch_0_fun/ppermute | solution.py:28
  143.9 2.1 %collective-permute-done.6 = bf16[64,2304]{1,0:T(8,128)(2,1)S(1)} collective-permute-done((bf16[64,2304]{1,0:T(8,128)(2,1)S(1)}, bf16[64,2304]{1,0:T(8,128)(2,1)S(1)}, u32[]{:S(2)}, u32[]{:S(2)}) %collective-permute-start.6) | collective-permute-done | bytes 294944 | tf_op jit(solution)/shard_map/cond/branch_0_fun/ppermute | solution.py:28
  146.1 1.9 collective-permute-start.7
  148.1 4.6 %collective-permute-start.14 = (bf16[64,2304]{1,0:T(8,128)(2,1)S(1)}, bf16[64,2304]{1,0:T(8,128)(2,1)S(1)}, u32[]{:S(2)}, u32[]{:S(2)}) collective-permute-start(bf16[64,2304]{1,0:T(8,128)(2,1)S(1)} %add_convert_fusion.1), channel_id=1, source_target_pairs={{0,15},{1,0},{2,1},{3,2},{4,3},{5,4},{6,5},{7,6},{8,7},{9,8},{10,9... | collective-permute-start | bytes 884744 | tf_op jit(solution)/shard_map/cond/branch_0_fun/ppermute | solution.py:28
  152.7 2.1 %collective-permute-done.7 = bf16[64,2304]{1,0:T(8,128)(2,1)S(1)} collective-permute-done((bf16[64,2304]{1,0:T(8,128)(2,1)S(1)}, bf16[64,2304]{1,0:T(8,128)(2,1)S(1)}, u32[]{:S(2)}, u32[]{:S(2)}) %collective-permute-start.7) | collective-permute-done | bytes 294944 | tf_op jit(solution)/shard_map/cond/branch_0_fun/ppermute | solution.py:28
  154.9 1.9 collective-permute-start.8
  156.9 4.6 %collective-permute-start.15 = (bf16[64,2304]{1,0:T(8,128)(2,1)S(1)}, bf16[64,2304]{1,0:T(8,128)(2,1)S(1)}, u32[]{:S(2)}, u32[]{:S(2)}) collective-permute-start(bf16[64,2304]{1,0:T(8,128)(2,1)S(1)} %add_convert_fusion), channel_id=1, source_target_pairs={{0,15},{1,0},{2,1},{3,2},{4,3},{5,4},{6,5},{7,6},{8,7},{9,8},{10,9... | collective-permute-start | bytes 884744 | tf_op jit(solution)/shard_map/cond/branch_0_fun/ppermute | solution.py:28
  161.5 2.1 %collective-permute-done.8 = bf16[64,2304]{1,0:T(8,128)(2,1)S(1)} collective-permute-done((bf16[64,2304]{1,0:T(8,128)(2,1)S(1)}, bf16[64,2304]{1,0:T(8,128)(2,1)S(1)}, u32[]{:S(2)}, u32[]{:S(2)}) %collective-permute-start.8) | collective-permute-done | bytes 294944 | tf_op jit(solution)/shard_map/cond/branch_0_fun/ppermute | solution.py:28
  166.4 26.3 %collective-permute-start.36 = (bf16[32,2304]{1,0:T(8,128)(2,1)S(1)}, bf16[32,2304]{1,0:T(8,128)(2,1)S(1)}, u32[]{:S(2)}, u32[]{:S(2)}) collective-permute-start(bf16[32,2304]{1,0:T(8,128)(2,1)S(1)} %get-tuple-element.95), channel_id=1, source_target_pairs={{16,32},{32,16},{48,64},{64,48},{80,96},{96,80},{112,128},{128,112... | collective-permute-start | bytes 442376 | tf_op jit(solution)/shard_map/ppermute | solution.py:36
  192.7 1.9 collective-permute-start.37
  (69 shorter events, 18.1 us)
Async XLA Ops:
  1.6 17.8 %collective-permute-start.21 = (bf16[64,2304]{1,0:T(8,128)(2,1)S(1)}, bf16[64,2304]{1,0:T(8,128)(2,1)S(1)}, u32[]{:S(2)}, u32[]{:S(2)}) collective-permute-start(bf16[64,2304]{1,0:T(8,128)(2,1)S(1)} %pad_maximum_fusion.refs_0_), channel_id=1, source_target_pairs={{0,1},{1,2},{2,3},{3,4},{4,5},{5,6},{6,7},{7,8},{8,9},{9,10},{10,1... | collective-permute-start | bytes 884744 | tf_op jit(solution)/shard_map/ppermute | solution.py:28
  5.2 16.2 %collective-permute-start.22 = (bf16[64,2304]{1,0:T(8,128)(2,1)S(1)}, bf16[64,2304]{1,0:T(8,128)(2,1)S(1)}, u32[]{:S(2)}, u32[]{:S(2)}) collective-permute-start(bf16[64,2304]{1,0:T(8,128)(2,1)S(1)} %pad_maximum_fusion.refs_0_), channel_id=1, source_target_pairs={{0,15},{1,0},{2,1},{3,2},{4,3},{5,4},{6,5},{7,6},{8,7},{9,8},{10,9... | collective-permute-start | bytes 884744 | tf_op jit(solution)/shard_map/ppermute | solution.py:28
  19.5 10.4 %collective-permute-start.23 = (bf16[64,2304]{1,0:T(8,128)(2,1)S(1)}, bf16[64,2304]{1,0:T(8,128)(2,1)S(1)}, u32[]{:S(2)}, u32[]{:S(2)}) collective-permute-start(bf16[64,2304]{1,0:T(8,128)(2,1)S(1)} %collective-permute-done.21.refs_1_), channel_id=1, source_target_pairs={{0,1},{1,2},{2,3},{3,4},{4,5},{5,6},{6,7},{7,8},{8,9},{9,10},{10,1... | collective-permute-start | bytes 884744 | tf_op jit(solution)/shard_map/ppermute | solution.py:28
  21.4 10.4 %collective-permute-start.24 = (bf16[64,2304]{1,0:T(8,128)(2,1)S(1)}, bf16[64,2304]{1,0:T(8,128)(2,1)S(1)}, u32[]{:S(2)}, u32[]{:S(2)}) collective-permute-start(bf16[64,2304]{1,0:T(8,128)(2,1)S(1)} %collective-permute-done.22.refs_2_), channel_id=1, source_target_pairs={{0,15},{1,0},{2,1},{3,2},{4,3},{5,4},{6,5},{7,6},{8,7},{9,8},{10,9... | collective-permute-start | bytes 884744 | tf_op jit(solution)/shard_map/ppermute | solution.py:28
  29.9 9.4 %collective-permute-start.25 = (bf16[64,2304]{1,0:T(8,128)(2,1)S(1)}, bf16[64,2304]{1,0:T(8,128)(2,1)S(1)}, u32[]{:S(2)}, u32[]{:S(2)}) collective-permute-start(bf16[64,2304]{1,0:T(8,128)(2,1)S(1)} %collective-permute-done.23.refs_3_), channel_id=1, source_target_pairs={{0,1},{1,2},{2,3},{3,4},{4,5},{5,6},{6,7},{7,8},{8,9},{9,10},{10,1... | collective-permute-start | bytes 884744 | tf_op jit(solution)/shard_map/ppermute | solution.py:28
  31.8 9.4 %collective-permute-start.26 = (bf16[64,2304]{1,0:T(8,128)(2,1)S(1)}, bf16[64,2304]{1,0:T(8,128)(2,1)S(1)}, u32[]{:S(2)}, u32[]{:S(2)}) collective-permute-start(bf16[64,2304]{1,0:T(8,128)(2,1)S(1)} %collective-permute-done.24.refs_4_), channel_id=1, source_target_pairs={{0,15},{1,0},{2,1},{3,2},{4,3},{5,4},{6,5},{7,6},{8,7},{9,8},{10,9... | collective-permute-start | bytes 884744 | tf_op jit(solution)/shard_map/ppermute | solution.py:28
  39.3 8.7 %collective-permute-start.27 = (bf16[64,2304]{1,0:T(8,128)(2,1)S(1)}, bf16[64,2304]{1,0:T(8,128)(2,1)S(1)}, u32[]{:S(2)}, u32[]{:S(2)}) collective-permute-start(bf16[64,2304]{1,0:T(8,128)(2,1)S(1)} %collective-permute-done.25.refs_5_), channel_id=1, source_target_pairs={{0,1},{1,2},{2,3},{3,4},{4,5},{5,6},{6,7},{7,8},{8,9},{9,10},{10,1... | collective-permute-start | bytes 884744 | tf_op jit(solution)/shard_map/ppermute | solution.py:28
  41.2 8.7 %collective-permute-start.28 = (bf16[64,2304]{1,0:T(8,128)(2,1)S(1)}, bf16[64,2304]{1,0:T(8,128)(2,1)S(1)}, u32[]{:S(2)}, u32[]{:S(2)}) collective-permute-start(bf16[64,2304]{1,0:T(8,128)(2,1)S(1)} %collective-permute-done.26.refs_6_), channel_id=1, source_target_pairs={{0,15},{1,0},{2,1},{3,2},{4,3},{5,4},{6,5},{7,6},{8,7},{9,8},{10,9... | collective-permute-start | bytes 884744 | tf_op jit(solution)/shard_map/ppermute | solution.py:28
  48.0 8.7 %collective-permute-start.29 = (bf16[64,2304]{1,0:T(8,128)(2,1)S(1)}, bf16[64,2304]{1,0:T(8,128)(2,1)S(1)}, u32[]{:S(2)}, u32[]{:S(2)}) collective-permute-start(bf16[64,2304]{1,0:T(8,128)(2,1)S(1)} %collective-permute-done.27.refs_7_), channel_id=1, source_target_pairs={{0,1},{1,2},{2,3},{3,4},{4,5},{5,6},{6,7},{7,8},{8,9},{9,10},{10,1... | collective-permute-start | bytes 884744 | tf_op jit(solution)/shard_map/ppermute | solution.py:28
  49.9 8.7 %collective-permute-start.30 = (bf16[64,2304]{1,0:T(8,128)(2,1)S(1)}, bf16[64,2304]{1,0:T(8,128)(2,1)S(1)}, u32[]{:S(2)}, u32[]{:S(2)}) collective-permute-start(bf16[64,2304]{1,0:T(8,128)(2,1)S(1)} %collective-permute-done.28.refs_8_), channel_id=1, source_target_pairs={{0,15},{1,0},{2,1},{3,2},{4,3},{5,4},{6,5},{7,6},{8,7},{9,8},{10,9... | collective-permute-start | bytes 884744 | tf_op jit(solution)/shard_map/ppermute | solution.py:28
  56.6 8.7 %collective-permute-start.31 = (bf16[64,2304]{1,0:T(8,128)(2,1)S(1)}, bf16[64,2304]{1,0:T(8,128)(2,1)S(1)}, u32[]{:S(2)}, u32[]{:S(2)}) collective-permute-start(bf16[64,2304]{1,0:T(8,128)(2,1)S(1)} %collective-permute-done.29.refs_9_), channel_id=1, source_target_pairs={{0,1},{1,2},{2,3},{3,4},{4,5},{5,6},{6,7},{7,8},{8,9},{9,10},{10,1... | collective-permute-start | bytes 884744 | tf_op jit(solution)/shard_map/ppermute | solution.py:28
  58.6 9.4 %collective-permute-start.32 = (bf16[64,2304]{1,0:T(8,128)(2,1)S(1)}, bf16[64,2304]{1,0:T(8,128)(2,1)}, u32[]{:S(2)}, u32[]{:S(2)}) collective-permute-start(bf16[64,2304]{1,0:T(8,128)(2,1)S(1)} %collective-permute-done.30.refs_10_), channel_id=1, source_target_pairs={{0,15},{1,0},{2,1},{3,2},{4,3},{5,4},{6,5},{7,6},{8,7},{9,8},{10,9... | collective-permute-start | bytes 884744 | tf_op jit(solution)/shard_map/ppermute | solution.py:28
  65.3 9.1 %collective-permute-start.33 = (bf16[64,2304]{1,0:T(8,128)(2,1)S(1)}, bf16[64,2304]{1,0:T(8,128)(2,1)}, u32[]{:S(2)}, u32[]{:S(2)}) collective-permute-start(bf16[64,2304]{1,0:T(8,128)(2,1)S(1)} %collective-permute-done.31.refs_11_), channel_id=1, source_target_pairs={{0,1},{1,2},{2,3},{3,4},{4,5},{5,6},{6,7},{7,8},{8,9},{9,10},{10,1... | collective-permute-start | bytes 884744 | tf_op jit(solution)/shard_map/ppermute | solution.py:28
  68.0 8.5 %collective-permute-start.34 = (bf16[64,2304]{1,0:T(8,128)(2,1)}, bf16[64,2304]{1,0:T(8,128)(2,1)}, u32[]{:S(2)}, u32[]{:S(2)}) collective-permute-start(bf16[64,2304]{1,0:T(8,128)(2,1)} %collective-permute-done.32.refs_12_), channel_id=1, source_target_pairs={{0,15},{1,0},{2,1},{3,2},{4,3},{5,4},{6,5},{7,6},{8,7},{9,8},{10,9... | collective-permute-start | bytes 884744 | tf_op jit(solution)/shard_map/ppermute | solution.py:28
  74.4 10.1 %collective-permute-start.35 = (bf16[64,2304]{1,0:T(8,128)(2,1)}, bf16[64,2304]{1,0:T(8,128)(2,1)}, u32[]{:S(2)}, u32[]{:S(2)}) collective-permute-start(bf16[64,2304]{1,0:T(8,128)(2,1)} %collective-permute-done.33.refs_13_), channel_id=1, source_target_pairs={{0,1},{1,2},{2,3},{3,4},{4,5},{5,6},{6,7},{7,8},{8,9},{9,10},{10,1... | collective-permute-start | bytes 884744 | tf_op jit(solution)/shard_map/ppermute | solution.py:28
  76.4 8.1 %copy-start.10 = (s32[3]{0:T(128)}, s32[3]{0:T(128)S(1)}, u32[]{:S(2)}) copy-start(s32[3]{0:T(128)S(1)} %pad_add_fusion.me_ref) | copy-start | bytes 40
  76.5 8.0 %copy-start.1 = (bf16[1,2304,256]{2,1,0:T(8,128)(2,1)S(1)}, bf16[1,2304,256]{2,1,0:T(8,128)(2,1)}, u32[]{:S(2)}) copy-start(bf16[1,2304,256]{2,1,0:T(8,128)(2,1)} %param.16) | copy-start | bytes 3538948
  76.5 8.0 %copy-start.2 = (bf16[1,256,2304]{2,1,0:T(8,128)(2,1)S(1)}, bf16[1,256,2304]{2,1,0:T(8,128)(2,1)}, u32[]{:S(2)}) copy-start(bf16[1,256,2304]{2,1,0:T(8,128)(2,1)} %param.19) | copy-start | bytes 3538948
  76.5 8.0 %copy-start.3 = (bf16[1,2304,128]{2,1,0:T(8,128)(2,1)S(1)}, bf16[1,2304,128]{2,1,0:T(8,128)(2,1)}, u32[]{:S(2)}) copy-start(bf16[1,2304,128]{2,1,0:T(8,128)(2,1)} %param.17) | copy-start | bytes 1769476
  76.5 8.0 %copy-start.4 = (bf16[1,2304,128]{2,1,0:T(8,128)(2,1)S(1)}, bf16[1,2304,128]{2,1,0:T(8,128)(2,1)}, u32[]{:S(2)}) copy-start(bf16[1,2304,128]{2,1,0:T(8,128)(2,1)} %param.18) | copy-start | bytes 1769476
  76.5 8.0 %copy-start.5 = (bf16[1,1,32,2304]{3,2,1,0:T(8,128)(2,1)S(1)}, bf16[1,1,32,2304]{3,2,1,0:T(8,128)(2,1)}, u32[]{:S(2)}) copy-start(bf16[1,1,32,2304]{3,2,1,0:T(8,128)(2,1)} %param.13) | copy-start | bytes 442372
  76.5 8.0 %copy-start.9 = (bf16[1,2304]{1,0:T(2,128)(2,1)S(1)}, bf16[1,2304]{1,0:T(2,128)(2,1)}, u32[]{:S(2)}) copy-start(bf16[1,2304]{1,0:T(2,128)(2,1)} %gain_ref.3) | copy-start | bytes 13828
  76.5 8.0 %copy-start.11 = (bf16[2304]{0:T(1024)(128)(2,1)S(1)}, bf16[2304]{0:T(1024)(128)(2,1)}, u32[]{:S(2)}) copy-start(bf16[2304]{0:T(1024)(128)(2,1)} %param.20) | copy-start | bytes 13828
  76.5 8.0 %copy-start.12 = (bf16[2304]{0:T(1024)(128)(2,1)S(1)}, bf16[2304]{0:T(1024)(128)(2,1)}, u32[]{:S(2)}) copy-start(bf16[2304]{0:T(1024)(128)(2,1)} %param.21) | copy-start | bytes 13828
  76.5 8.0 %copy-start.13 = (s32[1,8]{1,0:T(1,128)S(1)}, s32[1,8]{1,0:T(1,128)}, u32[]{:S(2)}) copy-start(s32[1,8]{1,0:T(1,128)} %param.22) | copy-start | bytes 100
  84.5 80.9 %copy-start = (bf16[1,1,32,2304]{3,2,1,0:T(8,128)(2,1)S(1)}, bf16[1,1,32,2304]{3,2,1,0:T(8,128)(2,1)}, u32[]{:S(2)}) copy-start(bf16[1,1,32,2304]{3,2,1,0:T(8,128)(2,1)} %param.14) | copy-start | bytes 442372
  84.5 80.9 %copy-start.6 = (bf16[1,1,32,2304]{3,2,1,0:T(8,128)(2,1)S(1)}, bf16[1,1,32,2304]{3,2,1,0:T(8,128)(2,1)}, u32[]{:S(2)}) copy-start(bf16[1,1,32,2304]{3,2,1,0:T(8,128)(2,1)} %param.13) | copy-start | bytes 442372
  88.6 6.4 %collective-permute-start.1 = (bf16[32,2304]{1,0:T(8,128)(2,1)S(1)}, bf16[32,2304]{1,0:T(8,128)(2,1)S(1)}, u32[]{:S(2)}, u32[]{:S(2)}) collective-permute-start(bf16[32,2304]{1,0:T(8,128)(2,1)S(1)} %get-tuple-element.53), channel_id=1, source_target_pairs={{0,15},{1,0},{2,1},{3,2},{4,3},{5,4},{6,5},{7,6},{8,7},{9,8},{10,9... | collective-permute-start | bytes 442376 | tf_op jit(solution)/shard_map/cond/branch_0_fun/ppermute | solution.py:28
  90.6 7.1 %collective-permute-start = (bf16[32,2304]{1,0:T(8,128)(2,1)S(1)}, bf16[32,2304]{1,0:T(8,128)(2,1)S(1)}, u32[]{:S(2)}, u32[]{:S(2)}) collective-permute-start(bf16[32,2304]{1,0:T(8,128)(2,1)S(1)} %get-tuple-element.50), channel_id=1, source_target_pairs={{0,1},{1,2},{2,3},{3,4},{4,5},{5,6},{6,7},{7,8},{8,9},{9,10},{10,1... | collective-permute-start | bytes 442376 | tf_op jit(solution)/shard_map/cond/branch_0_fun/ppermute | solution.py:28
  97.7 10.1 %collective-permute-start.2 = (bf16[64,2304]{1,0:T(8,128)(2,1)S(1)}, bf16[64,2304]{1,0:T(8,128)(2,1)S(1)}, u32[]{:S(2)}, u32[]{:S(2)}) collective-permute-start(bf16[64,2304]{1,0:T(8,128)(2,1)S(1)} %add_convert_fusion.13), channel_id=1, source_target_pairs={{0,1},{1,2},{2,3},{3,4},{4,5},{5,6},{6,7},{7,8},{8,9},{9,10},{10,1... | collective-permute-start | bytes 884744 | tf_op jit(solution)/shard_map/cond/branch_0_fun/ppermute | solution.py:28
  99.9 9.9 %collective-permute-start.9 = (bf16[64,2304]{1,0:T(8,128)(2,1)S(1)}, bf16[64,2304]{1,0:T(8,128)(2,1)S(1)}, u32[]{:S(2)}, u32[]{:S(2)}) collective-permute-start(bf16[64,2304]{1,0:T(8,128)(2,1)S(1)} %add_convert_fusion.12), channel_id=1, source_target_pairs={{0,15},{1,0},{2,1},{3,2},{4,3},{5,4},{6,5},{7,6},{8,7},{9,8},{10,9... | collective-permute-start | bytes 884744 | tf_op jit(solution)/shard_map/cond/branch_0_fun/ppermute | solution.py:28
  107.8 10.8 %collective-permute-start.3 = (bf16[64,2304]{1,0:T(8,128)(2,1)S(1)}, bf16[64,2304]{1,0:T(8,128)(2,1)S(1)}, u32[]{:S(2)}, u32[]{:S(2)}) collective-permute-start(bf16[64,2304]{1,0:T(8,128)(2,1)S(1)} %add_convert_fusion.11), channel_id=1, source_target_pairs={{0,1},{1,2},{2,3},{3,4},{4,5},{5,6},{6,7},{7,8},{8,9},{9,10},{10,1... | collective-permute-start | bytes 884744 | tf_op jit(solution)/shard_map/cond/branch_0_fun/ppermute | solution.py:28
  109.8 10.8 %collective-permute-start.10 = (bf16[64,2304]{1,0:T(8,128)(2,1)S(1)}, bf16[64,2304]{1,0:T(8,128)(2,1)S(1)}, u32[]{:S(2)}, u32[]{:S(2)}) collective-permute-start(bf16[64,2304]{1,0:T(8,128)(2,1)S(1)} %add_convert_fusion.5), channel_id=1, source_target_pairs={{0,15},{1,0},{2,1},{3,2},{4,3},{5,4},{6,5},{7,6},{8,7},{9,8},{10,9... | collective-permute-start | bytes 884744 | tf_op jit(solution)/shard_map/cond/branch_0_fun/ppermute | solution.py:28
  118.7 9.9 %collective-permute-start.4 = (bf16[64,2304]{1,0:T(8,128)(2,1)S(1)}, bf16[64,2304]{1,0:T(8,128)(2,1)S(1)}, u32[]{:S(2)}, u32[]{:S(2)}) collective-permute-start(bf16[64,2304]{1,0:T(8,128)(2,1)S(1)} %add_convert_fusion.10), channel_id=1, source_target_pairs={{0,1},{1,2},{2,3},{3,4},{4,5},{5,6},{6,7},{7,8},{8,9},{9,10},{10,1... | collective-permute-start | bytes 884744 | tf_op jit(solution)/shard_map/cond/branch_0_fun/ppermute | solution.py:28
  120.7 9.8 %collective-permute-start.11 = (bf16[64,2304]{1,0:T(8,128)(2,1)S(1)}, bf16[64,2304]{1,0:T(8,128)(2,1)S(1)}, u32[]{:S(2)}, u32[]{:S(2)}) collective-permute-start(bf16[64,2304]{1,0:T(8,128)(2,1)S(1)} %add_convert_fusion.4), channel_id=1, source_target_pairs={{0,15},{1,0},{2,1},{3,2},{4,3},{5,4},{6,5},{7,6},{8,7},{9,8},{10,9... | collective-permute-start | bytes 884744 | tf_op jit(solution)/shard_map/cond/branch_0_fun/ppermute | solution.py:28
  128.6 8.7 %collective-permute-start.5 = (bf16[64,2304]{1,0:T(8,128)(2,1)S(1)}, bf16[64,2304]{1,0:T(8,128)(2,1)S(1)}, u32[]{:S(2)}, u32[]{:S(2)}) collective-permute-start(bf16[64,2304]{1,0:T(8,128)(2,1)S(1)} %add_convert_fusion.9), channel_id=1, source_target_pairs={{0,1},{1,2},{2,3},{3,4},{4,5},{5,6},{6,7},{7,8},{8,9},{9,10},{10,1... | collective-permute-start | bytes 884744 | tf_op jit(solution)/shard_map/cond/branch_0_fun/ppermute | solution.py:28
  130.6 8.7 %collective-permute-start.12 = (bf16[64,2304]{1,0:T(8,128)(2,1)S(1)}, bf16[64,2304]{1,0:T(8,128)(2,1)S(1)}, u32[]{:S(2)}, u32[]{:S(2)}) collective-permute-start(bf16[64,2304]{1,0:T(8,128)(2,1)S(1)} %add_convert_fusion.3), channel_id=1, source_target_pairs={{0,15},{1,0},{2,1},{3,2},{4,3},{5,4},{6,5},{7,6},{8,7},{9,8},{10,9... | collective-permute-start | bytes 884744 | tf_op jit(solution)/shard_map/cond/branch_0_fun/ppermute | solution.py:28
  137.4 8.7 %collective-permute-start.6 = (bf16[64,2304]{1,0:T(8,128)(2,1)S(1)}, bf16[64,2304]{1,0:T(8,128)(2,1)S(1)}, u32[]{:S(2)}, u32[]{:S(2)}) collective-permute-start(bf16[64,2304]{1,0:T(8,128)(2,1)S(1)} %add_convert_fusion.8), channel_id=1, source_target_pairs={{0,1},{1,2},{2,3},{3,4},{4,5},{5,6},{6,7},{7,8},{8,9},{9,10},{10,1... | collective-permute-start | bytes 884744 | tf_op jit(solution)/shard_map/cond/branch_0_fun/ppermute | solution.py:28
  139.4 8.7 %collective-permute-start.13 = (bf16[64,2304]{1,0:T(8,128)(2,1)S(1)}, bf16[64,2304]{1,0:T(8,128)(2,1)S(1)}, u32[]{:S(2)}, u32[]{:S(2)}) collective-permute-start(bf16[64,2304]{1,0:T(8,128)(2,1)S(1)} %add_convert_fusion.2), channel_id=1, source_target_pairs={{0,15},{1,0},{2,1},{3,2},{4,3},{5,4},{6,5},{7,6},{8,7},{9,8},{10,9... | collective-permute-start | bytes 884744 | tf_op jit(solution)/shard_map/cond/branch_0_fun/ppermute | solution.py:28
  146.1 8.7 %collective-permute-start.7 = (bf16[64,2304]{1,0:T(8,128)(2,1)S(1)}, bf16[64,2304]{1,0:T(8,128)(2,1)S(1)}, u32[]{:S(2)}, u32[]{:S(2)}) collective-permute-start(bf16[64,2304]{1,0:T(8,128)(2,1)S(1)} %add_convert_fusion.7), channel_id=1, source_target_pairs={{0,1},{1,2},{2,3},{3,4},{4,5},{5,6},{6,7},{7,8},{8,9},{9,10},{10,1... | collective-permute-start | bytes 884744 | tf_op jit(solution)/shard_map/cond/branch_0_fun/ppermute | solution.py:28
  148.1 8.7 %collective-permute-start.14 = (bf16[64,2304]{1,0:T(8,128)(2,1)S(1)}, bf16[64,2304]{1,0:T(8,128)(2,1)S(1)}, u32[]{:S(2)}, u32[]{:S(2)}) collective-permute-start(bf16[64,2304]{1,0:T(8,128)(2,1)S(1)} %add_convert_fusion.1), channel_id=1, source_target_pairs={{0,15},{1,0},{2,1},{3,2},{4,3},{5,4},{6,5},{7,6},{8,7},{9,8},{10,9... | collective-permute-start | bytes 884744 | tf_op jit(solution)/shard_map/cond/branch_0_fun/ppermute | solution.py:28
  154.9 8.7 %collective-permute-start.8 = (bf16[64,2304]{1,0:T(8,128)(2,1)S(1)}, bf16[64,2304]{1,0:T(8,128)(2,1)S(1)}, u32[]{:S(2)}, u32[]{:S(2)}) collective-permute-start(bf16[64,2304]{1,0:T(8,128)(2,1)S(1)} %add_convert_fusion.6), channel_id=1, source_target_pairs={{0,1},{1,2},{2,3},{3,4},{4,5},{5,6},{6,7},{7,8},{8,9},{9,10},{10,1... | collective-permute-start | bytes 884744 | tf_op jit(solution)/shard_map/cond/branch_0_fun/ppermute | solution.py:28
  156.9 8.4 %collective-permute-start.15 = (bf16[64,2304]{1,0:T(8,128)(2,1)S(1)}, bf16[64,2304]{1,0:T(8,128)(2,1)S(1)}, u32[]{:S(2)}, u32[]{:S(2)}) collective-permute-start(bf16[64,2304]{1,0:T(8,128)(2,1)S(1)} %add_convert_fusion), channel_id=1, source_target_pairs={{0,15},{1,0},{2,1},{3,2},{4,3},{5,4},{6,5},{7,6},{8,7},{9,8},{10,9... | collective-permute-start | bytes 884744 | tf_op jit(solution)/shard_map/cond/branch_0_fun/ppermute | solution.py:28
  166.4 29.1 %collective-permute-start.36 = (bf16[32,2304]{1,0:T(8,128)(2,1)S(1)}, bf16[32,2304]{1,0:T(8,128)(2,1)S(1)}, u32[]{:S(2)}, u32[]{:S(2)}) collective-permute-start(bf16[32,2304]{1,0:T(8,128)(2,1)S(1)} %get-tuple-element.95), channel_id=1, source_target_pairs={{16,32},{32,16},{48,64},{64,48},{80,96},{96,80},{112,128},{128,112... | collective-permute-start | bytes 442376 | tf_op jit(solution)/shard_map/ppermute | solution.py:36
  192.7 3.3 %collective-permute-start.37 = (bf16[32,2304]{1,0:T(8,128)(2,1)S(1)}, bf16[32,2304]{1,0:T(8,128)(2,1)S(1)}, u32[]{:S(2)}, u32[]{:S(2)}) collective-permute-start(bf16[32,2304]{1,0:T(8,128)(2,1)S(1)} %get-tuple-element.96), channel_id=1, source_target_pairs={{0,16},{16,0},{32,48},{48,32},{64,80},{80,64},{96,112},{112,96},{1... | collective-permute-start | bytes 442376 | tf_op jit(solution)/shard_map/ppermute | solution.py:36

commit v6 on v5

--- a/solution.py
+++ b/solution.py
@@ -330,6 +330,7 @@
     wv_ref,
     wo_ref,
     parcels_ref,
+    packed,
 ):
     rows = qkv_ref.shape[0]
     feats = wq_ref.shape[0]
@@ -360,51 +361,94 @@
     fold_col = lax.broadcasted_iota(jnp.int32, (rows, length), 1)
     fold = (fold_row % length == fold_col).astype(BF16)
     shares = [dot(c, fold) for c in raws + [p.astype(BF16) for p in probs] + [picks]]
-    kinds = len(vectors)
-    vectors = jnp.concatenate(vectors, axis=0).astype(BF16)
+    owners = length // own
+    lanes, slots, width, half = parcel_shape(len(vectors), feats, owners)
+    stride = owners * slots
+    packed[...] = jnp.zeros(packed.shape, F32)
+    for i in range(len(vectors) * feats // lanes):
+        vector, place = divmod(i * lanes, feats)
+        owner, block = divmod(i, half)
+        slot, at = divmod(block * lanes, width)
+        packed[at // lanes, pl.ds(owner * slots + slot, RESP, stride=stride), :] = vectors[vector][
+            :, place : place + lanes
+        ]
+    per = lanes // own
+    for owner in range(owners):
+        for first in range(0, len(shares), per):
+            slot, at = divmod((half + first // per) * lanes, width)
+            some = [s[:, owner * own : (owner + 1) * own] for s in shares[first : first + per]]
+            some += [jnp.zeros((RESP, own), F32)] * (per - len(some))
+            packed[at // lanes, pl.ds(owner * slots + slot, RESP, stride=stride), :] = (
+                jnp.concatenate(some, axis=1)
+            )
+    for i in range(width // lanes):
+        parcels_ref[:, i * lanes : (i + 1) * lanes] = packed[i].astype(BF16)
+
+
+def parcel_shape(kinds, feats, owners):
+    lanes, slots = 128, 8
+    half = kinds * feats // lanes // owners
+    blocks = half + 2
+    return lanes, slots, -(-blocks // slots) * lanes, half
+
+
+def unpack_kernel(kinds, me_ref, mine_ref, theirs_ref, out_ref, mine, theirs):
+    own, feats = out_ref.shape
+    owners = 2
+    lanes, slots, width, half = parcel_shape(kinds, feats, owners)
+    count = mine_ref.shape[0] // slots
+    for i in range(width // lanes):
+        mine[i] = mine_ref[:, i * lanes : (i + 1) * lanes].astype(F32)
+        theirs[i] = theirs_ref[:, i * lanes : (i + 1) * lanes].astype(F32)
+    second = lax.rem(me_ref[0], owners) == 1
+
+    def block_of(ref, block):
+        slot, at = divmod(block * lanes, width)
+        return ref[at // lanes, pl.ds(slot, count, stride=slots), :]
+
+    per = lanes // own
+    shares = [block_of(mine, half + k // per)[:, k % per * own : (k % per + 1) * own] for k in range(kinds)]
     shares = jnp.concatenate(shares, axis=0).astype(BF16)
-    slots = parcels_ref.shape[0] // count
-    out_row = lax.broadcasted_iota(jnp.int32, (count * slots, kinds * RESP), 0)
-    source = lax.broadcasted_iota(jnp.int32, (count * slots, kinds * RESP), 1)
-    owner, slot = out_row // slots, out_row % slots
-    choose = ((slot == source // RESP) & (owner // (length // own) == source % RESP)).astype(BF16)
-    share = length // own
-    half = (lax.broadcasted_iota(jnp.int32, (count * slots, 1), 0) // slots) % share
-    width = feats // share
-    lanes = jnp.zeros((count * slots, width), F32)
-    chosen = dot(choose, shares)
-    part = jnp.zeros((count * slots, own), F32)
-    for i in range(share):
-        lanes = jnp.where(half == i, dot(choose, vectors[:, i * width : (i + 1) * width]), lanes)
-        part = jnp.where(half == i, chosen[:, i * own : (i + 1) * own], part)
-    parcels_ref[:, :width] = lanes.astype(BF16)
-    tail = jnp.zeros((count * slots, 128 - own), F32)
-    parcels_ref[:, width:] = jnp.concatenate([part, tail], axis=1).astype(BF16)
-
-
-def scored_part(positions, row_grads, qkv, weights, count, length, section):
-    width = row_grads.shape[1] // 2
+    for place in range(0, feats, lanes):
+        parts = []
+        for vector in range(kinds):
+            owner, block = divmod((vector * feats + place) // lanes, half)
+            here, there = block_of(mine, block), block_of(theirs, block)
+            swap = second if owner == 0 else jnp.logical_not(second)
+            parts.append(jnp.where(swap, there, here))
+        out_ref[:, place : place + lanes] = dot_tn(shares, jnp.concatenate(parts, axis=0).astype(BF16))
+
+
+def scored_part(me, positions, row_grads, qkv, weights, count, length, section):
+    feats = row_grads.shape[1]
     own = qkv.shape[0] // count
     vmem = pl.BlockSpec(memory_space=pltpu.VMEM)
-    slots = 8
+    smem = pl.BlockSpec(memory_space=pltpu.SMEM)
+    kinds = 2 * (weights[0].shape[1] // HEAD_DIM) + 1
+    lanes, slots, width, _ = parcel_shape(kinds, feats, length // own)
+    shape = (count * slots, width)
+    blocks = pltpu.VMEM((width // lanes, count * slots, lanes), F32)
     parcels = pl.pallas_call(
         functools.partial(scored_kernel, count, length),
-        out_shape=jax.ShapeDtypeStruct((count * slots, width + 128), BF16),
+        out_shape=jax.ShapeDtypeStruct(shape, BF16),
         in_specs=[vmem] * 7,
         out_specs=vmem,
+        scratch_shapes=[blocks],
         compiler_params=pltpu.CompilerParams(vmem_limit_bytes=VMEM_LIMIT),
         name="scored_backward",
     )(positions, row_grads, qkv, *weights)
-    parcels = lax.all_to_all(parcels.reshape(count, slots, -1), "tensor", 0, 0)
-    parcels = parcels.reshape(count * slots, -1)
-    vectors, shares = parcels[:, :width], parcels[:, width : width + own]
+    mine = lax.all_to_all(parcels.reshape(count, slots, width), "tensor", 0, 0).reshape(shape)
     swaps = [(section * count + i, section * count + (i ^ 1)) for i in range(count)]
-    swapped = lax.ppermute(vectors, ("section", "tensor"), swaps)
-    mine, theirs = dot_tn(shares, vectors), dot_tn(shares, swapped)
-    second = lax.axis_index("tensor") % 2 == 1
-    return jnp.concatenate(
-        [jnp.where(second, theirs, mine), jnp.where(second, mine, theirs)], axis=1
-    )
+    theirs = lax.ppermute(mine, ("section", "tensor"), swaps)
+    return pl.pallas_call(
+        functools.partial(unpack_kernel, kinds),
+        out_shape=jax.ShapeDtypeStruct((own, feats), F32),
+        in_specs=[smem, vmem, vmem],
+        out_specs=vmem,
+        scratch_shapes=[blocks] * 2,
+        compiler_params=pltpu.CompilerParams(vmem_limit_bytes=VMEM_LIMIT),
+        name="scored_sums",
+    )(me, mine, theirs)
 
 
 def finish_kernel(
@@ -477,7 +521,7 @@
         up = (up.astype(F32) + terms[left].astype(F32)).astype(BF16)
         down = (down.astype(F32) + terms[-left].astype(F32)).astype(BF16)
         if left == far - 1:
-            up, down, rest_rows = lax.optimization_barrier((up, down, rest_rows))
+            up, rest_rows = lax.optimization_barrier((up, rest_rows))
             terms.update(zip(back_offsets[3:], terms_of(weights, rest_rows, own)))
         up, down = shift(up, 1, sections), shift(down, -1, sections)
     return terms[0].astype(F32) + up.astype(F32) + down.astype(F32)
@@ -543,7 +587,7 @@
         )
         row_grads = row_grads.astype(BF16).astype(F32)
         back_own = scored_part(
-            places, row_grads, qkv, weights, tensor_count, length, last
+            me, places, row_grads, qkv, weights, tensor_count, length, last
         )
         return jnp.concatenate([jnp.zeros_like(back_own), back_own]), row_grads
 

time: 198 us -> 193 us (0.975)
  the two profiles are of different devices: /device:TPU:23 before, /device:TPU:1 now
where the time goes in v6:
time: 193 us; the launch traced here: 192 us
  starting transfers between devices  128 us (66%)
  waiting for transfers between devices  46.1 us (24%)
  Pallas kernels  12.4 us (6%)
  other arithmetic  2.86 us (1%)
    ppermute x31, starting transfers between devices, shift(): return lax.ppermute(value, ('section', 'tensor'), pairs)  107 us
    ppermute x31, waiting for transfers between devices, shift(): return lax.ppermute(value, ('section', 'tensor'), pairs)  44.8 us
    ppermute x2, starting transfers between devices, swap_sections(): return lax.ppermute(value, 'section', pairs)  21.4 us
    pallas_call x1, Pallas kernels, early_part(): pl.pallas_call(early_kernel, out_shape=jax.ShapeDtypeStruct((rows, cols),...  4.66 us
    pallas_call x1, Pallas kernels, layer_part(): pl.pallas_call(functools.partial(layer_kernel, offsets, back_offsets, len...  4.03 us
  transfers between devices with their start and end apart: 33, of which 19 were waited for; matrix products, arithmetic and copies ran while one was open for 1% of the time, Pallas kernels for 4%

profile of v6, /device:TPU:1, one launch (start us, length us, event | category | flops | bytes accessed | tf_op | source)
XLA Modules:
  0.0 191.5 jit_solution(15708827640458913098)
XLA Ops:
  1.6 4.4 %collective-permute-start.21 = (bf16[64,2304]{1,0:T(8,128)(2,1)S(1)}, bf16[64,2304]{1,0:T(8,128)(2,1)S(1)}, u32[]{:S(2)}, u32[]{:S(2)}) collective-permute-start(bf16[64,2304]{1,0:T(8,128)(2,1)S(1)} %pad_maximum_fusion.refs_0_), channel_id=1, source_target_pairs={{0,1},{1,2},{2,3},{3,4},{4,5},{5,6},{6,7},{7,8},{8,9},{9,10},{10,1... | collective-permute-start | bytes 884744 | tf_op jit(solution)/shard_map/ppermute | solution.py:28
  6.0 9.5 %collective-permute-start.22 = (bf16[64,2304]{1,0:T(8,128)(2,1)S(1)}, bf16[64,2304]{1,0:T(8,128)(2,1)S(1)}, u32[]{:S(2)}, u32[]{:S(2)}) collective-permute-start(bf16[64,2304]{1,0:T(8,128)(2,1)S(1)} %pad_maximum_fusion.refs_0_), channel_id=1, source_target_pairs={{0,15},{1,0},{2,1},{3,2},{4,3},{5,4},{6,5},{7,6},{8,7},{9,8},{10,9... | collective-permute-start | bytes 884744 | tf_op jit(solution)/shard_map/ppermute | solution.py:28
  15.5 4.8 %collective-permute-done.21.refs_1_ = bf16[64,2304]{1,0:T(8,128)(2,1)S(1)} collective-permute-done((bf16[64,2304]{1,0:T(8,128)(2,1)S(1)}, bf16[64,2304]{1,0:T(8,128)(2,1)S(1)}, u32[]{:S(2)}, u32[]{:S(2)}) %collective-permute-start.21) | collective-permute-done | bytes 294944 | tf_op jit(solution)/shard_map/ppermute | solution.py:28
  20.3 1.9 collective-permute-start.23
  22.2 4.6 %collective-permute-start.24 = (bf16[64,2304]{1,0:T(8,128)(2,1)S(1)}, bf16[64,2304]{1,0:T(8,128)(2,1)S(1)}, u32[]{:S(2)}, u32[]{:S(2)}) collective-permute-start(bf16[64,2304]{1,0:T(8,128)(2,1)S(1)} %collective-permute-done.22.refs_2_), channel_id=1, source_target_pairs={{0,15},{1,0},{2,1},{3,2},{4,3},{5,4},{6,5},{7,6},{8,7},{9,8},{10,9... | collective-permute-start | bytes 884744 | tf_op jit(solution)/shard_map/ppermute | solution.py:28
  26.8 3.9 %collective-permute-done.23.refs_3_ = bf16[64,2304]{1,0:T(8,128)(2,1)S(1)} collective-permute-done((bf16[64,2304]{1,0:T(8,128)(2,1)S(1)}, bf16[64,2304]{1,0:T(8,128)(2,1)S(1)}, u32[]{:S(2)}, u32[]{:S(2)}) %collective-permute-start.23) | collective-permute-done | bytes 294944 | tf_op jit(solution)/shard_map/ppermute | solution.py:28
  30.7 1.9 collective-permute-start.25
  32.6 4.6 %collective-permute-start.26 = (bf16[64,2304]{1,0:T(8,128)(2,1)S(1)}, bf16[64,2304]{1,0:T(8,128)(2,1)S(1)}, u32[]{:S(2)}, u32[]{:S(2)}) collective-permute-start(bf16[64,2304]{1,0:T(8,128)(2,1)S(1)} %collective-permute-done.24.refs_4_), channel_id=1, source_target_pairs={{0,15},{1,0},{2,1},{3,2},{4,3},{5,4},{6,5},{7,6},{8,7},{9,8},{10,9... | collective-permute-start | bytes 884744 | tf_op jit(solution)/shard_map/ppermute | solution.py:28
  37.2 2.9 %collective-permute-done.25.refs_5_ = bf16[64,2304]{1,0:T(8,128)(2,1)S(1)} collective-permute-done((bf16[64,2304]{1,0:T(8,128)(2,1)S(1)}, bf16[64,2304]{1,0:T(8,128)(2,1)S(1)}, u32[]{:S(2)}, u32[]{:S(2)}) %collective-permute-start.25) | collective-permute-done | bytes 294944 | tf_op jit(solution)/shard_map/ppermute | solution.py:28
  40.1 1.9 collective-permute-start.27
  42.1 4.6 %collective-permute-start.28 = (bf16[64,2304]{1,0:T(8,128)(2,1)S(1)}, bf16[64,2304]{1,0:T(8,128)(2,1)S(1)}, u32[]{:S(2)}, u32[]{:S(2)}) collective-permute-start(bf16[64,2304]{1,0:T(8,128)(2,1)S(1)} %collective-permute-done.26.refs_6_), channel_id=1, source_target_pairs={{0,15},{1,0},{2,1},{3,2},{4,3},{5,4},{6,5},{7,6},{8,7},{9,8},{10,9... | collective-permute-start | bytes 884744 | tf_op jit(solution)/shard_map/ppermute | solution.py:28
  46.6 2.2 %collective-permute-done.27.refs_7_ = bf16[64,2304]{1,0:T(8,128)(2,1)S(1)} collective-permute-done((bf16[64,2304]{1,0:T(8,128)(2,1)S(1)}, bf16[64,2304]{1,0:T(8,128)(2,1)S(1)}, u32[]{:S(2)}, u32[]{:S(2)}) %collective-permute-start.27) | collective-permute-done | bytes 294944 | tf_op jit(solution)/shard_map/ppermute | solution.py:28
  50.7 4.6 %collective-permute-start.30 = (bf16[64,2304]{1,0:T(8,128)(2,1)S(1)}, bf16[64,2304]{1,0:T(8,128)(2,1)S(1)}, u32[]{:S(2)}, u32[]{:S(2)}) collective-permute-start(bf16[64,2304]{1,0:T(8,128)(2,1)S(1)} %collective-permute-done.28.refs_8_), channel_id=1, source_target_pairs={{0,15},{1,0},{2,1},{3,2},{4,3},{5,4},{6,5},{7,6},{8,7},{9,8},{10,9... | collective-permute-start | bytes 884744 | tf_op jit(solution)/shard_map/ppermute | solution.py:28
  55.3 2.2 %collective-permute-done.29.refs_9_ = bf16[64,2304]{1,0:T(8,128)(2,1)S(1)} collective-permute-done((bf16[64,2304]{1,0:T(8,128)(2,1)S(1)}, bf16[64,2304]{1,0:T(8,128)(2,1)S(1)}, u32[]{:S(2)}, u32[]{:S(2)}) %collective-permute-start.29) | collective-permute-done | bytes 294944 | tf_op jit(solution)/shard_map/ppermute | solution.py:28
  59.4 4.6 %collective-permute-start.32 = (bf16[64,2304]{1,0:T(8,128)(2,1)S(1)}, bf16[64,2304]{1,0:T(8,128)(2,1)}, u32[]{:S(2)}, u32[]{:S(2)}) collective-permute-start(bf16[64,2304]{1,0:T(8,128)(2,1)S(1)} %collective-permute-done.30.refs_10_), channel_id=1, source_target_pairs={{0,15},{1,0},{2,1},{3,2},{4,3},{5,4},{6,5},{7,6},{8,7},{9,8},{10,9... | collective-permute-start | bytes 884744 | tf_op jit(solution)/shard_map/ppermute | solution.py:28
  64.0 2.2 %collective-permute-done.31.refs_11_ = bf16[64,2304]{1,0:T(8,128)(2,1)S(1)} collective-permute-done((bf16[64,2304]{1,0:T(8,128)(2,1)S(1)}, bf16[64,2304]{1,0:T(8,128)(2,1)S(1)}, u32[]{:S(2)}, u32[]{:S(2)}) %collective-permute-start.31) | collective-permute-done | bytes 294944 | tf_op jit(solution)/shard_map/ppermute | solution.py:28
  66.1 1.9 collective-permute-start.33
  68.8 4.6 %collective-permute-start.34 = (bf16[64,2304]{1,0:T(8,128)(2,1)}, bf16[64,2304]{1,0:T(8,128)(2,1)}, u32[]{:S(2)}, u32[]{:S(2)}) collective-permute-start(bf16[64,2304]{1,0:T(8,128)(2,1)} %collective-permute-done.32.refs_12_), channel_id=1, source_target_pairs={{0,15},{1,0},{2,1},{3,2},{4,3},{5,4},{6,5},{7,6},{8,7},{9,8},{10,9... | collective-permute-start | bytes 884744 | tf_op jit(solution)/shard_map/ppermute | solution.py:28
  75.2 1.9 collective-permute-start.35
  77.4 4.7 %early_rows.1 = bf16[480,768]{1,0:T(8,128)(2,1)S(1)} custom-call(bf16[1,2304]{1,0:T(2,128)(2,1)} %gain_ref.3, bf16[2304,256]{1,0:T(8,128)(2,1)} %bitcast.22, bf16[2304,128]{1,0:T(8,128)(2,1)} %bitcast.28, bf16[2304,128]{1,0:T(8,128)(2,1)} %bitcast.31, bf16[256,2304]{1,0:T(8,128)(2,1)} %bitcast.25, bf16[64,2304]{1,0:T(8,128)(2,1)S(1)} %pad_maximum_fusion.refs_0_, ...), custom_call_target="tpu_custom_call" | custom-call | flops 1698693120 | bytes 4423680 | tf_op jit(solution)/shard_map/early_rows/pallas_call | solution.py:104
  82.0 3.2 %collective-permute-done.35 = bf16[64,2304]{1,0:T(8,128)(2,1)} collective-permute-done((bf16[64,2304]{1,0:T(8,128)(2,1)}, bf16[64,2304]{1,0:T(8,128)(2,1)}, u32[]{:S(2)}, u32[]{:S(2)}) %collective-permute-start.35) | collective-permute-done | bytes 294944 | tf_op jit(solution)/shard_map/ppermute | solution.py:28
  85.4 81.6 %conditional.1 = (f32[64,2304]{1,0:T(8,128)S(1)}, f32[8,2304]{1,0:T(8,128)S(1)}) conditional(s32[]{:T(128)} %convert_element_type.155, (s32[3]{0:T(128)S(1)}, bf16[1,2304]{1,0:T(2,128)(2,1)S(1)}, bf16[2304,256]{1,0:T(8,128)(2,1)S(1)}, bf16[2304,128]{1,0:T(8,128)(2,1)S(1)}, bf16[2304,128]{1,0:T(8,128)(2,1)S(1)}, ...), branch_computations={%region_0.1_spmd, %region_1.9_spmd} | conditional | flops 1707687936 | bytes 31335060 | solution.py:594
  85.4 4.0 %layer_both_ways.1 = (bf16[32,2304]{1,0:T(8,128)(2,1)S(1)}, bf16[32,2304]{1,0:T(8,128)(2,1)S(1)}, bf16[64,768]{1,0:T(8,128)(2,1)S(1)}, bf16[416,768]{1,0:T(8,128)(2,1)S(1)}) custom-call(s32[3]{0:T(128)S(1)} %get-tuple-element.46.me_ref, bf16[1,2304]{1,0:T(2,128)(2,1)S(1)} %get-tuple-element.47.gain_ref, bf16[2304,256]{1,0:T(8,128)(2,1)S(1)} %get-tuple-element.42.wq_ref, ...), custom_call_target="tpu_custom_call" | custom-call | tf_op jit(solution)/shard_map/cond/branch_0_fun/layer_both_ways/pallas_call | solution.py:285
  89.4 1.9 %collective-permute-start = (bf16[32,2304]{1,0:T(8,128)(2,1)S(1)}, bf16[32,2304]{1,0:T(8,128)(2,1)S(1)}, u32[]{:S(2)}, u32[]{:S(2)}) collective-permute-start(bf16[32,2304]{1,0:T(8,128)(2,1)S(1)} %get-tuple-element.50), channel_id=1, source_target_pairs={{0,1},{1,2},{2,3},{3,4},{4,5},{5,6},{6,7},{7,8},{8,9},{9,10},{10,1... | collective-permute-start | bytes 442376 | tf_op jit(solution)/shard_map/cond/branch_0_fun/ppermute | solution.py:28
  91.4 4.6 %collective-permute-start.8 = (bf16[32,2304]{1,0:T(8,128)(2,1)S(1)}, bf16[32,2304]{1,0:T(8,128)(2,1)S(1)}, u32[]{:S(2)}, u32[]{:S(2)}) collective-permute-start(bf16[32,2304]{1,0:T(8,128)(2,1)S(1)} %get-tuple-element.63), channel_id=1, source_target_pairs={{0,15},{1,0},{2,1},{3,2},{4,3},{5,4},{6,5},{7,6},{8,7},{9,8},{10,9... | collective-permute-start | bytes 442376 | tf_op jit(solution)/shard_map/cond/branch_0_fun/ppermute | solution.py:28
  97.1 1.9 %collective-permute-start.1 = (bf16[64,2304]{1,0:T(8,128)(2,1)S(1)}, bf16[64,2304]{1,0:T(8,128)(2,1)S(1)}, u32[]{:S(2)}, u32[]{:S(2)}) collective-permute-start(bf16[64,2304]{1,0:T(8,128)(2,1)S(1)} %add_convert_fusion.13), channel_id=1, source_target_pairs={{0,1},{1,2},{2,3},{3,4},{4,5},{5,6},{6,7},{7,8},{8,9},{9,10},{10,1... | collective-permute-start | bytes 884744 | tf_op jit(solution)/shard_map/cond/branch_0_fun/ppermute | solution.py:28
  99.1 4.6 %collective-permute-start.9 = (bf16[64,2304]{1,0:T(8,128)(2,1)S(1)}, bf16[64,2304]{1,0:T(8,128)(2,1)S(1)}, u32[]{:S(2)}, u32[]{:S(2)}) collective-permute-start(bf16[64,2304]{1,0:T(8,128)(2,1)S(1)} %add_convert_fusion.6), channel_id=1, source_target_pairs={{0,15},{1,0},{2,1},{3,2},{4,3},{5,4},{6,5},{7,6},{8,7},{9,8},{10,9... | collective-permute-start | bytes 884744 | tf_op jit(solution)/shard_map/cond/branch_0_fun/ppermute | solution.py:28
  105.3 2.3 %collective-permute-done.1 = bf16[64,2304]{1,0:T(8,128)(2,1)S(1)} collective-permute-done((bf16[64,2304]{1,0:T(8,128)(2,1)S(1)}, bf16[64,2304]{1,0:T(8,128)(2,1)S(1)}, u32[]{:S(2)}, u32[]{:S(2)}) %collective-permute-start.1) | collective-permute-done | bytes 294944 | tf_op jit(solution)/shard_map/cond/branch_0_fun/ppermute | solution.py:28
  107.7 1.9 %collective-permute-start.2 = (bf16[64,2304]{1,0:T(8,128)(2,1)S(1)}, bf16[64,2304]{1,0:T(8,128)(2,1)S(1)}, u32[]{:S(2)}, u32[]{:S(2)}) collective-permute-start(bf16[64,2304]{1,0:T(8,128)(2,1)S(1)} %add_convert_fusion.12), channel_id=1, source_target_pairs={{0,1},{1,2},{2,3},{3,4},{4,5},{5,6},{6,7},{7,8},{8,9},{9,10},{10,1... | collective-permute-start | bytes 884744 | tf_op jit(solution)/shard_map/cond/branch_0_fun/ppermute | solution.py:28
  109.7 4.6 %collective-permute-start.10 = (bf16[64,2304]{1,0:T(8,128)(2,1)S(1)}, bf16[64,2304]{1,0:T(8,128)(2,1)S(1)}, u32[]{:S(2)}, u32[]{:S(2)}) collective-permute-start(bf16[64,2304]{1,0:T(8,128)(2,1)S(1)} %add_convert_fusion.5), channel_id=1, source_target_pairs={{0,15},{1,0},{2,1},{3,2},{4,3},{5,4},{6,5},{7,6},{8,7},{9,8},{10,9... | collective-permute-start | bytes 884744 | tf_op jit(solution)/shard_map/cond/branch_0_fun/ppermute | solution.py:28
  114.3 4.7 %collective-permute-done.2 = bf16[64,2304]{1,0:T(8,128)(2,1)S(1)} collective-permute-done((bf16[64,2304]{1,0:T(8,128)(2,1)S(1)}, bf16[64,2304]{1,0:T(8,128)(2,1)S(1)}, u32[]{:S(2)}, u32[]{:S(2)}) %collective-permute-start.2) | collective-permute-done | bytes 294944 | tf_op jit(solution)/shard_map/cond/branch_0_fun/ppermute | solution.py:28
  119.1 1.9 %collective-permute-start.3 = (bf16[64,2304]{1,0:T(8,128)(2,1)S(1)}, bf16[64,2304]{1,0:T(8,128)(2,1)S(1)}, u32[]{:S(2)}, u32[]{:S(2)}) collective-permute-start(bf16[64,2304]{1,0:T(8,128)(2,1)S(1)} %add_convert_fusion.11), channel_id=1, source_target_pairs={{0,1},{1,2},{2,3},{3,4},{4,5},{5,6},{6,7},{7,8},{8,9},{9,10},{10,1... | collective-permute-start | bytes 884744 | tf_op jit(solution)/shard_map/cond/branch_0_fun/ppermute | solution.py:28
  121.1 4.6 %collective-permute-start.11 = (bf16[64,2304]{1,0:T(8,128)(2,1)S(1)}, bf16[64,2304]{1,0:T(8,128)(2,1)S(1)}, u32[]{:S(2)}, u32[]{:S(2)}) collective-permute-start(bf16[64,2304]{1,0:T(8,128)(2,1)S(1)} %add_convert_fusion.4), channel_id=1, source_target_pairs={{0,15},{1,0},{2,1},{3,2},{4,3},{5,4},{6,5},{7,6},{8,7},{9,8},{10,9... | collective-permute-start | bytes 884744 | tf_op jit(solution)/shard_map/cond/branch_0_fun/ppermute | solution.py:28
  125.7 3.8 %collective-permute-done.3 = bf16[64,2304]{1,0:T(8,128)(2,1)S(1)} collective-permute-done((bf16[64,2304]{1,0:T(8,128)(2,1)S(1)}, bf16[64,2304]{1,0:T(8,128)(2,1)S(1)}, u32[]{:S(2)}, u32[]{:S(2)}) %collective-permute-start.3) | collective-permute-done | bytes 294944 | tf_op jit(solution)/shard_map/cond/branch_0_fun/ppermute | solution.py:28
  129.6 1.9 %collective-permute-start.4 = (bf16[64,2304]{1,0:T(8,128)(2,1)S(1)}, bf16[64,2304]{1,0:T(8,128)(2,1)S(1)}, u32[]{:S(2)}, u32[]{:S(2)}) collective-permute-start(bf16[64,2304]{1,0:T(8,128)(2,1)S(1)} %add_convert_fusion.10), channel_id=1, source_target_pairs={{0,1},{1,2},{2,3},{3,4},{4,5},{5,6},{6,7},{7,8},{8,9},{9,10},{10,1... | collective-permute-start | bytes 884744 | tf_op jit(solution)/shard_map/cond/branch_0_fun/ppermute | solution.py:28
  131.6 4.6 %collective-permute-start.12 = (bf16[64,2304]{1,0:T(8,128)(2,1)S(1)}, bf16[64,2304]{1,0:T(8,128)(2,1)S(1)}, u32[]{:S(2)}, u32[]{:S(2)}) collective-permute-start(bf16[64,2304]{1,0:T(8,128)(2,1)S(1)} %add_convert_fusion.3), channel_id=1, source_target_pairs={{0,15},{1,0},{2,1},{3,2},{4,3},{5,4},{6,5},{7,6},{8,7},{9,8},{10,9... | collective-permute-start | bytes 884744 | tf_op jit(solution)/shard_map/cond/branch_0_fun/ppermute | solution.py:28
  136.2 2.9 %collective-permute-done.4 = bf16[64,2304]{1,0:T(8,128)(2,1)S(1)} collective-permute-done((bf16[64,2304]{1,0:T(8,128)(2,1)S(1)}, bf16[64,2304]{1,0:T(8,128)(2,1)S(1)}, u32[]{:S(2)}, u32[]{:S(2)}) %collective-permute-start.4) | collective-permute-done | bytes 294944 | tf_op jit(solution)/shard_map/cond/branch_0_fun/ppermute | solution.py:28
  139.2 1.9 %collective-permute-start.5 = (bf16[64,2304]{1,0:T(8,128)(2,1)S(1)}, bf16[64,2304]{1,0:T(8,128)(2,1)S(1)}, u32[]{:S(2)}, u32[]{:S(2)}) collective-permute-start(bf16[64,2304]{1,0:T(8,128)(2,1)S(1)} %add_convert_fusion.9), channel_id=1, source_target_pairs={{0,1},{1,2},{2,3},{3,4},{4,5},{5,6},{6,7},{7,8},{8,9},{9,10},{10,1... | collective-permute-start | bytes 884744 | tf_op jit(solution)/shard_map/cond/branch_0_fun/ppermute | solution.py:28
  141.2 4.6 %collective-permute-start.13 = (bf16[64,2304]{1,0:T(8,128)(2,1)S(1)}, bf16[64,2304]{1,0:T(8,128)(2,1)S(1)}, u32[]{:S(2)}, u32[]{:S(2)}) collective-permute-start(bf16[64,2304]{1,0:T(8,128)(2,1)S(1)} %add_convert_fusion.2), channel_id=1, source_target_pairs={{0,15},{1,0},{2,1},{3,2},{4,3},{5,4},{6,5},{7,6},{8,7},{9,8},{10,9... | collective-permute-start | bytes 884744 | tf_op jit(solution)/shard_map/cond/branch_0_fun/ppermute | solution.py:28
  145.8 2.1 %collective-permute-done.5 = bf16[64,2304]{1,0:T(8,128)(2,1)S(1)} collective-permute-done((bf16[64,2304]{1,0:T(8,128)(2,1)S(1)}, bf16[64,2304]{1,0:T(8,128)(2,1)S(1)}, u32[]{:S(2)}, u32[]{:S(2)}) %collective-permute-start.5) | collective-permute-done | bytes 294944 | tf_op jit(solution)/shard_map/cond/branch_0_fun/ppermute | solution.py:28
  147.9 1.9 %collective-permute-start.6 = (bf16[64,2304]{1,0:T(8,128)(2,1)S(1)}, bf16[64,2304]{1,0:T(8,128)(2,1)S(1)}, u32[]{:S(2)}, u32[]{:S(2)}) collective-permute-start(bf16[64,2304]{1,0:T(8,128)(2,1)S(1)} %add_convert_fusion.8), channel_id=1, source_target_pairs={{0,1},{1,2},{2,3},{3,4},{4,5},{5,6},{6,7},{7,8},{8,9},{9,10},{10,1... | collective-permute-start | bytes 884744 | tf_op jit(solution)/shard_map/cond/branch_0_fun/ppermute | solution.py:28
  149.9 4.6 %collective-permute-start.14 = (bf16[64,2304]{1,0:T(8,128)(2,1)S(1)}, bf16[64,2304]{1,0:T(8,128)(2,1)S(1)}, u32[]{:S(2)}, u32[]{:S(2)}) collective-permute-start(bf16[64,2304]{1,0:T(8,128)(2,1)S(1)} %add_convert_fusion.1), channel_id=1, source_target_pairs={{0,15},{1,0},{2,1},{3,2},{4,3},{5,4},{6,5},{7,6},{8,7},{9,8},{10,9... | collective-permute-start | bytes 884744 | tf_op jit(solution)/shard_map/cond/branch_0_fun/ppermute | solution.py:28
  154.5 2.1 %collective-permute-done.6 = bf16[64,2304]{1,0:T(8,128)(2,1)S(1)} collective-permute-done((bf16[64,2304]{1,0:T(8,128)(2,1)S(1)}, bf16[64,2304]{1,0:T(8,128)(2,1)S(1)}, u32[]{:S(2)}, u32[]{:S(2)}) %collective-permute-start.6) | collective-permute-done | bytes 294944 | tf_op jit(solution)/shard_map/cond/branch_0_fun/ppermute | solution.py:28
  156.7 1.9 %collective-permute-start.7 = (bf16[64,2304]{1,0:T(8,128)(2,1)S(1)}, bf16[64,2304]{1,0:T(8,128)(2,1)S(1)}, u32[]{:S(2)}, u32[]{:S(2)}) collective-permute-start(bf16[64,2304]{1,0:T(8,128)(2,1)S(1)} %add_convert_fusion.7), channel_id=1, source_target_pairs={{0,1},{1,2},{2,3},{3,4},{4,5},{5,6},{6,7},{7,8},{8,9},{9,10},{10,1... | collective-permute-start | bytes 884744 | tf_op jit(solution)/shard_map/cond/branch_0_fun/ppermute | solution.py:28
  158.7 4.6 %collective-permute-start.15 = (bf16[64,2304]{1,0:T(8,128)(2,1)S(1)}, bf16[64,2304]{1,0:T(8,128)(2,1)S(1)}, u32[]{:S(2)}, u32[]{:S(2)}) collective-permute-start(bf16[64,2304]{1,0:T(8,128)(2,1)S(1)} %add_convert_fusion), channel_id=1, source_target_pairs={{0,15},{1,0},{2,1},{3,2},{4,3},{5,4},{6,5},{7,6},{8,7},{9,8},{10,9... | collective-permute-start | bytes 884744 | tf_op jit(solution)/shard_map/cond/branch_0_fun/ppermute | solution.py:28
  163.3 2.1 %collective-permute-done.7 = bf16[64,2304]{1,0:T(8,128)(2,1)S(1)} collective-permute-done((bf16[64,2304]{1,0:T(8,128)(2,1)S(1)}, bf16[64,2304]{1,0:T(8,128)(2,1)S(1)}, u32[]{:S(2)}, u32[]{:S(2)}) %collective-permute-start.7) | collective-permute-done | bytes 294944 | tf_op jit(solution)/shard_map/cond/branch_0_fun/ppermute | solution.py:28
  168.1 19.5 %collective-permute-start.36 = (bf16[32,2304]{1,0:T(8,128)(2,1)S(1)}, bf16[32,2304]{1,0:T(8,128)(2,1)S(1)}, u32[]{:S(2)}, u32[]{:S(2)}) collective-permute-start(bf16[32,2304]{1,0:T(8,128)(2,1)S(1)} %get-tuple-element.94), channel_id=1, source_target_pairs={{16,32},{32,16},{48,64},{64,48},{80,96},{96,80},{112,128},{128,112... | collective-permute-start | bytes 442376 | tf_op jit(solution)/shard_map/ppermute | solution.py:36
  187.5 1.9 %collective-permute-start.37 = (bf16[32,2304]{1,0:T(8,128)(2,1)S(1)}, bf16[32,2304]{1,0:T(8,128)(2,1)S(1)}, u32[]{:S(2)}, u32[]{:S(2)}) collective-permute-start(bf16[32,2304]{1,0:T(8,128)(2,1)S(1)} %get-tuple-element.95), channel_id=1, source_target_pairs={{0,16},{16,0},{32,48},{48,32},{64,80},{80,64},{96,112},{112,96},{1... | collective-permute-start | bytes 442376 | tf_op jit(solution)/shard_map/ppermute | solution.py:36
  (69 shorter events, 16.1 us)
Async XLA Ops:
  1.6 18.7 %collective-permute-start.21 = (bf16[64,2304]{1,0:T(8,128)(2,1)S(1)}, bf16[64,2304]{1,0:T(8,128)(2,1)S(1)}, u32[]{:S(2)}, u32[]{:S(2)}) collective-permute-start(bf16[64,2304]{1,0:T(8,128)(2,1)S(1)} %pad_maximum_fusion.refs_0_), channel_id=1, source_target_pairs={{0,1},{1,2},{2,3},{3,4},{4,5},{5,6},{6,7},{7,8},{8,9},{9,10},{10,1... | collective-permute-start | bytes 884744 | tf_op jit(solution)/shard_map/ppermute | solution.py:28
  6.0 16.2 %collective-permute-start.22 = (bf16[64,2304]{1,0:T(8,128)(2,1)S(1)}, bf16[64,2304]{1,0:T(8,128)(2,1)S(1)}, u32[]{:S(2)}, u32[]{:S(2)}) collective-permute-start(bf16[64,2304]{1,0:T(8,128)(2,1)S(1)} %pad_maximum_fusion.refs_0_), channel_id=1, source_target_pairs={{0,15},{1,0},{2,1},{3,2},{4,3},{5,4},{6,5},{7,6},{8,7},{9,8},{10,9... | collective-permute-start | bytes 884744 | tf_op jit(solution)/shard_map/ppermute | solution.py:28
  20.3 10.4 %collective-permute-start.23 = (bf16[64,2304]{1,0:T(8,128)(2,1)S(1)}, bf16[64,2304]{1,0:T(8,128)(2,1)S(1)}, u32[]{:S(2)}, u32[]{:S(2)}) collective-permute-start(bf16[64,2304]{1,0:T(8,128)(2,1)S(1)} %collective-permute-done.21.refs_1_), channel_id=1, source_target_pairs={{0,1},{1,2},{2,3},{3,4},{4,5},{5,6},{6,7},{7,8},{8,9},{9,10},{10,1... | collective-permute-start | bytes 884744 | tf_op jit(solution)/shard_map/ppermute | solution.py:28
  22.2 10.4 %collective-permute-start.24 = (bf16[64,2304]{1,0:T(8,128)(2,1)S(1)}, bf16[64,2304]{1,0:T(8,128)(2,1)S(1)}, u32[]{:S(2)}, u32[]{:S(2)}) collective-permute-start(bf16[64,2304]{1,0:T(8,128)(2,1)S(1)} %collective-permute-done.22.refs_2_), channel_id=1, source_target_pairs={{0,15},{1,0},{2,1},{3,2},{4,3},{5,4},{6,5},{7,6},{8,7},{9,8},{10,9... | collective-permute-start | bytes 884744 | tf_op jit(solution)/shard_map/ppermute | solution.py:28
  30.7 9.4 %collective-permute-start.25 = (bf16[64,2304]{1,0:T(8,128)(2,1)S(1)}, bf16[64,2304]{1,0:T(8,128)(2,1)S(1)}, u32[]{:S(2)}, u32[]{:S(2)}) collective-permute-start(bf16[64,2304]{1,0:T(8,128)(2,1)S(1)} %collective-permute-done.23.refs_3_), channel_id=1, source_target_pairs={{0,1},{1,2},{2,3},{3,4},{4,5},{5,6},{6,7},{7,8},{8,9},{9,10},{10,1... | collective-permute-start | bytes 884744 | tf_op jit(solution)/shard_map/ppermute | solution.py:28
  32.6 9.4 %collective-permute-start.26 = (bf16[64,2304]{1,0:T(8,128)(2,1)S(1)}, bf16[64,2304]{1,0:T(8,128)(2,1)S(1)}, u32[]{:S(2)}, u32[]{:S(2)}) collective-permute-start(bf16[64,2304]{1,0:T(8,128)(2,1)S(1)} %collective-permute-done.24.refs_4_), channel_id=1, source_target_pairs={{0,15},{1,0},{2,1},{3,2},{4,3},{5,4},{6,5},{7,6},{8,7},{9,8},{10,9... | collective-permute-start | bytes 884744 | tf_op jit(solution)/shard_map/ppermute | solution.py:28
  40.1 8.7 %collective-permute-start.27 = (bf16[64,2304]{1,0:T(8,128)(2,1)S(1)}, bf16[64,2304]{1,0:T(8,128)(2,1)S(1)}, u32[]{:S(2)}, u32[]{:S(2)}) collective-permute-start(bf16[64,2304]{1,0:T(8,128)(2,1)S(1)} %collective-permute-done.25.refs_5_), channel_id=1, source_target_pairs={{0,1},{1,2},{2,3},{3,4},{4,5},{5,6},{6,7},{7,8},{8,9},{9,10},{10,1... | collective-permute-start | bytes 884744 | tf_op jit(solution)/shard_map/ppermute | solution.py:28
  42.1 8.7 %collective-permute-start.28 = (bf16[64,2304]{1,0:T(8,128)(2,1)S(1)}, bf16[64,2304]{1,0:T(8,128)(2,1)S(1)}, u32[]{:S(2)}, u32[]{:S(2)}) collective-permute-start(bf16[64,2304]{1,0:T(8,128)(2,1)S(1)} %collective-permute-done.26.refs_6_), channel_id=1, source_target_pairs={{0,15},{1,0},{2,1},{3,2},{4,3},{5,4},{6,5},{7,6},{8,7},{9,8},{10,9... | collective-permute-start | bytes 884744 | tf_op jit(solution)/shard_map/ppermute | solution.py:28
  48.8 8.7 %collective-permute-start.29 = (bf16[64,2304]{1,0:T(8,128)(2,1)S(1)}, bf16[64,2304]{1,0:T(8,128)(2,1)S(1)}, u32[]{:S(2)}, u32[]{:S(2)}) collective-permute-start(bf16[64,2304]{1,0:T(8,128)(2,1)S(1)} %collective-permute-done.27.refs_7_), channel_id=1, source_target_pairs={{0,1},{1,2},{2,3},{3,4},{4,5},{5,6},{6,7},{7,8},{8,9},{9,10},{10,1... | collective-permute-start | bytes 884744 | tf_op jit(solution)/shard_map/ppermute | solution.py:28
  50.7 8.7 %collective-permute-start.30 = (bf16[64,2304]{1,0:T(8,128)(2,1)S(1)}, bf16[64,2304]{1,0:T(8,128)(2,1)S(1)}, u32[]{:S(2)}, u32[]{:S(2)}) collective-permute-start(bf16[64,2304]{1,0:T(8,128)(2,1)S(1)} %collective-permute-done.28.refs_8_), channel_id=1, source_target_pairs={{0,15},{1,0},{2,1},{3,2},{4,3},{5,4},{6,5},{7,6},{8,7},{9,8},{10,9... | collective-permute-start | bytes 884744 | tf_op jit(solution)/shard_map/ppermute | solution.py:28
  57.5 8.7 %collective-permute-start.31 = (bf16[64,2304]{1,0:T(8,128)(2,1)S(1)}, bf16[64,2304]{1,0:T(8,128)(2,1)S(1)}, u32[]{:S(2)}, u32[]{:S(2)}) collective-permute-start(bf16[64,2304]{1,0:T(8,128)(2,1)S(1)} %collective-permute-done.29.refs_9_), channel_id=1, source_target_pairs={{0,1},{1,2},{2,3},{3,4},{4,5},{5,6},{6,7},{7,8},{8,9},{9,10},{10,1... | collective-permute-start | bytes 884744 | tf_op jit(solution)/shard_map/ppermute | solution.py:28
  59.4 9.4 %collective-permute-start.32 = (bf16[64,2304]{1,0:T(8,128)(2,1)S(1)}, bf16[64,2304]{1,0:T(8,128)(2,1)}, u32[]{:S(2)}, u32[]{:S(2)}) collective-permute-start(bf16[64,2304]{1,0:T(8,128)(2,1)S(1)} %collective-permute-done.30.refs_10_), channel_id=1, source_target_pairs={{0,15},{1,0},{2,1},{3,2},{4,3},{5,4},{6,5},{7,6},{8,7},{9,8},{10,9... | collective-permute-start | bytes 884744 | tf_op jit(solution)/shard_map/ppermute | solution.py:28
  66.1 9.1 %collective-permute-start.33 = (bf16[64,2304]{1,0:T(8,128)(2,1)S(1)}, bf16[64,2304]{1,0:T(8,128)(2,1)}, u32[]{:S(2)}, u32[]{:S(2)}) collective-permute-start(bf16[64,2304]{1,0:T(8,128)(2,1)S(1)} %collective-permute-done.31.refs_11_), channel_id=1, source_target_pairs={{0,1},{1,2},{2,3},{3,4},{4,5},{5,6},{6,7},{7,8},{8,9},{9,10},{10,1... | collective-permute-start | bytes 884744 | tf_op jit(solution)/shard_map/ppermute | solution.py:28
  68.8 8.5 %collective-permute-start.34 = (bf16[64,2304]{1,0:T(8,128)(2,1)}, bf16[64,2304]{1,0:T(8,128)(2,1)}, u32[]{:S(2)}, u32[]{:S(2)}) collective-permute-start(bf16[64,2304]{1,0:T(8,128)(2,1)} %collective-permute-done.32.refs_12_), channel_id=1, source_target_pairs={{0,15},{1,0},{2,1},{3,2},{4,3},{5,4},{6,5},{7,6},{8,7},{9,8},{10,9... | collective-permute-start | bytes 884744 | tf_op jit(solution)/shard_map/ppermute | solution.py:28
  75.2 10.1 %collective-permute-start.35 = (bf16[64,2304]{1,0:T(8,128)(2,1)}, bf16[64,2304]{1,0:T(8,128)(2,1)}, u32[]{:S(2)}, u32[]{:S(2)}) collective-permute-start(bf16[64,2304]{1,0:T(8,128)(2,1)} %collective-permute-done.33.refs_13_), channel_id=1, source_target_pairs={{0,1},{1,2},{2,3},{3,4},{4,5},{5,6},{6,7},{7,8},{8,9},{9,10},{10,1... | collective-permute-start | bytes 884744 | tf_op jit(solution)/shard_map/ppermute | solution.py:28
  77.2 8.1 %copy-start.10 = (s32[3]{0:T(128)}, s32[3]{0:T(128)S(1)}, u32[]{:S(2)}) copy-start(s32[3]{0:T(128)S(1)} %pad_add_fusion.me_ref) | copy-start | bytes 40
  77.3 8.0 %copy-start.1 = (bf16[1,2304,256]{2,1,0:T(8,128)(2,1)S(1)}, bf16[1,2304,256]{2,1,0:T(8,128)(2,1)}, u32[]{:S(2)}) copy-start(bf16[1,2304,256]{2,1,0:T(8,128)(2,1)} %param.16) | copy-start | bytes 3538948
  77.3 8.0 %copy-start.2 = (bf16[1,256,2304]{2,1,0:T(8,128)(2,1)S(1)}, bf16[1,256,2304]{2,1,0:T(8,128)(2,1)}, u32[]{:S(2)}) copy-start(bf16[1,256,2304]{2,1,0:T(8,128)(2,1)} %param.19) | copy-start | bytes 3538948
  77.3 8.0 %copy-start.3 = (bf16[1,2304,128]{2,1,0:T(8,128)(2,1)S(1)}, bf16[1,2304,128]{2,1,0:T(8,128)(2,1)}, u32[]{:S(2)}) copy-start(bf16[1,2304,128]{2,1,0:T(8,128)(2,1)} %param.17) | copy-start | bytes 1769476
  77.3 8.0 %copy-start.4 = (bf16[1,2304,128]{2,1,0:T(8,128)(2,1)S(1)}, bf16[1,2304,128]{2,1,0:T(8,128)(2,1)}, u32[]{:S(2)}) copy-start(bf16[1,2304,128]{2,1,0:T(8,128)(2,1)} %param.18) | copy-start | bytes 1769476
  77.3 8.0 %copy-start.5 = (bf16[1,1,32,2304]{3,2,1,0:T(8,128)(2,1)S(1)}, bf16[1,1,32,2304]{3,2,1,0:T(8,128)(2,1)}, u32[]{:S(2)}) copy-start(bf16[1,1,32,2304]{3,2,1,0:T(8,128)(2,1)} %param.13) | copy-start | bytes 442372
  77.3 8.0 %copy-start.9 = (bf16[1,2304]{1,0:T(2,128)(2,1)S(1)}, bf16[1,2304]{1,0:T(2,128)(2,1)}, u32[]{:S(2)}) copy-start(bf16[1,2304]{1,0:T(2,128)(2,1)} %gain_ref.3) | copy-start | bytes 13828
  77.3 8.0 %copy-start.11 = (bf16[2304]{0:T(1024)(128)(2,1)S(1)}, bf16[2304]{0:T(1024)(128)(2,1)}, u32[]{:S(2)}) copy-start(bf16[2304]{0:T(1024)(128)(2,1)} %param.20) | copy-start | bytes 13828
  77.4 8.0 %copy-start.12 = (bf16[2304]{0:T(1024)(128)(2,1)S(1)}, bf16[2304]{0:T(1024)(128)(2,1)}, u32[]{:S(2)}) copy-start(bf16[2304]{0:T(1024)(128)(2,1)} %param.21) | copy-start | bytes 13828
  77.4 8.0 %copy-start.13 = (s32[1,8]{1,0:T(1,128)S(1)}, s32[1,8]{1,0:T(1,128)}, u32[]{:S(2)}) copy-start(s32[1,8]{1,0:T(1,128)} %param.22) | copy-start | bytes 100
  85.4 81.7 %copy-start = (bf16[1,1,32,2304]{3,2,1,0:T(8,128)(2,1)S(1)}, bf16[1,1,32,2304]{3,2,1,0:T(8,128)(2,1)}, u32[]{:S(2)}) copy-start(bf16[1,1,32,2304]{3,2,1,0:T(8,128)(2,1)} %param.14) | copy-start | bytes 442372
  85.4 81.7 %copy-start.6 = (bf16[1,1,32,2304]{3,2,1,0:T(8,128)(2,1)S(1)}, bf16[1,1,32,2304]{3,2,1,0:T(8,128)(2,1)}, u32[]{:S(2)}) copy-start(bf16[1,1,32,2304]{3,2,1,0:T(8,128)(2,1)} %param.13) | copy-start | bytes 442372
  89.4 7.6 %collective-permute-start = (bf16[32,2304]{1,0:T(8,128)(2,1)S(1)}, bf16[32,2304]{1,0:T(8,128)(2,1)S(1)}, u32[]{:S(2)}, u32[]{:S(2)}) collective-permute-start(bf16[32,2304]{1,0:T(8,128)(2,1)S(1)} %get-tuple-element.50), channel_id=1, source_target_pairs={{0,1},{1,2},{2,3},{3,4},{4,5},{5,6},{6,7},{7,8},{8,9},{9,10},{10,1... | collective-permute-start | bytes 442376 | tf_op jit(solution)/shard_map/cond/branch_0_fun/ppermute | solution.py:28
  91.4 7.6 %collective-permute-start.8 = (bf16[32,2304]{1,0:T(8,128)(2,1)S(1)}, bf16[32,2304]{1,0:T(8,128)(2,1)S(1)}, u32[]{:S(2)}, u32[]{:S(2)}) collective-permute-start(bf16[32,2304]{1,0:T(8,128)(2,1)S(1)} %get-tuple-element.63), channel_id=1, source_target_pairs={{0,15},{1,0},{2,1},{3,2},{4,3},{5,4},{6,5},{7,6},{8,7},{9,8},{10,9... | collective-permute-start | bytes 442376 | tf_op jit(solution)/shard_map/cond/branch_0_fun/ppermute | solution.py:28
  97.1 10.5 %collective-permute-start.1 = (bf16[64,2304]{1,0:T(8,128)(2,1)S(1)}, bf16[64,2304]{1,0:T(8,128)(2,1)S(1)}, u32[]{:S(2)}, u32[]{:S(2)}) collective-permute-start(bf16[64,2304]{1,0:T(8,128)(2,1)S(1)} %add_convert_fusion.13), channel_id=1, source_target_pairs={{0,1},{1,2},{2,3},{3,4},{4,5},{5,6},{6,7},{7,8},{8,9},{9,10},{10,1... | collective-permute-start | bytes 884744 | tf_op jit(solution)/shard_map/cond/branch_0_fun/ppermute | solution.py:28
  99.1 10.6 %collective-permute-start.9 = (bf16[64,2304]{1,0:T(8,128)(2,1)S(1)}, bf16[64,2304]{1,0:T(8,128)(2,1)S(1)}, u32[]{:S(2)}, u32[]{:S(2)}) collective-permute-start(bf16[64,2304]{1,0:T(8,128)(2,1)S(1)} %add_convert_fusion.6), channel_id=1, source_target_pairs={{0,15},{1,0},{2,1},{3,2},{4,3},{5,4},{6,5},{7,6},{8,7},{9,8},{10,9... | collective-permute-start | bytes 884744 | tf_op jit(solution)/shard_map/cond/branch_0_fun/ppermute | solution.py:28
  107.7 11.3 %collective-permute-start.2 = (bf16[64,2304]{1,0:T(8,128)(2,1)S(1)}, bf16[64,2304]{1,0:T(8,128)(2,1)S(1)}, u32[]{:S(2)}, u32[]{:S(2)}) collective-permute-start(bf16[64,2304]{1,0:T(8,128)(2,1)S(1)} %add_convert_fusion.12), channel_id=1, source_target_pairs={{0,1},{1,2},{2,3},{3,4},{4,5},{5,6},{6,7},{7,8},{8,9},{9,10},{10,1... | collective-permute-start | bytes 884744 | tf_op jit(solution)/shard_map/cond/branch_0_fun/ppermute | solution.py:28
  109.7 11.3 %collective-permute-start.10 = (bf16[64,2304]{1,0:T(8,128)(2,1)S(1)}, bf16[64,2304]{1,0:T(8,128)(2,1)S(1)}, u32[]{:S(2)}, u32[]{:S(2)}) collective-permute-start(bf16[64,2304]{1,0:T(8,128)(2,1)S(1)} %add_convert_fusion.5), channel_id=1, source_target_pairs={{0,15},{1,0},{2,1},{3,2},{4,3},{5,4},{6,5},{7,6},{8,7},{9,8},{10,9... | collective-permute-start | bytes 884744 | tf_op jit(solution)/shard_map/cond/branch_0_fun/ppermute | solution.py:28
  119.1 10.4 %collective-permute-start.3 = (bf16[64,2304]{1,0:T(8,128)(2,1)S(1)}, bf16[64,2304]{1,0:T(8,128)(2,1)S(1)}, u32[]{:S(2)}, u32[]{:S(2)}) collective-permute-start(bf16[64,2304]{1,0:T(8,128)(2,1)S(1)} %add_convert_fusion.11), channel_id=1, source_target_pairs={{0,1},{1,2},{2,3},{3,4},{4,5},{5,6},{6,7},{7,8},{8,9},{9,10},{10,1... | collective-permute-start | bytes 884744 | tf_op jit(solution)/shard_map/cond/branch_0_fun/ppermute | solution.py:28
  121.1 10.4 %collective-permute-start.11 = (bf16[64,2304]{1,0:T(8,128)(2,1)S(1)}, bf16[64,2304]{1,0:T(8,128)(2,1)S(1)}, u32[]{:S(2)}, u32[]{:S(2)}) collective-permute-start(bf16[64,2304]{1,0:T(8,128)(2,1)S(1)} %add_convert_fusion.4), channel_id=1, source_target_pairs={{0,15},{1,0},{2,1},{3,2},{4,3},{5,4},{6,5},{7,6},{8,7},{9,8},{10,9... | collective-permute-start | bytes 884744 | tf_op jit(solution)/shard_map/cond/branch_0_fun/ppermute | solution.py:28
  129.6 9.5 %collective-permute-start.4 = (bf16[64,2304]{1,0:T(8,128)(2,1)S(1)}, bf16[64,2304]{1,0:T(8,128)(2,1)S(1)}, u32[]{:S(2)}, u32[]{:S(2)}) collective-permute-start(bf16[64,2304]{1,0:T(8,128)(2,1)S(1)} %add_convert_fusion.10), channel_id=1, source_target_pairs={{0,1},{1,2},{2,3},{3,4},{4,5},{5,6},{6,7},{7,8},{8,9},{9,10},{10,1... | collective-permute-start | bytes 884744 | tf_op jit(solution)/shard_map/cond/branch_0_fun/ppermute | solution.py:28
  131.6 9.5 %collective-permute-start.12 = (bf16[64,2304]{1,0:T(8,128)(2,1)S(1)}, bf16[64,2304]{1,0:T(8,128)(2,1)S(1)}, u32[]{:S(2)}, u32[]{:S(2)}) collective-permute-start(bf16[64,2304]{1,0:T(8,128)(2,1)S(1)} %add_convert_fusion.3), channel_id=1, source_target_pairs={{0,15},{1,0},{2,1},{3,2},{4,3},{5,4},{6,5},{7,6},{8,7},{9,8},{10,9... | collective-permute-start | bytes 884744 | tf_op jit(solution)/shard_map/cond/branch_0_fun/ppermute | solution.py:28
  139.2 8.7 %collective-permute-start.5 = (bf16[64,2304]{1,0:T(8,128)(2,1)S(1)}, bf16[64,2304]{1,0:T(8,128)(2,1)S(1)}, u32[]{:S(2)}, u32[]{:S(2)}) collective-permute-start(bf16[64,2304]{1,0:T(8,128)(2,1)S(1)} %add_convert_fusion.9), channel_id=1, source_target_pairs={{0,1},{1,2},{2,3},{3,4},{4,5},{5,6},{6,7},{7,8},{8,9},{9,10},{10,1... | collective-permute-start | bytes 884744 | tf_op jit(solution)/shard_map/cond/branch_0_fun/ppermute | solution.py:28
  141.2 8.7 %collective-permute-start.13 = (bf16[64,2304]{1,0:T(8,128)(2,1)S(1)}, bf16[64,2304]{1,0:T(8,128)(2,1)S(1)}, u32[]{:S(2)}, u32[]{:S(2)}) collective-permute-start(bf16[64,2304]{1,0:T(8,128)(2,1)S(1)} %add_convert_fusion.2), channel_id=1, source_target_pairs={{0,15},{1,0},{2,1},{3,2},{4,3},{5,4},{6,5},{7,6},{8,7},{9,8},{10,9... | collective-permute-start | bytes 884744 | tf_op jit(solution)/shard_map/cond/branch_0_fun/ppermute | solution.py:28
  147.9 8.7 %collective-permute-start.6 = (bf16[64,2304]{1,0:T(8,128)(2,1)S(1)}, bf16[64,2304]{1,0:T(8,128)(2,1)S(1)}, u32[]{:S(2)}, u32[]{:S(2)}) collective-permute-start(bf16[64,2304]{1,0:T(8,128)(2,1)S(1)} %add_convert_fusion.8), channel_id=1, source_target_pairs={{0,1},{1,2},{2,3},{3,4},{4,5},{5,6},{6,7},{7,8},{8,9},{9,10},{10,1... | collective-permute-start | bytes 884744 | tf_op jit(solution)/shard_map/cond/branch_0_fun/ppermute | solution.py:28
  149.9 8.7 %collective-permute-start.14 = (bf16[64,2304]{1,0:T(8,128)(2,1)S(1)}, bf16[64,2304]{1,0:T(8,128)(2,1)S(1)}, u32[]{:S(2)}, u32[]{:S(2)}) collective-permute-start(bf16[64,2304]{1,0:T(8,128)(2,1)S(1)} %add_convert_fusion.1), channel_id=1, source_target_pairs={{0,15},{1,0},{2,1},{3,2},{4,3},{5,4},{6,5},{7,6},{8,7},{9,8},{10,9... | collective-permute-start | bytes 884744 | tf_op jit(solution)/shard_map/cond/branch_0_fun/ppermute | solution.py:28
  156.7 8.7 %collective-permute-start.7 = (bf16[64,2304]{1,0:T(8,128)(2,1)S(1)}, bf16[64,2304]{1,0:T(8,128)(2,1)S(1)}, u32[]{:S(2)}, u32[]{:S(2)}) collective-permute-start(bf16[64,2304]{1,0:T(8,128)(2,1)S(1)} %add_convert_fusion.7), channel_id=1, source_target_pairs={{0,1},{1,2},{2,3},{3,4},{4,5},{5,6},{6,7},{7,8},{8,9},{9,10},{10,1... | collective-permute-start | bytes 884744 | tf_op jit(solution)/shard_map/cond/branch_0_fun/ppermute | solution.py:28
  158.7 8.2 %collective-permute-start.15 = (bf16[64,2304]{1,0:T(8,128)(2,1)S(1)}, bf16[64,2304]{1,0:T(8,128)(2,1)S(1)}, u32[]{:S(2)}, u32[]{:S(2)}) collective-permute-start(bf16[64,2304]{1,0:T(8,128)(2,1)S(1)} %add_convert_fusion), channel_id=1, source_target_pairs={{0,15},{1,0},{2,1},{3,2},{4,3},{5,4},{6,5},{7,6},{8,7},{9,8},{10,9... | collective-permute-start | bytes 884744 | tf_op jit(solution)/shard_map/cond/branch_0_fun/ppermute | solution.py:28
  168.1 22.3 %collective-permute-start.36 = (bf16[32,2304]{1,0:T(8,128)(2,1)S(1)}, bf16[32,2304]{1,0:T(8,128)(2,1)S(1)}, u32[]{:S(2)}, u32[]{:S(2)}) collective-permute-start(bf16[32,2304]{1,0:T(8,128)(2,1)S(1)} %get-tuple-element.94), channel_id=1, source_target_pairs={{16,32},{32,16},{48,64},{64,48},{80,96},{96,80},{112,128},{128,112... | collective-permute-start | bytes 442376 | tf_op jit(solution)/shard_map/ppermute | solution.py:36
  187.5 3.3 %collective-permute-start.37 = (bf16[32,2304]{1,0:T(8,128)(2,1)S(1)}, bf16[32,2304]{1,0:T(8,128)(2,1)S(1)}, u32[]{:S(2)}, u32[]{:S(2)}) collective-permute-start(bf16[32,2304]{1,0:T(8,128)(2,1)S(1)} %get-tuple-element.95), channel_id=1, source_target_pairs={{0,16},{16,0},{32,48},{48,32},{64,80},{80,64},{96,112},{112,96},{1... | collective-permute-start | bytes 442376 | tf_op jit(solution)/shard_map/ppermute | solution.py:36

commit v7 on v6

--- a/solution.py
+++ b/solution.py
@@ -56,6 +56,14 @@
     row = lax.broadcasted_iota(jnp.int32, (block, block), 0)
     col = lax.broadcasted_iota(jnp.int32, (block, block), 1)
     return ((row // length == col // length) & (col <= row)).astype(F32)
+
+
+def positions_of(lengths_ref, length):
+    response = lax.broadcasted_iota(jnp.int32, (RESP, 1), 0)
+    positions = jnp.zeros((RESP, 1), jnp.int32)
+    for i in range(RESP):
+        positions = jnp.where(response == i, i * length + lengths_ref[0, i] - 1, positions)
+    return positions
 
 
 def row_picks(positions, rows):
@@ -147,7 +155,7 @@
     offsets,
     length,
     me_ref,
-    positions_ref,
+    lengths_ref,
     gain_ref,
     wq_ref,
     wk_ref,
@@ -168,14 +176,15 @@
     _, probs = attention(queries, keys, pair_mask(2 * length, length))
     for (s, h), prob, value in zip(pairs, probs, values):
         context[s, h : h + HEAD_DIM] = dot(prob.astype(BF16), value).astype(BF16)
-    picks = row_picks(positions_ref[...], qkv_ref.shape[0])
-    own_picks = row_picks(positions_ref[...] - me_ref[0] * own, own)
+    positions = positions_of(lengths_ref, length)
+    picks = row_picks(positions, qkv_ref.shape[0])
+    own_picks = row_picks(positions - me_ref[0] * own, own)
     rows_ref[...] = dot(dot(picks, context[...]).astype(BF16), wo_ref[...]) + dot(
         own_picks, x_ref[...]
     )
 
 
-def rows_part_of(me, positions, gain, weights, early, x_own, late, offsets, length):
+def rows_part_of(me, lengths, gain, weights, early, x_own, late, offsets, length):
     own, feats = late.shape[0] // 2, late.shape[1]
     rows = own * len(offsets)
     vmem = pl.BlockSpec(memory_space=pltpu.VMEM)
@@ -187,12 +196,12 @@
             jax.ShapeDtypeStruct((rows, cols), BF16),
             jax.ShapeDtypeStruct((RESP, feats), F32),
         ),
-        in_specs=[smem] + [vmem] * 9,
+        in_specs=[smem] * 2 + [vmem] * 8,
         out_specs=[vmem] * 2,
         scratch_shapes=[pltpu.VMEM((rows, weights[0].shape[1]), BF16)],
         compiler_params=pltpu.CompilerParams(vmem_limit_bytes=VMEM_LIMIT),
         name="scored_rows",
-    )(me, positions, gain, *weights, early, x_own, late)
+    )(me, lengths, gain, *weights, early, x_own, late)
 
 
 def project_back(turned, wq_ref, wk_ref, wv_ref, wo_ref, mixed_outs, back_outs):
@@ -322,7 +331,7 @@
 def scored_kernel(
     count,
     length,
-    positions_ref,
+    lengths_ref,
     row_grads_ref,
     qkv_ref,
     wq_ref,
@@ -336,7 +345,7 @@
     feats = wq_ref.shape[0]
     own = rows // count
     q_cols, kv_cols = wq_ref.shape[1], wk_ref.shape[1]
-    positions = positions_ref[...]
+    positions = positions_of(lengths_ref, length)
     picks = row_picks(positions, rows)
     row = lax.broadcasted_iota(jnp.int32, (RESP, rows), 0)
     col = lax.broadcasted_iota(jnp.int32, (RESP, rows), 1)
@@ -419,7 +428,7 @@
         out_ref[:, place : place + lanes] = dot_tn(shares, jnp.concatenate(parts, axis=0).astype(BF16))
 
 
-def scored_part(me, positions, row_grads, qkv, weights, count, length, section):
+def scored_part(me, lengths, row_grads, qkv, weights, count, length, section):
     feats = row_grads.shape[1]
     own = qkv.shape[0] // count
     vmem = pl.BlockSpec(memory_space=pltpu.VMEM)
@@ -431,12 +440,12 @@
     parcels = pl.pallas_call(
         functools.partial(scored_kernel, count, length),
         out_shape=jax.ShapeDtypeStruct(shape, BF16),
-        in_specs=[vmem] * 7,
+        in_specs=[smem] + [vmem] * 6,
         out_specs=vmem,
         scratch_shapes=[blocks],
         compiler_params=pltpu.CompilerParams(vmem_limit_bytes=VMEM_LIMIT),
         name="scored_backward",
-    )(positions, row_grads, qkv, *weights)
+    )(lengths, row_grads, qkv, *weights)
     mine = lax.all_to_all(parcels.reshape(count, slots, width), "tensor", 0, 0).reshape(shape)
     swaps = [(section * count + i, section * count + (i ^ 1)) for i in range(count)]
     theirs = lax.ppermute(mine, ("section", "tensor"), swaps)
@@ -452,12 +461,21 @@
 
 
 def finish_kernel(
-    me_ref, positions_ref, gain_ref, x_ref, later_ref, sums_ref, row_grads_ref, between_ref, within_ref
+    length,
+    me_ref,
+    lengths_ref,
+    gain_ref,
+    x_ref,
+    later_ref,
+    sums_ref,
+    row_grads_ref,
+    between_ref,
+    within_ref,
 ):
     own = x_ref.shape[0]
     x = x_ref[...].astype(F32)
     hidden = x + sums_ref[:own]
-    picks = row_picks(positions_ref[...] - me_ref[0] * own, own)
+    picks = row_picks(positions_of(lengths_ref, length) - me_ref[0] * own, own)
     last = dot_tn(picks, row_grads_ref[...].astype(BF16))
     cotangent = jnp.where(me_ref[2] == 1, last, later_ref[...].astype(F32))
     inv_x = inv_rms(x)
@@ -469,17 +487,17 @@
     within_ref[...] = jnp.where(odd, returned, hidden).astype(BF16)
 
 
-def finish_part(me, positions, gain, x_own, later_own, sums, row_grads):
+def finish_part(me, lengths, gain, x_own, later_own, sums, row_grads, length):
     vmem = pl.BlockSpec(memory_space=pltpu.VMEM)
     smem = pl.BlockSpec(memory_space=pltpu.SMEM)
     return pl.pallas_call(
-        finish_kernel,
+        functools.partial(finish_kernel, length),
         out_shape=[jax.ShapeDtypeStruct(x_own.shape, BF16)] * 2,
-        in_specs=[smem] + [vmem] * 6,
+        in_specs=[smem] * 2 + [vmem] * 5,
         out_specs=[vmem] * 2,
         compiler_params=pltpu.CompilerParams(vmem_limit_bytes=VMEM_LIMIT),
         name="finish",
-    )(me, positions, gain, x_own, later_own, sums, row_grads)
+    )(me, lengths, gain, x_own, later_own, sums, row_grads)
 
 
 def rank_grad(reward_scores, rankings):
@@ -557,8 +575,6 @@
     length = total_rows // RESP
     weights = (w_query[0], w_key[0], w_value[0], w_out[0])
     at_end = lax.axis_index("section") == lax.axis_size("section") - 1
-    positions = jnp.arange(RESP) * length + lengths[0] - 1
-    places = positions[:, None].astype(jnp.int32)
     odd = lax.axis_index("section") % 2
     me = jnp.stack([tensor_pos, odd, at_end]).astype(jnp.int32)
 
@@ -575,7 +591,7 @@
 
     def last_section(early, late):
         qkv, rows_part = rows_part_of(
-            me, places, attn_gain, weights, early, x_own, late, offsets, length
+            me, lengths, attn_gain, weights, early, x_own, late, offsets, length
         )
         rows_hidden = sum_rows(rows_part, [last]).astype(BF16).astype(F32)
         inv_norm = inv_rms(rows_hidden)
@@ -587,12 +603,14 @@
         )
         row_grads = row_grads.astype(BF16).astype(F32)
         back_own = scored_part(
-            me, places, row_grads, qkv, weights, tensor_count, length, last
+            me, lengths, row_grads, qkv, weights, tensor_count, length, last
         )
         return jnp.concatenate([jnp.zeros_like(back_own), back_own]), row_grads
 
     sums, row_grads = lax.cond(at_end, last_section, inner_section, early, blocks[-1])
-    between, within = finish_part(me, places, attn_gain, x_own, later_own, sums, row_grads)
+    between, within = finish_part(
+        me, lengths, attn_gain, x_own, later_own, sums, row_grads, length
+    )
     between, within = swap_sections(between, 1), swap_sections(within, 0)
     even = lax.axis_index("section") % 2 == 0
     arrived = jnp.where(even, between, within)

time: 193 us -> 193 us (level)
  transfers between devices with their start and end apart: 33 -> 33, of which waited for: 19 -> 18; matrix products, arithmetic and copies ran while one was open for 1% -> 1% of each run, Pallas kernels for 4% -> 4%
where the time goes in v7:
time: 193 us; the launch traced here: 191 us
  starting transfers between devices  128 us (66%)
  waiting for transfers between devices  46.7 us (24%)
  Pallas kernels  12.2 us (6%)
  other arithmetic  2.85 us (1%)
    ppermute x31, starting transfers between devices, shift(): return lax.ppermute(value, ('section', 'tensor'), pairs)  107 us
    ppermute x31, waiting for transfers between devices, shift(): return lax.ppermute(value, ('section', 'tensor'), pairs)  45.4 us
    ppermute x2, starting transfers between devices, swap_sections(): return lax.ppermute(value, 'section', pairs)  21.4 us
    pallas_call x1, Pallas kernels, early_part(): pl.pallas_call(early_kernel, out_shape=jax.ShapeDtypeStruct((rows, cols),...  4.65 us
    pallas_call x1, Pallas kernels, layer_part(): pl.pallas_call(functools.partial(layer_kernel, offsets, back_offsets, len...  4.04 us
  transfers between devices with their start and end apart: 33, of which 18 were waited for; matrix products, arithmetic and copies ran while one was open for 1% of the time, Pallas kernels for 4%

profile of v7, /device:TPU:1, one launch (start us, length us, event | category | flops | bytes accessed | tf_op | source)
XLA Modules:
  0.0 191.4 jit_solution(1739192376317333831)
XLA Ops:
  1.6 4.4 %collective-permute-start.21 = (bf16[64,2304]{1,0:T(8,128)(2,1)S(1)}, bf16[64,2304]{1,0:T(8,128)(2,1)S(1)}, u32[]{:S(2)}, u32[]{:S(2)}) collective-permute-start(bf16[64,2304]{1,0:T(8,128)(2,1)S(1)} %pad_maximum_fusion.refs_0_), channel_id=1, source_target_pairs={{0,1},{1,2},{2,3},{3,4},{4,5},{5,6},{6,7},{7,8},{8,9},{9,10},{10,1... | collective-permute-start | bytes 884744 | tf_op jit(solution)/shard_map/ppermute | solution.py:28
  6.0 9.5 %collective-permute-start.22 = (bf16[64,2304]{1,0:T(8,128)(2,1)S(1)}, bf16[64,2304]{1,0:T(8,128)(2,1)S(1)}, u32[]{:S(2)}, u32[]{:S(2)}) collective-permute-start(bf16[64,2304]{1,0:T(8,128)(2,1)S(1)} %pad_maximum_fusion.refs_0_), channel_id=1, source_target_pairs={{0,15},{1,0},{2,1},{3,2},{4,3},{5,4},{6,5},{7,6},{8,7},{9,8},{10,9... | collective-permute-start | bytes 884744 | tf_op jit(solution)/shard_map/ppermute | solution.py:28
  15.5 4.8 %collective-permute-done.21.refs_1_ = bf16[64,2304]{1,0:T(8,128)(2,1)S(1)} collective-permute-done((bf16[64,2304]{1,0:T(8,128)(2,1)S(1)}, bf16[64,2304]{1,0:T(8,128)(2,1)S(1)}, u32[]{:S(2)}, u32[]{:S(2)}) %collective-permute-start.21) | collective-permute-done | bytes 294944 | tf_op jit(solution)/shard_map/ppermute | solution.py:28
  20.3 1.9 collective-permute-start.23
  22.2 4.6 %collective-permute-start.24 = (bf16[64,2304]{1,0:T(8,128)(2,1)S(1)}, bf16[64,2304]{1,0:T(8,128)(2,1)S(1)}, u32[]{:S(2)}, u32[]{:S(2)}) collective-permute-start(bf16[64,2304]{1,0:T(8,128)(2,1)S(1)} %collective-permute-done.22.refs_2_), channel_id=1, source_target_pairs={{0,15},{1,0},{2,1},{3,2},{4,3},{5,4},{6,5},{7,6},{8,7},{9,8},{10,9... | collective-permute-start | bytes 884744 | tf_op jit(solution)/shard_map/ppermute | solution.py:28
  26.8 3.9 %collective-permute-done.23.refs_3_ = bf16[64,2304]{1,0:T(8,128)(2,1)S(1)} collective-permute-done((bf16[64,2304]{1,0:T(8,128)(2,1)S(1)}, bf16[64,2304]{1,0:T(8,128)(2,1)S(1)}, u32[]{:S(2)}, u32[]{:S(2)}) %collective-permute-start.23) | collective-permute-done | bytes 294944 | tf_op jit(solution)/shard_map/ppermute | solution.py:28
  30.7 1.9 collective-permute-start.25
  32.6 4.6 %collective-permute-start.26 = (bf16[64,2304]{1,0:T(8,128)(2,1)S(1)}, bf16[64,2304]{1,0:T(8,128)(2,1)S(1)}, u32[]{:S(2)}, u32[]{:S(2)}) collective-permute-start(bf16[64,2304]{1,0:T(8,128)(2,1)S(1)} %collective-permute-done.24.refs_4_), channel_id=1, source_target_pairs={{0,15},{1,0},{2,1},{3,2},{4,3},{5,4},{6,5},{7,6},{8,7},{9,8},{10,9... | collective-permute-start | bytes 884744 | tf_op jit(solution)/shard_map/ppermute | solution.py:28
  37.2 2.9 %collective-permute-done.25.refs_5_ = bf16[64,2304]{1,0:T(8,128)(2,1)S(1)} collective-permute-done((bf16[64,2304]{1,0:T(8,128)(2,1)S(1)}, bf16[64,2304]{1,0:T(8,128)(2,1)S(1)}, u32[]{:S(2)}, u32[]{:S(2)}) %collective-permute-start.25) | collective-permute-done | bytes 294944 | tf_op jit(solution)/shard_map/ppermute | solution.py:28
  42.1 4.6 %collective-permute-start.28 = (bf16[64,2304]{1,0:T(8,128)(2,1)S(1)}, bf16[64,2304]{1,0:T(8,128)(2,1)S(1)}, u32[]{:S(2)}, u32[]{:S(2)}) collective-permute-start(bf16[64,2304]{1,0:T(8,128)(2,1)S(1)} %collective-permute-done.26.refs_6_), channel_id=1, source_target_pairs={{0,15},{1,0},{2,1},{3,2},{4,3},{5,4},{6,5},{7,6},{8,7},{9,8},{10,9... | collective-permute-start | bytes 884744 | tf_op jit(solution)/shard_map/ppermute | solution.py:28
  46.6 2.2 %collective-permute-done.27.refs_7_ = bf16[64,2304]{1,0:T(8,128)(2,1)S(1)} collective-permute-done((bf16[64,2304]{1,0:T(8,128)(2,1)S(1)}, bf16[64,2304]{1,0:T(8,128)(2,1)S(1)}, u32[]{:S(2)}, u32[]{:S(2)}) %collective-permute-start.27) | collective-permute-done | bytes 294944 | tf_op jit(solution)/shard_map/ppermute | solution.py:28
  50.7 4.6 %collective-permute-start.30 = (bf16[64,2304]{1,0:T(8,128)(2,1)S(1)}, bf16[64,2304]{1,0:T(8,128)(2,1)S(1)}, u32[]{:S(2)}, u32[]{:S(2)}) collective-permute-start(bf16[64,2304]{1,0:T(8,128)(2,1)S(1)} %collective-permute-done.28.refs_8_), channel_id=1, source_target_pairs={{0,15},{1,0},{2,1},{3,2},{4,3},{5,4},{6,5},{7,6},{8,7},{9,8},{10,9... | collective-permute-start | bytes 884744 | tf_op jit(solution)/shard_map/ppermute | solution.py:28
  55.3 2.2 %collective-permute-done.29.refs_9_ = bf16[64,2304]{1,0:T(8,128)(2,1)S(1)} collective-permute-done((bf16[64,2304]{1,0:T(8,128)(2,1)S(1)}, bf16[64,2304]{1,0:T(8,128)(2,1)S(1)}, u32[]{:S(2)}, u32[]{:S(2)}) %collective-permute-start.29) | collective-permute-done | bytes 294944 | tf_op jit(solution)/shard_map/ppermute | solution.py:28
  59.4 4.6 %collective-permute-start.32 = (bf16[64,2304]{1,0:T(8,128)(2,1)S(1)}, bf16[64,2304]{1,0:T(8,128)(2,1)}, u32[]{:S(2)}, u32[]{:S(2)}) collective-permute-start(bf16[64,2304]{1,0:T(8,128)(2,1)S(1)} %collective-permute-done.30.refs_10_), channel_id=1, source_target_pairs={{0,15},{1,0},{2,1},{3,2},{4,3},{5,4},{6,5},{7,6},{8,7},{9,8},{10,9... | collective-permute-start | bytes 884744 | tf_op jit(solution)/shard_map/ppermute | solution.py:28
  64.0 2.2 %collective-permute-done.31.refs_11_ = bf16[64,2304]{1,0:T(8,128)(2,1)S(1)} collective-permute-done((bf16[64,2304]{1,0:T(8,128)(2,1)S(1)}, bf16[64,2304]{1,0:T(8,128)(2,1)S(1)}, u32[]{:S(2)}, u32[]{:S(2)}) %collective-permute-start.31) | collective-permute-done | bytes 294944 | tf_op jit(solution)/shard_map/ppermute | solution.py:28
  66.1 1.9 collective-permute-start.33
  68.1 4.7 %collective-permute-start.34 = (bf16[64,2304]{1,0:T(8,128)(2,1)}, bf16[64,2304]{1,0:T(8,128)(2,1)}, u32[]{:S(2)}, u32[]{:S(2)}) collective-permute-start(bf16[64,2304]{1,0:T(8,128)(2,1)} %collective-permute-done.32.refs_12_), channel_id=1, source_target_pairs={{0,15},{1,0},{2,1},{3,2},{4,3},{5,4},{6,5},{7,6},{8,7},{9,8},{10,9... | collective-permute-start | bytes 884744 | tf_op jit(solution)/shard_map/ppermute | solution.py:28
  72.7 2.5 %collective-permute-done.33.refs_13_ = bf16[64,2304]{1,0:T(8,128)(2,1)} collective-permute-done((bf16[64,2304]{1,0:T(8,128)(2,1)S(1)}, bf16[64,2304]{1,0:T(8,128)(2,1)}, u32[]{:S(2)}, u32[]{:S(2)}) %collective-permute-start.33) | collective-permute-done | bytes 294944 | tf_op jit(solution)/shard_map/ppermute | solution.py:28
  75.2 1.9 collective-permute-start.35
  77.3 4.7 %early_rows.1 = bf16[480,768]{1,0:T(8,128)(2,1)S(1)} custom-call(bf16[1,2304]{1,0:T(2,128)(2,1)} %gain_ref.3, bf16[2304,256]{1,0:T(8,128)(2,1)} %bitcast.21, bf16[2304,128]{1,0:T(8,128)(2,1)} %bitcast.27, bf16[2304,128]{1,0:T(8,128)(2,1)} %bitcast.30, bf16[256,2304]{1,0:T(8,128)(2,1)} %bitcast.24, bf16[64,2304]{1,0:T(8,128)(2,1)S(1)} %pad_maximum_fusion.refs_0_, ...), custom_call_target="tpu_custom_call" | custom-call | flops 1698693120 | bytes 4423680 | tf_op jit(solution)/shard_map/early_rows/pallas_call | solution.py:112
  82.0 3.3 %collective-permute-done.35 = bf16[64,2304]{1,0:T(8,128)(2,1)} collective-permute-done((bf16[64,2304]{1,0:T(8,128)(2,1)}, bf16[64,2304]{1,0:T(8,128)(2,1)}, u32[]{:S(2)}, u32[]{:S(2)}) %collective-permute-start.35) | collective-permute-done | bytes 294944 | tf_op jit(solution)/shard_map/ppermute | solution.py:28
  85.4 81.6 %conditional.1 = (f32[64,2304]{1,0:T(8,128)S(1)}, f32[8,2304]{1,0:T(8,128)S(1)}) conditional(s32[]{:T(128)} %convert_element_type.155, (s32[3]{0:T(128)S(1)}, bf16[1,2304]{1,0:T(2,128)(2,1)S(1)}, bf16[2304,256]{1,0:T(8,128)(2,1)S(1)}, bf16[2304,128]{1,0:T(8,128)(2,1)S(1)}, bf16[2304,128]{1,0:T(8,128)(2,1)S(1)}, ...), branch_computations={%region_0.1_spmd, %region_1.9_spmd} | conditional | flops 1707687936 | bytes 31335060 | solution.py:610
  85.4 4.0 %layer_both_ways.1 = (bf16[32,2304]{1,0:T(8,128)(2,1)S(1)}, bf16[32,2304]{1,0:T(8,128)(2,1)S(1)}, bf16[64,768]{1,0:T(8,128)(2,1)S(1)}, bf16[416,768]{1,0:T(8,128)(2,1)S(1)}) custom-call(s32[3]{0:T(128)S(1)} %get-tuple-element.46.me_ref, bf16[1,2304]{1,0:T(2,128)(2,1)S(1)} %get-tuple-element.47.gain_ref, bf16[2304,256]{1,0:T(8,128)(2,1)S(1)} %get-tuple-element.42.wq_ref, ...), custom_call_target="tpu_custom_call" | custom-call | tf_op jit(solution)/shard_map/cond/branch_0_fun/layer_both_ways/pallas_call | solution.py:294
  89.5 1.9 %collective-permute-start = (bf16[32,2304]{1,0:T(8,128)(2,1)S(1)}, bf16[32,2304]{1,0:T(8,128)(2,1)S(1)}, u32[]{:S(2)}, u32[]{:S(2)}) collective-permute-start(bf16[32,2304]{1,0:T(8,128)(2,1)S(1)} %get-tuple-element.50), channel_id=1, source_target_pairs={{0,1},{1,2},{2,3},{3,4},{4,5},{5,6},{6,7},{7,8},{8,9},{9,10},{10,1... | collective-permute-start | bytes 442376 | tf_op jit(solution)/shard_map/cond/branch_0_fun/ppermute | solution.py:28
  91.4 4.6 %collective-permute-start.8 = (bf16[32,2304]{1,0:T(8,128)(2,1)S(1)}, bf16[32,2304]{1,0:T(8,128)(2,1)S(1)}, u32[]{:S(2)}, u32[]{:S(2)}) collective-permute-start(bf16[32,2304]{1,0:T(8,128)(2,1)S(1)} %get-tuple-element.63), channel_id=1, source_target_pairs={{0,15},{1,0},{2,1},{3,2},{4,3},{5,4},{6,5},{7,6},{8,7},{9,8},{10,9... | collective-permute-start | bytes 442376 | tf_op jit(solution)/shard_map/cond/branch_0_fun/ppermute | solution.py:28
  97.1 1.9 %collective-permute-start.1 = (bf16[64,2304]{1,0:T(8,128)(2,1)S(1)}, bf16[64,2304]{1,0:T(8,128)(2,1)S(1)}, u32[]{:S(2)}, u32[]{:S(2)}) collective-permute-start(bf16[64,2304]{1,0:T(8,128)(2,1)S(1)} %add_convert_fusion.13), channel_id=1, source_target_pairs={{0,1},{1,2},{2,3},{3,4},{4,5},{5,6},{6,7},{7,8},{8,9},{9,10},{10,1... | collective-permute-start | bytes 884744 | tf_op jit(solution)/shard_map/cond/branch_0_fun/ppermute | solution.py:28
  99.1 4.6 %collective-permute-start.9 = (bf16[64,2304]{1,0:T(8,128)(2,1)S(1)}, bf16[64,2304]{1,0:T(8,128)(2,1)S(1)}, u32[]{:S(2)}, u32[]{:S(2)}) collective-permute-start(bf16[64,2304]{1,0:T(8,128)(2,1)S(1)} %add_convert_fusion.6), channel_id=1, source_target_pairs={{0,15},{1,0},{2,1},{3,2},{4,3},{5,4},{6,5},{7,6},{8,7},{9,8},{10,9... | collective-permute-start | bytes 884744 | tf_op jit(solution)/shard_map/cond/branch_0_fun/ppermute | solution.py:28
  105.3 2.3 %collective-permute-done.1 = bf16[64,2304]{1,0:T(8,128)(2,1)S(1)} collective-permute-done((bf16[64,2304]{1,0:T(8,128)(2,1)S(1)}, bf16[64,2304]{1,0:T(8,128)(2,1)S(1)}, u32[]{:S(2)}, u32[]{:S(2)}) %collective-permute-start.1) | collective-permute-done | bytes 294944 | tf_op jit(solution)/shard_map/cond/branch_0_fun/ppermute | solution.py:28
  107.7 1.9 %collective-permute-start.2 = (bf16[64,2304]{1,0:T(8,128)(2,1)S(1)}, bf16[64,2304]{1,0:T(8,128)(2,1)S(1)}, u32[]{:S(2)}, u32[]{:S(2)}) collective-permute-start(bf16[64,2304]{1,0:T(8,128)(2,1)S(1)} %add_convert_fusion.12), channel_id=1, source_target_pairs={{0,1},{1,2},{2,3},{3,4},{4,5},{5,6},{6,7},{7,8},{8,9},{9,10},{10,1... | collective-permute-start | bytes 884744 | tf_op jit(solution)/shard_map/cond/branch_0_fun/ppermute | solution.py:28
  109.7 4.6 %collective-permute-start.10 = (bf16[64,2304]{1,0:T(8,128)(2,1)S(1)}, bf16[64,2304]{1,0:T(8,128)(2,1)S(1)}, u32[]{:S(2)}, u32[]{:S(2)}) collective-permute-start(bf16[64,2304]{1,0:T(8,128)(2,1)S(1)} %add_convert_fusion.5), channel_id=1, source_target_pairs={{0,15},{1,0},{2,1},{3,2},{4,3},{5,4},{6,5},{7,6},{8,7},{9,8},{10,9... | collective-permute-start | bytes 884744 | tf_op jit(solution)/shard_map/cond/branch_0_fun/ppermute | solution.py:28
  114.3 4.7 %collective-permute-done.2 = bf16[64,2304]{1,0:T(8,128)(2,1)S(1)} collective-permute-done((bf16[64,2304]{1,0:T(8,128)(2,1)S(1)}, bf16[64,2304]{1,0:T(8,128)(2,1)S(1)}, u32[]{:S(2)}, u32[]{:S(2)}) %collective-permute-start.2) | collective-permute-done | bytes 294944 | tf_op jit(solution)/shard_map/cond/branch_0_fun/ppermute | solution.py:28
  119.1 1.9 %collective-permute-start.3 = (bf16[64,2304]{1,0:T(8,128)(2,1)S(1)}, bf16[64,2304]{1,0:T(8,128)(2,1)S(1)}, u32[]{:S(2)}, u32[]{:S(2)}) collective-permute-start(bf16[64,2304]{1,0:T(8,128)(2,1)S(1)} %add_convert_fusion.11), channel_id=1, source_target_pairs={{0,1},{1,2},{2,3},{3,4},{4,5},{5,6},{6,7},{7,8},{8,9},{9,10},{10,1... | collective-permute-start | bytes 884744 | tf_op jit(solution)/shard_map/cond/branch_0_fun/ppermute | solution.py:28
  121.1 4.6 %collective-permute-start.11 = (bf16[64,2304]{1,0:T(8,128)(2,1)S(1)}, bf16[64,2304]{1,0:T(8,128)(2,1)S(1)}, u32[]{:S(2)}, u32[]{:S(2)}) collective-permute-start(bf16[64,2304]{1,0:T(8,128)(2,1)S(1)} %add_convert_fusion.4), channel_id=1, source_target_pairs={{0,15},{1,0},{2,1},{3,2},{4,3},{5,4},{6,5},{7,6},{8,7},{9,8},{10,9... | collective-permute-start | bytes 884744 | tf_op jit(solution)/shard_map/cond/branch_0_fun/ppermute | solution.py:28
  125.7 3.8 %collective-permute-done.3 = bf16[64,2304]{1,0:T(8,128)(2,1)S(1)} collective-permute-done((bf16[64,2304]{1,0:T(8,128)(2,1)S(1)}, bf16[64,2304]{1,0:T(8,128)(2,1)S(1)}, u32[]{:S(2)}, u32[]{:S(2)}) %collective-permute-start.3) | collective-permute-done | bytes 294944 | tf_op jit(solution)/shard_map/cond/branch_0_fun/ppermute | solution.py:28
  129.6 1.9 %collective-permute-start.4 = (bf16[64,2304]{1,0:T(8,128)(2,1)S(1)}, bf16[64,2304]{1,0:T(8,128)(2,1)S(1)}, u32[]{:S(2)}, u32[]{:S(2)}) collective-permute-start(bf16[64,2304]{1,0:T(8,128)(2,1)S(1)} %add_convert_fusion.10), channel_id=1, source_target_pairs={{0,1},{1,2},{2,3},{3,4},{4,5},{5,6},{6,7},{7,8},{8,9},{9,10},{10,1... | collective-permute-start | bytes 884744 | tf_op jit(solution)/shard_map/cond/branch_0_fun/ppermute | solution.py:28
  131.6 4.6 %collective-permute-start.12 = (bf16[64,2304]{1,0:T(8,128)(2,1)S(1)}, bf16[64,2304]{1,0:T(8,128)(2,1)S(1)}, u32[]{:S(2)}, u32[]{:S(2)}) collective-permute-start(bf16[64,2304]{1,0:T(8,128)(2,1)S(1)} %add_convert_fusion.3), channel_id=1, source_target_pairs={{0,15},{1,0},{2,1},{3,2},{4,3},{5,4},{6,5},{7,6},{8,7},{9,8},{10,9... | collective-permute-start | bytes 884744 | tf_op jit(solution)/shard_map/cond/branch_0_fun/ppermute | solution.py:28
  136.2 2.9 %collective-permute-done.4 = bf16[64,2304]{1,0:T(8,128)(2,1)S(1)} collective-permute-done((bf16[64,2304]{1,0:T(8,128)(2,1)S(1)}, bf16[64,2304]{1,0:T(8,128)(2,1)S(1)}, u32[]{:S(2)}, u32[]{:S(2)}) %collective-permute-start.4) | collective-permute-done | bytes 294944 | tf_op jit(solution)/shard_map/cond/branch_0_fun/ppermute | solution.py:28
  139.2 1.9 %collective-permute-start.5 = (bf16[64,2304]{1,0:T(8,128)(2,1)S(1)}, bf16[64,2304]{1,0:T(8,128)(2,1)S(1)}, u32[]{:S(2)}, u32[]{:S(2)}) collective-permute-start(bf16[64,2304]{1,0:T(8,128)(2,1)S(1)} %add_convert_fusion.9), channel_id=1, source_target_pairs={{0,1},{1,2},{2,3},{3,4},{4,5},{5,6},{6,7},{7,8},{8,9},{9,10},{10,1... | collective-permute-start | bytes 884744 | tf_op jit(solution)/shard_map/cond/branch_0_fun/ppermute | solution.py:28
  141.2 4.6 %collective-permute-start.13 = (bf16[64,2304]{1,0:T(8,128)(2,1)S(1)}, bf16[64,2304]{1,0:T(8,128)(2,1)S(1)}, u32[]{:S(2)}, u32[]{:S(2)}) collective-permute-start(bf16[64,2304]{1,0:T(8,128)(2,1)S(1)} %add_convert_fusion.2), channel_id=1, source_target_pairs={{0,15},{1,0},{2,1},{3,2},{4,3},{5,4},{6,5},{7,6},{8,7},{9,8},{10,9... | collective-permute-start | bytes 884744 | tf_op jit(solution)/shard_map/cond/branch_0_fun/ppermute | solution.py:28
  145.8 2.1 %collective-permute-done.5 = bf16[64,2304]{1,0:T(8,128)(2,1)S(1)} collective-permute-done((bf16[64,2304]{1,0:T(8,128)(2,1)S(1)}, bf16[64,2304]{1,0:T(8,128)(2,1)S(1)}, u32[]{:S(2)}, u32[]{:S(2)}) %collective-permute-start.5) | collective-permute-done | bytes 294944 | tf_op jit(solution)/shard_map/cond/branch_0_fun/ppermute | solution.py:28
  147.9 1.9 %collective-permute-start.6 = (bf16[64,2304]{1,0:T(8,128)(2,1)S(1)}, bf16[64,2304]{1,0:T(8,128)(2,1)S(1)}, u32[]{:S(2)}, u32[]{:S(2)}) collective-permute-start(bf16[64,2304]{1,0:T(8,128)(2,1)S(1)} %add_convert_fusion.8), channel_id=1, source_target_pairs={{0,1},{1,2},{2,3},{3,4},{4,5},{5,6},{6,7},{7,8},{8,9},{9,10},{10,1... | collective-permute-start | bytes 884744 | tf_op jit(solution)/shard_map/cond/branch_0_fun/ppermute | solution.py:28
  149.9 4.6 %collective-permute-start.14 = (bf16[64,2304]{1,0:T(8,128)(2,1)S(1)}, bf16[64,2304]{1,0:T(8,128)(2,1)S(1)}, u32[]{:S(2)}, u32[]{:S(2)}) collective-permute-start(bf16[64,2304]{1,0:T(8,128)(2,1)S(1)} %add_convert_fusion.1), channel_id=1, source_target_pairs={{0,15},{1,0},{2,1},{3,2},{4,3},{5,4},{6,5},{7,6},{8,7},{9,8},{10,9... | collective-permute-start | bytes 884744 | tf_op jit(solution)/shard_map/cond/branch_0_fun/ppermute | solution.py:28
  154.5 2.1 %collective-permute-done.6 = bf16[64,2304]{1,0:T(8,128)(2,1)S(1)} collective-permute-done((bf16[64,2304]{1,0:T(8,128)(2,1)S(1)}, bf16[64,2304]{1,0:T(8,128)(2,1)S(1)}, u32[]{:S(2)}, u32[]{:S(2)}) %collective-permute-start.6) | collective-permute-done | bytes 294944 | tf_op jit(solution)/shard_map/cond/branch_0_fun/ppermute | solution.py:28
  156.7 1.9 %collective-permute-start.7 = (bf16[64,2304]{1,0:T(8,128)(2,1)S(1)}, bf16[64,2304]{1,0:T(8,128)(2,1)S(1)}, u32[]{:S(2)}, u32[]{:S(2)}) collective-permute-start(bf16[64,2304]{1,0:T(8,128)(2,1)S(1)} %add_convert_fusion.7), channel_id=1, source_target_pairs={{0,1},{1,2},{2,3},{3,4},{4,5},{5,6},{6,7},{7,8},{8,9},{9,10},{10,1... | collective-permute-start | bytes 884744 | tf_op jit(solution)/shard_map/cond/branch_0_fun/ppermute | solution.py:28
  158.7 4.6 %collective-permute-start.15 = (bf16[64,2304]{1,0:T(8,128)(2,1)S(1)}, bf16[64,2304]{1,0:T(8,128)(2,1)S(1)}, u32[]{:S(2)}, u32[]{:S(2)}) collective-permute-start(bf16[64,2304]{1,0:T(8,128)(2,1)S(1)} %add_convert_fusion), channel_id=1, source_target_pairs={{0,15},{1,0},{2,1},{3,2},{4,3},{5,4},{6,5},{7,6},{8,7},{9,8},{10,9... | collective-permute-start | bytes 884744 | tf_op jit(solution)/shard_map/cond/branch_0_fun/ppermute | solution.py:28
  163.3 2.1 %collective-permute-done.7 = bf16[64,2304]{1,0:T(8,128)(2,1)S(1)} collective-permute-done((bf16[64,2304]{1,0:T(8,128)(2,1)S(1)}, bf16[64,2304]{1,0:T(8,128)(2,1)S(1)}, u32[]{:S(2)}, u32[]{:S(2)}) %collective-permute-start.7) | collective-permute-done | bytes 294944 | tf_op jit(solution)/shard_map/cond/branch_0_fun/ppermute | solution.py:28
  167.9 19.5 %collective-permute-start.36 = (bf16[32,2304]{1,0:T(8,128)(2,1)S(1)}, bf16[32,2304]{1,0:T(8,128)(2,1)S(1)}, u32[]{:S(2)}, u32[]{:S(2)}) collective-permute-start(bf16[32,2304]{1,0:T(8,128)(2,1)S(1)} %get-tuple-element.94), channel_id=1, source_target_pairs={{16,32},{32,16},{48,64},{64,48},{80,96},{96,80},{112,128},{128,112... | collective-permute-start | bytes 442376 | tf_op jit(solution)/shard_map/ppermute | solution.py:36
  187.4 1.9 %collective-permute-start.37 = (bf16[32,2304]{1,0:T(8,128)(2,1)S(1)}, bf16[32,2304]{1,0:T(8,128)(2,1)S(1)}, u32[]{:S(2)}, u32[]{:S(2)}) collective-permute-start(bf16[32,2304]{1,0:T(8,128)(2,1)S(1)} %get-tuple-element.95), channel_id=1, source_target_pairs={{0,16},{16,0},{32,48},{48,32},{64,80},{80,64},{96,112},{112,96},{1... | collective-permute-start | bytes 442376 | tf_op jit(solution)/shard_map/ppermute | solution.py:36
  (69 shorter events, 15.1 us)
Async XLA Ops:
  1.6 18.7 %collective-permute-start.21 = (bf16[64,2304]{1,0:T(8,128)(2,1)S(1)}, bf16[64,2304]{1,0:T(8,128)(2,1)S(1)}, u32[]{:S(2)}, u32[]{:S(2)}) collective-permute-start(bf16[64,2304]{1,0:T(8,128)(2,1)S(1)} %pad_maximum_fusion.refs_0_), channel_id=1, source_target_pairs={{0,1},{1,2},{2,3},{3,4},{4,5},{5,6},{6,7},{7,8},{8,9},{9,10},{10,1... | collective-permute-start | bytes 884744 | tf_op jit(solution)/shard_map/ppermute | solution.py:28
  6.0 16.2 %collective-permute-start.22 = (bf16[64,2304]{1,0:T(8,128)(2,1)S(1)}, bf16[64,2304]{1,0:T(8,128)(2,1)S(1)}, u32[]{:S(2)}, u32[]{:S(2)}) collective-permute-start(bf16[64,2304]{1,0:T(8,128)(2,1)S(1)} %pad_maximum_fusion.refs_0_), channel_id=1, source_target_pairs={{0,15},{1,0},{2,1},{3,2},{4,3},{5,4},{6,5},{7,6},{8,7},{9,8},{10,9... | collective-permute-start | bytes 884744 | tf_op jit(solution)/shard_map/ppermute | solution.py:28
  20.3 10.4 %collective-permute-start.23 = (bf16[64,2304]{1,0:T(8,128)(2,1)S(1)}, bf16[64,2304]{1,0:T(8,128)(2,1)S(1)}, u32[]{:S(2)}, u32[]{:S(2)}) collective-permute-start(bf16[64,2304]{1,0:T(8,128)(2,1)S(1)} %collective-permute-done.21.refs_1_), channel_id=1, source_target_pairs={{0,1},{1,2},{2,3},{3,4},{4,5},{5,6},{6,7},{7,8},{8,9},{9,10},{10,1... | collective-permute-start | bytes 884744 | tf_op jit(solution)/shard_map/ppermute | solution.py:28
  22.2 10.4 %collective-permute-start.24 = (bf16[64,2304]{1,0:T(8,128)(2,1)S(1)}, bf16[64,2304]{1,0:T(8,128)(2,1)S(1)}, u32[]{:S(2)}, u32[]{:S(2)}) collective-permute-start(bf16[64,2304]{1,0:T(8,128)(2,1)S(1)} %collective-permute-done.22.refs_2_), channel_id=1, source_target_pairs={{0,15},{1,0},{2,1},{3,2},{4,3},{5,4},{6,5},{7,6},{8,7},{9,8},{10,9... | collective-permute-start | bytes 884744 | tf_op jit(solution)/shard_map/ppermute | solution.py:28
  30.7 9.4 %collective-permute-start.25 = (bf16[64,2304]{1,0:T(8,128)(2,1)S(1)}, bf16[64,2304]{1,0:T(8,128)(2,1)S(1)}, u32[]{:S(2)}, u32[]{:S(2)}) collective-permute-start(bf16[64,2304]{1,0:T(8,128)(2,1)S(1)} %collective-permute-done.23.refs_3_), channel_id=1, source_target_pairs={{0,1},{1,2},{2,3},{3,4},{4,5},{5,6},{6,7},{7,8},{8,9},{9,10},{10,1... | collective-permute-start | bytes 884744 | tf_op jit(solution)/shard_map/ppermute | solution.py:28
  32.6 9.4 %collective-permute-start.26 = (bf16[64,2304]{1,0:T(8,128)(2,1)S(1)}, bf16[64,2304]{1,0:T(8,128)(2,1)S(1)}, u32[]{:S(2)}, u32[]{:S(2)}) collective-permute-start(bf16[64,2304]{1,0:T(8,128)(2,1)S(1)} %collective-permute-done.24.refs_4_), channel_id=1, source_target_pairs={{0,15},{1,0},{2,1},{3,2},{4,3},{5,4},{6,5},{7,6},{8,7},{9,8},{10,9... | collective-permute-start | bytes 884744 | tf_op jit(solution)/shard_map/ppermute | solution.py:28
  40.1 8.7 %collective-permute-start.27 = (bf16[64,2304]{1,0:T(8,128)(2,1)S(1)}, bf16[64,2304]{1,0:T(8,128)(2,1)S(1)}, u32[]{:S(2)}, u32[]{:S(2)}) collective-permute-start(bf16[64,2304]{1,0:T(8,128)(2,1)S(1)} %collective-permute-done.25.refs_5_), channel_id=1, source_target_pairs={{0,1},{1,2},{2,3},{3,4},{4,5},{5,6},{6,7},{7,8},{8,9},{9,10},{10,1... | collective-permute-start | bytes 884744 | tf_op jit(solution)/shard_map/ppermute | solution.py:28
  42.1 8.7 %collective-permute-start.28 = (bf16[64,2304]{1,0:T(8,128)(2,1)S(1)}, bf16[64,2304]{1,0:T(8,128)(2,1)S(1)}, u32[]{:S(2)}, u32[]{:S(2)}) collective-permute-start(bf16[64,2304]{1,0:T(8,128)(2,1)S(1)} %collective-permute-done.26.refs_6_), channel_id=1, source_target_pairs={{0,15},{1,0},{2,1},{3,2},{4,3},{5,4},{6,5},{7,6},{8,7},{9,8},{10,9... | collective-permute-start | bytes 884744 | tf_op jit(solution)/shard_map/ppermute | solution.py:28
  48.8 8.7 %collective-permute-start.29 = (bf16[64,2304]{1,0:T(8,128)(2,1)S(1)}, bf16[64,2304]{1,0:T(8,128)(2,1)S(1)}, u32[]{:S(2)}, u32[]{:S(2)}) collective-permute-start(bf16[64,2304]{1,0:T(8,128)(2,1)S(1)} %collective-permute-done.27.refs_7_), channel_id=1, source_target_pairs={{0,1},{1,2},{2,3},{3,4},{4,5},{5,6},{6,7},{7,8},{8,9},{9,10},{10,1... | collective-permute-start | bytes 884744 | tf_op jit(solution)/shard_map/ppermute | solution.py:28
  50.7 8.7 %collective-permute-start.30 = (bf16[64,2304]{1,0:T(8,128)(2,1)S(1)}, bf16[64,2304]{1,0:T(8,128)(2,1)S(1)}, u32[]{:S(2)}, u32[]{:S(2)}) collective-permute-start(bf16[64,2304]{1,0:T(8,128)(2,1)S(1)} %collective-permute-done.28.refs_8_), channel_id=1, source_target_pairs={{0,15},{1,0},{2,1},{3,2},{4,3},{5,4},{6,5},{7,6},{8,7},{9,8},{10,9... | collective-permute-start | bytes 884744 | tf_op jit(solution)/shard_map/ppermute | solution.py:28
  57.5 8.7 %collective-permute-start.31 = (bf16[64,2304]{1,0:T(8,128)(2,1)S(1)}, bf16[64,2304]{1,0:T(8,128)(2,1)S(1)}, u32[]{:S(2)}, u32[]{:S(2)}) collective-permute-start(bf16[64,2304]{1,0:T(8,128)(2,1)S(1)} %collective-permute-done.29.refs_9_), channel_id=1, source_target_pairs={{0,1},{1,2},{2,3},{3,4},{4,5},{5,6},{6,7},{7,8},{8,9},{9,10},{10,1... | collective-permute-start | bytes 884744 | tf_op jit(solution)/shard_map/ppermute | solution.py:28
  59.4 8.7 %collective-permute-start.32 = (bf16[64,2304]{1,0:T(8,128)(2,1)S(1)}, bf16[64,2304]{1,0:T(8,128)(2,1)}, u32[]{:S(2)}, u32[]{:S(2)}) collective-permute-start(bf16[64,2304]{1,0:T(8,128)(2,1)S(1)} %collective-permute-done.30.refs_10_), channel_id=1, source_target_pairs={{0,15},{1,0},{2,1},{3,2},{4,3},{5,4},{6,5},{7,6},{8,7},{9,8},{10,9... | collective-permute-start | bytes 884744 | tf_op jit(solution)/shard_map/ppermute | solution.py:28
  66.1 9.1 %collective-permute-start.33 = (bf16[64,2304]{1,0:T(8,128)(2,1)S(1)}, bf16[64,2304]{1,0:T(8,128)(2,1)}, u32[]{:S(2)}, u32[]{:S(2)}) collective-permute-start(bf16[64,2304]{1,0:T(8,128)(2,1)S(1)} %collective-permute-done.31.refs_11_), channel_id=1, source_target_pairs={{0,1},{1,2},{2,3},{3,4},{4,5},{5,6},{6,7},{7,8},{8,9},{9,10},{10,1... | collective-permute-start | bytes 884744 | tf_op jit(solution)/shard_map/ppermute | solution.py:28
  68.1 9.2 %collective-permute-start.34 = (bf16[64,2304]{1,0:T(8,128)(2,1)}, bf16[64,2304]{1,0:T(8,128)(2,1)}, u32[]{:S(2)}, u32[]{:S(2)}) collective-permute-start(bf16[64,2304]{1,0:T(8,128)(2,1)} %collective-permute-done.32.refs_12_), channel_id=1, source_target_pairs={{0,15},{1,0},{2,1},{3,2},{4,3},{5,4},{6,5},{7,6},{8,7},{9,8},{10,9... | collective-permute-start | bytes 884744 | tf_op jit(solution)/shard_map/ppermute | solution.py:28
  75.2 10.1 %collective-permute-start.35 = (bf16[64,2304]{1,0:T(8,128)(2,1)}, bf16[64,2304]{1,0:T(8,128)(2,1)}, u32[]{:S(2)}, u32[]{:S(2)}) collective-permute-start(bf16[64,2304]{1,0:T(8,128)(2,1)} %collective-permute-done.33.refs_13_), channel_id=1, source_target_pairs={{0,1},{1,2},{2,3},{3,4},{4,5},{5,6},{6,7},{7,8},{8,9},{9,10},{10,1... | collective-permute-start | bytes 884744 | tf_op jit(solution)/shard_map/ppermute | solution.py:28
  77.2 8.1 %copy-start.1 = (bf16[1,2304,256]{2,1,0:T(8,128)(2,1)S(1)}, bf16[1,2304,256]{2,1,0:T(8,128)(2,1)}, u32[]{:S(2)}) copy-start(bf16[1,2304,256]{2,1,0:T(8,128)(2,1)} %param.16) | copy-start | bytes 3538948
  77.2 8.1 %copy-start.2 = (bf16[1,256,2304]{2,1,0:T(8,128)(2,1)S(1)}, bf16[1,256,2304]{2,1,0:T(8,128)(2,1)}, u32[]{:S(2)}) copy-start(bf16[1,256,2304]{2,1,0:T(8,128)(2,1)} %param.19) | copy-start | bytes 3538948
  77.2 8.1 %copy-start.3 = (bf16[1,2304,128]{2,1,0:T(8,128)(2,1)S(1)}, bf16[1,2304,128]{2,1,0:T(8,128)(2,1)}, u32[]{:S(2)}) copy-start(bf16[1,2304,128]{2,1,0:T(8,128)(2,1)} %param.17) | copy-start | bytes 1769476
  77.3 8.0 %copy-start.4 = (bf16[1,2304,128]{2,1,0:T(8,128)(2,1)S(1)}, bf16[1,2304,128]{2,1,0:T(8,128)(2,1)}, u32[]{:S(2)}) copy-start(bf16[1,2304,128]{2,1,0:T(8,128)(2,1)} %param.18) | copy-start | bytes 1769476
  77.3 8.0 %copy-start.5 = (bf16[1,1,32,2304]{3,2,1,0:T(8,128)(2,1)S(1)}, bf16[1,1,32,2304]{3,2,1,0:T(8,128)(2,1)}, u32[]{:S(2)}) copy-start(bf16[1,1,32,2304]{3,2,1,0:T(8,128)(2,1)} %param.13) | copy-start | bytes 442372
  77.3 8.0 %copy-start.9 = (bf16[1,2304]{1,0:T(2,128)(2,1)S(1)}, bf16[1,2304]{1,0:T(2,128)(2,1)}, u32[]{:S(2)}) copy-start(bf16[1,2304]{1,0:T(2,128)(2,1)} %gain_ref.3) | copy-start | bytes 13828
  77.3 8.0 %copy-start.10 = (bf16[2304]{0:T(1024)(128)(2,1)S(1)}, bf16[2304]{0:T(1024)(128)(2,1)}, u32[]{:S(2)}) copy-start(bf16[2304]{0:T(1024)(128)(2,1)} %param.20) | copy-start | bytes 13828
  77.3 8.0 %copy-start.11 = (bf16[2304]{0:T(1024)(128)(2,1)S(1)}, bf16[2304]{0:T(1024)(128)(2,1)}, u32[]{:S(2)}) copy-start(bf16[2304]{0:T(1024)(128)(2,1)} %param.21) | copy-start | bytes 13828
  77.3 8.0 %copy-start.12 = (s32[1,8]{1,0:T(1,128)S(1)}, s32[1,8]{1,0:T(1,128)}, u32[]{:S(2)}) copy-start(s32[1,8]{1,0:T(1,128)} %lengths_ref.1) | copy-start | bytes 100
  77.3 8.0 %copy-start.14 = (s32[1,8]{1,0:T(1,128)S(1)}, s32[1,8]{1,0:T(1,128)}, u32[]{:S(2)}) copy-start(s32[1,8]{1,0:T(1,128)} %param.22) | copy-start | bytes 100
  85.4 81.7 %copy-start = (bf16[1,1,32,2304]{3,2,1,0:T(8,128)(2,1)S(1)}, bf16[1,1,32,2304]{3,2,1,0:T(8,128)(2,1)}, u32[]{:S(2)}) copy-start(bf16[1,1,32,2304]{3,2,1,0:T(8,128)(2,1)} %param.14) | copy-start | bytes 442372
  85.4 81.7 %copy-start.6 = (bf16[1,1,32,2304]{3,2,1,0:T(8,128)(2,1)S(1)}, bf16[1,1,32,2304]{3,2,1,0:T(8,128)(2,1)}, u32[]{:S(2)}) copy-start(bf16[1,1,32,2304]{3,2,1,0:T(8,128)(2,1)} %param.13) | copy-start | bytes 442372
  85.4 81.7 %copy-start.13 = (s32[1,8]{1,0:T(1,128)S(1)}, s32[1,8]{1,0:T(1,128)}, u32[]{:S(2)}) copy-start(s32[1,8]{1,0:T(1,128)} %lengths_ref.1) | copy-start | bytes 100
  89.5 7.6 %collective-permute-start = (bf16[32,2304]{1,0:T(8,128)(2,1)S(1)}, bf16[32,2304]{1,0:T(8,128)(2,1)S(1)}, u32[]{:S(2)}, u32[]{:S(2)}) collective-permute-start(bf16[32,2304]{1,0:T(8,128)(2,1)S(1)} %get-tuple-element.50), channel_id=1, source_target_pairs={{0,1},{1,2},{2,3},{3,4},{4,5},{5,6},{6,7},{7,8},{8,9},{9,10},{10,1... | collective-permute-start | bytes 442376 | tf_op jit(solution)/shard_map/cond/branch_0_fun/ppermute | solution.py:28
  91.4 7.6 %collective-permute-start.8 = (bf16[32,2304]{1,0:T(8,128)(2,1)S(1)}, bf16[32,2304]{1,0:T(8,128)(2,1)S(1)}, u32[]{:S(2)}, u32[]{:S(2)}) collective-permute-start(bf16[32,2304]{1,0:T(8,128)(2,1)S(1)} %get-tuple-element.63), channel_id=1, source_target_pairs={{0,15},{1,0},{2,1},{3,2},{4,3},{5,4},{6,5},{7,6},{8,7},{9,8},{10,9... | collective-permute-start | bytes 442376 | tf_op jit(solution)/shard_map/cond/branch_0_fun/ppermute | solution.py:28
  97.1 10.5 %collective-permute-start.1 = (bf16[64,2304]{1,0:T(8,128)(2,1)S(1)}, bf16[64,2304]{1,0:T(8,128)(2,1)S(1)}, u32[]{:S(2)}, u32[]{:S(2)}) collective-permute-start(bf16[64,2304]{1,0:T(8,128)(2,1)S(1)} %add_convert_fusion.13), channel_id=1, source_target_pairs={{0,1},{1,2},{2,3},{3,4},{4,5},{5,6},{6,7},{7,8},{8,9},{9,10},{10,1... | collective-permute-start | bytes 884744 | tf_op jit(solution)/shard_map/cond/branch_0_fun/ppermute | solution.py:28
  99.1 10.6 %collective-permute-start.9 = (bf16[64,2304]{1,0:T(8,128)(2,1)S(1)}, bf16[64,2304]{1,0:T(8,128)(2,1)S(1)}, u32[]{:S(2)}, u32[]{:S(2)}) collective-permute-start(bf16[64,2304]{1,0:T(8,128)(2,1)S(1)} %add_convert_fusion.6), channel_id=1, source_target_pairs={{0,15},{1,0},{2,1},{3,2},{4,3},{5,4},{6,5},{7,6},{8,7},{9,8},{10,9... | collective-permute-start | bytes 884744 | tf_op jit(solution)/shard_map/cond/branch_0_fun/ppermute | solution.py:28
  107.7 11.3 %collective-permute-start.2 = (bf16[64,2304]{1,0:T(8,128)(2,1)S(1)}, bf16[64,2304]{1,0:T(8,128)(2,1)S(1)}, u32[]{:S(2)}, u32[]{:S(2)}) collective-permute-start(bf16[64,2304]{1,0:T(8,128)(2,1)S(1)} %add_convert_fusion.12), channel_id=1, source_target_pairs={{0,1},{1,2},{2,3},{3,4},{4,5},{5,6},{6,7},{7,8},{8,9},{9,10},{10,1... | collective-permute-start | bytes 884744 | tf_op jit(solution)/shard_map/cond/branch_0_fun/ppermute | solution.py:28
  109.7 11.3 %collective-permute-start.10 = (bf16[64,2304]{1,0:T(8,128)(2,1)S(1)}, bf16[64,2304]{1,0:T(8,128)(2,1)S(1)}, u32[]{:S(2)}, u32[]{:S(2)}) collective-permute-start(bf16[64,2304]{1,0:T(8,128)(2,1)S(1)} %add_convert_fusion.5), channel_id=1, source_target_pairs={{0,15},{1,0},{2,1},{3,2},{4,3},{5,4},{6,5},{7,6},{8,7},{9,8},{10,9... | collective-permute-start | bytes 884744 | tf_op jit(solution)/shard_map/cond/branch_0_fun/ppermute | solution.py:28
  119.1 10.4 %collective-permute-start.3 = (bf16[64,2304]{1,0:T(8,128)(2,1)S(1)}, bf16[64,2304]{1,0:T(8,128)(2,1)S(1)}, u32[]{:S(2)}, u32[]{:S(2)}) collective-permute-start(bf16[64,2304]{1,0:T(8,128)(2,1)S(1)} %add_convert_fusion.11), channel_id=1, source_target_pairs={{0,1},{1,2},{2,3},{3,4},{4,5},{5,6},{6,7},{7,8},{8,9},{9,10},{10,1... | collective-permute-start | bytes 884744 | tf_op jit(solution)/shard_map/cond/branch_0_fun/ppermute | solution.py:28
  121.1 10.4 %collective-permute-start.11 = (bf16[64,2304]{1,0:T(8,128)(2,1)S(1)}, bf16[64,2304]{1,0:T(8,128)(2,1)S(1)}, u32[]{:S(2)}, u32[]{:S(2)}) collective-permute-start(bf16[64,2304]{1,0:T(8,128)(2,1)S(1)} %add_convert_fusion.4), channel_id=1, source_target_pairs={{0,15},{1,0},{2,1},{3,2},{4,3},{5,4},{6,5},{7,6},{8,7},{9,8},{10,9... | collective-permute-start | bytes 884744 | tf_op jit(solution)/shard_map/cond/branch_0_fun/ppermute | solution.py:28
  129.6 9.5 %collective-permute-start.4 = (bf16[64,2304]{1,0:T(8,128)(2,1)S(1)}, bf16[64,2304]{1,0:T(8,128)(2,1)S(1)}, u32[]{:S(2)}, u32[]{:S(2)}) collective-permute-start(bf16[64,2304]{1,0:T(8,128)(2,1)S(1)} %add_convert_fusion.10), channel_id=1, source_target_pairs={{0,1},{1,2},{2,3},{3,4},{4,5},{5,6},{6,7},{7,8},{8,9},{9,10},{10,1... | collective-permute-start | bytes 884744 | tf_op jit(solution)/shard_map/cond/branch_0_fun/ppermute | solution.py:28
  131.6 9.5 %collective-permute-start.12 = (bf16[64,2304]{1,0:T(8,128)(2,1)S(1)}, bf16[64,2304]{1,0:T(8,128)(2,1)S(1)}, u32[]{:S(2)}, u32[]{:S(2)}) collective-permute-start(bf16[64,2304]{1,0:T(8,128)(2,1)S(1)} %add_convert_fusion.3), channel_id=1, source_target_pairs={{0,15},{1,0},{2,1},{3,2},{4,3},{5,4},{6,5},{7,6},{8,7},{9,8},{10,9... | collective-permute-start | bytes 884744 | tf_op jit(solution)/shard_map/cond/branch_0_fun/ppermute | solution.py:28
  139.2 8.7 %collective-permute-start.5 = (bf16[64,2304]{1,0:T(8,128)(2,1)S(1)}, bf16[64,2304]{1,0:T(8,128)(2,1)S(1)}, u32[]{:S(2)}, u32[]{:S(2)}) collective-permute-start(bf16[64,2304]{1,0:T(8,128)(2,1)S(1)} %add_convert_fusion.9), channel_id=1, source_target_pairs={{0,1},{1,2},{2,3},{3,4},{4,5},{5,6},{6,7},{7,8},{8,9},{9,10},{10,1... | collective-permute-start | bytes 884744 | tf_op jit(solution)/shard_map/cond/branch_0_fun/ppermute | solution.py:28
  141.2 8.7 %collective-permute-start.13 = (bf16[64,2304]{1,0:T(8,128)(2,1)S(1)}, bf16[64,2304]{1,0:T(8,128)(2,1)S(1)}, u32[]{:S(2)}, u32[]{:S(2)}) collective-permute-start(bf16[64,2304]{1,0:T(8,128)(2,1)S(1)} %add_convert_fusion.2), channel_id=1, source_target_pairs={{0,15},{1,0},{2,1},{3,2},{4,3},{5,4},{6,5},{7,6},{8,7},{9,8},{10,9... | collective-permute-start | bytes 884744 | tf_op jit(solution)/shard_map/cond/branch_0_fun/ppermute | solution.py:28
  147.9 8.7 %collective-permute-start.6 = (bf16[64,2304]{1,0:T(8,128)(2,1)S(1)}, bf16[64,2304]{1,0:T(8,128)(2,1)S(1)}, u32[]{:S(2)}, u32[]{:S(2)}) collective-permute-start(bf16[64,2304]{1,0:T(8,128)(2,1)S(1)} %add_convert_fusion.8), channel_id=1, source_target_pairs={{0,1},{1,2},{2,3},{3,4},{4,5},{5,6},{6,7},{7,8},{8,9},{9,10},{10,1... | collective-permute-start | bytes 884744 | tf_op jit(solution)/shard_map/cond/branch_0_fun/ppermute | solution.py:28
  149.9 8.7 %collective-permute-start.14 = (bf16[64,2304]{1,0:T(8,128)(2,1)S(1)}, bf16[64,2304]{1,0:T(8,128)(2,1)S(1)}, u32[]{:S(2)}, u32[]{:S(2)}) collective-permute-start(bf16[64,2304]{1,0:T(8,128)(2,1)S(1)} %add_convert_fusion.1), channel_id=1, source_target_pairs={{0,15},{1,0},{2,1},{3,2},{4,3},{5,4},{6,5},{7,6},{8,7},{9,8},{10,9... | collective-permute-start | bytes 884744 | tf_op jit(solution)/shard_map/cond/branch_0_fun/ppermute | solution.py:28
  156.7 8.7 %collective-permute-start.7 = (bf16[64,2304]{1,0:T(8,128)(2,1)S(1)}, bf16[64,2304]{1,0:T(8,128)(2,1)S(1)}, u32[]{:S(2)}, u32[]{:S(2)}) collective-permute-start(bf16[64,2304]{1,0:T(8,128)(2,1)S(1)} %add_convert_fusion.7), channel_id=1, source_target_pairs={{0,1},{1,2},{2,3},{3,4},{4,5},{5,6},{6,7},{7,8},{8,9},{9,10},{10,1... | collective-permute-start | bytes 884744 | tf_op jit(solution)/shard_map/cond/branch_0_fun/ppermute | solution.py:28
  158.7 8.2 %collective-permute-start.15 = (bf16[64,2304]{1,0:T(8,128)(2,1)S(1)}, bf16[64,2304]{1,0:T(8,128)(2,1)S(1)}, u32[]{:S(2)}, u32[]{:S(2)}) collective-permute-start(bf16[64,2304]{1,0:T(8,128)(2,1)S(1)} %add_convert_fusion), channel_id=1, source_target_pairs={{0,15},{1,0},{2,1},{3,2},{4,3},{5,4},{6,5},{7,6},{8,7},{9,8},{10,9... | collective-permute-start | bytes 884744 | tf_op jit(solution)/shard_map/cond/branch_0_fun/ppermute | solution.py:28
  167.9 22.3 %collective-permute-start.36 = (bf16[32,2304]{1,0:T(8,128)(2,1)S(1)}, bf16[32,2304]{1,0:T(8,128)(2,1)S(1)}, u32[]{:S(2)}, u32[]{:S(2)}) collective-permute-start(bf16[32,2304]{1,0:T(8,128)(2,1)S(1)} %get-tuple-element.94), channel_id=1, source_target_pairs={{16,32},{32,16},{48,64},{64,48},{80,96},{96,80},{112,128},{128,112... | collective-permute-start | bytes 442376 | tf_op jit(solution)/shard_map/ppermute | solution.py:36
  187.4 3.3 %collective-permute-start.37 = (bf16[32,2304]{1,0:T(8,128)(2,1)S(1)}, bf16[32,2304]{1,0:T(8,128)(2,1)S(1)}, u32[]{:S(2)}, u32[]{:S(2)}) collective-permute-start(bf16[32,2304]{1,0:T(8,128)(2,1)S(1)} %get-tuple-element.95), channel_id=1, source_target_pairs={{0,16},{16,0},{32,48},{48,32},{64,80},{80,64},{96,112},{112,96},{1... | collective-permute-start | bytes 442376 | tf_op jit(solution)/shard_map/ppermute | solution.py:36

commit v8 on v6

--- a/solution.py
+++ b/solution.py
@@ -198,8 +198,8 @@
 def project_back(turned, wq_ref, wk_ref, wv_ref, wo_ref, mixed_outs, back_outs):
     own, feats = mixed_outs[0].shape[0], wq_ref.shape[0]
     at_mix = turned.shape[1] - wo_ref.shape[0]
-    for start in range(0, feats, 256):
-        cols = slice(start, start + 256)
+    for start in range(0, feats, 768):
+        cols = slice(start, start + 768)
         w_in = w_in_of(wq_ref.at[cols], wk_ref.at[cols], wv_ref.at[cols])
         back = dot_nt(turned[:, :at_mix], w_in).astype(BF16)
         mixed = dot(turned[:, at_mix:], wo_ref[:, cols]).astype(BF16)

time: 193 us -> 193 us (level)
  no operation moved by 1% of the time
where the time goes in v8:
time: 193 us; the launch traced here: 191 us
  starting transfers between devices  128 us (66%)
  waiting for transfers between devices  46 us (24%)
  Pallas kernels  12.4 us (6%)
  other arithmetic  2.86 us (1%)
    ppermute x31, starting transfers between devices, shift(): return lax.ppermute(value, ('section', 'tensor'), pairs)  107 us
    ppermute x31, waiting for transfers between devices, shift(): return lax.ppermute(value, ('section', 'tensor'), pairs)  44.7 us
    ppermute x2, starting transfers between devices, swap_sections(): return lax.ppermute(value, 'section', pairs)  21.4 us
    pallas_call x1, Pallas kernels, early_part(): pl.pallas_call(early_kernel, out_shape=jax.ShapeDtypeStruct((rows, cols),...  4.66 us
    pallas_call x1, Pallas kernels, layer_part(): pl.pallas_call(functools.partial(layer_kernel, offsets, back_offsets, len...  4.01 us
  transfers between devices with their start and end apart: 33, of which 19 were waited for; matrix products, arithmetic and copies ran while one was open for 1% of the time, Pallas kernels for 4%

profile of v8, /device:TPU:1, one launch (start us, length us, event | category | flops | bytes accessed | tf_op | source)
XLA Modules:
  0.0 191.4 jit_solution(1683396637722866745)
XLA Ops:
  1.6 4.4 %collective-permute-start.21 = (bf16[64,2304]{1,0:T(8,128)(2,1)S(1)}, bf16[64,2304]{1,0:T(8,128)(2,1)S(1)}, u32[]{:S(2)}, u32[]{:S(2)}) collective-permute-start(bf16[64,2304]{1,0:T(8,128)(2,1)S(1)} %pad_maximum_fusion.refs_0_), channel_id=1, source_target_pairs={{0,1},{1,2},{2,3},{3,4},{4,5},{5,6},{6,7},{7,8},{8,9},{9,10},{10,1... | collective-permute-start | bytes 884744 | tf_op jit(solution)/shard_map/ppermute | solution.py:28
  6.0 9.5 %collective-permute-start.22 = (bf16[64,2304]{1,0:T(8,128)(2,1)S(1)}, bf16[64,2304]{1,0:T(8,128)(2,1)S(1)}, u32[]{:S(2)}, u32[]{:S(2)}) collective-permute-start(bf16[64,2304]{1,0:T(8,128)(2,1)S(1)} %pad_maximum_fusion.refs_0_), channel_id=1, source_target_pairs={{0,15},{1,0},{2,1},{3,2},{4,3},{5,4},{6,5},{7,6},{8,7},{9,8},{10,9... | collective-permute-start | bytes 884744 | tf_op jit(solution)/shard_map/ppermute | solution.py:28
  15.5 4.8 %collective-permute-done.21.refs_1_ = bf16[64,2304]{1,0:T(8,128)(2,1)S(1)} collective-permute-done((bf16[64,2304]{1,0:T(8,128)(2,1)S(1)}, bf16[64,2304]{1,0:T(8,128)(2,1)S(1)}, u32[]{:S(2)}, u32[]{:S(2)}) %collective-permute-start.21) | collective-permute-done | bytes 294944 | tf_op jit(solution)/shard_map/ppermute | solution.py:28
  20.3 1.9 collective-permute-start.23
  22.2 4.6 %collective-permute-start.24 = (bf16[64,2304]{1,0:T(8,128)(2,1)S(1)}, bf16[64,2304]{1,0:T(8,128)(2,1)S(1)}, u32[]{:S(2)}, u32[]{:S(2)}) collective-permute-start(bf16[64,2304]{1,0:T(8,128)(2,1)S(1)} %collective-permute-done.22.refs_2_), channel_id=1, source_target_pairs={{0,15},{1,0},{2,1},{3,2},{4,3},{5,4},{6,5},{7,6},{8,7},{9,8},{10,9... | collective-permute-start | bytes 884744 | tf_op jit(solution)/shard_map/ppermute | solution.py:28
  26.8 3.9 %collective-permute-done.23.refs_3_ = bf16[64,2304]{1,0:T(8,128)(2,1)S(1)} collective-permute-done((bf16[64,2304]{1,0:T(8,128)(2,1)S(1)}, bf16[64,2304]{1,0:T(8,128)(2,1)S(1)}, u32[]{:S(2)}, u32[]{:S(2)}) %collective-permute-start.23) | collective-permute-done | bytes 294944 | tf_op jit(solution)/shard_map/ppermute | solution.py:28
  30.7 1.9 collective-permute-start.25
  32.6 4.6 %collective-permute-start.26 = (bf16[64,2304]{1,0:T(8,128)(2,1)S(1)}, bf16[64,2304]{1,0:T(8,128)(2,1)S(1)}, u32[]{:S(2)}, u32[]{:S(2)}) collective-permute-start(bf16[64,2304]{1,0:T(8,128)(2,1)S(1)} %collective-permute-done.24.refs_4_), channel_id=1, source_target_pairs={{0,15},{1,0},{2,1},{3,2},{4,3},{5,4},{6,5},{7,6},{8,7},{9,8},{10,9... | collective-permute-start | bytes 884744 | tf_op jit(solution)/shard_map/ppermute | solution.py:28
  37.2 2.9 %collective-permute-done.25.refs_5_ = bf16[64,2304]{1,0:T(8,128)(2,1)S(1)} collective-permute-done((bf16[64,2304]{1,0:T(8,128)(2,1)S(1)}, bf16[64,2304]{1,0:T(8,128)(2,1)S(1)}, u32[]{:S(2)}, u32[]{:S(2)}) %collective-permute-start.25) | collective-permute-done | bytes 294944 | tf_op jit(solution)/shard_map/ppermute | solution.py:28
  40.1 1.9 collective-permute-start.27
  42.1 4.6 %collective-permute-start.28 = (bf16[64,2304]{1,0:T(8,128)(2,1)S(1)}, bf16[64,2304]{1,0:T(8,128)(2,1)S(1)}, u32[]{:S(2)}, u32[]{:S(2)}) collective-permute-start(bf16[64,2304]{1,0:T(8,128)(2,1)S(1)} %collective-permute-done.26.refs_6_), channel_id=1, source_target_pairs={{0,15},{1,0},{2,1},{3,2},{4,3},{5,4},{6,5},{7,6},{8,7},{9,8},{10,9... | collective-permute-start | bytes 884744 | tf_op jit(solution)/shard_map/ppermute | solution.py:28
  46.6 2.2 %collective-permute-done.27.refs_7_ = bf16[64,2304]{1,0:T(8,128)(2,1)S(1)} collective-permute-done((bf16[64,2304]{1,0:T(8,128)(2,1)S(1)}, bf16[64,2304]{1,0:T(8,128)(2,1)S(1)}, u32[]{:S(2)}, u32[]{:S(2)}) %collective-permute-start.27) | collective-permute-done | bytes 294944 | tf_op jit(solution)/shard_map/ppermute | solution.py:28
  50.7 4.6 %collective-permute-start.30 = (bf16[64,2304]{1,0:T(8,128)(2,1)S(1)}, bf16[64,2304]{1,0:T(8,128)(2,1)S(1)}, u32[]{:S(2)}, u32[]{:S(2)}) collective-permute-start(bf16[64,2304]{1,0:T(8,128)(2,1)S(1)} %collective-permute-done.28.refs_8_), channel_id=1, source_target_pairs={{0,15},{1,0},{2,1},{3,2},{4,3},{5,4},{6,5},{7,6},{8,7},{9,8},{10,9... | collective-permute-start | bytes 884744 | tf_op jit(solution)/shard_map/ppermute | solution.py:28
  55.3 2.2 %collective-permute-done.29.refs_9_ = bf16[64,2304]{1,0:T(8,128)(2,1)S(1)} collective-permute-done((bf16[64,2304]{1,0:T(8,128)(2,1)S(1)}, bf16[64,2304]{1,0:T(8,128)(2,1)S(1)}, u32[]{:S(2)}, u32[]{:S(2)}) %collective-permute-start.29) | collective-permute-done | bytes 294944 | tf_op jit(solution)/shard_map/ppermute | solution.py:28
  59.4 4.6 %collective-permute-start.32 = (bf16[64,2304]{1,0:T(8,128)(2,1)S(1)}, bf16[64,2304]{1,0:T(8,128)(2,1)}, u32[]{:S(2)}, u32[]{:S(2)}) collective-permute-start(bf16[64,2304]{1,0:T(8,128)(2,1)S(1)} %collective-permute-done.30.refs_10_), channel_id=1, source_target_pairs={{0,15},{1,0},{2,1},{3,2},{4,3},{5,4},{6,5},{7,6},{8,7},{9,8},{10,9... | collective-permute-start | bytes 884744 | tf_op jit(solution)/shard_map/ppermute | solution.py:28
  64.0 2.2 %collective-permute-done.31.refs_11_ = bf16[64,2304]{1,0:T(8,128)(2,1)S(1)} collective-permute-done((bf16[64,2304]{1,0:T(8,128)(2,1)S(1)}, bf16[64,2304]{1,0:T(8,128)(2,1)S(1)}, u32[]{:S(2)}, u32[]{:S(2)}) %collective-permute-start.31) | collective-permute-done | bytes 294944 | tf_op jit(solution)/shard_map/ppermute | solution.py:28
  66.1 1.9 collective-permute-start.33
  68.8 4.6 %collective-permute-start.34 = (bf16[64,2304]{1,0:T(8,128)(2,1)}, bf16[64,2304]{1,0:T(8,128)(2,1)}, u32[]{:S(2)}, u32[]{:S(2)}) collective-permute-start(bf16[64,2304]{1,0:T(8,128)(2,1)} %collective-permute-done.32.refs_12_), channel_id=1, source_target_pairs={{0,15},{1,0},{2,1},{3,2},{4,3},{5,4},{6,5},{7,6},{8,7},{9,8},{10,9... | collective-permute-start | bytes 884744 | tf_op jit(solution)/shard_map/ppermute | solution.py:28
  75.2 1.9 collective-permute-start.35
  77.4 4.7 %early_rows.1 = bf16[480,768]{1,0:T(8,128)(2,1)S(1)} custom-call(bf16[1,2304]{1,0:T(2,128)(2,1)} %gain_ref.3, bf16[2304,256]{1,0:T(8,128)(2,1)} %bitcast.22, bf16[2304,128]{1,0:T(8,128)(2,1)} %bitcast.28, bf16[2304,128]{1,0:T(8,128)(2,1)} %bitcast.31, bf16[256,2304]{1,0:T(8,128)(2,1)} %bitcast.25, bf16[64,2304]{1,0:T(8,128)(2,1)S(1)} %pad_maximum_fusion.refs_0_, ...), custom_call_target="tpu_custom_call" | custom-call | flops 1698693120 | bytes 4423680 | tf_op jit(solution)/shard_map/early_rows/pallas_call | solution.py:104
  82.0 3.2 %collective-permute-done.35 = bf16[64,2304]{1,0:T(8,128)(2,1)} collective-permute-done((bf16[64,2304]{1,0:T(8,128)(2,1)}, bf16[64,2304]{1,0:T(8,128)(2,1)}, u32[]{:S(2)}, u32[]{:S(2)}) %collective-permute-start.35) | collective-permute-done | bytes 294944 | tf_op jit(solution)/shard_map/ppermute | solution.py:28
  85.4 81.5 %conditional.1 = (f32[64,2304]{1,0:T(8,128)S(1)}, f32[8,2304]{1,0:T(8,128)S(1)}) conditional(s32[]{:T(128)} %convert_element_type.155, (s32[3]{0:T(128)S(1)}, bf16[1,2304]{1,0:T(2,128)(2,1)S(1)}, bf16[2304,256]{1,0:T(8,128)(2,1)S(1)}, bf16[2304,128]{1,0:T(8,128)(2,1)S(1)}, bf16[2304,128]{1,0:T(8,128)(2,1)S(1)}, ...), branch_computations={%region_0.1_spmd, %region_1.9_spmd} | conditional | flops 1707687936 | bytes 31335060 | solution.py:594
  85.4 4.0 %layer_both_ways.1 = (bf16[32,2304]{1,0:T(8,128)(2,1)S(1)}, bf16[32,2304]{1,0:T(8,128)(2,1)S(1)}, bf16[64,768]{1,0:T(8,128)(2,1)S(1)}, bf16[416,768]{1,0:T(8,128)(2,1)S(1)}) custom-call(s32[3]{0:T(128)S(1)} %get-tuple-element.46.me_ref, bf16[1,2304]{1,0:T(2,128)(2,1)S(1)} %get-tuple-element.47.gain_ref, bf16[2304,256]{1,0:T(8,128)(2,1)S(1)} %get-tuple-element.42.wq_ref, ...), custom_call_target="tpu_custom_call" | custom-call | tf_op jit(solution)/shard_map/cond/branch_0_fun/layer_both_ways/pallas_call | solution.py:285
  89.4 1.9 %collective-permute-start = (bf16[32,2304]{1,0:T(8,128)(2,1)S(1)}, bf16[32,2304]{1,0:T(8,128)(2,1)S(1)}, u32[]{:S(2)}, u32[]{:S(2)}) collective-permute-start(bf16[32,2304]{1,0:T(8,128)(2,1)S(1)} %get-tuple-element.50), channel_id=1, source_target_pairs={{0,1},{1,2},{2,3},{3,4},{4,5},{5,6},{6,7},{7,8},{8,9},{9,10},{10,1... | collective-permute-start | bytes 442376 | tf_op jit(solution)/shard_map/cond/branch_0_fun/ppermute | solution.py:28
  91.4 4.6 %collective-permute-start.8 = (bf16[32,2304]{1,0:T(8,128)(2,1)S(1)}, bf16[32,2304]{1,0:T(8,128)(2,1)S(1)}, u32[]{:S(2)}, u32[]{:S(2)}) collective-permute-start(bf16[32,2304]{1,0:T(8,128)(2,1)S(1)} %get-tuple-element.63), channel_id=1, source_target_pairs={{0,15},{1,0},{2,1},{3,2},{4,3},{5,4},{6,5},{7,6},{8,7},{9,8},{10,9... | collective-permute-start | bytes 442376 | tf_op jit(solution)/shard_map/cond/branch_0_fun/ppermute | solution.py:28
  97.0 1.9 %collective-permute-start.1 = (bf16[64,2304]{1,0:T(8,128)(2,1)S(1)}, bf16[64,2304]{1,0:T(8,128)(2,1)S(1)}, u32[]{:S(2)}, u32[]{:S(2)}) collective-permute-start(bf16[64,2304]{1,0:T(8,128)(2,1)S(1)} %add_convert_fusion.13), channel_id=1, source_target_pairs={{0,1},{1,2},{2,3},{3,4},{4,5},{5,6},{6,7},{7,8},{8,9},{9,10},{10,1... | collective-permute-start | bytes 884744 | tf_op jit(solution)/shard_map/cond/branch_0_fun/ppermute | solution.py:28
  99.0 4.6 %collective-permute-start.9 = (bf16[64,2304]{1,0:T(8,128)(2,1)S(1)}, bf16[64,2304]{1,0:T(8,128)(2,1)S(1)}, u32[]{:S(2)}, u32[]{:S(2)}) collective-permute-start(bf16[64,2304]{1,0:T(8,128)(2,1)S(1)} %add_convert_fusion.6), channel_id=1, source_target_pairs={{0,15},{1,0},{2,1},{3,2},{4,3},{5,4},{6,5},{7,6},{8,7},{9,8},{10,9... | collective-permute-start | bytes 884744 | tf_op jit(solution)/shard_map/cond/branch_0_fun/ppermute | solution.py:28
  105.3 2.3 %collective-permute-done.1 = bf16[64,2304]{1,0:T(8,128)(2,1)S(1)} collective-permute-done((bf16[64,2304]{1,0:T(8,128)(2,1)S(1)}, bf16[64,2304]{1,0:T(8,128)(2,1)S(1)}, u32[]{:S(2)}, u32[]{:S(2)}) %collective-permute-start.1) | collective-permute-done | bytes 294944 | tf_op jit(solution)/shard_map/cond/branch_0_fun/ppermute | solution.py:28
  107.6 1.9 %collective-permute-start.2 = (bf16[64,2304]{1,0:T(8,128)(2,1)S(1)}, bf16[64,2304]{1,0:T(8,128)(2,1)S(1)}, u32[]{:S(2)}, u32[]{:S(2)}) collective-permute-start(bf16[64,2304]{1,0:T(8,128)(2,1)S(1)} %add_convert_fusion.12), channel_id=1, source_target_pairs={{0,1},{1,2},{2,3},{3,4},{4,5},{5,6},{6,7},{7,8},{8,9},{9,10},{10,1... | collective-permute-start | bytes 884744 | tf_op jit(solution)/shard_map/cond/branch_0_fun/ppermute | solution.py:28
  109.7 4.6 %collective-permute-start.10 = (bf16[64,2304]{1,0:T(8,128)(2,1)S(1)}, bf16[64,2304]{1,0:T(8,128)(2,1)S(1)}, u32[]{:S(2)}, u32[]{:S(2)}) collective-permute-start(bf16[64,2304]{1,0:T(8,128)(2,1)S(1)} %add_convert_fusion.5), channel_id=1, source_target_pairs={{0,15},{1,0},{2,1},{3,2},{4,3},{5,4},{6,5},{7,6},{8,7},{9,8},{10,9... | collective-permute-start | bytes 884744 | tf_op jit(solution)/shard_map/cond/branch_0_fun/ppermute | solution.py:28
  114.2 4.7 %collective-permute-done.2 = bf16[64,2304]{1,0:T(8,128)(2,1)S(1)} collective-permute-done((bf16[64,2304]{1,0:T(8,128)(2,1)S(1)}, bf16[64,2304]{1,0:T(8,128)(2,1)S(1)}, u32[]{:S(2)}, u32[]{:S(2)}) %collective-permute-start.2) | collective-permute-done | bytes 294944 | tf_op jit(solution)/shard_map/cond/branch_0_fun/ppermute | solution.py:28
  119.0 1.9 %collective-permute-start.3 = (bf16[64,2304]{1,0:T(8,128)(2,1)S(1)}, bf16[64,2304]{1,0:T(8,128)(2,1)S(1)}, u32[]{:S(2)}, u32[]{:S(2)}) collective-permute-start(bf16[64,2304]{1,0:T(8,128)(2,1)S(1)} %add_convert_fusion.11), channel_id=1, source_target_pairs={{0,1},{1,2},{2,3},{3,4},{4,5},{5,6},{6,7},{7,8},{8,9},{9,10},{10,1... | collective-permute-start | bytes 884744 | tf_op jit(solution)/shard_map/cond/branch_0_fun/ppermute | solution.py:28
  121.0 4.6 %collective-permute-start.11 = (bf16[64,2304]{1,0:T(8,128)(2,1)S(1)}, bf16[64,2304]{1,0:T(8,128)(2,1)S(1)}, u32[]{:S(2)}, u32[]{:S(2)}) collective-permute-start(bf16[64,2304]{1,0:T(8,128)(2,1)S(1)} %add_convert_fusion.4), channel_id=1, source_target_pairs={{0,15},{1,0},{2,1},{3,2},{4,3},{5,4},{6,5},{7,6},{8,7},{9,8},{10,9... | collective-permute-start | bytes 884744 | tf_op jit(solution)/shard_map/cond/branch_0_fun/ppermute | solution.py:28
  125.6 3.8 %collective-permute-done.3 = bf16[64,2304]{1,0:T(8,128)(2,1)S(1)} collective-permute-done((bf16[64,2304]{1,0:T(8,128)(2,1)S(1)}, bf16[64,2304]{1,0:T(8,128)(2,1)S(1)}, u32[]{:S(2)}, u32[]{:S(2)}) %collective-permute-start.3) | collective-permute-done | bytes 294944 | tf_op jit(solution)/shard_map/cond/branch_0_fun/ppermute | solution.py:28
  129.5 1.9 %collective-permute-start.4 = (bf16[64,2304]{1,0:T(8,128)(2,1)S(1)}, bf16[64,2304]{1,0:T(8,128)(2,1)S(1)}, u32[]{:S(2)}, u32[]{:S(2)}) collective-permute-start(bf16[64,2304]{1,0:T(8,128)(2,1)S(1)} %add_convert_fusion.10), channel_id=1, source_target_pairs={{0,1},{1,2},{2,3},{3,4},{4,5},{5,6},{6,7},{7,8},{8,9},{9,10},{10,1... | collective-permute-start | bytes 884744 | tf_op jit(solution)/shard_map/cond/branch_0_fun/ppermute | solution.py:28
  131.5 4.6 %collective-permute-start.12 = (bf16[64,2304]{1,0:T(8,128)(2,1)S(1)}, bf16[64,2304]{1,0:T(8,128)(2,1)S(1)}, u32[]{:S(2)}, u32[]{:S(2)}) collective-permute-start(bf16[64,2304]{1,0:T(8,128)(2,1)S(1)} %add_convert_fusion.3), channel_id=1, source_target_pairs={{0,15},{1,0},{2,1},{3,2},{4,3},{5,4},{6,5},{7,6},{8,7},{9,8},{10,9... | collective-permute-start | bytes 884744 | tf_op jit(solution)/shard_map/cond/branch_0_fun/ppermute | solution.py:28
  136.1 2.9 %collective-permute-done.4 = bf16[64,2304]{1,0:T(8,128)(2,1)S(1)} collective-permute-done((bf16[64,2304]{1,0:T(8,128)(2,1)S(1)}, bf16[64,2304]{1,0:T(8,128)(2,1)S(1)}, u32[]{:S(2)}, u32[]{:S(2)}) %collective-permute-start.4) | collective-permute-done | bytes 294944 | tf_op jit(solution)/shard_map/cond/branch_0_fun/ppermute | solution.py:28
  139.0 1.9 %collective-permute-start.5 = (bf16[64,2304]{1,0:T(8,128)(2,1)S(1)}, bf16[64,2304]{1,0:T(8,128)(2,1)S(1)}, u32[]{:S(2)}, u32[]{:S(2)}) collective-permute-start(bf16[64,2304]{1,0:T(8,128)(2,1)S(1)} %add_convert_fusion.9), channel_id=1, source_target_pairs={{0,1},{1,2},{2,3},{3,4},{4,5},{5,6},{6,7},{7,8},{8,9},{9,10},{10,1... | collective-permute-start | bytes 884744 | tf_op jit(solution)/shard_map/cond/branch_0_fun/ppermute | solution.py:28
  141.0 4.6 %collective-permute-start.13 = (bf16[64,2304]{1,0:T(8,128)(2,1)S(1)}, bf16[64,2304]{1,0:T(8,128)(2,1)S(1)}, u32[]{:S(2)}, u32[]{:S(2)}) collective-permute-start(bf16[64,2304]{1,0:T(8,128)(2,1)S(1)} %add_convert_fusion.2), channel_id=1, source_target_pairs={{0,15},{1,0},{2,1},{3,2},{4,3},{5,4},{6,5},{7,6},{8,7},{9,8},{10,9... | collective-permute-start | bytes 884744 | tf_op jit(solution)/shard_map/cond/branch_0_fun/ppermute | solution.py:28
  145.6 2.1 %collective-permute-done.5 = bf16[64,2304]{1,0:T(8,128)(2,1)S(1)} collective-permute-done((bf16[64,2304]{1,0:T(8,128)(2,1)S(1)}, bf16[64,2304]{1,0:T(8,128)(2,1)S(1)}, u32[]{:S(2)}, u32[]{:S(2)}) %collective-permute-start.5) | collective-permute-done | bytes 294944 | tf_op jit(solution)/shard_map/cond/branch_0_fun/ppermute | solution.py:28
  147.8 1.9 %collective-permute-start.6 = (bf16[64,2304]{1,0:T(8,128)(2,1)S(1)}, bf16[64,2304]{1,0:T(8,128)(2,1)S(1)}, u32[]{:S(2)}, u32[]{:S(2)}) collective-permute-start(bf16[64,2304]{1,0:T(8,128)(2,1)S(1)} %add_convert_fusion.8), channel_id=1, source_target_pairs={{0,1},{1,2},{2,3},{3,4},{4,5},{5,6},{6,7},{7,8},{8,9},{9,10},{10,1... | collective-permute-start | bytes 884744 | tf_op jit(solution)/shard_map/cond/branch_0_fun/ppermute | solution.py:28
  149.8 4.6 %collective-permute-start.14 = (bf16[64,2304]{1,0:T(8,128)(2,1)S(1)}, bf16[64,2304]{1,0:T(8,128)(2,1)S(1)}, u32[]{:S(2)}, u32[]{:S(2)}) collective-permute-start(bf16[64,2304]{1,0:T(8,128)(2,1)S(1)} %add_convert_fusion.1), channel_id=1, source_target_pairs={{0,15},{1,0},{2,1},{3,2},{4,3},{5,4},{6,5},{7,6},{8,7},{9,8},{10,9... | collective-permute-start | bytes 884744 | tf_op jit(solution)/shard_map/cond/branch_0_fun/ppermute | solution.py:28
  154.4 2.1 %collective-permute-done.6 = bf16[64,2304]{1,0:T(8,128)(2,1)S(1)} collective-permute-done((bf16[64,2304]{1,0:T(8,128)(2,1)S(1)}, bf16[64,2304]{1,0:T(8,128)(2,1)S(1)}, u32[]{:S(2)}, u32[]{:S(2)}) %collective-permute-start.6) | collective-permute-done | bytes 294944 | tf_op jit(solution)/shard_map/cond/branch_0_fun/ppermute | solution.py:28
  156.5 1.9 %collective-permute-start.7 = (bf16[64,2304]{1,0:T(8,128)(2,1)S(1)}, bf16[64,2304]{1,0:T(8,128)(2,1)S(1)}, u32[]{:S(2)}, u32[]{:S(2)}) collective-permute-start(bf16[64,2304]{1,0:T(8,128)(2,1)S(1)} %add_convert_fusion.7), channel_id=1, source_target_pairs={{0,1},{1,2},{2,3},{3,4},{4,5},{5,6},{6,7},{7,8},{8,9},{9,10},{10,1... | collective-permute-start | bytes 884744 | tf_op jit(solution)/shard_map/cond/branch_0_fun/ppermute | solution.py:28
  158.5 4.6 %collective-permute-start.15 = (bf16[64,2304]{1,0:T(8,128)(2,1)S(1)}, bf16[64,2304]{1,0:T(8,128)(2,1)S(1)}, u32[]{:S(2)}, u32[]{:S(2)}) collective-permute-start(bf16[64,2304]{1,0:T(8,128)(2,1)S(1)} %add_convert_fusion), channel_id=1, source_target_pairs={{0,15},{1,0},{2,1},{3,2},{4,3},{5,4},{6,5},{7,6},{8,7},{9,8},{10,9... | collective-permute-start | bytes 884744 | tf_op jit(solution)/shard_map/cond/branch_0_fun/ppermute | solution.py:28
  163.1 2.1 %collective-permute-done.7 = bf16[64,2304]{1,0:T(8,128)(2,1)S(1)} collective-permute-done((bf16[64,2304]{1,0:T(8,128)(2,1)S(1)}, bf16[64,2304]{1,0:T(8,128)(2,1)S(1)}, u32[]{:S(2)}, u32[]{:S(2)}) %collective-permute-start.7) | collective-permute-done | bytes 294944 | tf_op jit(solution)/shard_map/cond/branch_0_fun/ppermute | solution.py:28
  167.9 19.5 %collective-permute-start.36 = (bf16[32,2304]{1,0:T(8,128)(2,1)S(1)}, bf16[32,2304]{1,0:T(8,128)(2,1)S(1)}, u32[]{:S(2)}, u32[]{:S(2)}) collective-permute-start(bf16[32,2304]{1,0:T(8,128)(2,1)S(1)} %get-tuple-element.94), channel_id=1, source_target_pairs={{16,32},{32,16},{48,64},{64,48},{80,96},{96,80},{112,128},{128,112... | collective-permute-start | bytes 442376 | tf_op jit(solution)/shard_map/ppermute | solution.py:36
  187.4 1.9 %collective-permute-start.37 = (bf16[32,2304]{1,0:T(8,128)(2,1)S(1)}, bf16[32,2304]{1,0:T(8,128)(2,1)S(1)}, u32[]{:S(2)}, u32[]{:S(2)}) collective-permute-start(bf16[32,2304]{1,0:T(8,128)(2,1)S(1)} %get-tuple-element.95), channel_id=1, source_target_pairs={{0,16},{16,0},{32,48},{48,32},{64,80},{80,64},{96,112},{112,96},{1... | collective-permute-start | bytes 442376 | tf_op jit(solution)/shard_map/ppermute | solution.py:36
  (69 shorter events, 16.1 us)
Async XLA Ops:
  1.6 18.7 %collective-permute-start.21 = (bf16[64,2304]{1,0:T(8,128)(2,1)S(1)}, bf16[64,2304]{1,0:T(8,128)(2,1)S(1)}, u32[]{:S(2)}, u32[]{:S(2)}) collective-permute-start(bf16[64,2304]{1,0:T(8,128)(2,1)S(1)} %pad_maximum_fusion.refs_0_), channel_id=1, source_target_pairs={{0,1},{1,2},{2,3},{3,4},{4,5},{5,6},{6,7},{7,8},{8,9},{9,10},{10,1... | collective-permute-start | bytes 884744 | tf_op jit(solution)/shard_map/ppermute | solution.py:28
  6.0 16.2 %collective-permute-start.22 = (bf16[64,2304]{1,0:T(8,128)(2,1)S(1)}, bf16[64,2304]{1,0:T(8,128)(2,1)S(1)}, u32[]{:S(2)}, u32[]{:S(2)}) collective-permute-start(bf16[64,2304]{1,0:T(8,128)(2,1)S(1)} %pad_maximum_fusion.refs_0_), channel_id=1, source_target_pairs={{0,15},{1,0},{2,1},{3,2},{4,3},{5,4},{6,5},{7,6},{8,7},{9,8},{10,9... | collective-permute-start | bytes 884744 | tf_op jit(solution)/shard_map/ppermute | solution.py:28
  20.3 10.4 %collective-permute-start.23 = (bf16[64,2304]{1,0:T(8,128)(2,1)S(1)}, bf16[64,2304]{1,0:T(8,128)(2,1)S(1)}, u32[]{:S(2)}, u32[]{:S(2)}) collective-permute-start(bf16[64,2304]{1,0:T(8,128)(2,1)S(1)} %collective-permute-done.21.refs_1_), channel_id=1, source_target_pairs={{0,1},{1,2},{2,3},{3,4},{4,5},{5,6},{6,7},{7,8},{8,9},{9,10},{10,1... | collective-permute-start | bytes 884744 | tf_op jit(solution)/shard_map/ppermute | solution.py:28
  22.2 10.4 %collective-permute-start.24 = (bf16[64,2304]{1,0:T(8,128)(2,1)S(1)}, bf16[64,2304]{1,0:T(8,128)(2,1)S(1)}, u32[]{:S(2)}, u32[]{:S(2)}) collective-permute-start(bf16[64,2304]{1,0:T(8,128)(2,1)S(1)} %collective-permute-done.22.refs_2_), channel_id=1, source_target_pairs={{0,15},{1,0},{2,1},{3,2},{4,3},{5,4},{6,5},{7,6},{8,7},{9,8},{10,9... | collective-permute-start | bytes 884744 | tf_op jit(solution)/shard_map/ppermute | solution.py:28
  30.7 9.4 %collective-permute-start.25 = (bf16[64,2304]{1,0:T(8,128)(2,1)S(1)}, bf16[64,2304]{1,0:T(8,128)(2,1)S(1)}, u32[]{:S(2)}, u32[]{:S(2)}) collective-permute-start(bf16[64,2304]{1,0:T(8,128)(2,1)S(1)} %collective-permute-done.23.refs_3_), channel_id=1, source_target_pairs={{0,1},{1,2},{2,3},{3,4},{4,5},{5,6},{6,7},{7,8},{8,9},{9,10},{10,1... | collective-permute-start | bytes 884744 | tf_op jit(solution)/shard_map/ppermute | solution.py:28
  32.6 9.4 %collective-permute-start.26 = (bf16[64,2304]{1,0:T(8,128)(2,1)S(1)}, bf16[64,2304]{1,0:T(8,128)(2,1)S(1)}, u32[]{:S(2)}, u32[]{:S(2)}) collective-permute-start(bf16[64,2304]{1,0:T(8,128)(2,1)S(1)} %collective-permute-done.24.refs_4_), channel_id=1, source_target_pairs={{0,15},{1,0},{2,1},{3,2},{4,3},{5,4},{6,5},{7,6},{8,7},{9,8},{10,9... | collective-permute-start | bytes 884744 | tf_op jit(solution)/shard_map/ppermute | solution.py:28
  40.1 8.7 %collective-permute-start.27 = (bf16[64,2304]{1,0:T(8,128)(2,1)S(1)}, bf16[64,2304]{1,0:T(8,128)(2,1)S(1)}, u32[]{:S(2)}, u32[]{:S(2)}) collective-permute-start(bf16[64,2304]{1,0:T(8,128)(2,1)S(1)} %collective-permute-done.25.refs_5_), channel_id=1, source_target_pairs={{0,1},{1,2},{2,3},{3,4},{4,5},{5,6},{6,7},{7,8},{8,9},{9,10},{10,1... | collective-permute-start | bytes 884744 | tf_op jit(solution)/shard_map/ppermute | solution.py:28
  42.1 8.7 %collective-permute-start.28 = (bf16[64,2304]{1,0:T(8,128)(2,1)S(1)}, bf16[64,2304]{1,0:T(8,128)(2,1)S(1)}, u32[]{:S(2)}, u32[]{:S(2)}) collective-permute-start(bf16[64,2304]{1,0:T(8,128)(2,1)S(1)} %collective-permute-done.26.refs_6_), channel_id=1, source_target_pairs={{0,15},{1,0},{2,1},{3,2},{4,3},{5,4},{6,5},{7,6},{8,7},{9,8},{10,9... | collective-permute-start | bytes 884744 | tf_op jit(solution)/shard_map/ppermute | solution.py:28
  48.8 8.7 %collective-permute-start.29 = (bf16[64,2304]{1,0:T(8,128)(2,1)S(1)}, bf16[64,2304]{1,0:T(8,128)(2,1)S(1)}, u32[]{:S(2)}, u32[]{:S(2)}) collective-permute-start(bf16[64,2304]{1,0:T(8,128)(2,1)S(1)} %collective-permute-done.27.refs_7_), channel_id=1, source_target_pairs={{0,1},{1,2},{2,3},{3,4},{4,5},{5,6},{6,7},{7,8},{8,9},{9,10},{10,1... | collective-permute-start | bytes 884744 | tf_op jit(solution)/shard_map/ppermute | solution.py:28
  50.7 8.7 %collective-permute-start.30 = (bf16[64,2304]{1,0:T(8,128)(2,1)S(1)}, bf16[64,2304]{1,0:T(8,128)(2,1)S(1)}, u32[]{:S(2)}, u32[]{:S(2)}) collective-permute-start(bf16[64,2304]{1,0:T(8,128)(2,1)S(1)} %collective-permute-done.28.refs_8_), channel_id=1, source_target_pairs={{0,15},{1,0},{2,1},{3,2},{4,3},{5,4},{6,5},{7,6},{8,7},{9,8},{10,9... | collective-permute-start | bytes 884744 | tf_op jit(solution)/shard_map/ppermute | solution.py:28
  57.5 8.7 %collective-permute-start.31 = (bf16[64,2304]{1,0:T(8,128)(2,1)S(1)}, bf16[64,2304]{1,0:T(8,128)(2,1)S(1)}, u32[]{:S(2)}, u32[]{:S(2)}) collective-permute-start(bf16[64,2304]{1,0:T(8,128)(2,1)S(1)} %collective-permute-done.29.refs_9_), channel_id=1, source_target_pairs={{0,1},{1,2},{2,3},{3,4},{4,5},{5,6},{6,7},{7,8},{8,9},{9,10},{10,1... | collective-permute-start | bytes 884744 | tf_op jit(solution)/shard_map/ppermute | solution.py:28
  59.4 9.4 %collective-permute-start.32 = (bf16[64,2304]{1,0:T(8,128)(2,1)S(1)}, bf16[64,2304]{1,0:T(8,128)(2,1)}, u32[]{:S(2)}, u32[]{:S(2)}) collective-permute-start(bf16[64,2304]{1,0:T(8,128)(2,1)S(1)} %collective-permute-done.30.refs_10_), channel_id=1, source_target_pairs={{0,15},{1,0},{2,1},{3,2},{4,3},{5,4},{6,5},{7,6},{8,7},{9,8},{10,9... | collective-permute-start | bytes 884744 | tf_op jit(solution)/shard_map/ppermute | solution.py:28
  66.1 9.1 %collective-permute-start.33 = (bf16[64,2304]{1,0:T(8,128)(2,1)S(1)}, bf16[64,2304]{1,0:T(8,128)(2,1)}, u32[]{:S(2)}, u32[]{:S(2)}) collective-permute-start(bf16[64,2304]{1,0:T(8,128)(2,1)S(1)} %collective-permute-done.31.refs_11_), channel_id=1, source_target_pairs={{0,1},{1,2},{2,3},{3,4},{4,5},{5,6},{6,7},{7,8},{8,9},{9,10},{10,1... | collective-permute-start | bytes 884744 | tf_op jit(solution)/shard_map/ppermute | solution.py:28
  68.8 8.5 %collective-permute-start.34 = (bf16[64,2304]{1,0:T(8,128)(2,1)}, bf16[64,2304]{1,0:T(8,128)(2,1)}, u32[]{:S(2)}, u32[]{:S(2)}) collective-permute-start(bf16[64,2304]{1,0:T(8,128)(2,1)} %collective-permute-done.32.refs_12_), channel_id=1, source_target_pairs={{0,15},{1,0},{2,1},{3,2},{4,3},{5,4},{6,5},{7,6},{8,7},{9,8},{10,9... | collective-permute-start | bytes 884744 | tf_op jit(solution)/shard_map/ppermute | solution.py:28
  75.2 10.1 %collective-permute-start.35 = (bf16[64,2304]{1,0:T(8,128)(2,1)}, bf16[64,2304]{1,0:T(8,128)(2,1)}, u32[]{:S(2)}, u32[]{:S(2)}) collective-permute-start(bf16[64,2304]{1,0:T(8,128)(2,1)} %collective-permute-done.33.refs_13_), channel_id=1, source_target_pairs={{0,1},{1,2},{2,3},{3,4},{4,5},{5,6},{6,7},{7,8},{8,9},{9,10},{10,1... | collective-permute-start | bytes 884744 | tf_op jit(solution)/shard_map/ppermute | solution.py:28
  77.2 8.1 %copy-start.10 = (s32[3]{0:T(128)}, s32[3]{0:T(128)S(1)}, u32[]{:S(2)}) copy-start(s32[3]{0:T(128)S(1)} %pad_add_fusion.me_ref) | copy-start | bytes 40
  77.3 8.0 %copy-start.1 = (bf16[1,2304,256]{2,1,0:T(8,128)(2,1)S(1)}, bf16[1,2304,256]{2,1,0:T(8,128)(2,1)}, u32[]{:S(2)}) copy-start(bf16[1,2304,256]{2,1,0:T(8,128)(2,1)} %param.16) | copy-start | bytes 3538948
  77.3 8.0 %copy-start.2 = (bf16[1,256,2304]{2,1,0:T(8,128)(2,1)S(1)}, bf16[1,256,2304]{2,1,0:T(8,128)(2,1)}, u32[]{:S(2)}) copy-start(bf16[1,256,2304]{2,1,0:T(8,128)(2,1)} %param.19) | copy-start | bytes 3538948
  77.3 8.0 %copy-start.3 = (bf16[1,2304,128]{2,1,0:T(8,128)(2,1)S(1)}, bf16[1,2304,128]{2,1,0:T(8,128)(2,1)}, u32[]{:S(2)}) copy-start(bf16[1,2304,128]{2,1,0:T(8,128)(2,1)} %param.17) | copy-start | bytes 1769476
  77.3 8.0 %copy-start.4 = (bf16[1,2304,128]{2,1,0:T(8,128)(2,1)S(1)}, bf16[1,2304,128]{2,1,0:T(8,128)(2,1)}, u32[]{:S(2)}) copy-start(bf16[1,2304,128]{2,1,0:T(8,128)(2,1)} %param.18) | copy-start | bytes 1769476
  77.3 8.0 %copy-start.5 = (bf16[1,1,32,2304]{3,2,1,0:T(8,128)(2,1)S(1)}, bf16[1,1,32,2304]{3,2,1,0:T(8,128)(2,1)}, u32[]{:S(2)}) copy-start(bf16[1,1,32,2304]{3,2,1,0:T(8,128)(2,1)} %param.13) | copy-start | bytes 442372
  77.3 8.0 %copy-start.9 = (bf16[1,2304]{1,0:T(2,128)(2,1)S(1)}, bf16[1,2304]{1,0:T(2,128)(2,1)}, u32[]{:S(2)}) copy-start(bf16[1,2304]{1,0:T(2,128)(2,1)} %gain_ref.3) | copy-start | bytes 13828
  77.3 8.0 %copy-start.11 = (bf16[2304]{0:T(1024)(128)(2,1)S(1)}, bf16[2304]{0:T(1024)(128)(2,1)}, u32[]{:S(2)}) copy-start(bf16[2304]{0:T(1024)(128)(2,1)} %param.20) | copy-start | bytes 13828
  77.4 8.0 %copy-start.12 = (bf16[2304]{0:T(1024)(128)(2,1)S(1)}, bf16[2304]{0:T(1024)(128)(2,1)}, u32[]{:S(2)}) copy-start(bf16[2304]{0:T(1024)(128)(2,1)} %param.21) | copy-start | bytes 13828
  77.4 8.0 %copy-start.13 = (s32[1,8]{1,0:T(1,128)S(1)}, s32[1,8]{1,0:T(1,128)}, u32[]{:S(2)}) copy-start(s32[1,8]{1,0:T(1,128)} %param.22) | copy-start | bytes 100
  85.4 81.5 %copy-start = (bf16[1,1,32,2304]{3,2,1,0:T(8,128)(2,1)S(1)}, bf16[1,1,32,2304]{3,2,1,0:T(8,128)(2,1)}, u32[]{:S(2)}) copy-start(bf16[1,1,32,2304]{3,2,1,0:T(8,128)(2,1)} %param.14) | copy-start | bytes 442372
  85.4 81.5 %copy-start.6 = (bf16[1,1,32,2304]{3,2,1,0:T(8,128)(2,1)S(1)}, bf16[1,1,32,2304]{3,2,1,0:T(8,128)(2,1)}, u32[]{:S(2)}) copy-start(bf16[1,1,32,2304]{3,2,1,0:T(8,128)(2,1)} %param.13) | copy-start | bytes 442372
  89.4 7.6 %collective-permute-start = (bf16[32,2304]{1,0:T(8,128)(2,1)S(1)}, bf16[32,2304]{1,0:T(8,128)(2,1)S(1)}, u32[]{:S(2)}, u32[]{:S(2)}) collective-permute-start(bf16[32,2304]{1,0:T(8,128)(2,1)S(1)} %get-tuple-element.50), channel_id=1, source_target_pairs={{0,1},{1,2},{2,3},{3,4},{4,5},{5,6},{6,7},{7,8},{8,9},{9,10},{10,1... | collective-permute-start | bytes 442376 | tf_op jit(solution)/shard_map/cond/branch_0_fun/ppermute | solution.py:28
  91.4 7.6 %collective-permute-start.8 = (bf16[32,2304]{1,0:T(8,128)(2,1)S(1)}, bf16[32,2304]{1,0:T(8,128)(2,1)S(1)}, u32[]{:S(2)}, u32[]{:S(2)}) collective-permute-start(bf16[32,2304]{1,0:T(8,128)(2,1)S(1)} %get-tuple-element.63), channel_id=1, source_target_pairs={{0,15},{1,0},{2,1},{3,2},{4,3},{5,4},{6,5},{7,6},{8,7},{9,8},{10,9... | collective-permute-start | bytes 442376 | tf_op jit(solution)/shard_map/cond/branch_0_fun/ppermute | solution.py:28
  97.0 10.5 %collective-permute-start.1 = (bf16[64,2304]{1,0:T(8,128)(2,1)S(1)}, bf16[64,2304]{1,0:T(8,128)(2,1)S(1)}, u32[]{:S(2)}, u32[]{:S(2)}) collective-permute-start(bf16[64,2304]{1,0:T(8,128)(2,1)S(1)} %add_convert_fusion.13), channel_id=1, source_target_pairs={{0,1},{1,2},{2,3},{3,4},{4,5},{5,6},{6,7},{7,8},{8,9},{9,10},{10,1... | collective-permute-start | bytes 884744 | tf_op jit(solution)/shard_map/cond/branch_0_fun/ppermute | solution.py:28
  99.0 10.5 %collective-permute-start.9 = (bf16[64,2304]{1,0:T(8,128)(2,1)S(1)}, bf16[64,2304]{1,0:T(8,128)(2,1)S(1)}, u32[]{:S(2)}, u32[]{:S(2)}) collective-permute-start(bf16[64,2304]{1,0:T(8,128)(2,1)S(1)} %add_convert_fusion.6), channel_id=1, source_target_pairs={{0,15},{1,0},{2,1},{3,2},{4,3},{5,4},{6,5},{7,6},{8,7},{9,8},{10,9... | collective-permute-start | bytes 884744 | tf_op jit(solution)/shard_map/cond/branch_0_fun/ppermute | solution.py:28
  107.6 11.3 %collective-permute-start.2 = (bf16[64,2304]{1,0:T(8,128)(2,1)S(1)}, bf16[64,2304]{1,0:T(8,128)(2,1)S(1)}, u32[]{:S(2)}, u32[]{:S(2)}) collective-permute-start(bf16[64,2304]{1,0:T(8,128)(2,1)S(1)} %add_convert_fusion.12), channel_id=1, source_target_pairs={{0,1},{1,2},{2,3},{3,4},{4,5},{5,6},{6,7},{7,8},{8,9},{9,10},{10,1... | collective-permute-start | bytes 884744 | tf_op jit(solution)/shard_map/cond/branch_0_fun/ppermute | solution.py:28
  109.7 11.3 %collective-permute-start.10 = (bf16[64,2304]{1,0:T(8,128)(2,1)S(1)}, bf16[64,2304]{1,0:T(8,128)(2,1)S(1)}, u32[]{:S(2)}, u32[]{:S(2)}) collective-permute-start(bf16[64,2304]{1,0:T(8,128)(2,1)S(1)} %add_convert_fusion.5), channel_id=1, source_target_pairs={{0,15},{1,0},{2,1},{3,2},{4,3},{5,4},{6,5},{7,6},{8,7},{9,8},{10,9... | collective-permute-start | bytes 884744 | tf_op jit(solution)/shard_map/cond/branch_0_fun/ppermute | solution.py:28
  119.0 10.4 %collective-permute-start.3 = (bf16[64,2304]{1,0:T(8,128)(2,1)S(1)}, bf16[64,2304]{1,0:T(8,128)(2,1)S(1)}, u32[]{:S(2)}, u32[]{:S(2)}) collective-permute-start(bf16[64,2304]{1,0:T(8,128)(2,1)S(1)} %add_convert_fusion.11), channel_id=1, source_target_pairs={{0,1},{1,2},{2,3},{3,4},{4,5},{5,6},{6,7},{7,8},{8,9},{9,10},{10,1... | collective-permute-start | bytes 884744 | tf_op jit(solution)/shard_map/cond/branch_0_fun/ppermute | solution.py:28
  121.0 10.4 %collective-permute-start.11 = (bf16[64,2304]{1,0:T(8,128)(2,1)S(1)}, bf16[64,2304]{1,0:T(8,128)(2,1)S(1)}, u32[]{:S(2)}, u32[]{:S(2)}) collective-permute-start(bf16[64,2304]{1,0:T(8,128)(2,1)S(1)} %add_convert_fusion.4), channel_id=1, source_target_pairs={{0,15},{1,0},{2,1},{3,2},{4,3},{5,4},{6,5},{7,6},{8,7},{9,8},{10,9... | collective-permute-start | bytes 884744 | tf_op jit(solution)/shard_map/cond/branch_0_fun/ppermute | solution.py:28
  129.5 9.5 %collective-permute-start.4 = (bf16[64,2304]{1,0:T(8,128)(2,1)S(1)}, bf16[64,2304]{1,0:T(8,128)(2,1)S(1)}, u32[]{:S(2)}, u32[]{:S(2)}) collective-permute-start(bf16[64,2304]{1,0:T(8,128)(2,1)S(1)} %add_convert_fusion.10), channel_id=1, source_target_pairs={{0,1},{1,2},{2,3},{3,4},{4,5},{5,6},{6,7},{7,8},{8,9},{9,10},{10,1... | collective-permute-start | bytes 884744 | tf_op jit(solution)/shard_map/cond/branch_0_fun/ppermute | solution.py:28
  131.5 9.4 %collective-permute-start.12 = (bf16[64,2304]{1,0:T(8,128)(2,1)S(1)}, bf16[64,2304]{1,0:T(8,128)(2,1)S(1)}, u32[]{:S(2)}, u32[]{:S(2)}) collective-permute-start(bf16[64,2304]{1,0:T(8,128)(2,1)S(1)} %add_convert_fusion.3), channel_id=1, source_target_pairs={{0,15},{1,0},{2,1},{3,2},{4,3},{5,4},{6,5},{7,6},{8,7},{9,8},{10,9... | collective-permute-start | bytes 884744 | tf_op jit(solution)/shard_map/cond/branch_0_fun/ppermute | solution.py:28
  139.0 8.7 %collective-permute-start.5 = (bf16[64,2304]{1,0:T(8,128)(2,1)S(1)}, bf16[64,2304]{1,0:T(8,128)(2,1)S(1)}, u32[]{:S(2)}, u32[]{:S(2)}) collective-permute-start(bf16[64,2304]{1,0:T(8,128)(2,1)S(1)} %add_convert_fusion.9), channel_id=1, source_target_pairs={{0,1},{1,2},{2,3},{3,4},{4,5},{5,6},{6,7},{7,8},{8,9},{9,10},{10,1... | collective-permute-start | bytes 884744 | tf_op jit(solution)/shard_map/cond/branch_0_fun/ppermute | solution.py:28
  141.0 8.7 %collective-permute-start.13 = (bf16[64,2304]{1,0:T(8,128)(2,1)S(1)}, bf16[64,2304]{1,0:T(8,128)(2,1)S(1)}, u32[]{:S(2)}, u32[]{:S(2)}) collective-permute-start(bf16[64,2304]{1,0:T(8,128)(2,1)S(1)} %add_convert_fusion.2), channel_id=1, source_target_pairs={{0,15},{1,0},{2,1},{3,2},{4,3},{5,4},{6,5},{7,6},{8,7},{9,8},{10,9... | collective-permute-start | bytes 884744 | tf_op jit(solution)/shard_map/cond/branch_0_fun/ppermute | solution.py:28
  147.8 8.7 %collective-permute-start.6 = (bf16[64,2304]{1,0:T(8,128)(2,1)S(1)}, bf16[64,2304]{1,0:T(8,128)(2,1)S(1)}, u32[]{:S(2)}, u32[]{:S(2)}) collective-permute-start(bf16[64,2304]{1,0:T(8,128)(2,1)S(1)} %add_convert_fusion.8), channel_id=1, source_target_pairs={{0,1},{1,2},{2,3},{3,4},{4,5},{5,6},{6,7},{7,8},{8,9},{9,10},{10,1... | collective-permute-start | bytes 884744 | tf_op jit(solution)/shard_map/cond/branch_0_fun/ppermute | solution.py:28
  149.8 8.7 %collective-permute-start.14 = (bf16[64,2304]{1,0:T(8,128)(2,1)S(1)}, bf16[64,2304]{1,0:T(8,128)(2,1)S(1)}, u32[]{:S(2)}, u32[]{:S(2)}) collective-permute-start(bf16[64,2304]{1,0:T(8,128)(2,1)S(1)} %add_convert_fusion.1), channel_id=1, source_target_pairs={{0,15},{1,0},{2,1},{3,2},{4,3},{5,4},{6,5},{7,6},{8,7},{9,8},{10,9... | collective-permute-start | bytes 884744 | tf_op jit(solution)/shard_map/cond/branch_0_fun/ppermute | solution.py:28
  156.5 8.7 %collective-permute-start.7 = (bf16[64,2304]{1,0:T(8,128)(2,1)S(1)}, bf16[64,2304]{1,0:T(8,128)(2,1)S(1)}, u32[]{:S(2)}, u32[]{:S(2)}) collective-permute-start(bf16[64,2304]{1,0:T(8,128)(2,1)S(1)} %add_convert_fusion.7), channel_id=1, source_target_pairs={{0,1},{1,2},{2,3},{3,4},{4,5},{5,6},{6,7},{7,8},{8,9},{9,10},{10,1... | collective-permute-start | bytes 884744 | tf_op jit(solution)/shard_map/cond/branch_0_fun/ppermute | solution.py:28
  158.5 8.2 %collective-permute-start.15 = (bf16[64,2304]{1,0:T(8,128)(2,1)S(1)}, bf16[64,2304]{1,0:T(8,128)(2,1)S(1)}, u32[]{:S(2)}, u32[]{:S(2)}) collective-permute-start(bf16[64,2304]{1,0:T(8,128)(2,1)S(1)} %add_convert_fusion), channel_id=1, source_target_pairs={{0,15},{1,0},{2,1},{3,2},{4,3},{5,4},{6,5},{7,6},{8,7},{9,8},{10,9... | collective-permute-start | bytes 884744 | tf_op jit(solution)/shard_map/cond/branch_0_fun/ppermute | solution.py:28
  167.9 22.3 %collective-permute-start.36 = (bf16[32,2304]{1,0:T(8,128)(2,1)S(1)}, bf16[32,2304]{1,0:T(8,128)(2,1)S(1)}, u32[]{:S(2)}, u32[]{:S(2)}) collective-permute-start(bf16[32,2304]{1,0:T(8,128)(2,1)S(1)} %get-tuple-element.94), channel_id=1, source_target_pairs={{16,32},{32,16},{48,64},{64,48},{80,96},{96,80},{112,128},{128,112... | collective-permute-start | bytes 442376 | tf_op jit(solution)/shard_map/ppermute | solution.py:36
  187.4 3.3 %collective-permute-start.37 = (bf16[32,2304]{1,0:T(8,128)(2,1)S(1)}, bf16[32,2304]{1,0:T(8,128)(2,1)S(1)}, u32[]{:S(2)}, u32[]{:S(2)}) collective-permute-start(bf16[32,2304]{1,0:T(8,128)(2,1)S(1)} %get-tuple-element.95), channel_id=1, source_target_pairs={{0,16},{16,0},{32,48},{48,32},{64,80},{80,64},{96,112},{112,96},{1... | collective-permute-start | bytes 442376 | tf_op jit(solution)/shard_map/ppermute | solution.py:36
